TPU v7x, 32 devices: a whole 2x2x4 slice. The times are simulated.
32 devices in a mesh: samp: 4 (over y, x), snp: 8 (over z, core).
Axes of the slice: x: 2, y: 2, z: 4, core: 2. Of those that a mesh axis runs over, the one named last changes fastest.
Arguments:
- dosage: bfloat16 [8192, 4096], P('samp', 'snp'), may hold values from 0 to 2
- band_width: int32 [8], P('snp'), may hold values from 1 to 3, as said below
- marginal: float32 [4096, 64], P('snp'), may hold values from -6 to 6
- penalty: float32 [64], replicated, may hold values from 4 to 16
Outputs:
- effects: float32 [4096, 64], P('snp')
- residual: float32 [4096, 64], P('snp')
Inputs may be any that keep to these rules, and one draw needn't show every extreme that they name: `band_width`: every draw has a block with 3 neighbours and one with a single neighbour.
All inputs are finite; a program needn't handle non-finite values.
Results may differ from a plain program's by a relative error of at most 0.00087.
Values may be sent and summed in bfloat16 or wider, within the bound.
No kernel may reach another device: no remote copies, remote signals or barrier semaphores. Data moves between devices by JAX's collectives and lax.ppermute only.
A program may use at most 64 MiB of HBM per device.

v0:
```python
import jax
import jax.numpy as jnp
from jax import lax
from jax.sharding import PartitionSpec as P

WMAX = 3
TRAITS = 64
ITERS = 2


def from_behind(block, axis, distance):
    devices = range(lax.axis_size(axis))
    route = [(i - distance, i) for i in devices if i - distance in devices]
    return lax.ppermute(block, axis, route)


def gram_pair(scaled, other):
    return lax.dot_general(
        scaled, other, (((0,), (0,)), ((), ())), preferred_element_type=jnp.float32
    )


def exact_dot(left_mat, right_mat):
    return jnp.dot(left_mat, right_mat, precision=lax.Precision.HIGHEST)


def exact_tdot(left_mat, right_mat):
    return lax.dot_general(
        left_mat, right_mat, (((0,), (0,)), ((), ())), precision=lax.Precision.HIGHEST
    )


def residual_sum(vector):
    return lax.psum(jnp.sum(vector * vector, 0), "snp")


def search_sum(direction, imaged):
    return lax.psum(jnp.sum(direction * imaged, 0), "snp")


def shards(dosage, band_width, marginal, penalty):
    block_size = dosage.shape[1]
    samples = dosage.shape[0] * lax.axis_size("samp")
    genotype = dosage.astype(jnp.float32)
    col_sum, col_sq = lax.psum((jnp.sum(genotype, 0), jnp.sum(genotype * genotype, 0)), "samp")
    center = col_sum / samples
    spread = col_sq / samples - center * center
    scaled = ((genotype - center) * lax.rsqrt(spread + 1e-05)).astype(jnp.bfloat16)
    own_width = band_width[0]
    pieces = [gram_pair(scaled, scaled)]
    for offset in range(1, WMAX + 1):
        ahead_cols = from_behind(scaled, "snp", -offset)
        gram_piece = jnp.where(offset <= own_width, gram_pair(scaled, ahead_cols), 0.0)
        pieces.append(gram_piece)
    partial_band = jnp.concatenate(pieces, 1)
    ld_band = lax.psum(partial_band, "samp") / samples
    share_count = TRAITS // lax.axis_size("samp")
    first_trait = lax.axis_index("samp") * share_count
    target = lax.dynamic_slice_in_dim(marginal, first_trait, share_count, 1)
    shrink = lax.dynamic_slice_in_dim(penalty, first_trait, share_count, 0)
    effects = jnp.zeros_like(target)
    residual = target
    direction = target
    norm_now = residual_sum(residual)
    for sweep in range(ITERS):
        result = exact_dot(ld_band[:, :block_size], direction)
        for operate_offset in range(1, WMAX + 1):
            ld_block = ld_band[:, operate_offset * block_size : (operate_offset + 1) * block_size]
            ahead_dir = from_behind(direction, "snp", -operate_offset)
            result = result + exact_dot(ld_block, ahead_dir)
            result = result + from_behind(exact_tdot(ld_block, direction), "snp", operate_offset)
        imaged = result + shrink * direction
        step_size = norm_now / search_sum(direction, imaged)
        effects = effects + step_size * direction
        residual = residual - step_size * imaged
        norm_next = residual_sum(residual)
        direction = residual + norm_next / norm_now * direction
        norm_now = norm_next
    effects, residual = (
        lax.all_gather(effects, "samp", axis=1, tiled=True),
        lax.all_gather(residual, "samp", axis=1, tiled=True),
    )
    return (effects, residual)


def solution(mesh):
    in_specs = (P("samp", "snp"), P("snp"), P("snp", None), P())
    out_specs = (P("snp", None), P("snp", None))
    return jax.shard_map(shards, mesh=mesh, in_specs=in_specs, out_specs=out_specs, check_vma=False)
```

profile of v0, /device:TPU:0, one launch (start us, length us, event | category | flops | bytes accessed | tf_op | source)
XLA Modules:
  0.0 379.8 jit_solution(2802639933544557806)
XLA Ops:
  7.2 0.0 all-reduce.4.cloned.1.call-start
  7.2 2.2 convert_reduce_fusion
  9.4 11.4 %all-reduce.1 = (f32[512]{0:T(512)S(1)}, f32[512]{0:T(512)S(1)}) all-reduce(f32[512]{0:T(512)S(1)} %get-tuple-element.3, f32[512]{0:T(512)S(1)} %get-tuple-element.2), channel_id=1, replica_groups=mesh['samp'=4,'snp'=8] {'samp'}, use_global_device_ids=true, to_apply=%region_5.6 | all-reduce | flops 1024 | bytes 8192 | tf_op jit(solution)/shard_map/psum | solution.py:45
  20.8 2.1 fusion.1
  22.9 1.3 collective-permute-start.1
  24.2 1.3 collective-permute-start
  25.5 1.3 collective-permute-start.2
  27.4 1.3 fusion.41
  28.7 44.6 %collective-permute-done.1 = bf16[2048,512]{1,0:T(8,128)(2,1)S(1)} collective-permute-done((bf16[2048,512]{1,0:T(8,128)(2,1)S(1)}, bf16[2048,512]{1,0:T(8,128)(2,1)S(1)}, u32[]{:S(2)}, u32[]{:S(2)}) %collective-permute-start.1) | collective-permute-done | bytes 2097184 | tf_op jit(solution)/shard_map/ppermute | solution.py:14
  73.3 1.3 convolution_select_fusion.1
  74.7 0.0 collective-permute-done
  74.7 1.3 convolution_select_fusion.2
  76.0 35.9 %collective-permute-done.2 = bf16[2048,512]{1,0:T(8,128)(2,1)S(1)} collective-permute-done((bf16[2048,512]{1,0:T(8,128)(2,1)S(1)}, bf16[2048,512]{1,0:T(8,128)(2,1)S(1)}, u32[]{:S(2)}, u32[]{:S(2)}) %collective-permute-start.2) | collective-permute-done | bytes 2097184 | tf_op jit(solution)/shard_map/ppermute | solution.py:14
  111.9 1.3 convolution_select_fusion
  113.2 2.4 pad_maximum_fusion
  115.6 0.0 all-reduce.4.cloned.1.call-update
  115.6 0.9 copy-done.2
  116.5 1.3 collective-permute-start.7
  117.8 1.3 collective-permute-start.5
  119.1 1.3 collective-permute-start.3
  120.4 0.1 dynamic_slice.7
  120.5 145.4 %all-reduce.4.cloned.1.call-done = f32[512,2048]{0,1:T(8,128)} async-done(((f32[512,2048]{0,1:T(8,128)}), f32[512,2048]{0,1:T(8,128)}) %all-reduce.4.cloned.1.call-update) | async-done | bytes 4194320 | tf_op jit(solution)/shard_map/psum | solution.py:56
  265.8 2.7 broadcast_multiply_fusion
  268.5 1.0 fusion.38
  269.5 1.0 fusion.31
  270.5 1.0 fusion.23
  271.5 0.7 fusion.17
  272.2 1.7 collective-permute-start.4
  273.9 3.6 collective-permute-start.6
  277.5 0.0 collective-permute-done.7
  277.5 4.5 %collective-permute-start.8 = (f32[512,16]{0,1:T(8,128)S(1)}, f32[512,16]{0,1:T(8,128)S(1)}, u32[]{:S(2)}, u32[]{:S(2)}) collective-permute-start(f32[512,16]{0,1:T(8,128)S(1)} %fusion.23), channel_id=1, source_target_pairs={{0,3},{1,4},{2,5},{3,6},{4,7},{8,11},{9,12},{10,13},{11,14},{12,15... | collective-permute-start | bytes 98312 | tf_op jit(solution)/shard_map/ppermute | solution.py:14
  282.0 0.7 fusion.25
  282.7 0.0 collective-permute-done.5
  282.7 0.7 fusion.33
  283.3 0.0 collective-permute-done.4
  283.3 0.0 collective-permute-done.6
  283.4 0.0 collective-permute-done.8
  283.4 0.8 multiply_reduce_fusion.2
  284.2 14.8 %all-reduce = (f32[16]{0:T(128)S(1)}, f32[16]{0:T(128)S(1)}) all-reduce(f32[16]{0:T(128)S(1)} %get-tuple-element.5, f32[16]{0:T(128)S(1)} %get-tuple-element.4), channel_id=1, replica_groups=mesh['samp'=4,'snp'=8] {'snp'}, use_global_device_ids=true, to_apply=%region_1.0 | all-reduce | flops 32 | bytes 256 | tf_op jit(solution)/shard_map/psum | solution.py:34
  299.0 0.2 multiply_reduce_fusion.1
  299.2 13.6 %psum.54 = f32[16]{0:T(128)S(1)} all-reduce(f32[16]{0:T(128)S(1)} %multiply_reduce_fusion.1), channel_id=1, replica_groups=mesh['samp'=4,'snp'=8] {'snp'}, use_global_device_ids=true, to_apply=%region_10.11 | all-reduce | flops 16 | bytes 128 | tf_op jit(solution)/shard_map/psum | solution.py:34
  312.8 0.1 multiply_add_fusion.1
  312.9 2.0 fusion.15
  314.9 2.2 fusion.35
  317.1 1.3 collective-permute-start.11
  318.4 2.2 fusion.27
  320.6 1.3 collective-permute-start.13
  321.9 2.2 fusion.19
  324.1 1.3 collective-permute-start.9
  325.5 3.0 collective-permute-start.10
  328.5 4.6 %collective-permute-start.12 = (f32[512,16]{0,1:T(8,128)S(1)}, f32[512,16]{0,1:T(8,128)S(1)}, u32[]{:S(2)}, u32[]{:S(2)}) collective-permute-start(f32[512,16]{0,1:T(8,128)S(1)} %fusion.27), channel_id=1, source_target_pairs={{0,2},{1,3},{2,4},{3,5},{4,6},{5,7},{8,10},{9,11},{10,12},{11,13},... | collective-permute-start | bytes 98312 | tf_op jit(solution)/shard_map/ppermute | solution.py:14
  333.0 0.0 collective-permute-done.11
  333.1 5.2 %collective-permute-start.14 = (f32[512,16]{0,1:T(8,128)S(1)}, f32[512,16]{0,1:T(8,128)S(1)}, u32[]{:S(2)}, u32[]{:S(2)}) collective-permute-start(f32[512,16]{0,1:T(8,128)S(1)} %fusion.19), channel_id=1, source_target_pairs={{0,3},{1,4},{2,5},{3,6},{4,7},{8,11},{9,12},{10,13},{11,14},{12,15... | collective-permute-start | bytes 98312 | tf_op jit(solution)/shard_map/ppermute | solution.py:14
  338.3 0.7 fusion.29
  339.0 0.7 fusion.21
  339.6 0.0 collective-permute-done.10
  339.6 0.2 collective-permute-done.14
  339.9 0.8 multiply_reduce_fusion
  340.6 14.8 %psum.55 = f32[16]{0:T(128)S(1)} all-reduce(f32[16]{0:T(128)S(1)} %get-tuple-element.15), channel_id=1, replica_groups=mesh['samp'=4,'snp'=8] {'snp'}, use_global_device_ids=true, to_apply=%region_12.13 | all-reduce | flops 16 | bytes 128 | tf_op jit(solution)/shard_map/psum | solution.py:38
  355.5 0.1 multiply_subtract_fusion
  355.6 8.4 %all_gather.6 = f32[512,64]{0,1:T(8,128)S(1)} all-gather(f32[512,16]{0,1:T(8,128)S(1)} %get-tuple-element.11), channel_id=1, replica_groups=mesh['samp'=4,'snp'=8] {'samp'}, dimensions={1}, use_global_device_ids=true | all-gather | bytes 163840 | tf_op jit(solution)/shard_map/all_gather | solution.py:80
  364.0 7.7 %all_gather.7 = f32[512,64]{0,1:T(8,128)S(1)} all-gather(f32[512,16]{0,1:T(8,128)S(1)} %get-tuple-element.10), channel_id=1, replica_groups=mesh['samp'=4,'snp'=8] {'samp'}, dimensions={1}, use_global_device_ids=true | all-gather | bytes 163840 | tf_op jit(solution)/shard_map/all_gather | solution.py:81
  371.7 0.7 copy.10
  372.3 0.7 copy.11
  (16 shorter events, 0.1 us)
Async XLA Ops:
  7.2 258.6 %all-reduce.4.cloned.1.call-start = ((), (), s32[]{:S(2)}) async-start(), calls=%async_computation | async-start | bytes 8388608 | tf_op jit(solution)/shard_map/psum | solution.py:56
  22.9 50.5 %collective-permute-start.1 = (bf16[2048,512]{1,0:T(8,128)(2,1)S(1)}, bf16[2048,512]{1,0:T(8,128)(2,1)S(1)}, u32[]{:S(2)}, u32[]{:S(2)}) collective-permute-start(bf16[2048,512]{1,0:T(8,128)(2,1)S(1)} %fusion.1), channel_id=1, source_target_pairs={{2,0},{3,1},{4,2},{5,3},{6,4},{7,5},{10,8},{11,9},{12,10},{13,11},... | collective-permute-start | bytes 6291464 | tf_op jit(solution)/shard_map/ppermute | solution.py:14
  24.2 50.5 %collective-permute-start = (bf16[2048,512]{1,0:T(8,128)(2,1)S(1)}, bf16[2048,512]{1,0:T(8,128)(2,1)S(1)}, u32[]{:S(2)}, u32[]{:S(2)}) collective-permute-start(bf16[2048,512]{1,0:T(8,128)(2,1)S(1)} %fusion.1), channel_id=1, source_target_pairs={{1,0},{2,1},{3,2},{4,3},{5,4},{6,5},{7,6},{9,8},{10,9},{11,10},{12... | collective-permute-start | bytes 6291464 | tf_op jit(solution)/shard_map/ppermute | solution.py:14
  25.5 86.4 %collective-permute-start.2 = (bf16[2048,512]{1,0:T(8,128)(2,1)S(1)}, bf16[2048,512]{1,0:T(8,128)(2,1)S(1)}, u32[]{:S(2)}, u32[]{:S(2)}) collective-permute-start(bf16[2048,512]{1,0:T(8,128)(2,1)S(1)} %fusion.1), channel_id=1, source_target_pairs={{3,0},{4,1},{5,2},{6,3},{7,4},{11,8},{12,9},{13,10},{14,11},{15,12... | collective-permute-start | bytes 6291464 | tf_op jit(solution)/shard_map/ppermute | solution.py:14
  115.6 0.9 copy-start.2
  115.6 4.8 %copy-start.3 = (f32[64]{0:T(128)S(1)}, f32[64]{0:T(128)}, u32[]{:S(2)}) copy-start(f32[64]{0:T(128)} %param.7) | copy-start | bytes 772
  116.5 161.0 %collective-permute-start.7 = (f32[512,16]{0,1:T(8,128)S(1)}, f32[512,16]{0,1:T(8,128)S(1)}, u32[]{:S(2)}, u32[]{:S(2)}) collective-permute-start(f32[512,16]{0,1:T(8,128)S(1)} %constant_dynamic-slice_fusion), channel_id=1, source_target_pairs={{3,0},{4,1},{5,2},{6,3},{7,4},{11,8},{12,9},{13,10},{14,11},{15,12... | collective-permute-start | bytes 98312 | tf_op jit(solution)/shard_map/ppermute | solution.py:14
  117.8 164.9 %collective-permute-start.5 = (f32[512,16]{0,1:T(8,128)S(1)}, f32[512,16]{0,1:T(8,128)S(1)}, u32[]{:S(2)}, u32[]{:S(2)}) collective-permute-start(f32[512,16]{0,1:T(8,128)S(1)} %constant_dynamic-slice_fusion), channel_id=1, source_target_pairs={{2,0},{3,1},{4,2},{5,3},{6,4},{7,5},{10,8},{11,9},{12,10},{13,11},... | collective-permute-start | bytes 98312 | tf_op jit(solution)/shard_map/ppermute | solution.py:14
  119.1 164.3 %collective-permute-start.3 = (f32[512,16]{0,1:T(8,128)S(1)}, f32[512,16]{0,1:T(8,128)S(1)}, u32[]{:S(2)}, u32[]{:S(2)}) collective-permute-start(f32[512,16]{0,1:T(8,128)S(1)} %constant_dynamic-slice_fusion), channel_id=1, source_target_pairs={{1,0},{2,1},{3,2},{4,3},{5,4},{6,5},{7,6},{9,8},{10,9},{11,10},{12... | collective-permute-start | bytes 98312 | tf_op jit(solution)/shard_map/ppermute | solution.py:14
  268.5 14.9 %copy-start = (f32[512,2048]{0,1:T(8,128)}, f32[512,2048]{0,1:T(8,128)S(1)}, u32[]{:S(2)}) copy-start(f32[512,2048]{0,1:T(8,128)S(1)} %broadcast_multiply_fusion) | copy-start | bytes 12582916
  272.2 11.2 %collective-permute-start.4 = (f32[512,16]{0,1:T(8,128)S(1)}, f32[512,16]{0,1:T(8,128)S(1)}, u32[]{:S(2)}, u32[]{:S(2)}) collective-permute-start(f32[512,16]{0,1:T(8,128)S(1)} %fusion.38), channel_id=1, source_target_pairs={{0,1},{1,2},{2,3},{3,4},{4,5},{5,6},{6,7},{8,9},{9,10},{10,11},{11... | collective-permute-start | bytes 98312 | tf_op jit(solution)/shard_map/ppermute | solution.py:14
  273.9 9.4 %collective-permute-start.6 = (f32[512,16]{0,1:T(8,128)S(1)}, f32[512,16]{0,1:T(8,128)S(1)}, u32[]{:S(2)}, u32[]{:S(2)}) collective-permute-start(f32[512,16]{0,1:T(8,128)S(1)} %fusion.31), channel_id=1, source_target_pairs={{0,2},{1,3},{2,4},{3,5},{4,6},{5,7},{8,10},{9,11},{10,12},{11,13},... | collective-permute-start | bytes 98312 | tf_op jit(solution)/shard_map/ppermute | solution.py:14
  277.5 5.9 %collective-permute-start.8 = (f32[512,16]{0,1:T(8,128)S(1)}, f32[512,16]{0,1:T(8,128)S(1)}, u32[]{:S(2)}, u32[]{:S(2)}) collective-permute-start(f32[512,16]{0,1:T(8,128)S(1)} %fusion.23), channel_id=1, source_target_pairs={{0,3},{1,4},{2,5},{3,6},{4,7},{8,11},{9,12},{10,13},{11,14},{12,15... | collective-permute-start | bytes 98312 | tf_op jit(solution)/shard_map/ppermute | solution.py:14
  312.8 25.5 %copy-start.1 = (f32[512,2048]{0,1:T(8,128)S(1)}, f32[512,2048]{0,1:T(8,128)}, u32[]{:S(2)}) copy-start(f32[512,2048]{0,1:T(8,128)} %copy-done) | copy-start | bytes 12582916
  317.1 15.9 %collective-permute-start.11 = (f32[512,16]{0,1:T(8,128)S(1)}, f32[512,16]{0,1:T(8,128)S(1)}, u32[]{:S(2)}, u32[]{:S(2)}) collective-permute-start(f32[512,16]{0,1:T(8,128)S(1)} %multiply_add_fusion.1), channel_id=1, source_target_pairs={{2,0},{3,1},{4,2},{5,3},{6,4},{7,5},{10,8},{11,9},{12,10},{13,11},... | collective-permute-start | bytes 98312 | tf_op jit(solution)/shard_map/ppermute | solution.py:14
  320.6 18.3 %collective-permute-start.13 = (f32[512,16]{0,1:T(8,128)S(1)}, f32[512,16]{0,1:T(8,128)S(1)}, u32[]{:S(2)}, u32[]{:S(2)}) collective-permute-start(f32[512,16]{0,1:T(8,128)S(1)} %multiply_add_fusion.1), channel_id=1, source_target_pairs={{3,0},{4,1},{5,2},{6,3},{7,4},{11,8},{12,9},{13,10},{14,11},{15,12... | collective-permute-start | bytes 98312 | tf_op jit(solution)/shard_map/ppermute | solution.py:14
  324.1 15.7 %collective-permute-start.9 = (f32[512,16]{0,1:T(8,128)S(1)}, f32[512,16]{0,1:T(8,128)S(1)}, u32[]{:S(2)}, u32[]{:S(2)}) collective-permute-start(f32[512,16]{0,1:T(8,128)S(1)} %multiply_add_fusion.1), channel_id=1, source_target_pairs={{1,0},{2,1},{3,2},{4,3},{5,4},{6,5},{7,6},{9,8},{10,9},{11,10},{12... | collective-permute-start | bytes 98312 | tf_op jit(solution)/shard_map/ppermute | solution.py:14
  325.5 14.2 %collective-permute-start.10 = (f32[512,16]{0,1:T(8,128)S(1)}, f32[512,16]{0,1:T(8,128)S(1)}, u32[]{:S(2)}, u32[]{:S(2)}) collective-permute-start(f32[512,16]{0,1:T(8,128)S(1)} %fusion.35), channel_id=1, source_target_pairs={{0,1},{1,2},{2,3},{3,4},{4,5},{5,6},{6,7},{8,9},{9,10},{10,11},{11... | collective-permute-start | bytes 98312 | tf_op jit(solution)/shard_map/ppermute | solution.py:14
  328.5 11.1 %collective-permute-start.12 = (f32[512,16]{0,1:T(8,128)S(1)}, f32[512,16]{0,1:T(8,128)S(1)}, u32[]{:S(2)}, u32[]{:S(2)}) collective-permute-start(f32[512,16]{0,1:T(8,128)S(1)} %fusion.27), channel_id=1, source_target_pairs={{0,2},{1,3},{2,4},{3,5},{4,6},{5,7},{8,10},{9,11},{10,12},{11,13},... | collective-permute-start | bytes 98312 | tf_op jit(solution)/shard_map/ppermute | solution.py:14
  333.1 6.8 %collective-permute-start.14 = (f32[512,16]{0,1:T(8,128)S(1)}, f32[512,16]{0,1:T(8,128)S(1)}, u32[]{:S(2)}, u32[]{:S(2)}) collective-permute-start(f32[512,16]{0,1:T(8,128)S(1)} %fusion.19), channel_id=1, source_target_pairs={{0,3},{1,4},{2,5},{3,6},{4,7},{8,11},{9,12},{10,13},{11,14},{12,15... | collective-permute-start | bytes 98312 | tf_op jit(solution)/shard_map/ppermute | solution.py:14
Sparse Core Ops, SparseCore 0:
  115.7 150.0 all-reduce.3
where the time goes:
time: 381 us; the launch traced here: 380 us
  waiting for transfers between devices  226 us (59%)
  blocking collectives  70.7 us (19%)
  starting transfers between devices  34.3 us (9%)
  matrix products  21.6 us (6%)
  between operations  15 us (4%)
  other arithmetic  9.79 us (3%)
    psum x1, waiting for transfers between devices, shards(): ld_band = lax.psum(partial_band, 'samp') / samples  145 us
    ppermute x15, waiting for transfers between devices, from_behind(): return lax.ppermute(block, axis, route)  80.8 us
    ppermute x15, starting transfers between devices, from_behind(): return lax.ppermute(block, axis, route)  34.2 us
    psum x2, blocking collectives, residual_sum(): return lax.psum(jnp.sum(vector * vector, 0), 'snp')  28.4 us
    psum x1, blocking collectives, search_sum(): return lax.psum(jnp.sum(direction * imaged, 0), 'snp')  14.8 us
    psum x1, blocking collectives, shards(): lax.psum((jnp.sum(genotype, 0), jnp.sum(genotype * genotype, 0)), 'samp')  11.4 us
    dot_general x6, matrix products, exact_tdot(): lax.dot_general(left_mat, right_mat, (((0,), (0,)), ((), ())), precision=...  9.6 us
    all_gather x1, blocking collectives, shards(): lax.all_gather(effects, 'samp', axis=1, tiled=True)  8.42 us
  transfers between devices with their start and end apart: 16, of which 4 were waited for; matrix products, arithmetic and copies ran while one was open for 5% of the time, Pallas kernels for 0%

commit v1 on v0

v1 whole, which is shorter than its diff:
```python
import jax
import jax.numpy as jnp
from jax import lax
from jax.sharding import PartitionSpec as P


AUX = 128


def permute(value, axis, pairs):
    return lax.ppermute(value, axis, pairs)


def swap(value, axis, bit):
    return permute(value, axis, [(i, i ^ bit) for i in range(lax.axis_size(axis))])


def shift(value, distance):
    count = lax.axis_size("snp")
    return permute(value, "snp", [(i, i + distance) for i in range(count) if 0 <= i + distance < count])


def far_shift(value):
    count = lax.axis_size("snp")
    up = [(i, i + 3) for i in range(1, count, 2) if i + 3 < count]
    down = [(i, i - 3) for i in range(0, count, 2) if i - 3 >= 0]
    return permute(value, "snp", up + down)


def sum_over(value, axis):
    count = lax.axis_size(axis)
    if count & (count - 1):
        return lax.psum(value, axis)
    bit = 1
    while bit < count:
        value = value + swap(value, axis, bit)
        bit *= 2
    return value


def two_terms(value):
    high = lax.reduce_precision(value, 8, 7)
    low = value - high
    return jnp.concatenate([high.astype(jnp.bfloat16), low.astype(jnp.bfloat16)], 0)


def product(value, scaled, contract):
    rows = value.shape[0]
    both = lax.dot_general(
        two_terms(value), scaled, (((1,), (contract,)), ((), ())), preferred_element_type=jnp.float32
    )
    return both[:rows] + both[rows:]


def pack(value, width):
    peak = jnp.maximum(jnp.max(jnp.abs(value), 1, keepdims=True), 1e-30)
    exponent = jnp.floor(jnp.log2(peak))
    coded = (value * jnp.exp2(-exponent)).astype(jnp.float16)
    lane = lax.broadcasted_iota(jnp.int32, (value.shape[0], AUX), 1)
    extra = jnp.where(lane == 0, exponent, jnp.where(lane == 1, width, 0.0)).astype(jnp.float16)
    return jnp.concatenate([coded, extra], 1)


def unpack(coded):
    count = coded.shape[1] - AUX
    exponent = coded[:, count : count + 1].astype(jnp.float32)
    width = coded[:, count + 1 : count + 2].astype(jnp.float32)
    return coded[:, :count].astype(jnp.float32) * jnp.exp2(exponent), width


def window(own, width, partner_width, odd):
    coded = pack(own, width)
    below = shift(coded, 2)
    above = shift(coded, -2)
    far = far_shift(coded)
    below, below_width = unpack(below)
    above, _ = unpack(above)
    pick = lambda even_case, odd_case: jnp.where(odd, odd_case, even_case)
    give = (
        own * (pick(width, partner_width) >= 1)
        + below * (below_width >= pick(3.0, 1.0))
        + above * (partner_width >= pick(1.0, 3.0))
    )
    given = swap(give, "snp", 1)
    far, far_width = unpack(far)
    return (
        own
        + below * (below_width >= 2)
        + above * (width >= 2)
        + given
        + far * (pick(far_width, width) >= 3)
    )


def shards(dosage, band_width, marginal, penalty):
    samples = dosage.shape[0] * lax.axis_size("samp")
    odd = lax.axis_index("snp") % 2 == 1
    width = band_width.astype(jnp.float32).reshape(1, 1)
    partner_width = swap(jnp.broadcast_to(width, (8, 128)), "snp", 1)[:1, :1]
    genotype = dosage.astype(jnp.float32)
    sums = sum_over(jnp.stack([jnp.sum(genotype, 0), jnp.sum(genotype * genotype, 0)]), "samp")
    center = sums[0] / samples
    spread = sums[1] / samples - center * center
    scaled = ((genotype - center) * lax.rsqrt(spread + 1e-05)).astype(jnp.bfloat16)
    start = marginal.T
    shrink = penalty[:, None]

    def operate(value):
        mixed = window(product(value, scaled, 1), width, partner_width, odd)
        return sum_over(product(mixed, scaled, 0), "samp") / samples

    first = operate(start)
    second = operate(first)
    dot = lambda a, b: jnp.sum(a * b, 1, keepdims=True)
    parts = jnp.concatenate([dot(start, start), dot(start, first), dot(first, first), dot(first, second)], 1)
    parts = sum_over(parts, "snp")
    bb, bw, ww, wu = (parts[:, k : k + 1] for k in range(4))
    ratio = bw / bb
    step = 1.0 / (ratio + shrink)
    norm = step * step * (ww - ratio * bw)
    bend = norm / bb
    curve = step * step * (ratio * (ratio * bw - 2.0 * ww) + wu) + shrink * norm - bend * norm / step
    step2 = jnp.where(curve > 0, norm / curve, 0.0)
    rest = step * (ratio * start - first)
    direction = rest + bend * start
    image = step * (ratio * first - second) + bend * first + shrink * direction
    effects = step * start + step2 * direction
    residual = rest - step2 * image
    return (effects.T, residual.T)


def solution(mesh):
    in_specs = (P("samp", "snp"), P("snp"), P("snp", None), P())
    out_specs = (P("snp", None), P("snp", None))
    return jax.shard_map(shards, mesh=mesh, in_specs=in_specs, out_specs=out_specs, check_vma=False)
```

time: 381 us -> 98.8 us (0.26)
  waiting for transfers between devices: 226 us -> 49.2 us
  blocking collectives: 70.7 us -> 0 us
  matrix products: 21.6 us -> 3.02 us
  between operations: 15 us -> 3.06 us
    psum x1 -> x0, waiting for transfers between devices: 145 us -> none  [shards(): ld_band = lax.psum(partial_band, 'samp') / samples]
    psum x4 -> x0, blocking collectives: 54.6 us -> none  [the longest x2 28.4 us: residual_sum(): return lax.psum(jnp.sum(vector * vector, 0), 'snp')]
    ppermute x15 -> x18, waiting for transfers between devices: 80.8 us -> 49.2 us  [permute(): return lax.ppermute(value, axis, pairs)]
    dot_general x18 -> x4, matrix products: 21.6 us -> 3.02 us  [product(): lax.dot_general(two_terms(value), scaled, (((1,), (contract,)), ((), ()))...]
    all_gather x2 -> x0, blocking collectives: 16.1 us -> none  [the longest x1 8.42 us: shards(): lax.all_gather(effects, 'samp', axis=1, tiled=True)]
    ppermute x15 -> x18, starting transfers between devices: 34.2 us -> 34.1 us  [permute(): return lax.ppermute(value, axis, pairs)]
  transfers between devices with their start and end apart: 16 -> 18, of which waited for: 4 -> 14; matrix products, arithmetic and copies ran while one was open for 5% -> 2% of each run, Pallas kernels for 0% -> 0%
where the time goes in v1:
time: 98.8 us; the launch traced here: 98.5 us
  waiting for transfers between devices  49.2 us (50%)
  starting transfers between devices  34.1 us (35%)
  other arithmetic  8.24 us (8%)
  between operations  3.06 us (3%)
  matrix products  3.02 us (3%)
    ppermute x18, waiting for transfers between devices, permute(): return lax.ppermute(value, axis, pairs)  49.2 us
    ppermute x18, starting transfers between devices, permute(): return lax.ppermute(value, axis, pairs)  34.1 us
    dot_general x4, matrix products, product(): lax.dot_general(two_terms(value), scaled, (((1,), (contract,)), ((), ()))...  3.02 us
    reduce_sum x1, other arithmetic, shards(): jnp.sum(genotype, 0)  2.34 us
  transfers between devices with their start and end apart: 18, of which 14 were waited for; matrix products, arithmetic and copies ran while one was open for 2% of the time, Pallas kernels for 0%

profile of v1, /device:TPU:0, one launch (start us, length us, event | category | flops | bytes accessed | tf_op | source)
XLA Modules:
  0.0 98.5 jit_solution(2966233525433758116)
XLA Ops:
  0.6 2.3 %convert_reduce_fusion = (f32[512]{0:T(512)S(1)}, f32[512]{0:T(512)S(1)}) fusion(bf16[2048,512]{1,0:T(8,128)(2,1)} %param.4), kind=kLoop, calls=%fused_computation.2 | loop fusion | flops 4193280 | bytes 2101248 | tf_op jit(solution)/shard_map/reduce_sum | solution.py:101
  3.0 3.0 %collective-permute-start = (f32[2,512]{1,0:T(2,128)S(1)}, f32[2,512]{1,0:T(2,128)S(1)}, u32[]{:S(2)}, u32[]{:S(2)}) collective-permute-start(f32[2,512]{1,0:T(2,128)S(1)} %pad_maximum_fusion.2), channel_id=1, source_target_pairs={{0,8},{8,0},{16,24},{24,16},{1,9},{9,1},{17,25},{25,17},{2,10},{10... | collective-permute-start | bytes 12296 | tf_op jit(solution)/shard_map/ppermute | solution.py:11
  6.0 0.9 reduce-precision_convert_fusion.3
  7.6 2.1 %collective-permute-start.1 = (f32[2,512]{1,0:T(2,128)S(1)}, f32[2,512]{1,0:T(2,128)S(1)}, u32[]{:S(2)}, u32[]{:S(2)}) collective-permute-start(f32[2,512]{1,0:T(2,128)S(1)} %fusion.47), channel_id=1, source_target_pairs={{0,16},{8,24},{16,0},{24,8},{1,17},{9,25},{17,1},{25,9},{2,18},{10... | collective-permute-start | bytes 12296 | tf_op jit(solution)/shard_map/ppermute | solution.py:11
  9.7 1.6 %collective-permute-done.1 = f32[2,512]{1,0:T(2,128)S(1)} collective-permute-done((f32[2,512]{1,0:T(2,128)S(1)}, f32[2,512]{1,0:T(2,128)S(1)}, u32[]{:S(2)}, u32[]{:S(2)}) %collective-permute-start.1) | collective-permute-done | bytes 4128 | tf_op jit(solution)/shard_map/ppermute | solution.py:11
  11.3 0.9 fusion.9
  12.2 0.2 abs_reduce_fusion.1
  12.4 0.1 multiply_convert_fusion.1
  12.5 0.1 select_convert_fusion.1
  12.6 0.1 pad_maximum_fusion
  12.7 4.0 %collective-permute-start.2 = (f16[64,2176]{1,0:T(8,128)(2,1)S(1)}, f16[64,2176]{1,0:T(8,128)(2,1)S(1)}, u32[]{:S(2)}, u32[]{:S(2)}) collective-permute-start(f16[64,2176]{1,0:T(8,128)(2,1)S(1)} %pad_maximum_fusion), channel_id=1, source_target_pairs={{0,2},{1,3},{2,4},{3,5},{4,6},{5,7},{8,10},{9,11},{10,12},{11,13},... | collective-permute-start | bytes 835592 | tf_op jit(solution)/shard_map/ppermute | solution.py:11
  16.7 0.1 collective-permute-start.4
  16.8 1.1 %collective-permute-done.4 = f32[8,128]{1,0:T(8,128)S(1)} collective-permute-done((f32[8,128]{1,0:T(8,128)S(1)}, f32[8,128]{1,0:T(8,128)S(1)}, u32[]{:S(2)}, u32[]{:S(2)}) %collective-permute-start.4) | collective-permute-done | bytes 4128 | tf_op jit(solution)/shard_map/ppermute | solution.py:11
  17.9 0.6 slice.102
  19.9 1.3 %collective-permute-start.3 = (f16[64,2176]{1,0:T(8,128)(2,1)S(1)}, f16[64,2176]{1,0:T(8,128)(2,1)S(1)}, u32[]{:S(2)}, u32[]{:S(2)}) collective-permute-start(f16[64,2176]{1,0:T(8,128)(2,1)S(1)} %pad_maximum_fusion), channel_id=1, source_target_pairs={{2,0},{3,1},{4,2},{5,3},{6,4},{7,5},{10,8},{11,9},{12,10},{13,11},... | collective-permute-start | bytes 835592 | tf_op jit(solution)/shard_map/ppermute | solution.py:11
  21.2 0.1 exponential_reduce_fusion.5
  21.3 0.1 slice.130
  21.4 0.1 copy.28
  21.5 9.0 %collective-permute-done.3 = f16[64,2176]{1,0:T(8,128)(2,1)S(1)} collective-permute-done((f16[64,2176]{1,0:T(8,128)(2,1)S(1)}, f16[64,2176]{1,0:T(8,128)(2,1)S(1)}, u32[]{:S(2)}, u32[]{:S(2)}) %collective-permute-start.3) | collective-permute-done | bytes 278560 | tf_op jit(solution)/shard_map/ppermute | solution.py:11
  30.5 0.1 exponential_reduce_fusion.4
  30.6 0.2 multiply_add_fusion.3
  30.9 0.1 collective-permute-start.5
  31.0 0.7 collective-permute-start.6
  31.7 0.2 exponential_reduce_fusion.3
  31.8 1.0 %collective-permute-done.5 = f32[64,2048]{1,0:T(8,128)S(1)} collective-permute-done((f32[64,2048]{1,0:T(8,128)S(1)}, f32[64,2048]{1,0:T(8,128)S(1)}, u32[]{:S(2)}, u32[]{:S(2)}) %collective-permute-start.5) | collective-permute-done | bytes 524320 | tf_op jit(solution)/shard_map/ppermute | solution.py:11
  32.9 0.3 reduce-precision_convert_fusion.1
  33.2 0.1 fusion.11
  33.3 0.7 fusion.7
  34.0 1.6 %collective-permute-start.7 = (f32[64,512]{1,0:T(8,128)S(1)}, f32[64,512]{1,0:T(8,128)S(1)}, u32[]{:S(2)}, u32[]{:S(2)}) collective-permute-start(f32[64,512]{1,0:T(8,128)S(1)} %slice_add_fusion.3), channel_id=1, source_target_pairs={{0,8},{8,0},{16,24},{24,16},{1,9},{9,1},{17,25},{25,17},{2,10},{10... | collective-permute-start | bytes 393224 | tf_op jit(solution)/shard_map/ppermute | solution.py:11
  35.5 3.5 %collective-permute-done.7 = f32[64,512]{1,0:T(8,128)S(1)} collective-permute-done((f32[64,512]{1,0:T(8,128)S(1)}, f32[64,512]{1,0:T(8,128)S(1)}, u32[]{:S(2)}, u32[]{:S(2)}) %collective-permute-start.7) | collective-permute-done | bytes 131104 | tf_op jit(solution)/shard_map/ppermute | solution.py:11
  39.0 1.6 %collective-permute-start.8 = (f32[64,512]{1,0:T(8,128)S(1)}, f32[64,512]{1,0:T(8,128)S(1)}, u32[]{:S(2)}, u32[]{:S(2)}) collective-permute-start(f32[64,512]{1,0:T(8,128)S(1)} %fusion.50), channel_id=1, source_target_pairs={{0,16},{8,24},{16,0},{24,8},{1,17},{9,25},{17,1},{25,9},{2,18},{10... | collective-permute-start | bytes 393224 | tf_op jit(solution)/shard_map/ppermute | solution.py:11
  40.6 3.4 %collective-permute-done.8 = f32[64,512]{1,0:T(8,128)S(1)} collective-permute-done((f32[64,512]{1,0:T(8,128)S(1)}, f32[64,512]{1,0:T(8,128)S(1)}, u32[]{:S(2)}, u32[]{:S(2)}) %collective-permute-start.8) | collective-permute-done | bytes 131104 | tf_op jit(solution)/shard_map/ppermute | solution.py:11
  44.1 0.9 fusion.5
  45.0 0.2 abs_reduce_fusion
  45.1 0.1 select_convert_fusion
  45.2 0.1 multiply_convert_fusion
  45.3 0.8 pad_maximum_fusion.1
  46.1 3.5 %collective-permute-start.9 = (f16[64,2176]{1,0:T(8,128)(2,1)}, f16[64,2176]{1,0:T(8,128)(2,1)S(1)}, u32[]{:S(2)}, u32[]{:S(2)}) collective-permute-start(f16[64,2176]{1,0:T(8,128)(2,1)} %pad_maximum_fusion.1), channel_id=1, source_target_pairs={{0,2},{1,3},{2,4},{3,5},{4,6},{5,7},{8,10},{9,11},{10,12},{11,13},... | collective-permute-start | bytes 835592 | tf_op jit(solution)/shard_map/ppermute | solution.py:11
  49.6 1.3 %collective-permute-start.10 = (f16[64,2176]{1,0:T(8,128)(2,1)}, f16[64,2176]{1,0:T(8,128)(2,1)S(1)}, u32[]{:S(2)}, u32[]{:S(2)}) collective-permute-start(f16[64,2176]{1,0:T(8,128)(2,1)} %pad_maximum_fusion.1), channel_id=1, source_target_pairs={{2,0},{3,1},{4,2},{5,3},{6,4},{7,5},{10,8},{11,9},{12,10},{13,11},... | collective-permute-start | bytes 835592 | tf_op jit(solution)/shard_map/ppermute | solution.py:11
  50.9 3.0 %collective-permute-done.9 = f16[64,2176]{1,0:T(8,128)(2,1)S(1)} collective-permute-done((f16[64,2176]{1,0:T(8,128)(2,1)}, f16[64,2176]{1,0:T(8,128)(2,1)S(1)}, u32[]{:S(2)}, u32[]{:S(2)}) %collective-permute-start.9) | collective-permute-done | bytes 278560 | tf_op jit(solution)/shard_map/ppermute | solution.py:11
  53.9 0.1 exponential_reduce_fusion.2
  54.1 0.1 slice.142
  54.1 0.1 copy.29
  54.2 12.1 %collective-permute-done.10 = f16[64,2176]{1,0:T(8,128)(2,1)S(1)} collective-permute-done((f16[64,2176]{1,0:T(8,128)(2,1)}, f16[64,2176]{1,0:T(8,128)(2,1)S(1)}, u32[]{:S(2)}, u32[]{:S(2)}) %collective-permute-start.10) | collective-permute-done | bytes 278560 | tf_op jit(solution)/shard_map/ppermute | solution.py:11
  66.3 0.1 exponential_reduce_fusion.1
  66.4 0.2 multiply_add_fusion.1
  66.7 0.1 collective-permute-start.11
  66.8 0.7 collective-permute-start.12
  67.5 0.2 exponential_reduce_fusion
  67.6 1.0 %collective-permute-done.11 = f32[64,2048]{1,0:T(8,128)S(1)} collective-permute-done((f32[64,2048]{1,0:T(8,128)S(1)}, f32[64,2048]{1,0:T(8,128)S(1)}, u32[]{:S(2)}, u32[]{:S(2)}) %collective-permute-start.11) | collective-permute-done | bytes 524320 | tf_op jit(solution)/shard_map/ppermute | solution.py:11
  68.7 0.3 reduce-precision_convert_fusion
  69.1 0.7 fusion.3
  69.8 1.6 %collective-permute-start.13 = (f32[64,512]{1,0:T(8,128)S(1)}, f32[64,512]{1,0:T(8,128)S(1)}, u32[]{:S(2)}, u32[]{:S(2)}) collective-permute-start(f32[64,512]{1,0:T(8,128)S(1)} %slice_add_fusion.2), channel_id=1, source_target_pairs={{0,8},{8,0},{16,24},{24,16},{1,9},{9,1},{17,25},{25,17},{2,10},{10... | collective-permute-start | bytes 393224 | tf_op jit(solution)/shard_map/ppermute | solution.py:11
  71.3 3.5 %collective-permute-done.13 = f32[64,512]{1,0:T(8,128)S(1)} collective-permute-done((f32[64,512]{1,0:T(8,128)S(1)}, f32[64,512]{1,0:T(8,128)S(1)}, u32[]{:S(2)}, u32[]{:S(2)}) %collective-permute-start.13) | collective-permute-done | bytes 131104 | tf_op jit(solution)/shard_map/ppermute | solution.py:11
  74.8 1.6 %collective-permute-start.14 = (f32[64,512]{1,0:T(8,128)S(1)}, f32[64,512]{1,0:T(8,128)S(1)}, u32[]{:S(2)}, u32[]{:S(2)}) collective-permute-start(f32[64,512]{1,0:T(8,128)S(1)} %fusion.49), channel_id=1, source_target_pairs={{0,16},{8,24},{16,0},{24,8},{1,17},{9,25},{17,1},{25,9},{2,18},{10... | collective-permute-start | bytes 393224 | tf_op jit(solution)/shard_map/ppermute | solution.py:11
  76.4 3.4 %collective-permute-done.14 = f32[64,512]{1,0:T(8,128)S(1)} collective-permute-done((f32[64,512]{1,0:T(8,128)S(1)}, f32[64,512]{1,0:T(8,128)S(1)}, u32[]{:S(2)}, u32[]{:S(2)}) %collective-permute-start.14) | collective-permute-done | bytes 131104 | tf_op jit(solution)/shard_map/ppermute | solution.py:11
  79.9 0.2 fusion.27
  80.1 8.5 %collective-permute-start.15 = (f32[64,4]{0,1:T(4,128)S(1)}, f32[64,4]{0,1:T(4,128)S(1)}, u32[]{:S(2)}, u32[]{:S(2)}) collective-permute-start(f32[64,4]{0,1:T(4,128)S(1)} %pad_maximum_fusion.3), channel_id=1, source_target_pairs={{0,1},{1,0},{2,3},{3,2},{4,5},{5,4},{6,7},{7,6},{8,9},{9,8},{10,11... | collective-permute-start | bytes 3080 | tf_op jit(solution)/shard_map/ppermute | solution.py:11
  88.6 0.8 collective-permute-done.15
  89.4 0.1 collective-permute-start.16
  89.5 3.6 %collective-permute-done.16 = f32[64,4]{0,1:T(4,128)S(1)} collective-permute-done((f32[64,4]{0,1:T(4,128)S(1)}, f32[64,4]{0,1:T(4,128)S(1)}, u32[]{:S(2)}, u32[]{:S(2)}) %collective-permute-start.16) | collective-permute-done | bytes 1056 | tf_op jit(solution)/shard_map/ppermute | solution.py:11
  93.1 2.5 %collective-permute-start.17 = (f32[64,4]{0,1:T(4,128)S(1)}, f32[64,4]{0,1:T(4,128)S(1)}, u32[]{:S(2)}, u32[]{:S(2)}) collective-permute-start(f32[64,4]{0,1:T(4,128)S(1)} %fusion.48), channel_id=1, source_target_pairs={{0,4},{1,5},{2,6},{3,7},{4,0},{5,1},{6,2},{7,3},{8,12},{9,13},{10,... | collective-permute-start | bytes 3080 | tf_op jit(solution)/shard_map/ppermute | solution.py:11
  95.6 2.0 %collective-permute-done.17 = f32[64,4]{0,1:T(4,128)S(1)} collective-permute-done((f32[64,4]{0,1:T(4,128)S(1)}, f32[64,4]{0,1:T(4,128)S(1)}, u32[]{:S(2)}, u32[]{:S(2)}) %collective-permute-start.17) | collective-permute-done | bytes 1056 | tf_op jit(solution)/shard_map/ppermute | solution.py:11
  97.7 0.9 subtract_bitcast_fusion
  (35 shorter events, 0.4 us)
Async XLA Ops:
  0.6 10.7 %copy-start = (bf16[2048,512]{1,0:T(8,128)(2,1)S(1)}, bf16[2048,512]{1,0:T(8,128)(2,1)}, u32[]{:S(2)}) copy-start(bf16[2048,512]{1,0:T(8,128)(2,1)} %param.4) | copy-start | bytes 6291460
  3.0 4.6 %collective-permute-start = (f32[2,512]{1,0:T(2,128)S(1)}, f32[2,512]{1,0:T(2,128)S(1)}, u32[]{:S(2)}, u32[]{:S(2)}) collective-permute-start(f32[2,512]{1,0:T(2,128)S(1)} %pad_maximum_fusion.2), channel_id=1, source_target_pairs={{0,8},{8,0},{16,24},{24,16},{1,9},{9,1},{17,25},{25,17},{2,10},{10... | collective-permute-start | bytes 12296 | tf_op jit(solution)/shard_map/ppermute | solution.py:11
  7.6 3.7 %collective-permute-start.1 = (f32[2,512]{1,0:T(2,128)S(1)}, f32[2,512]{1,0:T(2,128)S(1)}, u32[]{:S(2)}, u32[]{:S(2)}) collective-permute-start(f32[2,512]{1,0:T(2,128)S(1)} %fusion.47), channel_id=1, source_target_pairs={{0,16},{8,24},{16,0},{24,8},{1,17},{9,25},{17,1},{25,9},{2,18},{10... | collective-permute-start | bytes 12296 | tf_op jit(solution)/shard_map/ppermute | solution.py:11
  12.7 8.5 %collective-permute-start.2 = (f16[64,2176]{1,0:T(8,128)(2,1)S(1)}, f16[64,2176]{1,0:T(8,128)(2,1)S(1)}, u32[]{:S(2)}, u32[]{:S(2)}) collective-permute-start(f16[64,2176]{1,0:T(8,128)(2,1)S(1)} %pad_maximum_fusion), channel_id=1, source_target_pairs={{0,2},{1,3},{2,4},{3,5},{4,6},{5,7},{8,10},{9,11},{10,12},{11,13},... | collective-permute-start | bytes 835592 | tf_op jit(solution)/shard_map/ppermute | solution.py:11
  16.7 1.2 %collective-permute-start.4 = (f32[8,128]{1,0:T(8,128)S(1)}, f32[8,128]{1,0:T(8,128)S(1)}, u32[]{:S(2)}, u32[]{:S(2)}) collective-permute-start(f32[8,128]{1,0:T(8,128)S(1)} %broadcast_in_dim.73), channel_id=1, source_target_pairs={{0,1},{1,0},{2,3},{3,2},{4,5},{5,4},{6,7},{7,6},{8,9},{9,8},{10,11... | collective-permute-start | bytes 12296 | tf_op jit(solution)/shard_map/ppermute | solution.py:11
  19.9 10.6 %collective-permute-start.3 = (f16[64,2176]{1,0:T(8,128)(2,1)S(1)}, f16[64,2176]{1,0:T(8,128)(2,1)S(1)}, u32[]{:S(2)}, u32[]{:S(2)}) collective-permute-start(f16[64,2176]{1,0:T(8,128)(2,1)S(1)} %pad_maximum_fusion), channel_id=1, source_target_pairs={{2,0},{3,1},{4,2},{5,3},{6,4},{7,5},{10,8},{11,9},{12,10},{13,11},... | collective-permute-start | bytes 835592 | tf_op jit(solution)/shard_map/ppermute | solution.py:11
  30.9 2.0 %collective-permute-start.5 = (f32[64,2048]{1,0:T(8,128)S(1)}, f32[64,2048]{1,0:T(8,128)S(1)}, u32[]{:S(2)}, u32[]{:S(2)}) collective-permute-start(f32[64,2048]{1,0:T(8,128)S(1)} %multiply_add_fusion.3), channel_id=1, source_target_pairs={{0,1},{1,0},{2,3},{3,2},{4,5},{5,4},{6,7},{7,6},{8,9},{9,8},{10,11... | collective-permute-start | bytes 1572872 | tf_op jit(solution)/shard_map/ppermute | solution.py:11
  31.0 0.7 collective-permute-start.6
  34.0 5.0 %collective-permute-start.7 = (f32[64,512]{1,0:T(8,128)S(1)}, f32[64,512]{1,0:T(8,128)S(1)}, u32[]{:S(2)}, u32[]{:S(2)}) collective-permute-start(f32[64,512]{1,0:T(8,128)S(1)} %slice_add_fusion.3), channel_id=1, source_target_pairs={{0,8},{8,0},{16,24},{24,16},{1,9},{9,1},{17,25},{25,17},{2,10},{10... | collective-permute-start | bytes 393224 | tf_op jit(solution)/shard_map/ppermute | solution.py:11
  39.0 5.0 %collective-permute-start.8 = (f32[64,512]{1,0:T(8,128)S(1)}, f32[64,512]{1,0:T(8,128)S(1)}, u32[]{:S(2)}, u32[]{:S(2)}) collective-permute-start(f32[64,512]{1,0:T(8,128)S(1)} %fusion.50), channel_id=1, source_target_pairs={{0,16},{8,24},{16,0},{24,8},{1,17},{9,25},{17,1},{25,9},{2,18},{10... | collective-permute-start | bytes 393224 | tf_op jit(solution)/shard_map/ppermute | solution.py:11
  46.1 7.8 %collective-permute-start.9 = (f16[64,2176]{1,0:T(8,128)(2,1)}, f16[64,2176]{1,0:T(8,128)(2,1)S(1)}, u32[]{:S(2)}, u32[]{:S(2)}) collective-permute-start(f16[64,2176]{1,0:T(8,128)(2,1)} %pad_maximum_fusion.1), channel_id=1, source_target_pairs={{0,2},{1,3},{2,4},{3,5},{4,6},{5,7},{8,10},{9,11},{10,12},{11,13},... | collective-permute-start | bytes 835592 | tf_op jit(solution)/shard_map/ppermute | solution.py:11
  49.6 16.7 %collective-permute-start.10 = (f16[64,2176]{1,0:T(8,128)(2,1)}, f16[64,2176]{1,0:T(8,128)(2,1)S(1)}, u32[]{:S(2)}, u32[]{:S(2)}) collective-permute-start(f16[64,2176]{1,0:T(8,128)(2,1)} %pad_maximum_fusion.1), channel_id=1, source_target_pairs={{2,0},{3,1},{4,2},{5,3},{6,4},{7,5},{10,8},{11,9},{12,10},{13,11},... | collective-permute-start | bytes 835592 | tf_op jit(solution)/shard_map/ppermute | solution.py:11
  66.7 2.0 %collective-permute-start.11 = (f32[64,2048]{1,0:T(8,128)S(1)}, f32[64,2048]{1,0:T(8,128)S(1)}, u32[]{:S(2)}, u32[]{:S(2)}) collective-permute-start(f32[64,2048]{1,0:T(8,128)S(1)} %multiply_add_fusion.1), channel_id=1, source_target_pairs={{0,1},{1,0},{2,3},{3,2},{4,5},{5,4},{6,7},{7,6},{8,9},{9,8},{10,11... | collective-permute-start | bytes 1572872 | tf_op jit(solution)/shard_map/ppermute | solution.py:11
  66.8 0.7 collective-permute-start.12
  69.1 10.8 %copy-start.1 = (f32[512,64]{0,1:T(8,128)S(1)}, f32[512,64]{0,1:T(8,128)}, u32[]{:S(2)}) copy-start(f32[512,64]{0,1:T(8,128)} %param.6) | copy-start | bytes 393220
  69.1 28.5 %copy-start.2 = (f32[64]{0:T(128)S(1)}, f32[64]{0:T(128)}, u32[]{:S(2)}) copy-start(f32[64]{0:T(128)} %param.7) | copy-start | bytes 772
  69.8 5.0 %collective-permute-start.13 = (f32[64,512]{1,0:T(8,128)S(1)}, f32[64,512]{1,0:T(8,128)S(1)}, u32[]{:S(2)}, u32[]{:S(2)}) collective-permute-start(f32[64,512]{1,0:T(8,128)S(1)} %slice_add_fusion.2), channel_id=1, source_target_pairs={{0,8},{8,0},{16,24},{24,16},{1,9},{9,1},{17,25},{25,17},{2,10},{10... | collective-permute-start | bytes 393224 | tf_op jit(solution)/shard_map/ppermute | solution.py:11
  74.8 5.0 %collective-permute-start.14 = (f32[64,512]{1,0:T(8,128)S(1)}, f32[64,512]{1,0:T(8,128)S(1)}, u32[]{:S(2)}, u32[]{:S(2)}) collective-permute-start(f32[64,512]{1,0:T(8,128)S(1)} %fusion.49), channel_id=1, source_target_pairs={{0,16},{8,24},{16,0},{24,8},{1,17},{9,25},{17,1},{25,9},{2,18},{10... | collective-permute-start | bytes 393224 | tf_op jit(solution)/shard_map/ppermute | solution.py:11
  80.1 9.3 %collective-permute-start.15 = (f32[64,4]{0,1:T(4,128)S(1)}, f32[64,4]{0,1:T(4,128)S(1)}, u32[]{:S(2)}, u32[]{:S(2)}) collective-permute-start(f32[64,4]{0,1:T(4,128)S(1)} %pad_maximum_fusion.3), channel_id=1, source_target_pairs={{0,1},{1,0},{2,3},{3,2},{4,5},{5,4},{6,7},{7,6},{8,9},{9,8},{10,11... | collective-permute-start | bytes 3080 | tf_op jit(solution)/shard_map/ppermute | solution.py:11
  89.4 3.7 %collective-permute-start.16 = (f32[64,4]{0,1:T(4,128)S(1)}, f32[64,4]{0,1:T(4,128)S(1)}, u32[]{:S(2)}, u32[]{:S(2)}) collective-permute-start(f32[64,4]{0,1:T(4,128)S(1)} %fusion.46), channel_id=1, source_target_pairs={{0,2},{1,3},{2,0},{3,1},{4,6},{5,7},{6,4},{7,5},{8,10},{9,11},{10,... | collective-permute-start | bytes 3080 | tf_op jit(solution)/shard_map/ppermute | solution.py:11
  93.1 4.5 %collective-permute-start.17 = (f32[64,4]{0,1:T(4,128)S(1)}, f32[64,4]{0,1:T(4,128)S(1)}, u32[]{:S(2)}, u32[]{:S(2)}) collective-permute-start(f32[64,4]{0,1:T(4,128)S(1)} %fusion.48), channel_id=1, source_target_pairs={{0,4},{1,5},{2,6},{3,7},{4,0},{5,1},{6,2},{7,3},{8,12},{9,13},{10,... | collective-permute-start | bytes 3080 | tf_op jit(solution)/shard_map/ppermute | solution.py:11

commit v2 on v1

--- a/solution.py
+++ b/solution.py
@@ -20,21 +20,36 @@
     return permute(value, "snp", [(i, i + distance) for i in range(count) if 0 <= i + distance < count])
 
 
-def far_shift(value):
+def forward(value):
     count = lax.axis_size("snp")
-    up = [(i, i + 3) for i in range(1, count, 2) if i + 3 < count]
-    down = [(i, i - 3) for i in range(0, count, 2) if i - 3 >= 0]
+    up = [(i, i + 1) for i in range(1, count, 2) if i + 1 < count]
+    down = [(i, i - 1) for i in range(0, count, 2) if i - 1 >= 0]
     return permute(value, "snp", up + down)
 
 
-def sum_over(value, axis):
-    count = lax.axis_size(axis)
+def snp_sum(value):
+    count = lax.axis_size("snp")
     if count & (count - 1):
-        return lax.psum(value, axis)
+        return lax.psum(value, "snp")
     bit = 1
     while bit < count:
-        value = value + swap(value, axis, bit)
+        value = value + swap(value, "snp", bit)
         bit *= 2
+    return value
+
+
+def samp_sum(value):
+    rows, count = lax.axis_size("samp"), lax.axis_size("snp")
+    if rows & (rows - 1):
+        return lax.psum(value, "samp")
+    bits = [1 << k for k in range(rows.bit_length() - 1)]
+    for even_bit, odd_bit in zip(bits, bits[::-1]):
+        pairs = [
+            (row * count + col, (row ^ (odd_bit if col % 2 else even_bit)) * count + col)
+            for row in range(rows)
+            for col in range(count)
+        ]
+        value = value + permute(value, ("samp", "snp"), pairs)
     return value
 
 
@@ -70,11 +85,11 @@
 
 def window(own, width, partner_width, odd):
     coded = pack(own, width)
-    below = shift(coded, 2)
-    above = shift(coded, -2)
-    far = far_shift(coded)
-    below, below_width = unpack(below)
-    above, _ = unpack(above)
+    below_coded = shift(coded, 2)
+    above_coded = shift(coded, -2)
+    far = forward(jnp.where(odd, below_coded, above_coded))
+    below, below_width = unpack(below_coded)
+    above, _ = unpack(above_coded)
     pick = lambda even_case, odd_case: jnp.where(odd, odd_case, even_case)
     give = (
         own * (pick(width, partner_width) >= 1)
@@ -98,7 +113,9 @@
     width = band_width.astype(jnp.float32).reshape(1, 1)
     partner_width = swap(jnp.broadcast_to(width, (8, 128)), "snp", 1)[:1, :1]
     genotype = dosage.astype(jnp.float32)
-    sums = sum_over(jnp.stack([jnp.sum(genotype, 0), jnp.sum(genotype * genotype, 0)]), "samp")
+    sums = jnp.stack([jnp.sum(genotype, 0), jnp.sum(genotype * genotype, 0)])
+    sums, partner_width = lax.optimization_barrier((sums, partner_width))
+    sums = samp_sum(sums)
     center = sums[0] / samples
     spread = sums[1] / samples - center * center
     scaled = ((genotype - center) * lax.rsqrt(spread + 1e-05)).astype(jnp.bfloat16)
@@ -107,13 +124,13 @@
 
     def operate(value):
         mixed = window(product(value, scaled, 1), width, partner_width, odd)
-        return sum_over(product(mixed, scaled, 0), "samp") / samples
+        return samp_sum(product(mixed, scaled, 0)) / samples
 
     first = operate(start)
     second = operate(first)
     dot = lambda a, b: jnp.sum(a * b, 1, keepdims=True)
     parts = jnp.concatenate([dot(start, start), dot(start, first), dot(first, first), dot(first, second)], 1)
-    parts = sum_over(parts, "snp")
+    parts = snp_sum(parts)
     bb, bw, ww, wu = (parts[:, k : k + 1] for k in range(4))
     ratio = bw / bb
     step = 1.0 / (ratio + shrink)

time: 98.8 us -> 93.4 us (0.945)
  waiting for transfers between devices: 49.2 us -> 39.8 us
  starting transfers between devices: 34.1 us -> 37.9 us
    ppermute x18, waiting for transfers between devices: 49.2 us -> 39.8 us  [permute(): return lax.ppermute(value, axis, pairs)]
    ppermute x18, starting transfers between devices: 34.1 us -> 37.9 us  [permute(): return lax.ppermute(value, axis, pairs)]
  transfers between devices with their start and end apart: 18 -> 18, of which waited for: 14 -> 15; matrix products, arithmetic and copies ran while one was open for 2% -> 5% of each run, Pallas kernels for 0% -> 0%
where the time goes in v2:
time: 93.4 us; the launch traced here: 93.1 us
  waiting for transfers between devices  39.8 us (43%)
  starting transfers between devices  37.9 us (41%)
  other arithmetic  8.25 us (9%)
  between operations  3.19 us (3%)
  matrix products  3.01 us (3%)
  local copies, waits for them, and re-layouts  0.94 us (1%)
    ppermute x18, waiting for transfers between devices, permute(): return lax.ppermute(value, axis, pairs)  39.8 us
    ppermute x18, starting transfers between devices, permute(): return lax.ppermute(value, axis, pairs)  37.9 us
    dot_general x4, matrix products, product(): lax.dot_general(two_terms(value), scaled, (((1,), (contract,)), ((), ()))...  3.01 us
    reduce_sum x1, other arithmetic, shards(): sums = jnp.stack([jnp.sum(genotype, 0), jnp.sum(genotype * genotype, 0)])  2.19 us
  transfers between devices with their start and end apart: 18, of which 15 were waited for; matrix products, arithmetic and copies ran while one was open for 5% of the time, Pallas kernels for 0%

profile of v2, /device:TPU:0, one launch (start us, length us, event | category | flops | bytes accessed | tf_op | source)
XLA Modules:
  0.0 93.1 jit_solution(16712650707212069141)
XLA Ops:
  1.4 0.5 collective-permute-start
  2.0 2.2 %convert_reduce_fusion = (f32[512]{0:T(512)S(1)}, f32[512]{0:T(512)S(1)}) fusion(bf16[2048,512]{1,0:T(8,128)(2,1)} %param.4), kind=kLoop, calls=%fused_computation.2 | loop fusion | flops 4193280 | bytes 2101248 | tf_op jit(solution)/shard_map/reduce_sum | solution.py:116
  4.2 0.9 reduce-precision_convert_fusion.3
  5.1 0.6 slice.93
  5.7 2.5 %collective-permute-start.1 = (f32[2,512]{1,0:T(2,128)S(1)}, f32[2,512]{1,0:T(2,128)S(1)}, u32[]{:S(2)}, u32[]{:S(2)}) collective-permute-start(f32[2,512]{1,0:T(2,128)S(1)} %pad_maximum_fusion.2), channel_id=1, source_target_pairs={{0,8},{1,17},{2,10},{3,19},{4,12},{5,21},{6,14},{7,23},{8,0},{9,25... | collective-permute-start | bytes 12296 | tf_op jit(solution)/shard_map/ppermute | solution.py:11
  8.2 1.6 %collective-permute-done.1 = f32[2,512]{1,0:T(2,128)S(1)} collective-permute-done((f32[2,512]{1,0:T(2,128)S(1)}, f32[2,512]{1,0:T(2,128)S(1)}, u32[]{:S(2)}, u32[]{:S(2)}) %collective-permute-start.1) | collective-permute-done | bytes 4128 | tf_op jit(solution)/shard_map/ppermute | solution.py:11
  9.8 2.1 %collective-permute-start.2 = (f32[2,512]{1,0:T(2,128)S(1)}, f32[2,512]{1,0:T(2,128)S(1)}, u32[]{:S(2)}, u32[]{:S(2)}) collective-permute-start(f32[2,512]{1,0:T(2,128)S(1)} %add.107), channel_id=1, source_target_pairs={{0,16},{1,9},{2,18},{3,11},{4,20},{5,13},{6,22},{7,15},{8,24},{9,1... | collective-permute-start | bytes 12296 | tf_op jit(solution)/shard_map/ppermute | solution.py:11
  11.9 1.6 %collective-permute-done.2 = f32[2,512]{1,0:T(2,128)S(1)} collective-permute-done((f32[2,512]{1,0:T(2,128)S(1)}, f32[2,512]{1,0:T(2,128)S(1)}, u32[]{:S(2)}, u32[]{:S(2)}) %collective-permute-start.2) | collective-permute-done | bytes 4128 | tf_op jit(solution)/shard_map/ppermute | solution.py:11
  13.5 0.9 fusion.9
  14.3 0.2 abs_reduce_fusion.1
  14.5 0.1 multiply_convert_fusion.1
  14.6 0.1 select_convert_fusion.1
  14.8 4.0 %collective-permute-start.3 = (f16[64,2176]{1,0:T(8,128)(2,1)S(1)}, f16[64,2176]{1,0:T(8,128)(2,1)S(1)}, u32[]{:S(2)}, u32[]{:S(2)}) collective-permute-start(f16[64,2176]{1,0:T(8,128)(2,1)S(1)} %pad_maximum_fusion), channel_id=1, source_target_pairs={{0,2},{1,3},{2,4},{3,5},{4,6},{5,7},{8,10},{9,11},{10,12},{11,13},... | collective-permute-start | bytes 835592 | tf_op jit(solution)/shard_map/ppermute | solution.py:11
  20.2 1.3 %collective-permute-start.4 = (f16[64,2176]{1,0:T(8,128)(2,1)S(1)}, f16[64,2176]{1,0:T(8,128)(2,1)S(1)}, u32[]{:S(2)}, u32[]{:S(2)}) collective-permute-start(f16[64,2176]{1,0:T(8,128)(2,1)S(1)} %pad_maximum_fusion), channel_id=1, source_target_pairs={{2,0},{3,1},{4,2},{5,3},{6,4},{7,5},{10,8},{11,9},{12,10},{13,11},... | collective-permute-start | bytes 835592 | tf_op jit(solution)/shard_map/ppermute | solution.py:11
  21.5 1.5 %collective-permute-done.3 = f16[64,2176]{1,0:T(8,128)(2,1)S(1)} collective-permute-done((f16[64,2176]{1,0:T(8,128)(2,1)S(1)}, f16[64,2176]{1,0:T(8,128)(2,1)S(1)}, u32[]{:S(2)}, u32[]{:S(2)}) %collective-permute-start.3) | collective-permute-done | bytes 278560 | tf_op jit(solution)/shard_map/ppermute | solution.py:11
  23.0 0.1 exponential_reduce_fusion.5
  23.1 0.1 slice.130
  23.2 0.1 copy.28
  23.3 5.3 %collective-permute-done.4 = f16[64,2176]{1,0:T(8,128)(2,1)S(1)} collective-permute-done((f16[64,2176]{1,0:T(8,128)(2,1)S(1)}, f16[64,2176]{1,0:T(8,128)(2,1)S(1)}, u32[]{:S(2)}, u32[]{:S(2)}) %collective-permute-start.4) | collective-permute-done | bytes 278560 | tf_op jit(solution)/shard_map/ppermute | solution.py:11
  28.6 0.1 exponential_reduce_fusion.4
  28.7 0.2 multiply_add_fusion.3
  29.0 0.1 collective-permute-start.5
  29.1 0.1 broadcast_select_fusion.1
  29.2 0.7 collective-permute-start.6
  29.9 0.2 exponential_reduce_fusion.3
  30.1 0.9 collective-permute-done.5
  31.0 0.3 reduce-precision_convert_fusion.1
  31.4 0.7 fusion.7
  32.1 1.6 %collective-permute-start.7 = (f32[64,512]{1,0:T(8,128)S(1)}, f32[64,512]{1,0:T(8,128)S(1)}, u32[]{:S(2)}, u32[]{:S(2)}) collective-permute-start(f32[64,512]{1,0:T(8,128)S(1)} %slice_add_fusion.3), channel_id=1, source_target_pairs={{0,8},{1,17},{2,10},{3,19},{4,12},{5,21},{6,14},{7,23},{8,0},{9,25... | collective-permute-start | bytes 393224 | tf_op jit(solution)/shard_map/ppermute | solution.py:11
  33.6 3.5 %collective-permute-done.7 = f32[64,512]{1,0:T(8,128)S(1)} collective-permute-done((f32[64,512]{1,0:T(8,128)S(1)}, f32[64,512]{1,0:T(8,128)S(1)}, u32[]{:S(2)}, u32[]{:S(2)}) %collective-permute-start.7) | collective-permute-done | bytes 131104 | tf_op jit(solution)/shard_map/ppermute | solution.py:11
  37.1 1.6 %collective-permute-start.8 = (f32[64,512]{1,0:T(8,128)S(1)}, f32[64,512]{1,0:T(8,128)S(1)}, u32[]{:S(2)}, u32[]{:S(2)}) collective-permute-start(f32[64,512]{1,0:T(8,128)S(1)} %fusion.49), channel_id=1, source_target_pairs={{0,16},{1,9},{2,18},{3,11},{4,20},{5,13},{6,22},{7,15},{8,24},{9,1... | collective-permute-start | bytes 393224 | tf_op jit(solution)/shard_map/ppermute | solution.py:11
  38.7 4.2 %collective-permute-done.8 = f32[64,512]{1,0:T(8,128)S(1)} collective-permute-done((f32[64,512]{1,0:T(8,128)S(1)}, f32[64,512]{1,0:T(8,128)S(1)}, u32[]{:S(2)}, u32[]{:S(2)}) %collective-permute-start.8) | collective-permute-done | bytes 131104 | tf_op jit(solution)/shard_map/ppermute | solution.py:11
  43.0 0.9 fusion.5
  43.8 0.2 abs_reduce_fusion
  44.0 0.1 select_convert_fusion
  44.1 0.1 multiply_convert_fusion
  44.2 0.8 pad_maximum_fusion.1
  45.0 9.0 %collective-permute-start.9 = (f16[64,2176]{1,0:T(8,128)(2,1)}, f16[64,2176]{1,0:T(8,128)(2,1)S(1)}, u32[]{:S(2)}, u32[]{:S(2)}) collective-permute-start(f16[64,2176]{1,0:T(8,128)(2,1)} %pad_maximum_fusion.1), channel_id=1, source_target_pairs={{0,2},{1,3},{2,4},{3,5},{4,6},{5,7},{8,10},{9,11},{10,12},{11,13},... | collective-permute-start | bytes 835592 | tf_op jit(solution)/shard_map/ppermute | solution.py:11
  54.0 1.3 %collective-permute-start.10 = (f16[64,2176]{1,0:T(8,128)(2,1)}, f16[64,2176]{1,0:T(8,128)(2,1)S(1)}, u32[]{:S(2)}, u32[]{:S(2)}) collective-permute-start(f16[64,2176]{1,0:T(8,128)(2,1)} %pad_maximum_fusion.1), channel_id=1, source_target_pairs={{2,0},{3,1},{4,2},{5,3},{6,4},{7,5},{10,8},{11,9},{12,10},{13,11},... | collective-permute-start | bytes 835592 | tf_op jit(solution)/shard_map/ppermute | solution.py:11
  55.3 3.8 %collective-permute-done.9 = f16[64,2176]{1,0:T(8,128)(2,1)S(1)} collective-permute-done((f16[64,2176]{1,0:T(8,128)(2,1)}, f16[64,2176]{1,0:T(8,128)(2,1)S(1)}, u32[]{:S(2)}, u32[]{:S(2)}) %collective-permute-start.9) | collective-permute-done | bytes 278560 | tf_op jit(solution)/shard_map/ppermute | solution.py:11
  59.1 0.1 exponential_reduce_fusion.2
  59.2 0.1 slice.142
  59.3 0.1 copy.29
  59.4 3.7 %collective-permute-done.10 = f16[64,2176]{1,0:T(8,128)(2,1)S(1)} collective-permute-done((f16[64,2176]{1,0:T(8,128)(2,1)}, f16[64,2176]{1,0:T(8,128)(2,1)S(1)}, u32[]{:S(2)}, u32[]{:S(2)}) %collective-permute-start.10) | collective-permute-done | bytes 278560 | tf_op jit(solution)/shard_map/ppermute | solution.py:11
  63.1 0.1 exponential_reduce_fusion.1
  63.3 0.2 multiply_add_fusion.1
  63.6 0.1 broadcast_select_fusion
  63.7 0.7 collective-permute-start.12
  64.4 0.2 exponential_reduce_fusion
  64.6 0.9 collective-permute-done.11
  65.5 0.3 reduce-precision_convert_fusion
  65.9 0.7 fusion.3
  66.6 1.6 %collective-permute-start.13 = (f32[64,512]{1,0:T(8,128)S(1)}, f32[64,512]{1,0:T(8,128)S(1)}, u32[]{:S(2)}, u32[]{:S(2)}) collective-permute-start(f32[64,512]{1,0:T(8,128)S(1)} %slice_add_fusion.2), channel_id=1, source_target_pairs={{0,8},{1,17},{2,10},{3,19},{4,12},{5,21},{6,14},{7,23},{8,0},{9,25... | collective-permute-start | bytes 393224 | tf_op jit(solution)/shard_map/ppermute | solution.py:11
  68.2 3.5 %collective-permute-done.13 = f32[64,512]{1,0:T(8,128)S(1)} collective-permute-done((f32[64,512]{1,0:T(8,128)S(1)}, f32[64,512]{1,0:T(8,128)S(1)}, u32[]{:S(2)}, u32[]{:S(2)}) %collective-permute-start.13) | collective-permute-done | bytes 131104 | tf_op jit(solution)/shard_map/ppermute | solution.py:11
  71.7 1.6 %collective-permute-start.14 = (f32[64,512]{1,0:T(8,128)S(1)}, f32[64,512]{1,0:T(8,128)S(1)}, u32[]{:S(2)}, u32[]{:S(2)}) collective-permute-start(f32[64,512]{1,0:T(8,128)S(1)} %fusion.48), channel_id=1, source_target_pairs={{0,16},{1,9},{2,18},{3,11},{4,20},{5,13},{6,22},{7,15},{8,24},{9,1... | collective-permute-start | bytes 393224 | tf_op jit(solution)/shard_map/ppermute | solution.py:11
  73.3 4.2 %collective-permute-done.14 = f32[64,512]{1,0:T(8,128)S(1)} collective-permute-done((f32[64,512]{1,0:T(8,128)S(1)}, f32[64,512]{1,0:T(8,128)S(1)}, u32[]{:S(2)}, u32[]{:S(2)}) %collective-permute-start.14) | collective-permute-done | bytes 131104 | tf_op jit(solution)/shard_map/ppermute | solution.py:11
  77.4 0.2 fusion.27
  77.6 4.5 %collective-permute-start.15 = (f32[64,4]{0,1:T(4,128)S(1)}, f32[64,4]{0,1:T(4,128)S(1)}, u32[]{:S(2)}, u32[]{:S(2)}) collective-permute-start(f32[64,4]{0,1:T(4,128)S(1)} %pad_maximum_fusion.3), channel_id=1, source_target_pairs={{0,1},{1,0},{2,3},{3,2},{4,5},{5,4},{6,7},{7,6},{8,9},{9,8},{10,11... | collective-permute-start | bytes 3080 | tf_op jit(solution)/shard_map/ppermute | solution.py:11
  82.1 0.8 collective-permute-done.15
  82.9 3.1 %collective-permute-start.16 = (f32[64,4]{0,1:T(4,128)S(1)}, f32[64,4]{0,1:T(4,128)S(1)}, u32[]{:S(2)}, u32[]{:S(2)}) collective-permute-start(f32[64,4]{0,1:T(4,128)S(1)} %fusion.46), channel_id=1, source_target_pairs={{0,2},{1,3},{2,0},{3,1},{4,6},{5,7},{6,4},{7,5},{8,10},{9,11},{10,... | collective-permute-start | bytes 3080 | tf_op jit(solution)/shard_map/ppermute | solution.py:11
  86.0 1.6 %collective-permute-done.16 = f32[64,4]{0,1:T(4,128)S(1)} collective-permute-done((f32[64,4]{0,1:T(4,128)S(1)}, f32[64,4]{0,1:T(4,128)S(1)}, u32[]{:S(2)}, u32[]{:S(2)}) %collective-permute-start.16) | collective-permute-done | bytes 1056 | tf_op jit(solution)/shard_map/ppermute | solution.py:11
  87.6 1.9 %collective-permute-start.17 = (f32[64,4]{0,1:T(4,128)S(1)}, f32[64,4]{0,1:T(4,128)S(1)}, u32[]{:S(2)}, u32[]{:S(2)}) collective-permute-start(f32[64,4]{0,1:T(4,128)S(1)} %fusion.47), channel_id=1, source_target_pairs={{0,4},{1,5},{2,6},{3,7},{4,0},{5,1},{6,2},{7,3},{8,12},{9,13},{10,... | collective-permute-start | bytes 3080 | tf_op jit(solution)/shard_map/ppermute | solution.py:11
  89.5 2.6 %collective-permute-done.17 = f32[64,4]{0,1:T(4,128)S(1)} collective-permute-done((f32[64,4]{0,1:T(4,128)S(1)}, f32[64,4]{0,1:T(4,128)S(1)}, u32[]{:S(2)}, u32[]{:S(2)}) %collective-permute-start.17) | collective-permute-done | bytes 1056 | tf_op jit(solution)/shard_map/ppermute | solution.py:11
  92.2 0.9 subtract_bitcast_fusion
  (37 shorter events, 0.6 us)
Async XLA Ops:
  0.6 12.8 %copy-start = (bf16[2048,512]{1,0:T(8,128)(2,1)S(1)}, bf16[2048,512]{1,0:T(8,128)(2,1)}, u32[]{:S(2)}) copy-start(bf16[2048,512]{1,0:T(8,128)(2,1)} %param.4) | copy-start | bytes 6291460
  1.4 3.7 %collective-permute-start = (f32[8,128]{1,0:T(8,128)S(1)}, f32[8,128]{1,0:T(8,128)S(1)}, u32[]{:S(2)}, u32[]{:S(2)}) collective-permute-start(f32[8,128]{1,0:T(8,128)S(1)} %broadcast_in_dim.70), channel_id=1, source_target_pairs={{0,1},{1,0},{2,3},{3,2},{4,5},{5,4},{6,7},{7,6},{8,9},{9,8},{10,11... | collective-permute-start | bytes 12296 | tf_op jit(solution)/shard_map/ppermute | solution.py:11
  5.7 4.1 %collective-permute-start.1 = (f32[2,512]{1,0:T(2,128)S(1)}, f32[2,512]{1,0:T(2,128)S(1)}, u32[]{:S(2)}, u32[]{:S(2)}) collective-permute-start(f32[2,512]{1,0:T(2,128)S(1)} %pad_maximum_fusion.2), channel_id=1, source_target_pairs={{0,8},{1,17},{2,10},{3,19},{4,12},{5,21},{6,14},{7,23},{8,0},{9,25... | collective-permute-start | bytes 12296 | tf_op jit(solution)/shard_map/ppermute | solution.py:11
  9.8 3.6 %collective-permute-start.2 = (f32[2,512]{1,0:T(2,128)S(1)}, f32[2,512]{1,0:T(2,128)S(1)}, u32[]{:S(2)}, u32[]{:S(2)}) collective-permute-start(f32[2,512]{1,0:T(2,128)S(1)} %add.107), channel_id=1, source_target_pairs={{0,16},{1,9},{2,18},{3,11},{4,20},{5,13},{6,22},{7,15},{8,24},{9,1... | collective-permute-start | bytes 12296 | tf_op jit(solution)/shard_map/ppermute | solution.py:11
  14.8 8.3 %collective-permute-start.3 = (f16[64,2176]{1,0:T(8,128)(2,1)S(1)}, f16[64,2176]{1,0:T(8,128)(2,1)S(1)}, u32[]{:S(2)}, u32[]{:S(2)}) collective-permute-start(f16[64,2176]{1,0:T(8,128)(2,1)S(1)} %pad_maximum_fusion), channel_id=1, source_target_pairs={{0,2},{1,3},{2,4},{3,5},{4,6},{5,7},{8,10},{9,11},{10,12},{11,13},... | collective-permute-start | bytes 835592 | tf_op jit(solution)/shard_map/ppermute | solution.py:11
  20.2 8.4 %collective-permute-start.4 = (f16[64,2176]{1,0:T(8,128)(2,1)S(1)}, f16[64,2176]{1,0:T(8,128)(2,1)S(1)}, u32[]{:S(2)}, u32[]{:S(2)}) collective-permute-start(f16[64,2176]{1,0:T(8,128)(2,1)S(1)} %pad_maximum_fusion), channel_id=1, source_target_pairs={{2,0},{3,1},{4,2},{5,3},{6,4},{7,5},{10,8},{11,9},{12,10},{13,11},... | collective-permute-start | bytes 835592 | tf_op jit(solution)/shard_map/ppermute | solution.py:11
  29.0 2.0 %collective-permute-start.5 = (f32[64,2048]{1,0:T(8,128)S(1)}, f32[64,2048]{1,0:T(8,128)S(1)}, u32[]{:S(2)}, u32[]{:S(2)}) collective-permute-start(f32[64,2048]{1,0:T(8,128)S(1)} %multiply_add_fusion.3), channel_id=1, source_target_pairs={{0,1},{1,0},{2,3},{3,2},{4,5},{5,4},{6,7},{7,6},{8,9},{9,8},{10,11... | collective-permute-start | bytes 1572872 | tf_op jit(solution)/shard_map/ppermute | solution.py:11
  29.2 0.7 collective-permute-start.6
  32.1 5.0 %collective-permute-start.7 = (f32[64,512]{1,0:T(8,128)S(1)}, f32[64,512]{1,0:T(8,128)S(1)}, u32[]{:S(2)}, u32[]{:S(2)}) collective-permute-start(f32[64,512]{1,0:T(8,128)S(1)} %slice_add_fusion.3), channel_id=1, source_target_pairs={{0,8},{1,17},{2,10},{3,19},{4,12},{5,21},{6,14},{7,23},{8,0},{9,25... | collective-permute-start | bytes 393224 | tf_op jit(solution)/shard_map/ppermute | solution.py:11
  37.1 5.8 %collective-permute-start.8 = (f32[64,512]{1,0:T(8,128)S(1)}, f32[64,512]{1,0:T(8,128)S(1)}, u32[]{:S(2)}, u32[]{:S(2)}) collective-permute-start(f32[64,512]{1,0:T(8,128)S(1)} %fusion.49), channel_id=1, source_target_pairs={{0,16},{1,9},{2,18},{3,11},{4,20},{5,13},{6,22},{7,15},{8,24},{9,1... | collective-permute-start | bytes 393224 | tf_op jit(solution)/shard_map/ppermute | solution.py:11
  45.0 14.1 %collective-permute-start.9 = (f16[64,2176]{1,0:T(8,128)(2,1)}, f16[64,2176]{1,0:T(8,128)(2,1)S(1)}, u32[]{:S(2)}, u32[]{:S(2)}) collective-permute-start(f16[64,2176]{1,0:T(8,128)(2,1)} %pad_maximum_fusion.1), channel_id=1, source_target_pairs={{0,2},{1,3},{2,4},{3,5},{4,6},{5,7},{8,10},{9,11},{10,12},{11,13},... | collective-permute-start | bytes 835592 | tf_op jit(solution)/shard_map/ppermute | solution.py:11
  54.0 9.2 %collective-permute-start.10 = (f16[64,2176]{1,0:T(8,128)(2,1)}, f16[64,2176]{1,0:T(8,128)(2,1)S(1)}, u32[]{:S(2)}, u32[]{:S(2)}) collective-permute-start(f16[64,2176]{1,0:T(8,128)(2,1)} %pad_maximum_fusion.1), channel_id=1, source_target_pairs={{2,0},{3,1},{4,2},{5,3},{6,4},{7,5},{10,8},{11,9},{12,10},{13,11},... | collective-permute-start | bytes 835592 | tf_op jit(solution)/shard_map/ppermute | solution.py:11
  63.5 2.0 %collective-permute-start.11 = (f32[64,2048]{1,0:T(8,128)S(1)}, f32[64,2048]{1,0:T(8,128)S(1)}, u32[]{:S(2)}, u32[]{:S(2)}) collective-permute-start(f32[64,2048]{1,0:T(8,128)S(1)} %multiply_add_fusion.1), channel_id=1, source_target_pairs={{0,1},{1,0},{2,3},{3,2},{4,5},{5,4},{6,7},{7,6},{8,9},{9,8},{10,11... | collective-permute-start | bytes 1572872 | tf_op jit(solution)/shard_map/ppermute | solution.py:11
  63.7 0.7 collective-permute-start.12
  65.9 11.5 %copy-start.1 = (f32[512,64]{0,1:T(8,128)S(1)}, f32[512,64]{0,1:T(8,128)}, u32[]{:S(2)}) copy-start(f32[512,64]{0,1:T(8,128)} %param.6) | copy-start | bytes 393220
  65.9 26.2 %copy-start.2 = (f32[64]{0:T(128)S(1)}, f32[64]{0:T(128)}, u32[]{:S(2)}) copy-start(f32[64]{0:T(128)} %param.7) | copy-start | bytes 772
  66.6 5.0 %collective-permute-start.13 = (f32[64,512]{1,0:T(8,128)S(1)}, f32[64,512]{1,0:T(8,128)S(1)}, u32[]{:S(2)}, u32[]{:S(2)}) collective-permute-start(f32[64,512]{1,0:T(8,128)S(1)} %slice_add_fusion.2), channel_id=1, source_target_pairs={{0,8},{1,17},{2,10},{3,19},{4,12},{5,21},{6,14},{7,23},{8,0},{9,25... | collective-permute-start | bytes 393224 | tf_op jit(solution)/shard_map/ppermute | solution.py:11
  71.7 5.8 %collective-permute-start.14 = (f32[64,512]{1,0:T(8,128)S(1)}, f32[64,512]{1,0:T(8,128)S(1)}, u32[]{:S(2)}, u32[]{:S(2)}) collective-permute-start(f32[64,512]{1,0:T(8,128)S(1)} %fusion.48), channel_id=1, source_target_pairs={{0,16},{1,9},{2,18},{3,11},{4,20},{5,13},{6,22},{7,15},{8,24},{9,1... | collective-permute-start | bytes 393224 | tf_op jit(solution)/shard_map/ppermute | solution.py:11
  77.6 5.3 %collective-permute-start.15 = (f32[64,4]{0,1:T(4,128)S(1)}, f32[64,4]{0,1:T(4,128)S(1)}, u32[]{:S(2)}, u32[]{:S(2)}) collective-permute-start(f32[64,4]{0,1:T(4,128)S(1)} %pad_maximum_fusion.3), channel_id=1, source_target_pairs={{0,1},{1,0},{2,3},{3,2},{4,5},{5,4},{6,7},{7,6},{8,9},{9,8},{10,11... | collective-permute-start | bytes 3080 | tf_op jit(solution)/shard_map/ppermute | solution.py:11
  82.9 4.7 %collective-permute-start.16 = (f32[64,4]{0,1:T(4,128)S(1)}, f32[64,4]{0,1:T(4,128)S(1)}, u32[]{:S(2)}, u32[]{:S(2)}) collective-permute-start(f32[64,4]{0,1:T(4,128)S(1)} %fusion.46), channel_id=1, source_target_pairs={{0,2},{1,3},{2,0},{3,1},{4,6},{5,7},{6,4},{7,5},{8,10},{9,11},{10,... | collective-permute-start | bytes 3080 | tf_op jit(solution)/shard_map/ppermute | solution.py:11
  87.6 4.5 %collective-permute-start.17 = (f32[64,4]{0,1:T(4,128)S(1)}, f32[64,4]{0,1:T(4,128)S(1)}, u32[]{:S(2)}, u32[]{:S(2)}) collective-permute-start(f32[64,4]{0,1:T(4,128)S(1)} %fusion.47), channel_id=1, source_target_pairs={{0,4},{1,5},{2,6},{3,7},{4,0},{5,1},{6,2},{7,3},{8,12},{9,13},{10,... | collective-permute-start | bytes 3080 | tf_op jit(solution)/shard_map/ppermute | solution.py:11

commit v3 on v1

v3 whole, which is shorter than its diff:
```python
import jax
import jax.numpy as jnp
from jax import lax
from jax.sharding import PartitionSpec as P


AUX = 128


def swap(value, axis, bits):
    return lax.ppermute(value, axis, [(i, i ^ bits) for i in range(lax.axis_size(axis))])


def crossing(value, rising):
    count = lax.axis_size("snp")
    pairs = []
    for i in range(count):
        target = i + 2 if i % 2 == rising else i - 2
        pairs.append((i, target if 0 <= target < count else i ^ 1))
    return lax.ppermute(value, "snp", pairs)


def forward(value):
    count = lax.axis_size("snp")
    pairs = [(i, i + 1) for i in range(1, count - 1, 2)] + [(i, i - 1) for i in range(2, count, 2)]
    return lax.ppermute(value, "snp", pairs)


def group_sum(value, axis, bits):
    for bit in bits:
        if isinstance(bit, int):
            value = value + swap(value, axis, bit)
        else:
            low, high = bit
            one, two, three = (swap(value, axis, k) for k in (low, high, low + high))
            value = (value + one) + (two + three)
    return value


def stages(bits):
    return [(bits[k], bits[k + 1]) if k + 1 < len(bits) else bits[k] for k in range(0, len(bits), 2)]


def axis_bits(axis):
    return [1 << k for k in range(lax.axis_size(axis).bit_length() - 1)]


def samp_sum(value):
    return group_sum(value, "samp", stages(axis_bits("samp")))


def snp_sum(value):
    bits = axis_bits("snp")
    return group_sum(value, "snp", bits[:1] + stages(bits[1:]))


def two_terms(value):
    high = lax.reduce_precision(value, 8, 7)
    low = value - high
    return jnp.concatenate([high.astype(jnp.bfloat16), low.astype(jnp.bfloat16)], 0)


def product(value, scaled, contract):
    rows = value.shape[0]
    both = lax.dot_general(
        two_terms(value), scaled, (((1,), (contract,)), ((), ())), preferred_element_type=jnp.float32
    )
    return both[:rows] + both[rows:]


def pack(value, width):
    peak = jnp.maximum(jnp.max(jnp.abs(value), 1, keepdims=True), 1e-30)
    exponent = jnp.floor(jnp.log2(peak))
    coded = (value * jnp.exp2(-exponent)).astype(jnp.float16)
    lane = lax.broadcasted_iota(jnp.int32, (value.shape[0], AUX), 1)
    extra = jnp.where(lane == 0, exponent, jnp.where(lane == 1, width, 0.0)).astype(jnp.float16)
    return jnp.concatenate([coded, extra], 1)


def unpack(coded):
    count = coded.shape[1] - AUX
    exponent = coded[:, count : count + 1].astype(jnp.float32)
    width = coded[:, count + 1 : count + 2].astype(jnp.float32)
    return coded[:, :count].astype(jnp.float32), jnp.exp2(exponent), width


def window(own, width, partner_width, place):
    odd, has_below, has_above, has_far = place
    coded = pack(own, width)
    outer_coded = crossing(coded, 1)
    inner_coded = crossing(coded, 0)
    far_coded = forward(outer_coded)
    inner_coded, far_coded = lax.optimization_barrier((inner_coded, far_coded))
    outer, outer_scale, outer_width = unpack(outer_coded)
    inner, inner_scale, inner_width = unpack(inner_coded)
    far, far_scale, far_width = unpack(far_coded)
    at_least = lambda value, least, use: jnp.where((value >= least) & use, 1.0, 0.0)
    choose = lambda even_case, odd_case: jnp.where(odd, odd_case, even_case)
    outer_use, inner_use = choose(has_above, has_below), choose(has_below, has_above)
    give_own = at_least(choose(width, partner_width), 1, True)
    give_outer = outer_scale * at_least(choose(partner_width, outer_width), 1, outer_use)
    give_inner = inner_scale * at_least(choose(inner_width, partner_width), 3, inner_use)
    take_outer = outer_scale * at_least(choose(width, outer_width), 2, outer_use)
    take_inner = inner_scale * at_least(choose(inner_width, width), 2, inner_use)
    take_far = far_scale * at_least(choose(far_width, width), 3, has_far)
    given = swap(own * give_own + outer * give_outer + inner * give_inner, "snp", 1)
    return own + outer * take_outer + inner * take_inner + given + far * take_far


def shards(dosage, band_width, marginal, penalty):
    groups, count = lax.axis_size("samp"), lax.axis_size("snp")
    samples = dosage.shape[0] * groups
    index = lax.axis_index("snp")
    odd = (index & 1) == 1
    has_below, has_above = index >= 2, index < count - 2
    place = (odd, has_below, has_above, jnp.where(odd, index < count - 3, index >= 3))
    genotype = dosage.astype(jnp.float32)
    sums = jnp.stack([jnp.sum(genotype, 0), jnp.sum(genotype * genotype, 0)])
    width = band_width.astype(jnp.float32).reshape(1, 1)
    sums, wide = lax.optimization_barrier((sums, jnp.broadcast_to(width, (8, 128))))
    partner_wide = swap(wide, "snp", 1)
    sums, partner_wide = lax.optimization_barrier((samp_sum(sums), partner_wide))
    partner_width = partner_wide[:1, :1]
    center = sums[0] / samples
    spread = sums[1] / samples - center * center
    scaled = ((genotype - center) * lax.rsqrt(spread + 1e-05)).astype(jnp.bfloat16)
    start = marginal.T
    shrink = penalty[:, None]
    dot = lambda a, b: jnp.sum(a * b, 1, keepdims=True)

    def operate(value):
        spanned = product(value, scaled, 1)
        mixed = window(spanned, width, partner_width, place)
        return samp_sum(product(mixed, scaled, 0)) / samples, dot(spanned, mixed) / samples

    first, _ = operate(start)
    second, curved = operate(first)
    parts = [dot(start, start) / groups, dot(start, first) / groups, dot(first, first) / groups, curved]
    parts = samp_sum(snp_sum(jnp.concatenate(parts, 1)))
    bb, bw, ww, wu = (parts[:, k : k + 1] for k in range(4))
    ratio = bw / bb
    step = 1.0 / (ratio + shrink)
    norm = step * step * (ww - ratio * bw)
    bend = norm / bb
    curve = step * step * (ratio * (ratio * bw - 2.0 * ww) + wu) + shrink * norm - bend * norm / step
    step2 = jnp.where(curve > 0, norm / curve, 0.0)
    rest = step * (ratio * start - first)
    direction = rest + bend * start
    image = step * (ratio * first - second) + bend * first + shrink * direction
    effects = step * start + step2 * direction
    residual = rest - step2 * image
    return (effects.T, residual.T)


def solution(mesh):
    in_specs = (P("samp", "snp"), P("snp"), P("snp", None), P())
    out_specs = (P("snp", None), P("snp", None))
    return jax.shard_map(shards, mesh=mesh, in_specs=in_specs, out_specs=out_specs, check_vma=False)
```

time: 98.8 us -> 90.7 us (0.918)
  waiting for transfers between devices: 49.2 us -> 33 us
  other arithmetic: 8.24 us -> 13.3 us
  starting transfers between devices: 34.1 us -> 37.9 us
    ppermute x18 -> x25, waiting for transfers between devices: 49.2 us -> 33 us  [the longest x19 20.1 us: swap(): lax.ppermute(value, axis, [(i, i ^ bits) for i in range(lax.axis_size(axi...]
    mul x3 -> x6, other arithmetic: 0.03 us -> 3.85 us  [the longest x2 1.75 us: window(): inner_scale * at_least(choose(inner_width, width), 2, inner_use)]
    ppermute x18 -> x25, starting transfers between devices: 34.1 us -> 37.9 us  [the longest x19 32 us: swap(): lax.ppermute(value, axis, [(i, i ^ bits) for i in range(lax.axis_size(axi...]
    convert_element_type x4, other arithmetic: 1.63 us -> 2.66 us  [two_terms(): high.astype(jnp.bfloat16)]
  transfers between devices with their start and end apart: 18 -> 25, of which waited for: 14 -> 15; matrix products, arithmetic and copies ran while one was open for 2% -> 5% of each run, Pallas kernels for 0% -> 0%
where the time goes in v3:
time: 90.7 us; the launch traced here: 90.4 us
  starting transfers between devices  37.9 us (42%)
  waiting for transfers between devices  33 us (36%)
  other arithmetic  13.3 us (15%)
  matrix products  3.01 us (3%)
  between operations  2.42 us (3%)
    ppermute x19, starting transfers between devices, swap(): lax.ppermute(value, axis, [(i, i ^ bits) for i in range(lax.axis_size(axi...  32 us
    ppermute x19, waiting for transfers between devices, swap(): lax.ppermute(value, axis, [(i, i ^ bits) for i in range(lax.axis_size(axi...  20.1 us
    ppermute x4, waiting for transfers between devices, crossing(): return lax.ppermute(value, 'snp', pairs)  12.9 us
    ppermute x4, starting transfers between devices, crossing(): return lax.ppermute(value, 'snp', pairs)  4.57 us
    dot_general x4, matrix products, product(): lax.dot_general(two_terms(value), scaled, (((1,), (contract,)), ((), ()))...  3.01 us
    convert_element_type x4, other arithmetic, two_terms(): high.astype(jnp.bfloat16)  2.66 us
    reduce_sum x1, other arithmetic, shards(): sums = jnp.stack([jnp.sum(genotype, 0), jnp.sum(genotype * genotype, 0)])  2.2 us
  transfers between devices with their start and end apart: 25, of which 15 were waited for; matrix products, arithmetic and copies ran while one was open for 5% of the time, Pallas kernels for 0%

profile of v3, /device:TPU:0, one launch (start us, length us, event | category | flops | bytes accessed | tf_op | source)
XLA Modules:
  0.0 90.4 jit_solution(13277876832402366408)
XLA Ops:
  1.4 2.2 %convert_reduce_fusion = (f32[512]{0:T(512)S(1)}, f32[512]{0:T(512)S(1)}) fusion(bf16[2048,512]{1,0:T(8,128)(2,1)} %param.4), kind=kLoop, calls=%fused_computation.2 | loop fusion | flops 4193280 | bytes 2101248 | tf_op jit(solution)/shard_map/reduce_sum | solution.py:118
  3.7 3.0 %collective-permute-start = (f32[2,512]{1,0:T(2,128)S(1)}, f32[2,512]{1,0:T(2,128)S(1)}, u32[]{:S(2)}, u32[]{:S(2)}) collective-permute-start(f32[2,512]{1,0:T(2,128)S(1)} %pad_maximum_fusion.2), channel_id=1, source_target_pairs={{0,8},{8,0},{16,24},{24,16},{1,9},{9,1},{17,25},{25,17},{2,10},{10... | collective-permute-start | bytes 12296 | tf_op jit(solution)/shard_map/ppermute | solution.py:11
  6.7 1.5 %collective-permute-start.1 = (f32[2,512]{1,0:T(2,128)S(1)}, f32[2,512]{1,0:T(2,128)S(1)}, u32[]{:S(2)}, u32[]{:S(2)}) collective-permute-start(f32[2,512]{1,0:T(2,128)S(1)} %pad_maximum_fusion.2), channel_id=1, source_target_pairs={{0,16},{8,24},{16,0},{24,8},{1,17},{9,25},{17,1},{25,9},{2,18},{10... | collective-permute-start | bytes 12296 | tf_op jit(solution)/shard_map/ppermute | solution.py:11
  8.2 0.9 %reduce-precision_convert_fusion.3 = (bf16[64,512]{1,0:T(8,128)(2,1)S(1)}, bf16[64,512]{1,0:T(8,128)(2,1)S(1)}) fusion(f32[512,64]{0,1:T(8,128)} %param.6), kind=kLoop, calls=%fused_computation.54 | loop fusion | flops 131072 | bytes 262144 | tf_op jit(solution)/shard_map/convert_element_type | solution.py:60
  9.2 1.1 %collective-permute-done.1 = f32[2,512]{1,0:T(2,128)S(1)} collective-permute-done((f32[2,512]{1,0:T(2,128)S(1)}, f32[2,512]{1,0:T(2,128)S(1)}, u32[]{:S(2)}, u32[]{:S(2)}) %collective-permute-start.1) | collective-permute-done | bytes 4128 | tf_op jit(solution)/shard_map/ppermute | solution.py:11
  10.3 2.4 %collective-permute-done.2 = f32[2,512]{1,0:T(2,128)S(1)} collective-permute-done((f32[2,512]{1,0:T(2,128)S(1)}, f32[2,512]{1,0:T(2,128)S(1)}, u32[]{:S(2)}, u32[]{:S(2)}) %collective-permute-start.2) | collective-permute-done | bytes 4128 | tf_op jit(solution)/shard_map/ppermute | solution.py:11
  12.7 0.9 fusion.9
  13.6 0.2 abs_reduce_fusion.1
  13.8 0.1 multiply_convert_fusion.1
  14.0 0.8 pad_maximum_fusion
  14.7 2.0 %collective-permute-start.5 = (f16[64,2176]{1,0:T(8,128)(2,1)}, f16[64,2176]{1,0:T(8,128)(2,1)S(1)}, u32[]{:S(2)}, u32[]{:S(2)}) collective-permute-start(f16[64,2176]{1,0:T(8,128)(2,1)} %pad_maximum_fusion), channel_id=1, source_target_pairs={{0,2},{1,0},{2,4},{3,1},{4,6},{5,3},{6,7},{7,5},{8,10},{9,8},{10,1... | collective-permute-start | bytes 835592 | tf_op jit(solution)/shard_map/ppermute | solution.py:20
  16.8 6.2 %collective-permute-done.4 = f16[64,2176]{1,0:T(8,128)(2,1)S(1)} collective-permute-done((f16[64,2176]{1,0:T(8,128)(2,1)}, f16[64,2176]{1,0:T(8,128)(2,1)S(1)}, u32[]{:S(2)}, u32[]{:S(2)}) %collective-permute-start.4) | collective-permute-done | bytes 278560 | tf_op jit(solution)/shard_map/ppermute | solution.py:20
  22.9 0.7 collective-permute-start.6
  23.6 0.6 slice.109
  24.9 0.9 multiply_reduce_fusion.11
  25.8 0.9 multiply_reduce_fusion.10
  26.7 1.0 %fusion.16 = f32[64,2048]{1,0:T(8,128)} fusion(f32[64,2048]{1,0:T(8,128)S(1)} %get-tuple-element.49, f32[64]{0:T(128)S(1)} %get-tuple-element.27, f32[64]{0:T(128)S(1)} %get-tuple-element.25, f32[]{:T(128)} %bitcast.9, f16[64,2176]{1,0:T(8,128)(2,1)S(1)} %collective-permute-done.4, f16[64,2176]{1,0:T(8,128)(2,1)S(1)} %collective-permute-done.5), kind=kLoop, calls=%fused_computation.27 | loop fusion | flops 917504 | bytes 1573380 | tf_op jit(solution)/shard_map/add | solution.py:106
  27.7 4.9 %collective-permute-start.7 = (f32[64,2048]{1,0:T(8,128)}, f32[64,2048]{1,0:T(8,128)}, u32[]{:S(2)}, u32[]{:S(2)}) collective-permute-start(f32[64,2048]{1,0:T(8,128)} %fusion.16), channel_id=1, source_target_pairs={{0,1},{1,0},{2,3},{3,2},{4,5},{5,4},{6,7},{7,6},{8,9},{9,8},{10,11... | collective-permute-start | bytes 1572872 | tf_op jit(solution)/shard_map/ppermute | solution.py:11
  32.7 0.2 multiply_reduce_fusion.7
  32.8 1.7 %collective-permute-done.7 = f32[64,2048]{1,0:T(8,128)} collective-permute-done((f32[64,2048]{1,0:T(8,128)}, f32[64,2048]{1,0:T(8,128)}, u32[]{:S(2)}, u32[]{:S(2)}) %collective-permute-start.7) | collective-permute-done | bytes 524320 | tf_op jit(solution)/shard_map/ppermute | solution.py:11
  34.5 1.4 %reduce-precision_convert_fusion.1 = (bf16[64,2048]{1,0:T(8,128)(2,1)S(1)}, f32[64,2048]{1,0:T(8,128)S(1)}) fusion(f32[64]{0:T(128)S(1)} %multiply_reduce_fusion.7, f16[64,2176]{1,0:T(8,128)(2,1)S(1)} %collective-permute-done.6, f32[64,2048]{1,0:T(8,128)} %collective-permute-done.7, f32[64]{0:T(128)S(1)} %get-tuple-element.26, ...), kind=kLoop, calls=%fused_computation.9 | loop fusion | flops 1572864 | bytes 2622208 | tf_op jit(solution)/shard_map/convert_element_type | solution.py:60
  36.0 0.7 fusion.7
  36.7 1.9 %collective-permute-start.10 = (f32[64,512]{1,0:T(8,128)S(1)}, f32[64,512]{1,0:T(8,128)S(1)}, u32[]{:S(2)}, u32[]{:S(2)}) collective-permute-start(f32[64,512]{1,0:T(8,128)S(1)} %slice_add_fusion.3), channel_id=1, source_target_pairs={{0,24},{8,16},{16,8},{24,0},{1,25},{9,17},{17,9},{25,1},{2,26},{10... | collective-permute-start | bytes 393224 | tf_op jit(solution)/shard_map/ppermute | solution.py:11
  38.6 0.5 collective-permute-start.8
  39.1 1.2 %collective-permute-start.9 = (f32[64,512]{1,0:T(8,128)S(1)}, f32[64,512]{1,0:T(8,128)S(1)}, u32[]{:S(2)}, u32[]{:S(2)}) collective-permute-start(f32[64,512]{1,0:T(8,128)S(1)} %slice_add_fusion.3), channel_id=1, source_target_pairs={{0,16},{8,24},{16,0},{24,8},{1,17},{9,25},{17,1},{25,9},{2,18},{10... | collective-permute-start | bytes 393224 | tf_op jit(solution)/shard_map/ppermute | solution.py:11
  40.3 3.7 %collective-permute-done.10 = f32[64,512]{1,0:T(8,128)S(1)} collective-permute-done((f32[64,512]{1,0:T(8,128)S(1)}, f32[64,512]{1,0:T(8,128)S(1)}, u32[]{:S(2)}, u32[]{:S(2)}) %collective-permute-start.10) | collective-permute-done | bytes 131104 | tf_op jit(solution)/shard_map/ppermute | solution.py:11
  44.0 1.7 %collective-permute-done.8 = f32[64,512]{1,0:T(8,128)S(1)} collective-permute-done((f32[64,512]{1,0:T(8,128)S(1)}, f32[64,512]{1,0:T(8,128)S(1)}, u32[]{:S(2)}, u32[]{:S(2)}) %collective-permute-start.8) | collective-permute-done | bytes 131104 | tf_op jit(solution)/shard_map/ppermute | solution.py:11
  45.6 0.6 collective-permute-done.9
  46.2 0.2 fusion.39
  46.4 0.8 fusion.5
  47.3 0.2 abs_reduce_fusion
  47.5 0.1 multiply_convert_fusion
  47.8 2.5 %collective-permute-start.12 = (f16[64,2176]{1,0:T(8,128)(2,1)S(1)}, f16[64,2176]{1,0:T(8,128)(2,1)S(1)}, u32[]{:S(2)}, u32[]{:S(2)}) collective-permute-start(f16[64,2176]{1,0:T(8,128)(2,1)S(1)} %pad_maximum_fusion.1), channel_id=1, source_target_pairs={{0,2},{1,0},{2,4},{3,1},{4,6},{5,3},{6,7},{7,5},{8,10},{9,8},{10,1... | collective-permute-start | bytes 835592 | tf_op jit(solution)/shard_map/ppermute | solution.py:20
  50.3 6.7 %collective-permute-done.11 = f16[64,2176]{1,0:T(8,128)(2,1)S(1)} collective-permute-done((f16[64,2176]{1,0:T(8,128)(2,1)S(1)}, f16[64,2176]{1,0:T(8,128)(2,1)S(1)}, u32[]{:S(2)}, u32[]{:S(2)}) %collective-permute-start.11) | collective-permute-done | bytes 278560 | tf_op jit(solution)/shard_map/ppermute | solution.py:20
  57.0 0.7 collective-permute-start.13
  57.7 0.9 multiply_reduce_fusion.6
  58.5 0.9 multiply_reduce_fusion.5
  59.4 0.2 fusion.22
  59.7 7.1 %collective-permute-start.14 = (f32[64,2048]{1,0:T(8,128)S(1)}, f32[64,2048]{1,0:T(8,128)S(1)}, u32[]{:S(2)}, u32[]{:S(2)}) collective-permute-start(f32[64,2048]{1,0:T(8,128)S(1)} %fusion.22), channel_id=1, source_target_pairs={{0,1},{1,0},{2,3},{3,2},{4,5},{5,4},{6,7},{7,6},{8,9},{9,8},{10,11... | collective-permute-start | bytes 1572872 | tf_op jit(solution)/shard_map/ppermute | solution.py:11
  66.7 0.2 multiply_reduce_fusion.2
  66.9 1.4 %collective-permute-done.14 = f32[64,2048]{1,0:T(8,128)S(1)} collective-permute-done((f32[64,2048]{1,0:T(8,128)S(1)}, f32[64,2048]{1,0:T(8,128)S(1)}, u32[]{:S(2)}, u32[]{:S(2)}) %collective-permute-start.14) | collective-permute-done | bytes 524320 | tf_op jit(solution)/shard_map/ppermute | solution.py:11
  68.3 0.3 reduce-precision_convert_fusion
  68.6 0.2 fusion.24
  68.8 0.1 copy.19
  68.9 0.4 collective-permute-start.15
  69.3 0.1 copy.20
  69.4 0.8 collective-permute-done.15
  70.2 2.0 %collective-permute-start.16 = (f32[64,4]{1,0:T(8,128)S(1)}, f32[64,4]{1,0:T(8,128)S(1)}, u32[]{:S(2)}, u32[]{:S(2)}) collective-permute-start(f32[64,4]{1,0:T(8,128)S(1)} %add.147), channel_id=1, source_target_pairs={{0,2},{1,3},{2,0},{3,1},{4,6},{5,7},{6,4},{7,5},{8,10},{9,11},{10,... | collective-permute-start | bytes 3080 | tf_op jit(solution)/shard_map/ppermute | solution.py:11
  72.1 0.8 collective-permute-start.17
  72.9 1.6 %collective-permute-start.18 = (f32[64,4]{1,0:T(8,128)S(1)}, f32[64,4]{1,0:T(8,128)S(1)}, u32[]{:S(2)}, u32[]{:S(2)}) collective-permute-start(f32[64,4]{1,0:T(8,128)S(1)} %add.147), channel_id=1, source_target_pairs={{0,6},{1,7},{2,4},{3,5},{4,2},{5,3},{6,0},{7,1},{8,14},{9,15},{10,... | collective-permute-start | bytes 3080 | tf_op jit(solution)/shard_map/ppermute | solution.py:11
  74.6 0.7 fusion.3
  75.2 2.0 %collective-permute-done.17 = f32[64,4]{1,0:T(8,128)S(1)} collective-permute-done((f32[64,4]{1,0:T(8,128)S(1)}, f32[64,4]{1,0:T(8,128)S(1)}, u32[]{:S(2)}, u32[]{:S(2)}) %collective-permute-start.17) | collective-permute-done | bytes 1056 | tf_op jit(solution)/shard_map/ppermute | solution.py:11
  77.3 1.4 %collective-permute-done.18 = f32[64,4]{1,0:T(8,128)S(1)} collective-permute-done((f32[64,4]{1,0:T(8,128)S(1)}, f32[64,4]{1,0:T(8,128)S(1)}, u32[]{:S(2)}, u32[]{:S(2)}) %collective-permute-start.18) | collective-permute-done | bytes 1056 | tf_op jit(solution)/shard_map/ppermute | solution.py:11
  78.7 0.5 collective-permute-start.19
  79.2 0.9 collective-permute-start.20
  80.1 2.1 %collective-permute-start.21 = (f32[64,4]{1,0:T(8,128)S(1)}, f32[64,4]{1,0:T(8,128)S(1)}, u32[]{:S(2)}, u32[]{:S(2)}) collective-permute-start(f32[64,4]{1,0:T(8,128)S(1)} %add_add_fusion.2), channel_id=1, source_target_pairs={{0,24},{8,16},{16,8},{24,0},{1,25},{9,17},{17,9},{25,1},{2,26},{10... | collective-permute-start | bytes 3080 | tf_op jit(solution)/shard_map/ppermute | solution.py:11
  82.2 0.5 collective-permute-start.22
  82.8 0.9 collective-permute-start.23
  83.7 2.1 %collective-permute-start.24 = (f32[64,512]{1,0:T(8,128)S(1)}, f32[64,512]{1,0:T(8,128)S(1)}, u32[]{:S(2)}, u32[]{:S(2)}) collective-permute-start(f32[64,512]{1,0:T(8,128)S(1)} %slice_add_fusion.2), channel_id=1, source_target_pairs={{0,24},{8,16},{16,8},{24,0},{1,25},{9,17},{17,9},{25,1},{2,26},{10... | collective-permute-start | bytes 393224 | tf_op jit(solution)/shard_map/ppermute | solution.py:11
  85.9 0.2 fusion.68
  86.2 1.2 %collective-permute-done.22 = f32[64,512]{1,0:T(8,128)S(1)} collective-permute-done((f32[64,512]{1,0:T(8,128)S(1)}, f32[64,512]{1,0:T(8,128)S(1)}, u32[]{:S(2)}, u32[]{:S(2)}) %collective-permute-start.22) | collective-permute-done | bytes 131104 | tf_op jit(solution)/shard_map/ppermute | solution.py:11
  87.4 0.5 collective-permute-done.23
  87.9 1.6 %collective-permute-done.24 = f32[64,512]{1,0:T(8,128)S(1)} collective-permute-done((f32[64,512]{1,0:T(8,128)S(1)}, f32[64,512]{1,0:T(8,128)S(1)}, u32[]{:S(2)}, u32[]{:S(2)}) %collective-permute-start.24) | collective-permute-done | bytes 131104 | tf_op jit(solution)/shard_map/ppermute | solution.py:11
  89.6 0.9 subtract_bitcast_fusion
  (45 shorter events, 0.6 us)
Async XLA Ops:
  0.6 12.1 %copy-start = (bf16[2048,512]{1,0:T(8,128)(2,1)S(1)}, bf16[2048,512]{1,0:T(8,128)(2,1)}, u32[]{:S(2)}) copy-start(bf16[2048,512]{1,0:T(8,128)(2,1)} %param.4) | copy-start | bytes 6291460
  3.7 5.5 %collective-permute-start = (f32[2,512]{1,0:T(2,128)S(1)}, f32[2,512]{1,0:T(2,128)S(1)}, u32[]{:S(2)}, u32[]{:S(2)}) collective-permute-start(f32[2,512]{1,0:T(2,128)S(1)} %pad_maximum_fusion.2), channel_id=1, source_target_pairs={{0,8},{8,0},{16,24},{24,16},{1,9},{9,1},{17,25},{25,17},{2,10},{10... | collective-permute-start | bytes 12296 | tf_op jit(solution)/shard_map/ppermute | solution.py:11
  6.7 3.6 %collective-permute-start.1 = (f32[2,512]{1,0:T(2,128)S(1)}, f32[2,512]{1,0:T(2,128)S(1)}, u32[]{:S(2)}, u32[]{:S(2)}) collective-permute-start(f32[2,512]{1,0:T(2,128)S(1)} %pad_maximum_fusion.2), channel_id=1, source_target_pairs={{0,16},{8,24},{16,0},{24,8},{1,17},{9,25},{17,1},{25,9},{2,18},{10... | collective-permute-start | bytes 12296 | tf_op jit(solution)/shard_map/ppermute | solution.py:11
  8.2 4.5 %collective-permute-start.2 = (f32[2,512]{1,0:T(2,128)S(1)}, f32[2,512]{1,0:T(2,128)S(1)}, u32[]{:S(2)}, u32[]{:S(2)}) collective-permute-start(f32[2,512]{1,0:T(2,128)S(1)} %pad_maximum_fusion.2), channel_id=1, source_target_pairs={{0,24},{8,16},{16,8},{24,0},{1,25},{9,17},{17,9},{25,1},{2,26},{10... | collective-permute-start | bytes 12296 | tf_op jit(solution)/shard_map/ppermute | solution.py:11
  8.2 4.5 %collective-permute-start.3 = (f32[8,128]{1,0:T(8,128)S(1)}, f32[8,128]{1,0:T(8,128)S(1)}, u32[]{:S(2)}, u32[]{:S(2)}) collective-permute-start(f32[8,128]{1,0:T(8,128)S(1)} %broadcast_in_dim.122), channel_id=1, source_target_pairs={{0,1},{1,0},{2,3},{3,2},{4,5},{5,4},{6,7},{7,6},{8,9},{9,8},{10,11... | collective-permute-start | bytes 12296 | tf_op jit(solution)/shard_map/ppermute | solution.py:11
  14.7 8.2 %collective-permute-start.4 = (f16[64,2176]{1,0:T(8,128)(2,1)}, f16[64,2176]{1,0:T(8,128)(2,1)S(1)}, u32[]{:S(2)}, u32[]{:S(2)}) collective-permute-start(f16[64,2176]{1,0:T(8,128)(2,1)} %pad_maximum_fusion), channel_id=1, source_target_pairs={{0,1},{1,3},{2,0},{3,5},{4,2},{5,7},{6,4},{7,6},{8,9},{9,11},{10,8... | collective-permute-start | bytes 835592 | tf_op jit(solution)/shard_map/ppermute | solution.py:20
  14.7 11.1 %collective-permute-start.5 = (f16[64,2176]{1,0:T(8,128)(2,1)}, f16[64,2176]{1,0:T(8,128)(2,1)S(1)}, u32[]{:S(2)}, u32[]{:S(2)}) collective-permute-start(f16[64,2176]{1,0:T(8,128)(2,1)} %pad_maximum_fusion), channel_id=1, source_target_pairs={{0,2},{1,0},{2,4},{3,1},{4,6},{5,3},{6,7},{7,5},{8,10},{9,8},{10,1... | collective-permute-start | bytes 835592 | tf_op jit(solution)/shard_map/ppermute | solution.py:20
  22.9 2.9 %collective-permute-start.6 = (f16[64,2176]{1,0:T(8,128)(2,1)S(1)}, f16[64,2176]{1,0:T(8,128)(2,1)S(1)}, u32[]{:S(2)}, u32[]{:S(2)}) collective-permute-start(f16[64,2176]{1,0:T(8,128)(2,1)S(1)} %collective-permute-done.4), channel_id=1, source_target_pairs={{1,2},{3,4},{5,6},{2,1},{4,3},{6,5},{9,10},{11,12},{13,14},{10,9},... | collective-permute-start | bytes 835592 | tf_op jit(solution)/shard_map/ppermute | solution.py:26
  27.7 6.8 %collective-permute-start.7 = (f32[64,2048]{1,0:T(8,128)}, f32[64,2048]{1,0:T(8,128)}, u32[]{:S(2)}, u32[]{:S(2)}) collective-permute-start(f32[64,2048]{1,0:T(8,128)} %fusion.16), channel_id=1, source_target_pairs={{0,1},{1,0},{2,3},{3,2},{4,5},{5,4},{6,7},{7,6},{8,9},{9,8},{10,11... | collective-permute-start | bytes 1572872 | tf_op jit(solution)/shard_map/ppermute | solution.py:11
  36.0 10.3 %copy-start.1 = (f32[512,64]{0,1:T(8,128)S(1)}, f32[512,64]{0,1:T(8,128)}, u32[]{:S(2)}) copy-start(f32[512,64]{0,1:T(8,128)} %param.6) | copy-start | bytes 393220
  36.7 7.3 %collective-permute-start.10 = (f32[64,512]{1,0:T(8,128)S(1)}, f32[64,512]{1,0:T(8,128)S(1)}, u32[]{:S(2)}, u32[]{:S(2)}) collective-permute-start(f32[64,512]{1,0:T(8,128)S(1)} %slice_add_fusion.3), channel_id=1, source_target_pairs={{0,24},{8,16},{16,8},{24,0},{1,25},{9,17},{17,9},{25,1},{2,26},{10... | collective-permute-start | bytes 393224 | tf_op jit(solution)/shard_map/ppermute | solution.py:11
  38.6 7.1 %collective-permute-start.8 = (f32[64,512]{1,0:T(8,128)S(1)}, f32[64,512]{1,0:T(8,128)S(1)}, u32[]{:S(2)}, u32[]{:S(2)}) collective-permute-start(f32[64,512]{1,0:T(8,128)S(1)} %slice_add_fusion.3), channel_id=1, source_target_pairs={{0,8},{8,0},{16,24},{24,16},{1,9},{9,1},{17,25},{25,17},{2,10},{10... | collective-permute-start | bytes 393224 | tf_op jit(solution)/shard_map/ppermute | solution.py:11
  39.1 7.2 %collective-permute-start.9 = (f32[64,512]{1,0:T(8,128)S(1)}, f32[64,512]{1,0:T(8,128)S(1)}, u32[]{:S(2)}, u32[]{:S(2)}) collective-permute-start(f32[64,512]{1,0:T(8,128)S(1)} %slice_add_fusion.3), channel_id=1, source_target_pairs={{0,16},{8,24},{16,0},{24,8},{1,17},{9,25},{17,1},{25,9},{2,18},{10... | collective-permute-start | bytes 393224 | tf_op jit(solution)/shard_map/ppermute | solution.py:11
  47.7 9.3 %collective-permute-start.11 = (f16[64,2176]{1,0:T(8,128)(2,1)S(1)}, f16[64,2176]{1,0:T(8,128)(2,1)S(1)}, u32[]{:S(2)}, u32[]{:S(2)}) collective-permute-start(f16[64,2176]{1,0:T(8,128)(2,1)S(1)} %pad_maximum_fusion.1), channel_id=1, source_target_pairs={{0,1},{1,3},{2,0},{3,5},{4,2},{5,7},{6,4},{7,6},{8,9},{9,11},{10,8... | collective-permute-start | bytes 835592 | tf_op jit(solution)/shard_map/ppermute | solution.py:20
  47.8 10.8 %collective-permute-start.12 = (f16[64,2176]{1,0:T(8,128)(2,1)S(1)}, f16[64,2176]{1,0:T(8,128)(2,1)S(1)}, u32[]{:S(2)}, u32[]{:S(2)}) collective-permute-start(f16[64,2176]{1,0:T(8,128)(2,1)S(1)} %pad_maximum_fusion.1), channel_id=1, source_target_pairs={{0,2},{1,0},{2,4},{3,1},{4,6},{5,3},{6,7},{7,5},{8,10},{9,8},{10,1... | collective-permute-start | bytes 835592 | tf_op jit(solution)/shard_map/ppermute | solution.py:20
  57.0 1.6 %collective-permute-start.13 = (f16[64,2176]{1,0:T(8,128)(2,1)S(1)}, f16[64,2176]{1,0:T(8,128)(2,1)S(1)}, u32[]{:S(2)}, u32[]{:S(2)}) collective-permute-start(f16[64,2176]{1,0:T(8,128)(2,1)S(1)} %collective-permute-done.11), channel_id=1, source_target_pairs={{1,2},{3,4},{5,6},{2,1},{4,3},{6,5},{9,10},{11,12},{13,14},{10,9},... | collective-permute-start | bytes 835592 | tf_op jit(solution)/shard_map/ppermute | solution.py:26
  59.7 9.6 %copy-start.2 = (f32[64]{0:T(128)S(1)}, f32[64]{0:T(128)}, u32[]{:S(2)}) copy-start(f32[64]{0:T(128)} %param.7) | copy-start | bytes 772
  59.7 8.6 %collective-permute-start.14 = (f32[64,2048]{1,0:T(8,128)S(1)}, f32[64,2048]{1,0:T(8,128)S(1)}, u32[]{:S(2)}, u32[]{:S(2)}) collective-permute-start(f32[64,2048]{1,0:T(8,128)S(1)} %fusion.22), channel_id=1, source_target_pairs={{0,1},{1,0},{2,3},{3,2},{4,5},{5,4},{6,7},{7,6},{8,9},{9,8},{10,11... | collective-permute-start | bytes 1572872 | tf_op jit(solution)/shard_map/ppermute | solution.py:11
  68.9 1.3 %collective-permute-start.15 = (f32[64,4]{1,0:T(8,128)S(1)}, f32[64,4]{1,0:T(8,128)S(1)}, u32[]{:S(2)}, u32[]{:S(2)}) collective-permute-start(f32[64,4]{1,0:T(8,128)S(1)} %copy.19), channel_id=1, source_target_pairs={{0,1},{1,0},{2,3},{3,2},{4,5},{5,4},{6,7},{7,6},{8,9},{9,8},{10,11... | collective-permute-start | bytes 3080 | tf_op jit(solution)/shard_map/ppermute | solution.py:11
  70.2 5.1 %collective-permute-start.16 = (f32[64,4]{1,0:T(8,128)S(1)}, f32[64,4]{1,0:T(8,128)S(1)}, u32[]{:S(2)}, u32[]{:S(2)}) collective-permute-start(f32[64,4]{1,0:T(8,128)S(1)} %add.147), channel_id=1, source_target_pairs={{0,2},{1,3},{2,0},{3,1},{4,6},{5,7},{6,4},{7,5},{8,10},{9,11},{10,... | collective-permute-start | bytes 3080 | tf_op jit(solution)/shard_map/ppermute | solution.py:11
  72.1 5.1 %collective-permute-start.17 = (f32[64,4]{1,0:T(8,128)S(1)}, f32[64,4]{1,0:T(8,128)S(1)}, u32[]{:S(2)}, u32[]{:S(2)}) collective-permute-start(f32[64,4]{1,0:T(8,128)S(1)} %add.147), channel_id=1, source_target_pairs={{0,4},{1,5},{2,6},{3,7},{4,0},{5,1},{6,2},{7,3},{8,12},{9,13},{10,... | collective-permute-start | bytes 3080 | tf_op jit(solution)/shard_map/ppermute | solution.py:11
  72.9 5.7 %collective-permute-start.18 = (f32[64,4]{1,0:T(8,128)S(1)}, f32[64,4]{1,0:T(8,128)S(1)}, u32[]{:S(2)}, u32[]{:S(2)}) collective-permute-start(f32[64,4]{1,0:T(8,128)S(1)} %add.147), channel_id=1, source_target_pairs={{0,6},{1,7},{2,4},{3,5},{4,2},{5,3},{6,0},{7,1},{8,14},{9,15},{10,... | collective-permute-start | bytes 3080 | tf_op jit(solution)/shard_map/ppermute | solution.py:11
  78.7 5.0 %collective-permute-start.19 = (f32[64,4]{1,0:T(8,128)S(1)}, f32[64,4]{1,0:T(8,128)S(1)}, u32[]{:S(2)}, u32[]{:S(2)}) collective-permute-start(f32[64,4]{1,0:T(8,128)S(1)} %add_add_fusion.2), channel_id=1, source_target_pairs={{0,8},{8,0},{16,24},{24,16},{1,9},{9,1},{17,25},{25,17},{2,10},{10... | collective-permute-start | bytes 3080 | tf_op jit(solution)/shard_map/ppermute | solution.py:11
  79.2 6.6 %collective-permute-start.20 = (f32[64,4]{1,0:T(8,128)S(1)}, f32[64,4]{1,0:T(8,128)S(1)}, u32[]{:S(2)}, u32[]{:S(2)}) collective-permute-start(f32[64,4]{1,0:T(8,128)S(1)} %add_add_fusion.2), channel_id=1, source_target_pairs={{0,16},{8,24},{16,0},{24,8},{1,17},{9,25},{17,1},{25,9},{2,18},{10... | collective-permute-start | bytes 3080 | tf_op jit(solution)/shard_map/ppermute | solution.py:11
  80.1 5.7 %collective-permute-start.21 = (f32[64,4]{1,0:T(8,128)S(1)}, f32[64,4]{1,0:T(8,128)S(1)}, u32[]{:S(2)}, u32[]{:S(2)}) collective-permute-start(f32[64,4]{1,0:T(8,128)S(1)} %add_add_fusion.2), channel_id=1, source_target_pairs={{0,24},{8,16},{16,8},{24,0},{1,25},{9,17},{17,9},{25,1},{2,26},{10... | collective-permute-start | bytes 3080 | tf_op jit(solution)/shard_map/ppermute | solution.py:11
  82.2 5.2 %collective-permute-start.22 = (f32[64,512]{1,0:T(8,128)S(1)}, f32[64,512]{1,0:T(8,128)S(1)}, u32[]{:S(2)}, u32[]{:S(2)}) collective-permute-start(f32[64,512]{1,0:T(8,128)S(1)} %slice_add_fusion.2), channel_id=1, source_target_pairs={{0,8},{8,0},{16,24},{24,16},{1,9},{9,1},{17,25},{25,17},{2,10},{10... | collective-permute-start | bytes 393224 | tf_op jit(solution)/shard_map/ppermute | solution.py:11
  82.8 5.2 %collective-permute-start.23 = (f32[64,512]{1,0:T(8,128)S(1)}, f32[64,512]{1,0:T(8,128)S(1)}, u32[]{:S(2)}, u32[]{:S(2)}) collective-permute-start(f32[64,512]{1,0:T(8,128)S(1)} %slice_add_fusion.2), channel_id=1, source_target_pairs={{0,16},{8,24},{16,0},{24,8},{1,17},{9,25},{17,1},{25,9},{2,18},{10... | collective-permute-start | bytes 393224 | tf_op jit(solution)/shard_map/ppermute | solution.py:11
  83.7 5.9 %collective-permute-start.24 = (f32[64,512]{1,0:T(8,128)S(1)}, f32[64,512]{1,0:T(8,128)S(1)}, u32[]{:S(2)}, u32[]{:S(2)}) collective-permute-start(f32[64,512]{1,0:T(8,128)S(1)} %slice_add_fusion.2), channel_id=1, source_target_pairs={{0,24},{8,16},{16,8},{24,0},{1,25},{9,17},{17,9},{25,1},{2,26},{10... | collective-permute-start | bytes 393224 | tf_op jit(solution)/shard_map/ppermute | solution.py:11

commit v4 on v0

v4 whole, which is shorter than its diff:
```python
import functools

import jax
import jax.numpy as jnp
from jax import lax
from jax.experimental import pallas as pl
from jax.experimental.pallas import tpu as pltpu
from jax.sharding import PartitionSpec as P


AUX = 128
CHUNK = 512
UNIT = 14


def swap(value, axis, bits):
    return lax.ppermute(value, axis, [(i, i ^ bits) for i in range(lax.axis_size(axis))])


def crossing(value, rising):
    count = lax.axis_size("snp")
    pairs = []
    for i in range(count):
        target = i + 2 if i % 2 == rising else i - 2
        pairs.append((i, target if 0 <= target < count else i ^ 1))
    return lax.ppermute(value, "snp", pairs)


def forward(value):
    count = lax.axis_size("snp")
    pairs = [(i, i + 1) for i in range(3, count - 1, 2)] + [(i, i - 1) for i in range(2, count - 2, 2)]
    pairs += [(1, 0), (0, 2), (count - 2, count - 1), (count - 1, count - 3)]
    return lax.ppermute(value, "snp", pairs)


def partners(value, axis, low, high):
    return [swap(value, axis, k) for k in (low, high, low + high)]


def total(parts):
    own, one, two, three = parts
    return (own + one) + (two + three)


def call(body, out_shape, *args, smem=()):
    specs = [
        pl.BlockSpec(memory_space=pltpu.SMEM if k in smem else pltpu.VMEM) for k in range(len(args))
    ]
    outs = [jax.ShapeDtypeStruct(shape, kind) for shape, kind in out_shape]
    return pl.pallas_call(
        body,
        out_shape=outs,
        in_specs=specs,
        out_specs=[pl.BlockSpec(memory_space=pltpu.VMEM) for _ in outs],
        compiler_params=pltpu.CompilerParams(vmem_limit_bytes=32 << 20),
    )(*args)


def two_terms(value):
    high = value.astype(jnp.bfloat16)
    low = (value - high.astype(jnp.float32)).astype(jnp.bfloat16)
    return jnp.concatenate([high, low], 0)


def stats_kernel(width_ref, dosage_ref, sums_ref):
    row = lax.broadcasted_iota(jnp.int32, (8, 1), 0)
    acc = jnp.zeros((8, dosage_ref.shape[1]), jnp.float32)
    square = acc
    rows = CHUNK // 4
    for k in range(dosage_ref.shape[0] // rows):
        part = dosage_ref[pl.ds(k * rows, rows)].astype(jnp.float32)
        part = part.reshape(rows // 8, 8, part.shape[1])
        acc = acc + jnp.sum(part, 0)
        square = square + jnp.sum(part * part, 0)
    first = jnp.sum(acc, 0, keepdims=True)
    second = jnp.sum(square, 0, keepdims=True)
    width = width_ref[0].astype(jnp.float32)
    sums_ref[...] = jnp.where(row == 0, first, jnp.where(row == 1, second, width))


def encode(own_ref, coded_ref, width):
    samples = own_ref.shape[1]
    peak = jnp.max(jnp.abs(own_ref[...]), 1, keepdims=True)
    exponent = jnp.floor(jnp.log2(jnp.maximum(peak, 1e-30)))
    scale = jnp.exp2(UNIT - exponent)
    for k in range(0, samples, CHUNK):
        part = jnp.clip(jnp.round(own_ref[:, pl.ds(k, CHUNK)] * scale), -32767.0, 32767.0)
        coded_ref[:, pl.ds(k, CHUNK)] = part.astype(jnp.int32).astype(jnp.int16)
    lane = lax.broadcasted_iota(jnp.int32, (own_ref.shape[0], AUX), 1)
    extra = jnp.where(lane == 0, exponent, jnp.where(lane == 1, width, 0.0))
    coded_ref[:, pl.ds(samples, AUX)] = extra.astype(jnp.int32).astype(jnp.int16)


def decode(coded_ref, use):
    samples = coded_ref.shape[1] - AUX
    extra = coded_ref[:, pl.ds(samples, AUX)].astype(jnp.int32).astype(jnp.float32)
    return jnp.where(use, jnp.exp2(extra[:, :1] - UNIT), 0.0), extra[:, 1:2]


def values(coded_ref, k):
    return coded_ref[:, pl.ds(k, CHUNK)].astype(jnp.int32).astype(jnp.float32)


def project(value, scaled_ref, own_ref):
    rows = value.shape[0]
    terms = two_terms(value)
    for k in range(0, scaled_ref.shape[0], CHUNK):
        both = lax.dot_general(
            terms, scaled_ref[pl.ds(k, CHUNK)], (((1,), (1,)), ((), ())), preferred_element_type=jnp.float32
        )
        own_ref[:, pl.ds(k, CHUNK)] = both[:rows] + both[rows:]


def first_kernel(samples, width_ref, s0, s1, s2, s3, dosage_ref, start_ref, scaled_ref, own_ref, coded_ref):
    sums = total([s[0:2] for s in (s0, s1, s2, s3)])
    center = sums[0:1] / samples
    spread = sums[1:2] / samples - center * center
    factor = lax.rsqrt(spread + 1e-05)
    for k in range(0, dosage_ref.shape[0], CHUNK):
        part = dosage_ref[pl.ds(k, CHUNK)].astype(jnp.float32)
        scaled_ref[pl.ds(k, CHUNK)] = ((part - center) * factor).astype(jnp.bfloat16)
    project(start_ref[...], scaled_ref, own_ref)
    encode(own_ref, coded_ref, width_ref[0].astype(jnp.float32))


def next_kernel(
    samples, groups, width_ref, z0, z1, z2, z3, start_ref, scaled_ref, first_ref, parts_ref, own_ref, coded_ref
):
    first = total([z[...] for z in (z0, z1, z2, z3)]) / samples
    first_ref[...] = first
    start = start_ref[...]
    lane = lax.broadcasted_iota(jnp.int32, parts_ref.shape, 1)
    parts = jnp.zeros(parts_ref.shape, jnp.float32)
    for k, (a, b) in enumerate(((start, start), (start, first), (first, first))):
        parts = jnp.where(lane == k, jnp.sum(a * b, 1, keepdims=True) / groups, parts)
    parts_ref[...] = parts
    project(first, scaled_ref, own_ref)
    encode(own_ref, coded_ref, width_ref[0].astype(jnp.float32))


def place(count):
    index = lax.axis_index("snp")
    odd = (index & 1) == 1
    below, above = index >= 2, index < count - 2
    outer = jnp.where(odd, below.astype(jnp.int32), above.astype(jnp.int32)) == 1
    inner = jnp.where(odd, above.astype(jnp.int32), below.astype(jnp.int32)) == 1
    far = jnp.where(odd, (index < count - 3).astype(jnp.int32), (index >= 3).astype(jnp.int32)) == 1
    return odd, outer, inner, far


def gate(scale, odd, even_width, odd_width, least):
    return jnp.where(jnp.where(odd, odd_width, even_width) >= least, scale, 0.0)


def give_kernel(count, width_ref, near_ref, own_ref, outer_ref, inner_ref, give_ref):
    odd, use_outer, use_inner, _ = place(count)
    width = width_ref[0].astype(jnp.float32)
    near = near_ref[2:3, 0:1]
    outer_scale, outer_width = decode(outer_ref, use_outer)
    inner_scale, inner_width = decode(inner_ref, use_inner)
    own_scale = gate(1.0, odd, width, near, 1)
    outer_scale = gate(outer_scale, odd, near, outer_width, 1)
    inner_scale = gate(inner_scale, odd, inner_width, near, 3)
    for k in range(0, own_ref.shape[1], CHUNK):
        give_ref[:, pl.ds(k, CHUNK)] = (
            own_ref[:, pl.ds(k, CHUNK)] * own_scale
            + values(outer_ref, k) * outer_scale
            + values(inner_ref, k) * inner_scale
        )


def window_kernel(
    samples, count, width_ref, own_ref, outer_ref, inner_ref, far_ref, given_ref, scaled_ref, *refs
):
    odd, use_outer, use_inner, use_far = place(count)
    width = width_ref[0].astype(jnp.float32)
    outer_scale, outer_width = decode(outer_ref, use_outer)
    inner_scale, inner_width = decode(inner_ref, use_inner)
    far_scale, far_width = decode(far_ref, use_far)
    outer_scale = gate(outer_scale, odd, width, outer_width, 2)
    inner_scale = gate(inner_scale, odd, inner_width, width, 2)
    far_scale = gate(far_scale, odd, far_width, width, 3)
    out_ref = refs[-1]
    rows = own_ref.shape[0]
    acc = jnp.zeros((2 * rows, scaled_ref.shape[1]), jnp.float32)
    curved = jnp.zeros((rows, CHUNK), jnp.float32)
    for k in range(0, own_ref.shape[1], CHUNK):
        own = own_ref[:, pl.ds(k, CHUNK)]
        mixed = (
            own
            + given_ref[:, pl.ds(k, CHUNK)]
            + values(outer_ref, k) * outer_scale
            + values(inner_ref, k) * inner_scale
            + values(far_ref, k) * far_scale
        )
        acc = acc + jnp.dot(
            two_terms(mixed), scaled_ref[pl.ds(k, CHUNK)], preferred_element_type=jnp.float32
        )
        curved = curved + own * mixed
    out_ref[...] = acc[:rows] + acc[rows:]
    if len(refs) == 3:
        parts_ref, sums_ref = refs[:2]
        lane = lax.broadcasted_iota(jnp.int32, parts_ref.shape, 1)
        sums_ref[...] = jnp.where(lane == 3, jnp.sum(curved, 1, keepdims=True) / samples, parts_ref[...])


def last_kernel(samples, shrink_ref, p0, p1, p2, p3, z0, z1, z2, z3, start_ref, first_ref, effects_ref, residual_ref):
    parts = total([p[...] for p in (p0, p1, p2, p3)])
    bb, bw, ww, wu = (parts[:, k : k + 1] for k in range(4))
    shrink = shrink_ref[...]
    start, first = start_ref[...], first_ref[...]
    second = total([z[...] for z in (z0, z1, z2, z3)]) / samples
    ratio = bw / bb
    step = 1.0 / (ratio + shrink)
    norm = step * step * (ww - ratio * bw)
    bend = norm / bb
    curve = step * step * (ratio * (ratio * bw - 2.0 * ww) + wu) + shrink * norm - bend * norm / step
    step2 = jnp.where(curve > 0, norm / curve, 0.0)
    rest = step * (ratio * start - first)
    direction = rest + bend * start
    image = step * (ratio * first - second) + bend * first + shrink * direction
    effects_ref[...] = step * start + step2 * direction
    residual_ref[...] = rest - step2 * image


def shards(dosage, band_width, marginal, penalty):
    groups, count = lax.axis_size("samp"), lax.axis_size("snp")
    samples, size, rows = dosage.shape[0] * groups, dosage.shape[1], marginal.shape[1]
    local = dosage.shape[0]
    start = marginal.T
    shrink = penalty[:, None]
    grid, coded_shape, own_shape = (rows, size), (rows, local + AUX), (rows, local)

    (sums,) = call(stats_kernel, [((8, size), jnp.float32)], band_width, dosage, smem=(0,))
    others = partners(sums, "samp", 1, 2)
    near = swap(sums, "snp", 1)
    others, near = lax.optimization_barrier((others, near))
    scaled, own, coded = call(
        functools.partial(first_kernel, samples),
        [(dosage.shape, jnp.bfloat16), (own_shape, jnp.float32), (coded_shape, jnp.int16)],
        band_width, sums, *others, dosage, start, smem=(0,),
    )

    def window(own, coded, extra, outs):
        outer = crossing(coded, 1)
        inner = crossing(coded, 0)
        far = forward(outer)
        inner, far = lax.optimization_barrier((inner, far))
        (give,) = call(
            functools.partial(give_kernel, count),
            [(own_shape, jnp.float32)],
            band_width, near, own, outer, inner, smem=(0,),
        )
        given = swap(give, "snp", 1)
        return call(
            functools.partial(window_kernel, samples, count),
            outs,
            band_width, own, outer, inner, far, given, scaled, *extra, smem=(0,),
        )

    (z,) = window(own, coded, (), [(grid, jnp.float32)])
    first, parts, own, coded = call(
        functools.partial(next_kernel, samples, groups),
        [(grid, jnp.float32), ((rows, AUX), jnp.float32), (own_shape, jnp.float32), (coded_shape, jnp.int16)],
        band_width, z, *partners(z, "samp", 1, 2), start, scaled, smem=(0,),
    )
    sums, z = window(own, coded, (parts,), [((rows, AUX), jnp.float32), (grid, jnp.float32)])
    zs = [z, *partners(z, "samp", 1, 2)]
    sums = sums + swap(sums, "snp", 1)
    bit = 2
    while bit < count:
        if 2 * bit < count:
            sums = total([sums, *partners(sums, "snp", bit, 2 * bit)])
        else:
            sums = sums + swap(sums, "snp", bit)
        bit *= 4
    effects, residual = call(
        functools.partial(last_kernel, samples),
        [(grid, jnp.float32), (grid, jnp.float32)],
        shrink, sums, *partners(sums, "samp", 1, 2), *zs, start, first,
    )
    return (effects.T, residual.T)


def solution(mesh):
    in_specs = (P("samp", "snp"), P("snp"), P("snp", None), P())
    out_specs = (P("snp", None), P("snp", None))
    return jax.shard_map(shards, mesh=mesh, in_specs=in_specs, out_specs=out_specs, check_vma=False)
```

time: 381 us -> 80.4 us (0.21)
  waiting for transfers between devices: 226 us -> 42.6 us
  blocking collectives: 70.7 us -> 0 us
  matrix products: 21.6 us -> 0 us
  between operations: 15 us -> 1.38 us
  other arithmetic: 9.79 us -> 0.01 us
  Pallas kernels: 0 us -> 5.36 us
  starting transfers between devices: 34.3 us -> 29.2 us
    psum x1 -> x0, waiting for transfers between devices: 145 us -> none  [shards(): ld_band = lax.psum(partial_band, 'samp') / samples]
    psum x4 -> x0, blocking collectives: 54.6 us -> none  [the longest x2 28.4 us: residual_sum(): return lax.psum(jnp.sum(vector * vector, 0), 'snp')]
    ppermute x15 -> x25, waiting for transfers between devices: 80.8 us -> 42.6 us  [the longest x19 21.9 us: swap(): lax.ppermute(value, axis, [(i, i ^ bits) for i in range(lax.axis_size(axi...]
    dot_general x18 -> x0, matrix products: 21.6 us -> none  [the longest x6 9.6 us: exact_tdot(): lax.dot_general(left_mat, right_mat, (((0,), (0,)), ((), ())), precision=...]
    all_gather x2 -> x0, blocking collectives: 16.1 us -> none  [the longest x1 8.42 us: shards(): lax.all_gather(effects, 'samp', axis=1, tiled=True)]
    pallas_call x0 -> x8, Pallas kernels: none -> 5.36 us  [call(): pl.pallas_call(body, out_shape=outs, in_specs=specs, out_specs=[pl.BlockS...]
    ppermute x15 -> x25, starting transfers between devices: 34.2 us -> 29.2 us  [the longest x19 20.1 us: swap(): lax.ppermute(value, axis, [(i, i ^ bits) for i in range(lax.axis_size(axi...]
  transfers between devices with their start and end apart: 16 -> 25, of which waited for: 4 -> 16; matrix products, arithmetic and copies ran while one was open for 5% -> 0% of each run, Pallas kernels for 0% -> 0%
where the time goes in v4:
time: 80.4 us; the launch traced here: 80.2 us
  waiting for transfers between devices  42.6 us (53%)
  starting transfers between devices  29.2 us (36%)
  Pallas kernels  5.36 us (7%)
  local copies, waits for them, and re-layouts  1.69 us (2%)
  between operations  1.38 us (2%)
    ppermute x19, waiting for transfers between devices, swap(): lax.ppermute(value, axis, [(i, i ^ bits) for i in range(lax.axis_size(axi...  21.9 us
    ppermute x19, starting transfers between devices, swap(): lax.ppermute(value, axis, [(i, i ^ bits) for i in range(lax.axis_size(axi...  20.1 us
    ppermute x4, waiting for transfers between devices, crossing(): return lax.ppermute(value, 'snp', pairs)  12.7 us
    ppermute x2, waiting for transfers between devices, forward(): return lax.ppermute(value, 'snp', pairs)  8.13 us
    pallas_call x8, Pallas kernels, call(): pl.pallas_call(body, out_shape=outs, in_specs=specs, out_specs=[pl.BlockS...  5.36 us
    ppermute x4, starting transfers between devices, crossing(): return lax.ppermute(value, 'snp', pairs)  5.15 us
    ppermute x2, starting transfers between devices, forward(): return lax.ppermute(value, 'snp', pairs)  3.91 us
  transfers between devices with their start and end apart: 25, of which 16 were waited for; matrix products, arithmetic and copies ran while one was open for 0% of the time, Pallas kernels for 0%

profile of v4, /device:TPU:0, one launch (start us, length us, event | category | flops | bytes accessed | tf_op | source)
XLA Modules:
  0.0 80.2 jit_solution(9980896182178337932)
XLA Ops:
  1.3 0.0 copy-start
  1.3 1.6 %copy-done = bf16[2048,512]{1,0:T(8,128)(2,1)S(1)} copy-done((bf16[2048,512]{1,0:T(8,128)(2,1)S(1)}, bf16[2048,512]{1,0:T(8,128)(2,1)}, u32[]{:S(2)}) %copy-start) | copy-done | bytes 2097176
  2.9 0.0 copy-start.1
  2.9 0.4 shard_map.59.s0
  3.3 3.0 %collective-permute-start = (f32[8,512]{1,0:T(8,128)S(1)}, f32[8,512]{1,0:T(8,128)S(1)}, u32[]{:S(2)}, u32[]{:S(2)}) collective-permute-start(f32[8,512]{1,0:T(8,128)S(1)} %shard_map.59.s0), channel_id=1, source_target_pairs={{0,8},{8,0},{16,24},{24,16},{1,9},{9,1},{17,25},{25,17},{2,10},{10... | collective-permute-start | bytes 49160 | tf_op jit(solution)/shard_map/ppermute | solution.py:17
  6.3 1.5 %collective-permute-start.1 = (f32[8,512]{1,0:T(8,128)S(1)}, f32[8,512]{1,0:T(8,128)S(1)}, u32[]{:S(2)}, u32[]{:S(2)}) collective-permute-start(f32[8,512]{1,0:T(8,128)S(1)} %shard_map.59.s0), channel_id=1, source_target_pairs={{0,16},{8,24},{16,0},{24,8},{1,17},{9,25},{17,1},{25,9},{2,18},{10... | collective-permute-start | bytes 49160 | tf_op jit(solution)/shard_map/ppermute | solution.py:17
  7.8 0.0 collective-permute-start.2
  7.8 0.0 collective-permute-start.3
  7.8 0.2 collective-permute-done.s1
  8.0 2.0 %collective-permute-done.1.s2 = f32[8,512]{1,0:T(8,128)S(1)} collective-permute-done((f32[8,512]{1,0:T(8,128)S(1)}, f32[8,512]{1,0:T(8,128)S(1)}, u32[]{:S(2)}, u32[]{:S(2)}) %collective-permute-start.1) | collective-permute-done | bytes 16416 | tf_op jit(solution)/shard_map/ppermute | solution.py:17
  10.0 2.4 %collective-permute-done.2.s3 = f32[8,512]{1,0:T(8,128)S(1)} collective-permute-done((f32[8,512]{1,0:T(8,128)S(1)}, f32[8,512]{1,0:T(8,128)S(1)}, u32[]{:S(2)}, u32[]{:S(2)}) %collective-permute-start.2) | collective-permute-done | bytes 16416 | tf_op jit(solution)/shard_map/ppermute | solution.py:17
  12.4 0.0 collective-permute-done.3.near_ref
  12.4 0.0 copy-done.1
  12.4 1.0 %shard_map.60 = (bf16[2048,512]{1,0:T(8,128)(2,1)S(1)}, f32[64,2048]{1,0:T(8,128)S(1)}, s16[64,2176]{1,0:T(8,128)(2,1)S(1)}) custom-call(s32[1]{0:T(128)S(6)} %copy.7.width_ref, f32[8,512]{1,0:T(8,128)S(1)} %shard_map.59.s0, f32[8,512]{1,0:T(8,128)S(1)} %collective-permute-done.s1, f32[8,512]{1,0:T(8,128)S(1)} %collective-permute-done.1.s2, ...), custom_call_target="tpu_custom_call" | custom-call | tf_op jit(solution)/shard_map/pallas_call | solution.py:50
  13.4 0.0 collective-permute-start.4
  13.5 2.0 %collective-permute-start.5 = (s16[64,2176]{1,0:T(8,128)(2,1)S(1)}, s16[64,2176]{1,0:T(8,128)(2,1)S(1)}, u32[]{:S(2)}, u32[]{:S(2)}) collective-permute-start(s16[64,2176]{1,0:T(8,128)(2,1)S(1)} %get-tuple-element.25), channel_id=1, source_target_pairs={{0,2},{1,0},{2,4},{3,1},{4,6},{5,3},{6,7},{7,5},{8,10},{9,8},{10,1... | collective-permute-start | bytes 835592 | tf_op jit(solution)/shard_map/ppermute | solution.py:26
  15.5 6.0 %collective-permute-done.4.outer_ref = s16[64,2176]{1,0:T(8,128)(2,1)S(1)} collective-permute-done((s16[64,2176]{1,0:T(8,128)(2,1)S(1)}, s16[64,2176]{1,0:T(8,128)(2,1)S(1)}, u32[]{:S(2)}, u32[]{:S(2)}) %collective-permute-start.4) | collective-permute-done | bytes 278560 | tf_op jit(solution)/shard_map/ppermute | solution.py:26
  21.4 1.6 %collective-permute-start.6 = (s16[64,2176]{1,0:T(8,128)(2,1)S(1)}, s16[64,2176]{1,0:T(8,128)(2,1)S(1)}, u32[]{:S(2)}, u32[]{:S(2)}) collective-permute-start(s16[64,2176]{1,0:T(8,128)(2,1)S(1)} %collective-permute-done.4.outer_ref), channel_id=1, source_target_pairs={{3,4},{5,6},{2,1},{4,3},{1,0},{0,2},{6,7},{7,5},{11,12},{13,14},{1... | collective-permute-start | bytes 835592 | tf_op jit(solution)/shard_map/ppermute | solution.py:33
  23.0 0.0 collective-permute-done.5.inner_ref
  23.0 4.1 %collective-permute-done.6.far_ref = s16[64,2176]{1,0:T(8,128)(2,1)S(1)} collective-permute-done((s16[64,2176]{1,0:T(8,128)(2,1)S(1)}, s16[64,2176]{1,0:T(8,128)(2,1)S(1)}, u32[]{:S(2)}, u32[]{:S(2)}) %collective-permute-start.6) | collective-permute-done | bytes 278560 | tf_op jit(solution)/shard_map/ppermute | solution.py:33
  27.1 0.3 shard_map.61
  27.3 0.3 collective-permute-start.7
  27.7 1.6 %collective-permute-done.7.given_ref = f32[64,2048]{1,0:T(8,128)S(1)} collective-permute-done((f32[64,2048]{1,0:T(8,128)S(1)}, f32[64,2048]{1,0:T(8,128)S(1)}, u32[]{:S(2)}, u32[]{:S(2)}) %collective-permute-start.7) | collective-permute-done | bytes 524320 | tf_op jit(solution)/shard_map/ppermute | solution.py:17
  29.3 0.6 shard_map.62.z0
  29.9 1.6 %collective-permute-start.10 = (f32[64,512]{1,0:T(8,128)S(1)}, f32[64,512]{1,0:T(8,128)S(1)}, u32[]{:S(2)}, u32[]{:S(2)}) collective-permute-start(f32[64,512]{1,0:T(8,128)S(1)} %shard_map.62.z0), channel_id=1, source_target_pairs={{0,24},{8,16},{16,8},{24,0},{1,25},{9,17},{17,9},{25,1},{2,26},{10... | collective-permute-start | bytes 393224 | tf_op jit(solution)/shard_map/ppermute | solution.py:17
  31.5 0.5 collective-permute-start.8
  32.0 1.5 %collective-permute-start.9 = (f32[64,512]{1,0:T(8,128)S(1)}, f32[64,512]{1,0:T(8,128)S(1)}, u32[]{:S(2)}, u32[]{:S(2)}) collective-permute-start(f32[64,512]{1,0:T(8,128)S(1)} %shard_map.62.z0), channel_id=1, source_target_pairs={{0,16},{8,24},{16,0},{24,8},{1,17},{9,25},{17,1},{25,9},{2,18},{10... | collective-permute-start | bytes 393224 | tf_op jit(solution)/shard_map/ppermute | solution.py:17
  33.5 3.7 %collective-permute-done.10.z3 = f32[64,512]{1,0:T(8,128)S(1)} collective-permute-done((f32[64,512]{1,0:T(8,128)S(1)}, f32[64,512]{1,0:T(8,128)S(1)}, u32[]{:S(2)}, u32[]{:S(2)}) %collective-permute-start.10) | collective-permute-done | bytes 131104 | tf_op jit(solution)/shard_map/ppermute | solution.py:17
  37.2 1.3 %collective-permute-done.8.z1 = f32[64,512]{1,0:T(8,128)S(1)} collective-permute-done((f32[64,512]{1,0:T(8,128)S(1)}, f32[64,512]{1,0:T(8,128)S(1)}, u32[]{:S(2)}, u32[]{:S(2)}) %collective-permute-start.8) | collective-permute-done | bytes 131104 | tf_op jit(solution)/shard_map/ppermute | solution.py:17
  38.5 0.9 %collective-permute-done.9.z2 = f32[64,512]{1,0:T(8,128)S(1)} collective-permute-done((f32[64,512]{1,0:T(8,128)S(1)}, f32[64,512]{1,0:T(8,128)S(1)}, u32[]{:S(2)}, u32[]{:S(2)}) %collective-permute-start.9) | collective-permute-done | bytes 131104 | tf_op jit(solution)/shard_map/ppermute | solution.py:17
  39.4 1.0 %shard_map.63 = (f32[64,512]{1,0:T(8,128)S(1)}, f32[64,128]{1,0:T(8,128)S(1)}, f32[64,2048]{1,0:T(8,128)S(1)}, s16[64,2176]{1,0:T(8,128)(2,1)S(1)}) custom-call(s32[1]{0:T(128)S(6)} %copy.7.width_ref, f32[64,512]{1,0:T(8,128)S(1)} %shard_map.62.z0, f32[64,512]{1,0:T(8,128)S(1)} %collective-permute-done.8.z1, f32[64,512]{1,0:T(8,128)S(1)} %collective-permute-done.9.z2, ...), custom_call_target="tpu_custom_call" | custom-call | tf_op jit(solution)/shard_map/pallas_call | solution.py:50
  40.3 0.0 collective-permute-start.11
  40.4 3.1 %collective-permute-start.12 = (s16[64,2176]{1,0:T(8,128)(2,1)S(1)}, s16[64,2176]{1,0:T(8,128)(2,1)S(1)}, u32[]{:S(2)}, u32[]{:S(2)}) collective-permute-start(s16[64,2176]{1,0:T(8,128)(2,1)S(1)} %get-tuple-element.31), channel_id=1, source_target_pairs={{0,2},{1,0},{2,4},{3,1},{4,6},{5,3},{6,7},{7,5},{8,10},{9,8},{10,1... | collective-permute-start | bytes 835592 | tf_op jit(solution)/shard_map/ppermute | solution.py:26
  43.4 6.7 %collective-permute-done.11.outer_ref = s16[64,2176]{1,0:T(8,128)(2,1)S(1)} collective-permute-done((s16[64,2176]{1,0:T(8,128)(2,1)S(1)}, s16[64,2176]{1,0:T(8,128)(2,1)S(1)}, u32[]{:S(2)}, u32[]{:S(2)}) %collective-permute-start.11) | collective-permute-done | bytes 278560 | tf_op jit(solution)/shard_map/ppermute | solution.py:26
  50.1 2.3 %collective-permute-start.13 = (s16[64,2176]{1,0:T(8,128)(2,1)S(1)}, s16[64,2176]{1,0:T(8,128)(2,1)S(1)}, u32[]{:S(2)}, u32[]{:S(2)}) collective-permute-start(s16[64,2176]{1,0:T(8,128)(2,1)S(1)} %collective-permute-done.11.outer_ref), channel_id=1, source_target_pairs={{3,4},{5,6},{2,1},{4,3},{1,0},{0,2},{6,7},{7,5},{11,12},{13,14},{1... | collective-permute-start | bytes 835592 | tf_op jit(solution)/shard_map/ppermute | solution.py:33
  52.5 0.0 collective-permute-done.12.inner_ref
  52.5 4.1 %collective-permute-done.13.far_ref = s16[64,2176]{1,0:T(8,128)(2,1)S(1)} collective-permute-done((s16[64,2176]{1,0:T(8,128)(2,1)S(1)}, s16[64,2176]{1,0:T(8,128)(2,1)S(1)}, u32[]{:S(2)}, u32[]{:S(2)}) %collective-permute-start.13) | collective-permute-done | bytes 278560 | tf_op jit(solution)/shard_map/ppermute | solution.py:33
  56.5 0.3 shard_map.64
  56.8 0.3 collective-permute-start.14
  57.1 1.6 %collective-permute-done.14.given_ref = f32[64,2048]{1,0:T(8,128)S(1)} collective-permute-done((f32[64,2048]{1,0:T(8,128)S(1)}, f32[64,2048]{1,0:T(8,128)S(1)}, u32[]{:S(2)}, u32[]{:S(2)}) %collective-permute-start.14) | collective-permute-done | bytes 524320 | tf_op jit(solution)/shard_map/ppermute | solution.py:17
  58.8 0.7 shard_map.65
  59.5 0.3 collective-permute-start.15
  59.9 0.9 %collective-permute-done.15 = f32[64,128]{1,0:T(8,128)S(1)} collective-permute-done((f32[64,128]{1,0:T(8,128)S(1)}, f32[64,128]{1,0:T(8,128)S(1)}, u32[]{:S(2)}, u32[]{:S(2)}) %collective-permute-start.15) | collective-permute-done | bytes 32800 | tf_op jit(solution)/shard_map/ppermute | solution.py:17
  60.8 2.5 %collective-permute-start.16 = (f32[64,128]{1,0:T(8,128)S(1)}, f32[64,128]{1,0:T(8,128)S(1)}, u32[]{:S(2)}, u32[]{:S(2)}) collective-permute-start(f32[64,128]{1,0:T(8,128)S(1)} %add.12), channel_id=1, source_target_pairs={{0,2},{1,3},{2,0},{3,1},{4,6},{5,7},{6,4},{7,5},{8,10},{9,11},{10,... | collective-permute-start | bytes 98312 | tf_op jit(solution)/shard_map/ppermute | solution.py:17
  63.3 0.2 collective-permute-start.17
  63.5 2.2 %collective-permute-start.18 = (f32[64,128]{1,0:T(8,128)S(1)}, f32[64,128]{1,0:T(8,128)S(1)}, u32[]{:S(2)}, u32[]{:S(2)}) collective-permute-start(f32[64,128]{1,0:T(8,128)S(1)} %add.12), channel_id=1, source_target_pairs={{0,6},{1,7},{2,4},{3,5},{4,2},{5,3},{6,0},{7,1},{8,14},{9,15},{10,... | collective-permute-start | bytes 98312 | tf_op jit(solution)/shard_map/ppermute | solution.py:17
  65.7 0.5 collective-permute-start.22
  66.3 1.1 %collective-permute-start.23 = (f32[64,512]{1,0:T(8,128)S(1)}, f32[64,512]{1,0:T(8,128)S(1)}, u32[]{:S(2)}, u32[]{:S(2)}) collective-permute-start(f32[64,512]{1,0:T(8,128)S(1)} %get-tuple-element.36.z0), channel_id=1, source_target_pairs={{0,16},{8,24},{16,0},{24,8},{1,17},{9,25},{17,1},{25,9},{2,18},{10... | collective-permute-start | bytes 393224 | tf_op jit(solution)/shard_map/ppermute | solution.py:17
  67.3 0.0 collective-permute-done.16
  67.3 1.9 %collective-permute-start.24 = (f32[64,512]{1,0:T(8,128)S(1)}, f32[64,512]{1,0:T(8,128)S(1)}, u32[]{:S(2)}, u32[]{:S(2)}) collective-permute-start(f32[64,512]{1,0:T(8,128)S(1)} %get-tuple-element.36.z0), channel_id=1, source_target_pairs={{0,24},{8,16},{16,8},{24,0},{1,25},{9,17},{17,9},{25,1},{2,26},{10... | collective-permute-start | bytes 393224 | tf_op jit(solution)/shard_map/ppermute | solution.py:17
  69.2 0.0 collective-permute-done.17
  69.2 0.1 collective-permute-done.18
  69.4 0.6 collective-permute-start.19
  70.0 1.0 %collective-permute-start.20 = (f32[64,128]{1,0:T(8,128)S(1)}, f32[64,128]{1,0:T(8,128)S(1)}, u32[]{:S(2)}, u32[]{:S(2)}) collective-permute-start(f32[64,128]{1,0:T(8,128)S(1)} %add_add_fusion.p0), channel_id=1, source_target_pairs={{0,16},{8,24},{16,0},{24,8},{1,17},{9,25},{17,1},{25,9},{2,18},{10... | collective-permute-start | bytes 98312 | tf_op jit(solution)/shard_map/ppermute | solution.py:17
  70.9 3.3 %collective-permute-done.19.p1 = f32[64,128]{1,0:T(8,128)S(1)} collective-permute-done((f32[64,128]{1,0:T(8,128)S(1)}, f32[64,128]{1,0:T(8,128)S(1)}, u32[]{:S(2)}, u32[]{:S(2)}) %collective-permute-start.19) | collective-permute-done | bytes 32800 | tf_op jit(solution)/shard_map/ppermute | solution.py:17
  74.3 1.0 %collective-permute-start.21 = (f32[64,128]{1,0:T(8,128)S(1)}, f32[64,128]{1,0:T(8,128)S(1)}, u32[]{:S(2)}, u32[]{:S(2)}) collective-permute-start(f32[64,128]{1,0:T(8,128)S(1)} %add_add_fusion.p0), channel_id=1, source_target_pairs={{0,24},{8,16},{16,8},{24,0},{1,25},{9,17},{17,9},{25,1},{2,26},{10... | collective-permute-start | bytes 98312 | tf_op jit(solution)/shard_map/ppermute | solution.py:17
  75.3 0.0 copy-done.2
  75.3 0.1 copy.6.shrink_ref
  75.4 0.0 collective-permute-done.20.p2
  75.4 3.7 %collective-permute-done.21.p3 = f32[64,128]{1,0:T(8,128)S(1)} collective-permute-done((f32[64,128]{1,0:T(8,128)S(1)}, f32[64,128]{1,0:T(8,128)S(1)}, u32[]{:S(2)}, u32[]{:S(2)}) %collective-permute-start.21) | collective-permute-done | bytes 32800 | tf_op jit(solution)/shard_map/ppermute | solution.py:17
  79.1 0.0 collective-permute-done.22.z1
  79.1 0.0 collective-permute-done.23.z2
  79.1 0.0 collective-permute-done.24.z3
  79.1 1.2 %shard_map.66 = (f32[64,512]{1,0:T(8,128)}, f32[64,512]{1,0:T(8,128)}) custom-call(f32[64,1]{1,0:T(8,128)S(1)} %copy.6.shrink_ref, f32[64,128]{1,0:T(8,128)S(1)} %add_add_fusion.p0, f32[64,128]{1,0:T(8,128)S(1)} %collective-permute-done.19.p1, f32[64,128]{1,0:T(8,128)S(1)} %collective-permute-done.20.p2, f32[64,128]{1,0:T(8,128)S(1)} %collective-permute-done.21.p3, ...), custom_call_target="tpu_custom_call" | custom-call | tf_op jit(solution)/shard_map/pallas_call | solution.py:50
  (3 shorter events, 0.0 us)
Async XLA Ops:
  1.3 1.6 %copy-start = (bf16[2048,512]{1,0:T(8,128)(2,1)S(1)}, bf16[2048,512]{1,0:T(8,128)(2,1)}, u32[]{:S(2)}) copy-start(bf16[2048,512]{1,0:T(8,128)(2,1)} %dosage_ref.3) | copy-start | bytes 6291460
  2.9 9.6 %copy-start.1 = (f32[512,64]{0,1:T(8,128)S(1)}, f32[512,64]{0,1:T(8,128)}, u32[]{:S(2)}) copy-start(f32[512,64]{0,1:T(8,128)} %param.6) | copy-start | bytes 393220
  3.3 4.7 %collective-permute-start = (f32[8,512]{1,0:T(8,128)S(1)}, f32[8,512]{1,0:T(8,128)S(1)}, u32[]{:S(2)}, u32[]{:S(2)}) collective-permute-start(f32[8,512]{1,0:T(8,128)S(1)} %shard_map.59.s0), channel_id=1, source_target_pairs={{0,8},{8,0},{16,24},{24,16},{1,9},{9,1},{17,25},{25,17},{2,10},{10... | collective-permute-start | bytes 49160 | tf_op jit(solution)/shard_map/ppermute | solution.py:17
  6.3 3.7 %collective-permute-start.1 = (f32[8,512]{1,0:T(8,128)S(1)}, f32[8,512]{1,0:T(8,128)S(1)}, u32[]{:S(2)}, u32[]{:S(2)}) collective-permute-start(f32[8,512]{1,0:T(8,128)S(1)} %shard_map.59.s0), channel_id=1, source_target_pairs={{0,16},{8,24},{16,0},{24,8},{1,17},{9,25},{17,1},{25,9},{2,18},{10... | collective-permute-start | bytes 49160 | tf_op jit(solution)/shard_map/ppermute | solution.py:17
  7.8 4.6 %collective-permute-start.2 = (f32[8,512]{1,0:T(8,128)S(1)}, f32[8,512]{1,0:T(8,128)S(1)}, u32[]{:S(2)}, u32[]{:S(2)}) collective-permute-start(f32[8,512]{1,0:T(8,128)S(1)} %shard_map.59.s0), channel_id=1, source_target_pairs={{0,24},{8,16},{16,8},{24,0},{1,25},{9,17},{17,9},{25,1},{2,26},{10... | collective-permute-start | bytes 49160 | tf_op jit(solution)/shard_map/ppermute | solution.py:17
  7.8 4.6 %collective-permute-start.3 = (f32[8,512]{1,0:T(8,128)S(1)}, f32[8,512]{1,0:T(8,128)S(1)}, u32[]{:S(2)}, u32[]{:S(2)}) collective-permute-start(f32[8,512]{1,0:T(8,128)S(1)} %shard_map.59.s0), channel_id=1, source_target_pairs={{0,1},{1,0},{2,3},{3,2},{4,5},{5,4},{6,7},{7,6},{8,9},{9,8},{10,11... | collective-permute-start | bytes 49160 | tf_op jit(solution)/shard_map/ppermute | solution.py:17
  13.4 8.0 %collective-permute-start.4 = (s16[64,2176]{1,0:T(8,128)(2,1)S(1)}, s16[64,2176]{1,0:T(8,128)(2,1)S(1)}, u32[]{:S(2)}, u32[]{:S(2)}) collective-permute-start(s16[64,2176]{1,0:T(8,128)(2,1)S(1)} %get-tuple-element.25), channel_id=1, source_target_pairs={{0,1},{1,3},{2,0},{3,5},{4,2},{5,7},{6,4},{7,6},{8,9},{9,11},{10,8... | collective-permute-start | bytes 835592 | tf_op jit(solution)/shard_map/ppermute | solution.py:26
  13.5 9.5 %collective-permute-start.5 = (s16[64,2176]{1,0:T(8,128)(2,1)S(1)}, s16[64,2176]{1,0:T(8,128)(2,1)S(1)}, u32[]{:S(2)}, u32[]{:S(2)}) collective-permute-start(s16[64,2176]{1,0:T(8,128)(2,1)S(1)} %get-tuple-element.25), channel_id=1, source_target_pairs={{0,2},{1,0},{2,4},{3,1},{4,6},{5,3},{6,7},{7,5},{8,10},{9,8},{10,1... | collective-permute-start | bytes 835592 | tf_op jit(solution)/shard_map/ppermute | solution.py:26
  21.4 5.6 %collective-permute-start.6 = (s16[64,2176]{1,0:T(8,128)(2,1)S(1)}, s16[64,2176]{1,0:T(8,128)(2,1)S(1)}, u32[]{:S(2)}, u32[]{:S(2)}) collective-permute-start(s16[64,2176]{1,0:T(8,128)(2,1)S(1)} %collective-permute-done.4.outer_ref), channel_id=1, source_target_pairs={{3,4},{5,6},{2,1},{4,3},{1,0},{0,2},{6,7},{7,5},{11,12},{13,14},{1... | collective-permute-start | bytes 835592 | tf_op jit(solution)/shard_map/ppermute | solution.py:33
  27.3 2.0 %collective-permute-start.7 = (f32[64,2048]{1,0:T(8,128)S(1)}, f32[64,2048]{1,0:T(8,128)S(1)}, u32[]{:S(2)}, u32[]{:S(2)}) collective-permute-start(f32[64,2048]{1,0:T(8,128)S(1)} %shard_map.61), channel_id=1, source_target_pairs={{0,1},{1,0},{2,3},{3,2},{4,5},{5,4},{6,7},{7,6},{8,9},{9,8},{10,11... | collective-permute-start | bytes 1572872 | tf_op jit(solution)/shard_map/ppermute | solution.py:17
  29.9 7.3 %collective-permute-start.10 = (f32[64,512]{1,0:T(8,128)S(1)}, f32[64,512]{1,0:T(8,128)S(1)}, u32[]{:S(2)}, u32[]{:S(2)}) collective-permute-start(f32[64,512]{1,0:T(8,128)S(1)} %shard_map.62.z0), channel_id=1, source_target_pairs={{0,24},{8,16},{16,8},{24,0},{1,25},{9,17},{17,9},{25,1},{2,26},{10... | collective-permute-start | bytes 393224 | tf_op jit(solution)/shard_map/ppermute | solution.py:17
  31.5 7.0 %collective-permute-start.8 = (f32[64,512]{1,0:T(8,128)S(1)}, f32[64,512]{1,0:T(8,128)S(1)}, u32[]{:S(2)}, u32[]{:S(2)}) collective-permute-start(f32[64,512]{1,0:T(8,128)S(1)} %shard_map.62.z0), channel_id=1, source_target_pairs={{0,8},{8,0},{16,24},{24,16},{1,9},{9,1},{17,25},{25,17},{2,10},{10... | collective-permute-start | bytes 393224 | tf_op jit(solution)/shard_map/ppermute | solution.py:17
  32.0 7.3 %collective-permute-start.9 = (f32[64,512]{1,0:T(8,128)S(1)}, f32[64,512]{1,0:T(8,128)S(1)}, u32[]{:S(2)}, u32[]{:S(2)}) collective-permute-start(f32[64,512]{1,0:T(8,128)S(1)} %shard_map.62.z0), channel_id=1, source_target_pairs={{0,16},{8,24},{16,0},{24,8},{1,17},{9,25},{17,1},{25,9},{2,18},{10... | collective-permute-start | bytes 393224 | tf_op jit(solution)/shard_map/ppermute | solution.py:17
  40.3 9.8 %collective-permute-start.11 = (s16[64,2176]{1,0:T(8,128)(2,1)S(1)}, s16[64,2176]{1,0:T(8,128)(2,1)S(1)}, u32[]{:S(2)}, u32[]{:S(2)}) collective-permute-start(s16[64,2176]{1,0:T(8,128)(2,1)S(1)} %get-tuple-element.31), channel_id=1, source_target_pairs={{0,1},{1,3},{2,0},{3,5},{4,2},{5,7},{6,4},{7,6},{8,9},{9,11},{10,8... | collective-permute-start | bytes 835592 | tf_op jit(solution)/shard_map/ppermute | solution.py:26
  40.4 12.1 %collective-permute-start.12 = (s16[64,2176]{1,0:T(8,128)(2,1)S(1)}, s16[64,2176]{1,0:T(8,128)(2,1)S(1)}, u32[]{:S(2)}, u32[]{:S(2)}) collective-permute-start(s16[64,2176]{1,0:T(8,128)(2,1)S(1)} %get-tuple-element.31), channel_id=1, source_target_pairs={{0,2},{1,0},{2,4},{3,1},{4,6},{5,3},{6,7},{7,5},{8,10},{9,8},{10,1... | collective-permute-start | bytes 835592 | tf_op jit(solution)/shard_map/ppermute | solution.py:26
  50.1 6.4 %collective-permute-start.13 = (s16[64,2176]{1,0:T(8,128)(2,1)S(1)}, s16[64,2176]{1,0:T(8,128)(2,1)S(1)}, u32[]{:S(2)}, u32[]{:S(2)}) collective-permute-start(s16[64,2176]{1,0:T(8,128)(2,1)S(1)} %collective-permute-done.11.outer_ref), channel_id=1, source_target_pairs={{3,4},{5,6},{2,1},{4,3},{1,0},{0,2},{6,7},{7,5},{11,12},{13,14},{1... | collective-permute-start | bytes 835592 | tf_op jit(solution)/shard_map/ppermute | solution.py:33
  56.8 2.0 %collective-permute-start.14 = (f32[64,2048]{1,0:T(8,128)S(1)}, f32[64,2048]{1,0:T(8,128)S(1)}, u32[]{:S(2)}, u32[]{:S(2)}) collective-permute-start(f32[64,2048]{1,0:T(8,128)S(1)} %shard_map.64), channel_id=1, source_target_pairs={{0,1},{1,0},{2,3},{3,2},{4,5},{5,4},{6,7},{7,6},{8,9},{9,8},{10,11... | collective-permute-start | bytes 1572872 | tf_op jit(solution)/shard_map/ppermute | solution.py:17
  58.8 16.5 %copy-start.2 = (f32[64]{0:T(128)S(1)}, f32[64]{0:T(128)}, u32[]{:S(2)}) copy-start(f32[64]{0:T(128)} %param.7) | copy-start | bytes 772
  59.5 1.3 %collective-permute-start.15 = (f32[64,128]{1,0:T(8,128)S(1)}, f32[64,128]{1,0:T(8,128)S(1)}, u32[]{:S(2)}, u32[]{:S(2)}) collective-permute-start(f32[64,128]{1,0:T(8,128)S(1)} %get-tuple-element.35), channel_id=1, source_target_pairs={{0,1},{1,0},{2,3},{3,2},{4,5},{5,4},{6,7},{7,6},{8,9},{9,8},{10,11... | collective-permute-start | bytes 98312 | tf_op jit(solution)/shard_map/ppermute | solution.py:17
  60.8 6.5 %collective-permute-start.16 = (f32[64,128]{1,0:T(8,128)S(1)}, f32[64,128]{1,0:T(8,128)S(1)}, u32[]{:S(2)}, u32[]{:S(2)}) collective-permute-start(f32[64,128]{1,0:T(8,128)S(1)} %add.12), channel_id=1, source_target_pairs={{0,2},{1,3},{2,0},{3,1},{4,6},{5,7},{6,4},{7,5},{8,10},{9,11},{10,... | collective-permute-start | bytes 98312 | tf_op jit(solution)/shard_map/ppermute | solution.py:17
  63.3 5.9 %collective-permute-start.17 = (f32[64,128]{1,0:T(8,128)S(1)}, f32[64,128]{1,0:T(8,128)S(1)}, u32[]{:S(2)}, u32[]{:S(2)}) collective-permute-start(f32[64,128]{1,0:T(8,128)S(1)} %add.12), channel_id=1, source_target_pairs={{0,4},{1,5},{2,6},{3,7},{4,0},{5,1},{6,2},{7,3},{8,12},{9,13},{10,... | collective-permute-start | bytes 98312 | tf_op jit(solution)/shard_map/ppermute | solution.py:17
  63.5 5.8 %collective-permute-start.18 = (f32[64,128]{1,0:T(8,128)S(1)}, f32[64,128]{1,0:T(8,128)S(1)}, u32[]{:S(2)}, u32[]{:S(2)}) collective-permute-start(f32[64,128]{1,0:T(8,128)S(1)} %add.12), channel_id=1, source_target_pairs={{0,6},{1,7},{2,4},{3,5},{4,2},{5,3},{6,0},{7,1},{8,14},{9,15},{10,... | collective-permute-start | bytes 98312 | tf_op jit(solution)/shard_map/ppermute | solution.py:17
  65.7 13.3 %collective-permute-start.22 = (f32[64,512]{1,0:T(8,128)S(1)}, f32[64,512]{1,0:T(8,128)S(1)}, u32[]{:S(2)}, u32[]{:S(2)}) collective-permute-start(f32[64,512]{1,0:T(8,128)S(1)} %get-tuple-element.36.z0), channel_id=1, source_target_pairs={{0,8},{8,0},{16,24},{24,16},{1,9},{9,1},{17,25},{25,17},{2,10},{10... | collective-permute-start | bytes 393224 | tf_op jit(solution)/shard_map/ppermute | solution.py:17
  66.3 12.8 %collective-permute-start.23 = (f32[64,512]{1,0:T(8,128)S(1)}, f32[64,512]{1,0:T(8,128)S(1)}, u32[]{:S(2)}, u32[]{:S(2)}) collective-permute-start(f32[64,512]{1,0:T(8,128)S(1)} %get-tuple-element.36.z0), channel_id=1, source_target_pairs={{0,16},{8,24},{16,0},{24,8},{1,17},{9,25},{17,1},{25,9},{2,18},{10... | collective-permute-start | bytes 393224 | tf_op jit(solution)/shard_map/ppermute | solution.py:17
  67.3 11.7 %collective-permute-start.24 = (f32[64,512]{1,0:T(8,128)S(1)}, f32[64,512]{1,0:T(8,128)S(1)}, u32[]{:S(2)}, u32[]{:S(2)}) collective-permute-start(f32[64,512]{1,0:T(8,128)S(1)} %get-tuple-element.36.z0), channel_id=1, source_target_pairs={{0,24},{8,16},{16,8},{24,0},{1,25},{9,17},{17,9},{25,1},{2,26},{10... | collective-permute-start | bytes 393224 | tf_op jit(solution)/shard_map/ppermute | solution.py:17
  69.4 4.9 %collective-permute-start.19 = (f32[64,128]{1,0:T(8,128)S(1)}, f32[64,128]{1,0:T(8,128)S(1)}, u32[]{:S(2)}, u32[]{:S(2)}) collective-permute-start(f32[64,128]{1,0:T(8,128)S(1)} %add_add_fusion.p0), channel_id=1, source_target_pairs={{0,8},{8,0},{16,24},{24,16},{1,9},{9,1},{17,25},{25,17},{2,10},{10... | collective-permute-start | bytes 98312 | tf_op jit(solution)/shard_map/ppermute | solution.py:17
  70.0 5.4 %collective-permute-start.20 = (f32[64,128]{1,0:T(8,128)S(1)}, f32[64,128]{1,0:T(8,128)S(1)}, u32[]{:S(2)}, u32[]{:S(2)}) collective-permute-start(f32[64,128]{1,0:T(8,128)S(1)} %add_add_fusion.p0), channel_id=1, source_target_pairs={{0,16},{8,24},{16,0},{24,8},{1,17},{9,25},{17,1},{25,9},{2,18},{10... | collective-permute-start | bytes 98312 | tf_op jit(solution)/shard_map/ppermute | solution.py:17
  74.3 4.8 %collective-permute-start.21 = (f32[64,128]{1,0:T(8,128)S(1)}, f32[64,128]{1,0:T(8,128)S(1)}, u32[]{:S(2)}, u32[]{:S(2)}) collective-permute-start(f32[64,128]{1,0:T(8,128)S(1)} %add_add_fusion.p0), channel_id=1, source_target_pairs={{0,24},{8,16},{16,8},{24,0},{1,25},{9,17},{17,9},{25,1},{2,26},{10... | collective-permute-start | bytes 98312 | tf_op jit(solution)/shard_map/ppermute | solution.py:17

commit v5 on v4

v5 whole, which is shorter than its diff:
```python
import functools

import jax
import jax.numpy as jnp
from jax import lax
from jax.experimental import pallas as pl
from jax.experimental.pallas import tpu as pltpu
from jax.sharding import PartitionSpec as P


AUX = 128
CHUNK = 512
UNIT = 14
ROWS = 128


def swap(value, axis, bits):
    return lax.ppermute(value, axis, [(i, i ^ bits) for i in range(lax.axis_size(axis))])


def crossing(value, rising):
    count = lax.axis_size("snp")
    pairs = []
    for i in range(count):
        target = i + 2 if i % 2 == rising else i - 2
        pairs.append((i, target if 0 <= target < count else i ^ 1))
    return lax.ppermute(value, "snp", pairs)


def distant(value):
    count = lax.axis_size("snp")
    both = [(i, i + 3) for i in range(1, count - 3, 2)] + [(0, 2), (count - 3, count - 1)]
    return lax.ppermute(value, "snp", both + [(j, i) for i, j in both])


def shifted(value):
    count = lax.axis_size("snp")
    return lax.ppermute(value, "snp", [(i, (i + 2) % count) for i in range(count)])


def partners(value, axis, low, high):
    return [swap(value, axis, k) for k in (low, high, low + high)]


def total(parts):
    own, one, two, three = parts
    return (own + one) + (two + three)


def call(body, out_shape, *args):
    specs = [pl.BlockSpec(memory_space=pltpu.VMEM) for _ in args]
    outs = [jax.ShapeDtypeStruct(shape, kind) for shape, kind in out_shape]
    return pl.pallas_call(
        body,
        out_shape=outs,
        in_specs=specs,
        out_specs=[pl.BlockSpec(memory_space=pltpu.VMEM) for _ in outs],
        compiler_params=pltpu.CompilerParams(vmem_limit_bytes=32 << 20),
    )(*args)


def two_terms(value):
    high = value.astype(jnp.bfloat16)
    low = (value - high.astype(jnp.float32)).astype(jnp.bfloat16)
    return jnp.concatenate([high, low], 0)


def stats_kernel(width_ref, dosage_ref, sums_ref):
    acc = jnp.zeros((8, dosage_ref.shape[1]), jnp.float32)
    square = acc
    for k in range(0, dosage_ref.shape[0], ROWS):
        part = dosage_ref[pl.ds(k, ROWS)].astype(jnp.float32)
        part = part.reshape(ROWS // 8, 8, part.shape[1])
        acc = acc + jnp.sum(part, 0)
        square = square + jnp.sum(part * part, 0)
    row = lax.broadcasted_iota(jnp.int32, (8, 1), 0)
    first = jnp.sum(acc, 0, keepdims=True)
    second = jnp.sum(square, 0, keepdims=True)
    width = width_ref[...].astype(jnp.float32).reshape(1, 1)
    sums_ref[...] = jnp.where(row == 0, first, jnp.where(row == 1, second, width))


def finish(coded_ref, exponent, width):
    lane = lax.broadcasted_iota(jnp.int32, (coded_ref.shape[0], AUX), 1)
    extra = jnp.where(lane == 0, exponent, jnp.where(lane == 1, width, 0.0))
    coded_ref[:, pl.ds(coded_ref.shape[1] - AUX, AUX)] = extra.astype(jnp.int32).astype(jnp.int16)


def fixed(value):
    return jnp.clip(jnp.round(value), -32767.0, 32767.0).astype(jnp.int32).astype(jnp.int16)


def encode(own_ref, coded_ref, width):
    peak = jnp.max(jnp.abs(own_ref[...]), 1, keepdims=True)
    exponent = jnp.floor(jnp.log2(jnp.maximum(peak, 1e-30)))
    scale = jnp.exp2(UNIT - exponent)
    for k in range(0, own_ref.shape[1], CHUNK):
        coded_ref[:, pl.ds(k, CHUNK)] = fixed(own_ref[:, pl.ds(k, CHUNK)] * scale)
    finish(coded_ref, exponent, width)


def aux(coded_ref):
    extra = coded_ref[:, pl.ds(coded_ref.shape[1] - AUX, AUX)].astype(jnp.int32).astype(jnp.float32)
    return extra[:, :1], extra[:, 1:2]


def unit(exponent, use):
    return jnp.where(use, jnp.exp2(exponent - UNIT), 0.0)


def values(coded_ref, k):
    return coded_ref[:, pl.ds(k, CHUNK)].astype(jnp.int32).astype(jnp.float32)


def project(value, scaled_ref, own_ref):
    rows = value.shape[0]
    terms = two_terms(value)
    for k in range(0, scaled_ref.shape[0], CHUNK):
        both = lax.dot_general(
            terms, scaled_ref[pl.ds(k, CHUNK)], (((1,), (1,)), ((), ())), preferred_element_type=jnp.float32
        )
        own_ref[:, pl.ds(k, CHUNK)] = both[:rows] + both[rows:]


def first_kernel(samples, s0, s1, s2, s3, dosage_ref, start_ref, scaled_ref, own_ref, coded_ref):
    sums = total([s[0:2] for s in (s0, s1, s2, s3)])
    width = s0[2:3, 0:1]
    center = sums[0:1] / samples
    spread = sums[1:2] / samples - center * center
    factor = lax.rsqrt(spread + 1e-05)
    for k in range(0, dosage_ref.shape[0], CHUNK):
        part = dosage_ref[pl.ds(k, CHUNK)].astype(jnp.float32)
        scaled_ref[pl.ds(k, CHUNK)] = ((part - center) * factor).astype(jnp.bfloat16)
    project(start_ref[...], scaled_ref, own_ref)
    encode(own_ref, coded_ref, width)


def next_kernel(
    samples, groups, sums_ref, z0, z1, z2, z3, start_ref, scaled_ref, first_ref, parts_ref, own_ref, coded_ref
):
    first = total([z[...] for z in (z0, z1, z2, z3)]) / samples
    first_ref[...] = first
    start = start_ref[...]
    lane = lax.broadcasted_iota(jnp.int32, parts_ref.shape, 1)
    parts = jnp.zeros(parts_ref.shape, jnp.float32)
    for k, (a, b) in enumerate(((start, start), (start, first), (first, first))):
        parts = jnp.where(lane == k, jnp.sum(a * b, 1, keepdims=True) / groups, parts)
    parts_ref[...] = parts
    project(first, scaled_ref, own_ref)
    encode(own_ref, coded_ref, sums_ref[2:3, 0:1])


def place(count):
    index = lax.axis_index("snp")
    odd = (index & 1) == 1
    below, above = (index >= 2).astype(jnp.int32), (index < count - 2).astype(jnp.int32)
    outer = jnp.where(odd, below, above) == 1
    inner = jnp.where(odd, above, below) == 1
    far = jnp.where(odd, (index < count - 3).astype(jnp.int32), (index >= 3).astype(jnp.int32)) == 1
    return odd, outer, inner, far


def give_kernel(count, near_ref, own_ref, coded_ref, partner_ref, outer_ref, inner_ref):
    odd = place(count)[0]
    exponent, width = aux(coded_ref)
    partner_exponent, partner_width = aux(partner_ref)
    near = near_ref[2:3, 0:1]
    sent = jnp.maximum(exponent, partner_exponent) + 1.0
    scale = jnp.exp2(UNIT - sent)
    partner_scale = scale * jnp.exp2(partner_exponent - UNIT)
    flag = lambda value, least: (value >= least).astype(jnp.float32)
    up_own = flag(width, 2.0) * scale
    up_partner = flag(partner_width, jnp.where(odd, 3.0, 1.0)) * partner_scale
    down_own = flag(near, 2.0) * scale
    down_partner = flag(near, jnp.where(odd, 1.0, 3.0)) * partner_scale
    choose = lambda even_case, odd_case: jnp.where(odd, odd_case, even_case)
    outer_own, outer_partner = choose(down_own, up_own), choose(down_partner, up_partner)
    inner_own, inner_partner = choose(up_own, down_own), choose(up_partner, down_partner)
    for k in range(0, own_ref.shape[1], CHUNK):
        own, partner = own_ref[:, pl.ds(k, CHUNK)], values(partner_ref, k)
        outer_ref[:, pl.ds(k, CHUNK)] = fixed(own * outer_own + partner * outer_partner)
        inner_ref[:, pl.ds(k, CHUNK)] = fixed(own * inner_own + partner * inner_partner)
    finish(outer_ref, sent, width)
    finish(inner_ref, sent, width)


def window_kernel(samples, count, own_ref, coded_ref, partner_ref, outer_ref, inner_ref, far_ref, scaled_ref, *refs):
    odd, use_outer, use_inner, use_far = place(count)
    _, width = aux(coded_ref)
    partner_exponent, partner_width = aux(partner_ref)
    far_exponent, far_width = aux(far_ref)
    partner_scale = unit(partner_exponent, jnp.where(odd, partner_width, width) >= 1)
    outer_scale = unit(aux(outer_ref)[0], use_outer)
    inner_scale = unit(aux(inner_ref)[0], use_inner)
    far_scale = jnp.where(jnp.where(odd, width, far_width) >= 3, unit(far_exponent, use_far), 0.0)
    out_ref = refs[-1]
    rows = own_ref.shape[0]
    acc = jnp.zeros((2 * rows, scaled_ref.shape[1]), jnp.float32)
    curved = jnp.zeros((rows, CHUNK), jnp.float32)
    for k in range(0, own_ref.shape[1], CHUNK):
        own = own_ref[:, pl.ds(k, CHUNK)]
        mixed = (
            own
            + values(partner_ref, k) * partner_scale
            + values(outer_ref, k) * outer_scale
            + values(inner_ref, k) * inner_scale
            + values(far_ref, k) * far_scale
        )
        acc = acc + jnp.dot(
            two_terms(mixed), scaled_ref[pl.ds(k, CHUNK)], preferred_element_type=jnp.float32
        )
        curved = curved + own * mixed
    out_ref[...] = acc[:rows] + acc[rows:]
    if len(refs) == 3:
        parts_ref, sums_ref = refs[:2]
        lane = lax.broadcasted_iota(jnp.int32, parts_ref.shape, 1)
        sums = jnp.where(lane == 3, jnp.sum(curved, 1, keepdims=True) / samples, parts_ref[...])
        filled = jnp.concatenate([sums, jnp.zeros((AUX - rows, AUX), jnp.float32)], 0)
        sums_ref[...] = filled.T[:8]


def last_kernel(samples, shrink_ref, p0, p1, p2, p3, z0, z1, start_ref, first_ref, effects_ref, residual_ref):
    rows = shrink_ref.shape[0]
    flat = total([p[...] for p in (p0, p1, p2, p3)])
    parts = jnp.concatenate([flat, jnp.zeros((AUX - 8, AUX), jnp.float32)], 0).T[:rows]
    bb, bw, ww, wu = (parts[:, k : k + 1] for k in range(4))
    shrink = shrink_ref[...]
    start, first = start_ref[...], first_ref[...]
    second = (z0[...] + z1[...]) / samples
    ratio = bw / bb
    step = 1.0 / (ratio + shrink)
    norm = step * step * (ww - ratio * bw)
    bend = norm / bb
    curve = step * step * (ratio * (ratio * bw - 2.0 * ww) + wu) + shrink * norm - bend * norm / step
    step2 = jnp.where(curve > 0, norm / curve, 0.0)
    rest = step * (ratio * start - first)
    direction = rest + bend * start
    image = step * (ratio * first - second) + bend * first + shrink * direction
    effects_ref[...] = step * start + step2 * direction
    residual_ref[...] = rest - step2 * image


def snp_sum(value):
    count = lax.axis_size("snp")
    value = value + swap(value, "snp", 1)
    bit = 2
    while bit < count:
        if 2 * bit < count:
            value = total([value, *partners(value, "snp", bit, 2 * bit)])
        else:
            value = value + swap(value, "snp", bit)
        bit *= 4
    return value


def shards(dosage, band_width, marginal, penalty):
    groups, count = lax.axis_size("samp"), lax.axis_size("snp")
    local, size, rows = dosage.shape[0], dosage.shape[1], marginal.shape[1]
    samples = local * groups
    start = marginal.T
    shrink = penalty[:, None]
    grid, own_shape, flat = (rows, size), (rows, local), (8, AUX)
    coded_out = ((rows, local + AUX), jnp.int16)

    (sums,) = call(stats_kernel, [((8, size), jnp.float32)], band_width, dosage)
    others = partners(sums, "samp", 1, 2)
    near = shifted(sums)
    others, near = lax.optimization_barrier((others, near))
    scaled, own, coded = call(
        functools.partial(first_kernel, samples),
        [(dosage.shape, jnp.bfloat16), (own_shape, jnp.float32), coded_out],
        sums, *others, dosage, start,
    )

    def window(own, coded, extra, outs):
        far = distant(coded)
        partner = swap(coded, "snp", 1)
        outer, inner = call(
            functools.partial(give_kernel, count), [coded_out, coded_out], near, own, coded, partner
        )
        return call(
            functools.partial(window_kernel, samples, count), outs,
            own, coded, partner, crossing(outer, 1), crossing(inner, 0), far, scaled, *extra,
        )

    (z,) = window(own, coded, (), [(grid, jnp.float32)])
    first, parts, own, coded = call(
        functools.partial(next_kernel, samples, groups),
        [(grid, jnp.float32), ((rows, AUX), jnp.float32), (own_shape, jnp.float32), coded_out],
        sums, z, *partners(z, "samp", 1, 2), start, scaled,
    )
    parts, z = window(own, coded, (parts,), [(flat, jnp.float32), (grid, jnp.float32)])
    z = z + swap(z, "samp", 1)
    z, parts = lax.optimization_barrier((z, snp_sum(parts)))
    effects, residual = call(
        functools.partial(last_kernel, samples),
        [(grid, jnp.float32), (grid, jnp.float32)],
        shrink, parts, *partners(parts, "samp", 1, 2), z, swap(z, "samp", 2), start, first,
    )
    return (effects.T, residual.T)


def solution(mesh):
    in_specs = (P("samp", "snp"), P("snp"), P("snp", None), P())
    out_specs = (P("snp", None), P("snp", None))
    return jax.shard_map(shards, mesh=mesh, in_specs=in_specs, out_specs=out_specs, check_vma=False)
```

time: 80.4 us -> 76.6 us (0.953)
  waiting for transfers between devices: 42.6 us -> 40.5 us
  starting transfers between devices: 29.2 us -> 27.1 us
    ppermute x19 -> x17, waiting for transfers between devices: 21.9 us -> 16.2 us  [swap(): lax.ppermute(value, axis, [(i, i ^ bits) for i in range(lax.axis_size(axi...]
    ppermute x2 -> x3, waiting for transfers between devices: 8.13 us -> 13.5 us  [the longest x2 12.4 us: distant(): return lax.ppermute(value, 'snp', both + [(j, i) for i, j in both])]
    ppermute x4, waiting for transfers between devices: 12.7 us -> 10.8 us  [crossing(): return lax.ppermute(value, 'snp', pairs)]
    ppermute x19 -> x17, starting transfers between devices: 20.1 us -> 18.9 us  [swap(): lax.ppermute(value, axis, [(i, i ^ bits) for i in range(lax.axis_size(axi...]
    ppermute x4, starting transfers between devices: 5.15 us -> 4.08 us  [crossing(): return lax.ppermute(value, 'snp', pairs)]
    ppermute x2 -> x3, starting transfers between devices: 3.91 us -> 4.08 us  [the longest x2 2.05 us: distant(): return lax.ppermute(value, 'snp', both + [(j, i) for i, j in both])]
  transfers between devices with their start and end apart: 25 -> 24, of which waited for: 16 -> 17; matrix products, arithmetic and copies ran while one was open for 0% -> 0% of each run, Pallas kernels for 0% -> 1%
where the time goes in v5:
time: 76.6 us; the launch traced here: 76.4 us
  waiting for transfers between devices  40.5 us (53%)
  starting transfers between devices  27.1 us (35%)
  Pallas kernels  5.75 us (8%)
  local copies, waits for them, and re-layouts  1.69 us (2%)
  between operations  1.39 us (2%)
    ppermute x17, starting transfers between devices, swap(): lax.ppermute(value, axis, [(i, i ^ bits) for i in range(lax.axis_size(axi...  18.9 us
    ppermute x17, waiting for transfers between devices, swap(): lax.ppermute(value, axis, [(i, i ^ bits) for i in range(lax.axis_size(axi...  16.2 us
    ppermute x2, waiting for transfers between devices, distant(): return lax.ppermute(value, 'snp', both + [(j, i) for i, j in both])  12.4 us
    ppermute x4, waiting for transfers between devices, crossing(): return lax.ppermute(value, 'snp', pairs)  10.8 us
    pallas_call x8, Pallas kernels, call(): pl.pallas_call(body, out_shape=outs, in_specs=specs, out_specs=[pl.BlockS...  5.75 us
    ppermute x4, starting transfers between devices, crossing(): return lax.ppermute(value, 'snp', pairs)  4.08 us
    ppermute x2, starting transfers between devices, distant(): return lax.ppermute(value, 'snp', both + [(j, i) for i, j in both])  2.05 us
    ppermute x1, starting transfers between devices, shifted(): lax.ppermute(value, 'snp', [(i, (i + 2) % count) for i in range(count)])  2.03 us
  transfers between devices with their start and end apart: 24, of which 17 were waited for; matrix products, arithmetic and copies ran while one was open for 0% of the time, Pallas kernels for 1%

profile of v5, /device:TPU:0, one launch (start us, length us, event | category | flops | bytes accessed | tf_op | source)
XLA Modules:
  0.0 76.4 jit_solution(8828990403417855711)
XLA Ops:
  1.3 0.0 copy-start
  1.3 1.6 %copy-done = bf16[2048,512]{1,0:T(8,128)(2,1)S(1)} copy-done((bf16[2048,512]{1,0:T(8,128)(2,1)S(1)}, bf16[2048,512]{1,0:T(8,128)(2,1)}, u32[]{:S(2)}) %copy-start) | copy-done | bytes 2097176
  2.9 0.0 copy-start.1
  2.9 0.4 shard_map.59.s0.sums_ref
  3.3 3.0 %collective-permute-start = (f32[8,512]{1,0:T(8,128)S(1)}, f32[8,512]{1,0:T(8,128)S(1)}, u32[]{:S(2)}, u32[]{:S(2)}) collective-permute-start(f32[8,512]{1,0:T(8,128)S(1)} %shard_map.59.s0.sums_ref), channel_id=1, source_target_pairs={{0,8},{8,0},{16,24},{24,16},{1,9},{9,1},{17,25},{25,17},{2,10},{10... | collective-permute-start | bytes 49160 | tf_op jit(solution)/shard_map/ppermute | solution.py:18
  6.3 1.5 %collective-permute-start.1 = (f32[8,512]{1,0:T(8,128)S(1)}, f32[8,512]{1,0:T(8,128)S(1)}, u32[]{:S(2)}, u32[]{:S(2)}) collective-permute-start(f32[8,512]{1,0:T(8,128)S(1)} %shard_map.59.s0.sums_ref), channel_id=1, source_target_pairs={{0,16},{8,24},{16,0},{24,8},{1,17},{9,25},{17,1},{25,9},{2,18},{10... | collective-permute-start | bytes 49160 | tf_op jit(solution)/shard_map/ppermute | solution.py:18
  7.8 0.0 collective-permute-start.2
  7.8 2.0 %collective-permute-start.3 = (f32[8,512]{1,0:T(8,128)S(1)}, f32[8,512]{1,0:T(8,128)S(1)}, u32[]{:S(2)}, u32[]{:S(2)}) collective-permute-start(f32[8,512]{1,0:T(8,128)S(1)} %shard_map.59.s0.sums_ref), channel_id=1, source_target_pairs={{0,2},{1,3},{2,4},{3,5},{4,6},{5,7},{6,0},{7,1},{8,10},{9,11},{10,... | collective-permute-start | bytes 49160 | tf_op jit(solution)/shard_map/ppermute | solution.py:38
  9.8 0.0 collective-permute-done.s1
  9.8 0.2 collective-permute-done.1.s2
  10.0 2.4 %collective-permute-done.2.s3 = f32[8,512]{1,0:T(8,128)S(1)} collective-permute-done((f32[8,512]{1,0:T(8,128)S(1)}, f32[8,512]{1,0:T(8,128)S(1)}, u32[]{:S(2)}, u32[]{:S(2)}) %collective-permute-start.2) | collective-permute-done | bytes 16416 | tf_op jit(solution)/shard_map/ppermute | solution.py:18
  12.4 1.2 %collective-permute-done.3.near_ref = f32[8,512]{1,0:T(8,128)S(1)} collective-permute-done((f32[8,512]{1,0:T(8,128)S(1)}, f32[8,512]{1,0:T(8,128)S(1)}, u32[]{:S(2)}, u32[]{:S(2)}) %collective-permute-start.3) | collective-permute-done | bytes 16416 | tf_op jit(solution)/shard_map/ppermute | solution.py:38
  13.6 0.0 copy-done.1
  13.6 1.0 %shard_map.60 = (bf16[2048,512]{1,0:T(8,128)(2,1)S(1)}, f32[64,2048]{1,0:T(8,128)S(1)}, s16[64,2176]{1,0:T(8,128)(2,1)S(1)}) custom-call(f32[8,512]{1,0:T(8,128)S(1)} %shard_map.59.s0.sums_ref, f32[8,512]{1,0:T(8,128)S(1)} %collective-permute-done.s1, f32[8,512]{1,0:T(8,128)S(1)} %collective-permute-done.1.s2, f32[8,512]{1,0:T(8,128)S(1)} %collective-permute-done.2.s3, ...), custom_call_target="tpu_custom_call" | custom-call | tf_op jit(solution)/shard_map/pallas_call | solution.py:53
  14.6 0.1 collective-permute-start.4
  14.7 0.5 collective-permute-start.7
  15.2 1.1 %collective-permute-done.4.partner_ref = s16[64,2176]{1,0:T(8,128)(2,1)S(1)} collective-permute-done((s16[64,2176]{1,0:T(8,128)(2,1)S(1)}, s16[64,2176]{1,0:T(8,128)(2,1)S(1)}, u32[]{:S(2)}, u32[]{:S(2)}) %collective-permute-start.4) | collective-permute-done | bytes 278560 | tf_op jit(solution)/shard_map/ppermute | solution.py:18
  16.2 0.4 shard_map.61
  16.6 0.2 collective-permute-start.5
  16.8 1.9 %collective-permute-start.6 = (s16[64,2176]{1,0:T(8,128)(2,1)S(1)}, s16[64,2176]{1,0:T(8,128)(2,1)S(1)}, u32[]{:S(2)}, u32[]{:S(2)}) collective-permute-start(s16[64,2176]{1,0:T(8,128)(2,1)S(1)} %get-tuple-element.30), channel_id=1, source_target_pairs={{0,2},{1,0},{2,4},{3,1},{4,6},{5,3},{6,7},{7,5},{8,10},{9,8},{10,1... | collective-permute-start | bytes 835592 | tf_op jit(solution)/shard_map/ppermute | solution.py:27
  18.7 5.5 %collective-permute-done.7.far_ref = s16[64,2176]{1,0:T(8,128)(2,1)S(1)} collective-permute-done((s16[64,2176]{1,0:T(8,128)(2,1)S(1)}, s16[64,2176]{1,0:T(8,128)(2,1)S(1)}, u32[]{:S(2)}, u32[]{:S(2)}) %collective-permute-start.7) | collective-permute-done | bytes 278560 | tf_op jit(solution)/shard_map/ppermute | solution.py:33
  24.2 6.0 %collective-permute-done.5.outer_ref = s16[64,2176]{1,0:T(8,128)(2,1)S(1)} collective-permute-done((s16[64,2176]{1,0:T(8,128)(2,1)S(1)}, s16[64,2176]{1,0:T(8,128)(2,1)S(1)}, u32[]{:S(2)}, u32[]{:S(2)}) %collective-permute-start.5) | collective-permute-done | bytes 278560 | tf_op jit(solution)/shard_map/ppermute | solution.py:27
  30.2 0.0 collective-permute-done.6.inner_ref
  30.2 0.6 shard_map.62.z0
  30.8 2.7 %collective-permute-start.10 = (f32[64,512]{1,0:T(8,128)S(1)}, f32[64,512]{1,0:T(8,128)S(1)}, u32[]{:S(2)}, u32[]{:S(2)}) collective-permute-start(f32[64,512]{1,0:T(8,128)S(1)} %shard_map.62.z0), channel_id=1, source_target_pairs={{0,24},{8,16},{16,8},{24,0},{1,25},{9,17},{17,9},{25,1},{2,26},{10... | collective-permute-start | bytes 393224 | tf_op jit(solution)/shard_map/ppermute | solution.py:18
  33.6 0.5 collective-permute-start.8
  34.1 0.3 collective-permute-start.9
  34.4 3.0 %collective-permute-done.10.z3 = f32[64,512]{1,0:T(8,128)S(1)} collective-permute-done((f32[64,512]{1,0:T(8,128)S(1)}, f32[64,512]{1,0:T(8,128)S(1)}, u32[]{:S(2)}, u32[]{:S(2)}) %collective-permute-start.10) | collective-permute-done | bytes 131104 | tf_op jit(solution)/shard_map/ppermute | solution.py:18
  37.4 1.3 %collective-permute-done.8.z1 = f32[64,512]{1,0:T(8,128)S(1)} collective-permute-done((f32[64,512]{1,0:T(8,128)S(1)}, f32[64,512]{1,0:T(8,128)S(1)}, u32[]{:S(2)}, u32[]{:S(2)}) %collective-permute-start.8) | collective-permute-done | bytes 131104 | tf_op jit(solution)/shard_map/ppermute | solution.py:18
  38.8 0.3 collective-permute-done.9.z2
  39.1 1.0 %shard_map.63 = (f32[64,512]{1,0:T(8,128)S(1)}, f32[64,128]{1,0:T(8,128)S(1)}, f32[64,2048]{1,0:T(8,128)S(1)}, s16[64,2176]{1,0:T(8,128)(2,1)S(1)}) custom-call(f32[8,512]{1,0:T(8,128)S(1)} %shard_map.59.s0.sums_ref, f32[64,512]{1,0:T(8,128)S(1)} %shard_map.62.z0, f32[64,512]{1,0:T(8,128)S(1)} %collective-permute-done.8.z1, ...), custom_call_target="tpu_custom_call" | custom-call | tf_op jit(solution)/shard_map/pallas_call | solution.py:53
  40.0 0.1 collective-permute-start.11
  40.1 1.6 %collective-permute-start.14 = (s16[64,2176]{1,0:T(8,128)(2,1)S(1)}, s16[64,2176]{1,0:T(8,128)(2,1)S(1)}, u32[]{:S(2)}, u32[]{:S(2)}) collective-permute-start(s16[64,2176]{1,0:T(8,128)(2,1)S(1)} %get-tuple-element.33.coded_ref), channel_id=1, source_target_pairs={{1,4},{3,6},{0,2},{5,7},{4,1},{6,3},{2,0},{7,5},{9,12},{11,14},{8,... | collective-permute-start | bytes 835592 | tf_op jit(solution)/shard_map/ppermute | solution.py:33
  41.7 0.0 collective-permute-done.11.partner_ref
  41.7 0.4 shard_map.64
  42.1 1.2 %collective-permute-start.12 = (s16[64,2176]{1,0:T(8,128)(2,1)S(1)}, s16[64,2176]{1,0:T(8,128)(2,1)S(1)}, u32[]{:S(2)}, u32[]{:S(2)}) collective-permute-start(s16[64,2176]{1,0:T(8,128)(2,1)S(1)} %get-tuple-element.34), channel_id=1, source_target_pairs={{0,1},{1,3},{2,0},{3,5},{4,2},{5,7},{6,4},{7,6},{8,9},{9,11},{10,8... | collective-permute-start | bytes 835592 | tf_op jit(solution)/shard_map/ppermute | solution.py:27
  43.3 0.9 %collective-permute-start.13 = (s16[64,2176]{1,0:T(8,128)(2,1)S(1)}, s16[64,2176]{1,0:T(8,128)(2,1)S(1)}, u32[]{:S(2)}, u32[]{:S(2)}) collective-permute-start(s16[64,2176]{1,0:T(8,128)(2,1)S(1)} %get-tuple-element.35), channel_id=1, source_target_pairs={{0,2},{1,0},{2,4},{3,1},{4,6},{5,3},{6,7},{7,5},{8,10},{9,8},{10,1... | collective-permute-start | bytes 835592 | tf_op jit(solution)/shard_map/ppermute | solution.py:27
  44.1 6.8 %collective-permute-done.14.far_ref = s16[64,2176]{1,0:T(8,128)(2,1)S(1)} collective-permute-done((s16[64,2176]{1,0:T(8,128)(2,1)S(1)}, s16[64,2176]{1,0:T(8,128)(2,1)S(1)}, u32[]{:S(2)}, u32[]{:S(2)}) %collective-permute-start.14) | collective-permute-done | bytes 278560 | tf_op jit(solution)/shard_map/ppermute | solution.py:33
  51.0 4.7 %collective-permute-done.12.outer_ref = s16[64,2176]{1,0:T(8,128)(2,1)S(1)} collective-permute-done((s16[64,2176]{1,0:T(8,128)(2,1)S(1)}, s16[64,2176]{1,0:T(8,128)(2,1)S(1)}, u32[]{:S(2)}, u32[]{:S(2)}) %collective-permute-start.12) | collective-permute-done | bytes 278560 | tf_op jit(solution)/shard_map/ppermute | solution.py:27
  55.7 0.0 collective-permute-done.13.inner_ref
  55.7 0.0 copy-start.2
  55.7 0.8 %shard_map.65 = (f32[8,128]{1,0:T(8,128)S(1)}, f32[64,512]{1,0:T(8,128)S(1)}) custom-call(f32[64,2048]{1,0:T(8,128)S(1)} %get-tuple-element.32.own_ref, s16[64,2176]{1,0:T(8,128)(2,1)S(1)} %get-tuple-element.33.coded_ref, s16[64,2176]{1,0:T(8,128)(2,1)S(1)} %collective-permute-done.11.partner_ref, s16[64,2176]{1,0:T(8,128)(2,1)S(1)} %collective-permute-done.12.outer_ref, ...), custom_call_target="tpu_custom_call" | custom-call | tf_op jit(solution)/shard_map/pallas_call | solution.py:53
  56.5 0.1 collective-permute-start.16
  56.6 1.2 %collective-permute-done.16 = f32[8,128]{1,0:T(8,128)S(1)} collective-permute-done((f32[8,128]{1,0:T(8,128)S(1)}, f32[8,128]{1,0:T(8,128)S(1)}, u32[]{:S(2)}, u32[]{:S(2)}) %collective-permute-start.16) | collective-permute-done | bytes 4128 | tf_op jit(solution)/shard_map/ppermute | solution.py:18
  57.7 1.5 %collective-permute-start.17 = (f32[8,128]{1,0:T(8,128)S(1)}, f32[8,128]{1,0:T(8,128)S(1)}, u32[]{:S(2)}, u32[]{:S(2)}) collective-permute-start(f32[8,128]{1,0:T(8,128)S(1)} %add.16), channel_id=1, source_target_pairs={{0,2},{1,3},{2,0},{3,1},{4,6},{5,7},{6,4},{7,5},{8,10},{9,11},{10,... | collective-permute-start | bytes 12296 | tf_op jit(solution)/shard_map/ppermute | solution.py:18
  59.2 0.7 collective-permute-start.18
  59.9 2.2 %collective-permute-start.19 = (f32[8,128]{1,0:T(8,128)S(1)}, f32[8,128]{1,0:T(8,128)S(1)}, u32[]{:S(2)}, u32[]{:S(2)}) collective-permute-start(f32[8,128]{1,0:T(8,128)S(1)} %add.16), channel_id=1, source_target_pairs={{0,6},{1,7},{2,4},{3,5},{4,2},{5,3},{6,0},{7,1},{8,14},{9,15},{10,... | collective-permute-start | bytes 12296 | tf_op jit(solution)/shard_map/ppermute | solution.py:18
  62.1 1.5 %collective-permute-start.15 = (f32[64,512]{1,0:T(8,128)S(1)}, f32[64,512]{1,0:T(8,128)S(1)}, u32[]{:S(2)}, u32[]{:S(2)}) collective-permute-start(f32[64,512]{1,0:T(8,128)S(1)} %get-tuple-element.37), channel_id=1, source_target_pairs={{0,8},{8,0},{16,24},{24,16},{1,9},{9,1},{17,25},{25,17},{2,10},{10... | collective-permute-start | bytes 393224 | tf_op jit(solution)/shard_map/ppermute | solution.py:18
  63.6 0.0 collective-permute-done.17
  63.6 0.1 collective-permute-done.18
  63.7 1.6 %collective-permute-done.19 = f32[8,128]{1,0:T(8,128)S(1)} collective-permute-done((f32[8,128]{1,0:T(8,128)S(1)}, f32[8,128]{1,0:T(8,128)S(1)}, u32[]{:S(2)}, u32[]{:S(2)}) %collective-permute-start.19) | collective-permute-done | bytes 4128 | tf_op jit(solution)/shard_map/ppermute | solution.py:18
  65.3 1.8 %collective-permute-done.15 = f32[64,512]{1,0:T(8,128)S(1)} collective-permute-done((f32[64,512]{1,0:T(8,128)S(1)}, f32[64,512]{1,0:T(8,128)S(1)}, u32[]{:S(2)}, u32[]{:S(2)}) %collective-permute-start.15) | collective-permute-done | bytes 131104 | tf_op jit(solution)/shard_map/ppermute | solution.py:18
  67.1 1.2 %collective-permute-start.23 = (f32[64,512]{1,0:T(8,128)S(1)}, f32[64,512]{1,0:T(8,128)S(1)}, u32[]{:S(2)}, u32[]{:S(2)}) collective-permute-start(f32[64,512]{1,0:T(8,128)S(1)} %add.15.z0), channel_id=1, source_target_pairs={{0,16},{8,24},{16,0},{24,8},{1,17},{9,25},{17,1},{25,9},{2,18},{10... | collective-permute-start | bytes 393224 | tf_op jit(solution)/shard_map/ppermute | solution.py:18
  68.4 1.5 %collective-permute-start.20 = (f32[8,128]{1,0:T(8,128)S(1)}, f32[8,128]{1,0:T(8,128)S(1)}, u32[]{:S(2)}, u32[]{:S(2)}) collective-permute-start(f32[8,128]{1,0:T(8,128)S(1)} %add_add_fusion.p0), channel_id=1, source_target_pairs={{0,8},{8,0},{16,24},{24,16},{1,9},{9,1},{17,25},{25,17},{2,10},{10... | collective-permute-start | bytes 12296 | tf_op jit(solution)/shard_map/ppermute | solution.py:18
  69.8 0.9 %collective-permute-start.21 = (f32[8,128]{1,0:T(8,128)S(1)}, f32[8,128]{1,0:T(8,128)S(1)}, u32[]{:S(2)}, u32[]{:S(2)}) collective-permute-start(f32[8,128]{1,0:T(8,128)S(1)} %add_add_fusion.p0), channel_id=1, source_target_pairs={{0,16},{8,24},{16,0},{24,8},{1,17},{9,25},{17,1},{25,9},{2,18},{10... | collective-permute-start | bytes 12296 | tf_op jit(solution)/shard_map/ppermute | solution.py:18
  70.7 1.1 %collective-permute-start.22 = (f32[8,128]{1,0:T(8,128)S(1)}, f32[8,128]{1,0:T(8,128)S(1)}, u32[]{:S(2)}, u32[]{:S(2)}) collective-permute-start(f32[8,128]{1,0:T(8,128)S(1)} %add_add_fusion.p0), channel_id=1, source_target_pairs={{0,24},{8,16},{16,8},{24,0},{1,25},{9,17},{17,9},{25,1},{2,26},{10... | collective-permute-start | bytes 12296 | tf_op jit(solution)/shard_map/ppermute | solution.py:18
  71.8 0.0 copy-done.2
  71.8 0.1 copy.6.shrink_ref
  71.9 0.0 collective-permute-done.20.p1
  72.0 1.5 %collective-permute-done.21.p2 = f32[8,128]{1,0:T(8,128)S(1)} collective-permute-done((f32[8,128]{1,0:T(8,128)S(1)}, f32[8,128]{1,0:T(8,128)S(1)}, u32[]{:S(2)}, u32[]{:S(2)}) %collective-permute-start.21) | collective-permute-done | bytes 4128 | tf_op jit(solution)/shard_map/ppermute | solution.py:18
  73.4 1.8 %collective-permute-done.22.p3 = f32[8,128]{1,0:T(8,128)S(1)} collective-permute-done((f32[8,128]{1,0:T(8,128)S(1)}, f32[8,128]{1,0:T(8,128)S(1)}, u32[]{:S(2)}, u32[]{:S(2)}) %collective-permute-start.22) | collective-permute-done | bytes 4128 | tf_op jit(solution)/shard_map/ppermute | solution.py:18
  75.2 0.0 collective-permute-done.23.z1
  75.2 1.2 %shard_map.66 = (f32[64,512]{1,0:T(8,128)}, f32[64,512]{1,0:T(8,128)}) custom-call(f32[64,1]{1,0:T(8,128)S(1)} %copy.6.shrink_ref, f32[8,128]{1,0:T(8,128)S(1)} %add_add_fusion.p0, f32[8,128]{1,0:T(8,128)S(1)} %collective-permute-done.20.p1, f32[8,128]{1,0:T(8,128)S(1)} %collective-permute-done.21.p2, f32[8,128]{1,0:T(8,128)S(1)} %collective-permute-done.22.p3, ...), custom_call_target="tpu_custom_call" | custom-call | tf_op jit(solution)/shard_map/pallas_call | solution.py:53
  (3 shorter events, 0.0 us)
Async XLA Ops:
  1.3 1.6 %copy-start = (bf16[2048,512]{1,0:T(8,128)(2,1)S(1)}, bf16[2048,512]{1,0:T(8,128)(2,1)}, u32[]{:S(2)}) copy-start(bf16[2048,512]{1,0:T(8,128)(2,1)} %dosage_ref.3) | copy-start | bytes 6291460
  2.9 10.7 %copy-start.1 = (f32[512,64]{0,1:T(8,128)S(1)}, f32[512,64]{0,1:T(8,128)}, u32[]{:S(2)}) copy-start(f32[512,64]{0,1:T(8,128)} %param.6) | copy-start | bytes 393220
  3.3 6.6 %collective-permute-start = (f32[8,512]{1,0:T(8,128)S(1)}, f32[8,512]{1,0:T(8,128)S(1)}, u32[]{:S(2)}, u32[]{:S(2)}) collective-permute-start(f32[8,512]{1,0:T(8,128)S(1)} %shard_map.59.s0.sums_ref), channel_id=1, source_target_pairs={{0,8},{8,0},{16,24},{24,16},{1,9},{9,1},{17,25},{25,17},{2,10},{10... | collective-permute-start | bytes 49160 | tf_op jit(solution)/shard_map/ppermute | solution.py:18
  6.3 3.7 %collective-permute-start.1 = (f32[8,512]{1,0:T(8,128)S(1)}, f32[8,512]{1,0:T(8,128)S(1)}, u32[]{:S(2)}, u32[]{:S(2)}) collective-permute-start(f32[8,512]{1,0:T(8,128)S(1)} %shard_map.59.s0.sums_ref), channel_id=1, source_target_pairs={{0,16},{8,24},{16,0},{24,8},{1,17},{9,25},{17,1},{25,9},{2,18},{10... | collective-permute-start | bytes 49160 | tf_op jit(solution)/shard_map/ppermute | solution.py:18
  7.8 4.6 %collective-permute-start.2 = (f32[8,512]{1,0:T(8,128)S(1)}, f32[8,512]{1,0:T(8,128)S(1)}, u32[]{:S(2)}, u32[]{:S(2)}) collective-permute-start(f32[8,512]{1,0:T(8,128)S(1)} %shard_map.59.s0.sums_ref), channel_id=1, source_target_pairs={{0,24},{8,16},{16,8},{24,0},{1,25},{9,17},{17,9},{25,1},{2,26},{10... | collective-permute-start | bytes 49160 | tf_op jit(solution)/shard_map/ppermute | solution.py:18
  7.8 5.8 %collective-permute-start.3 = (f32[8,512]{1,0:T(8,128)S(1)}, f32[8,512]{1,0:T(8,128)S(1)}, u32[]{:S(2)}, u32[]{:S(2)}) collective-permute-start(f32[8,512]{1,0:T(8,128)S(1)} %shard_map.59.s0.sums_ref), channel_id=1, source_target_pairs={{0,2},{1,3},{2,4},{3,5},{4,6},{5,7},{6,0},{7,1},{8,10},{9,11},{10,... | collective-permute-start | bytes 49160 | tf_op jit(solution)/shard_map/ppermute | solution.py:38
  14.6 1.6 %collective-permute-start.4 = (s16[64,2176]{1,0:T(8,128)(2,1)S(1)}, s16[64,2176]{1,0:T(8,128)(2,1)S(1)}, u32[]{:S(2)}, u32[]{:S(2)}) collective-permute-start(s16[64,2176]{1,0:T(8,128)(2,1)S(1)} %get-tuple-element.27.coded_ref), channel_id=1, source_target_pairs={{0,1},{1,0},{2,3},{3,2},{4,5},{5,4},{6,7},{7,6},{8,9},{9,8},{10,11... | collective-permute-start | bytes 835592 | tf_op jit(solution)/shard_map/ppermute | solution.py:18
  14.7 9.5 %collective-permute-start.7 = (s16[64,2176]{1,0:T(8,128)(2,1)S(1)}, s16[64,2176]{1,0:T(8,128)(2,1)S(1)}, u32[]{:S(2)}, u32[]{:S(2)}) collective-permute-start(s16[64,2176]{1,0:T(8,128)(2,1)S(1)} %get-tuple-element.27.coded_ref), channel_id=1, source_target_pairs={{1,4},{3,6},{0,2},{5,7},{4,1},{6,3},{2,0},{7,5},{9,12},{11,14},{8,... | collective-permute-start | bytes 835592 | tf_op jit(solution)/shard_map/ppermute | solution.py:33
  16.6 13.6 %collective-permute-start.5 = (s16[64,2176]{1,0:T(8,128)(2,1)S(1)}, s16[64,2176]{1,0:T(8,128)(2,1)S(1)}, u32[]{:S(2)}, u32[]{:S(2)}) collective-permute-start(s16[64,2176]{1,0:T(8,128)(2,1)S(1)} %get-tuple-element.29), channel_id=1, source_target_pairs={{0,1},{1,3},{2,0},{3,5},{4,2},{5,7},{6,4},{7,6},{8,9},{9,11},{10,8... | collective-permute-start | bytes 835592 | tf_op jit(solution)/shard_map/ppermute | solution.py:27
  16.8 13.5 %collective-permute-start.6 = (s16[64,2176]{1,0:T(8,128)(2,1)S(1)}, s16[64,2176]{1,0:T(8,128)(2,1)S(1)}, u32[]{:S(2)}, u32[]{:S(2)}) collective-permute-start(s16[64,2176]{1,0:T(8,128)(2,1)S(1)} %get-tuple-element.30), channel_id=1, source_target_pairs={{0,2},{1,0},{2,4},{3,1},{4,6},{5,3},{6,7},{7,5},{8,10},{9,8},{10,1... | collective-permute-start | bytes 835592 | tf_op jit(solution)/shard_map/ppermute | solution.py:27
  30.8 6.6 %collective-permute-start.10 = (f32[64,512]{1,0:T(8,128)S(1)}, f32[64,512]{1,0:T(8,128)S(1)}, u32[]{:S(2)}, u32[]{:S(2)}) collective-permute-start(f32[64,512]{1,0:T(8,128)S(1)} %shard_map.62.z0), channel_id=1, source_target_pairs={{0,24},{8,16},{16,8},{24,0},{1,25},{9,17},{17,9},{25,1},{2,26},{10... | collective-permute-start | bytes 393224 | tf_op jit(solution)/shard_map/ppermute | solution.py:18
  33.6 5.2 %collective-permute-start.8 = (f32[64,512]{1,0:T(8,128)S(1)}, f32[64,512]{1,0:T(8,128)S(1)}, u32[]{:S(2)}, u32[]{:S(2)}) collective-permute-start(f32[64,512]{1,0:T(8,128)S(1)} %shard_map.62.z0), channel_id=1, source_target_pairs={{0,8},{8,0},{16,24},{24,16},{1,9},{9,1},{17,25},{25,17},{2,10},{10... | collective-permute-start | bytes 393224 | tf_op jit(solution)/shard_map/ppermute | solution.py:18
  34.1 5.0 %collective-permute-start.9 = (f32[64,512]{1,0:T(8,128)S(1)}, f32[64,512]{1,0:T(8,128)S(1)}, u32[]{:S(2)}, u32[]{:S(2)}) collective-permute-start(f32[64,512]{1,0:T(8,128)S(1)} %shard_map.62.z0), channel_id=1, source_target_pairs={{0,16},{8,24},{16,0},{24,8},{1,17},{9,25},{17,1},{25,9},{2,18},{10... | collective-permute-start | bytes 393224 | tf_op jit(solution)/shard_map/ppermute | solution.py:18
  40.0 1.6 %collective-permute-start.11 = (s16[64,2176]{1,0:T(8,128)(2,1)S(1)}, s16[64,2176]{1,0:T(8,128)(2,1)S(1)}, u32[]{:S(2)}, u32[]{:S(2)}) collective-permute-start(s16[64,2176]{1,0:T(8,128)(2,1)S(1)} %get-tuple-element.33.coded_ref), channel_id=1, source_target_pairs={{0,1},{1,0},{2,3},{3,2},{4,5},{5,4},{6,7},{7,6},{8,9},{9,8},{10,11... | collective-permute-start | bytes 835592 | tf_op jit(solution)/shard_map/ppermute | solution.py:18
  40.1 10.8 %collective-permute-start.14 = (s16[64,2176]{1,0:T(8,128)(2,1)S(1)}, s16[64,2176]{1,0:T(8,128)(2,1)S(1)}, u32[]{:S(2)}, u32[]{:S(2)}) collective-permute-start(s16[64,2176]{1,0:T(8,128)(2,1)S(1)} %get-tuple-element.33.coded_ref), channel_id=1, source_target_pairs={{1,4},{3,6},{0,2},{5,7},{4,1},{6,3},{2,0},{7,5},{9,12},{11,14},{8,... | collective-permute-start | bytes 835592 | tf_op jit(solution)/shard_map/ppermute | solution.py:33
  42.1 13.6 %collective-permute-start.12 = (s16[64,2176]{1,0:T(8,128)(2,1)S(1)}, s16[64,2176]{1,0:T(8,128)(2,1)S(1)}, u32[]{:S(2)}, u32[]{:S(2)}) collective-permute-start(s16[64,2176]{1,0:T(8,128)(2,1)S(1)} %get-tuple-element.34), channel_id=1, source_target_pairs={{0,1},{1,3},{2,0},{3,5},{4,2},{5,7},{6,4},{7,6},{8,9},{9,11},{10,8... | collective-permute-start | bytes 835592 | tf_op jit(solution)/shard_map/ppermute | solution.py:27
  43.3 12.4 %collective-permute-start.13 = (s16[64,2176]{1,0:T(8,128)(2,1)S(1)}, s16[64,2176]{1,0:T(8,128)(2,1)S(1)}, u32[]{:S(2)}, u32[]{:S(2)}) collective-permute-start(s16[64,2176]{1,0:T(8,128)(2,1)S(1)} %get-tuple-element.35), channel_id=1, source_target_pairs={{0,2},{1,0},{2,4},{3,1},{4,6},{5,3},{6,7},{7,5},{8,10},{9,8},{10,1... | collective-permute-start | bytes 835592 | tf_op jit(solution)/shard_map/ppermute | solution.py:27
  55.7 16.2 %copy-start.2 = (f32[64]{0:T(128)S(1)}, f32[64]{0:T(128)}, u32[]{:S(2)}) copy-start(f32[64]{0:T(128)} %param.7) | copy-start | bytes 772
  56.5 1.2 %collective-permute-start.16 = (f32[8,128]{1,0:T(8,128)S(1)}, f32[8,128]{1,0:T(8,128)S(1)}, u32[]{:S(2)}, u32[]{:S(2)}) collective-permute-start(f32[8,128]{1,0:T(8,128)S(1)} %get-tuple-element.38), channel_id=1, source_target_pairs={{0,1},{1,0},{2,3},{3,2},{4,5},{5,4},{6,7},{7,6},{8,9},{9,8},{10,11... | collective-permute-start | bytes 12296 | tf_op jit(solution)/shard_map/ppermute | solution.py:18
  57.7 5.9 %collective-permute-start.17 = (f32[8,128]{1,0:T(8,128)S(1)}, f32[8,128]{1,0:T(8,128)S(1)}, u32[]{:S(2)}, u32[]{:S(2)}) collective-permute-start(f32[8,128]{1,0:T(8,128)S(1)} %add.16), channel_id=1, source_target_pairs={{0,2},{1,3},{2,0},{3,1},{4,6},{5,7},{6,4},{7,5},{8,10},{9,11},{10,... | collective-permute-start | bytes 12296 | tf_op jit(solution)/shard_map/ppermute | solution.py:18
  59.2 4.5 %collective-permute-start.18 = (f32[8,128]{1,0:T(8,128)S(1)}, f32[8,128]{1,0:T(8,128)S(1)}, u32[]{:S(2)}, u32[]{:S(2)}) collective-permute-start(f32[8,128]{1,0:T(8,128)S(1)} %add.16), channel_id=1, source_target_pairs={{0,4},{1,5},{2,6},{3,7},{4,0},{5,1},{6,2},{7,3},{8,12},{9,13},{10,... | collective-permute-start | bytes 12296 | tf_op jit(solution)/shard_map/ppermute | solution.py:18
  59.9 5.4 %collective-permute-start.19 = (f32[8,128]{1,0:T(8,128)S(1)}, f32[8,128]{1,0:T(8,128)S(1)}, u32[]{:S(2)}, u32[]{:S(2)}) collective-permute-start(f32[8,128]{1,0:T(8,128)S(1)} %add.16), channel_id=1, source_target_pairs={{0,6},{1,7},{2,4},{3,5},{4,2},{5,3},{6,0},{7,1},{8,14},{9,15},{10,... | collective-permute-start | bytes 12296 | tf_op jit(solution)/shard_map/ppermute | solution.py:18
  62.1 5.0 %collective-permute-start.15 = (f32[64,512]{1,0:T(8,128)S(1)}, f32[64,512]{1,0:T(8,128)S(1)}, u32[]{:S(2)}, u32[]{:S(2)}) collective-permute-start(f32[64,512]{1,0:T(8,128)S(1)} %get-tuple-element.37), channel_id=1, source_target_pairs={{0,8},{8,0},{16,24},{24,16},{1,9},{9,1},{17,25},{25,17},{2,10},{10... | collective-permute-start | bytes 393224 | tf_op jit(solution)/shard_map/ppermute | solution.py:18
  67.1 8.1 %collective-permute-start.23 = (f32[64,512]{1,0:T(8,128)S(1)}, f32[64,512]{1,0:T(8,128)S(1)}, u32[]{:S(2)}, u32[]{:S(2)}) collective-permute-start(f32[64,512]{1,0:T(8,128)S(1)} %add.15.z0), channel_id=1, source_target_pairs={{0,16},{8,24},{16,0},{24,8},{1,17},{9,25},{17,1},{25,9},{2,18},{10... | collective-permute-start | bytes 393224 | tf_op jit(solution)/shard_map/ppermute | solution.py:18
  68.4 3.6 %collective-permute-start.20 = (f32[8,128]{1,0:T(8,128)S(1)}, f32[8,128]{1,0:T(8,128)S(1)}, u32[]{:S(2)}, u32[]{:S(2)}) collective-permute-start(f32[8,128]{1,0:T(8,128)S(1)} %add_add_fusion.p0), channel_id=1, source_target_pairs={{0,8},{8,0},{16,24},{24,16},{1,9},{9,1},{17,25},{25,17},{2,10},{10... | collective-permute-start | bytes 12296 | tf_op jit(solution)/shard_map/ppermute | solution.py:18
  69.8 3.6 %collective-permute-start.21 = (f32[8,128]{1,0:T(8,128)S(1)}, f32[8,128]{1,0:T(8,128)S(1)}, u32[]{:S(2)}, u32[]{:S(2)}) collective-permute-start(f32[8,128]{1,0:T(8,128)S(1)} %add_add_fusion.p0), channel_id=1, source_target_pairs={{0,16},{8,24},{16,0},{24,8},{1,17},{9,25},{17,1},{25,9},{2,18},{10... | collective-permute-start | bytes 12296 | tf_op jit(solution)/shard_map/ppermute | solution.py:18
  70.7 4.5 %collective-permute-start.22 = (f32[8,128]{1,0:T(8,128)S(1)}, f32[8,128]{1,0:T(8,128)S(1)}, u32[]{:S(2)}, u32[]{:S(2)}) collective-permute-start(f32[8,128]{1,0:T(8,128)S(1)} %add_add_fusion.p0), channel_id=1, source_target_pairs={{0,24},{8,16},{16,8},{24,0},{1,25},{9,17},{17,9},{25,1},{2,26},{10... | collective-permute-start | bytes 12296 | tf_op jit(solution)/shard_map/ppermute | solution.py:18

commit v6 on v5

--- a/solution.py
+++ b/solution.py
@@ -65,7 +65,7 @@
     return jnp.concatenate([high, low], 0)
 
 
-def stats_kernel(width_ref, dosage_ref, sums_ref):
+def stats_kernel(dosage_ref, sums_ref):
     acc = jnp.zeros((8, dosage_ref.shape[1]), jnp.float32)
     square = acc
     for k in range(0, dosage_ref.shape[0], ROWS):
@@ -76,13 +76,14 @@
     row = lax.broadcasted_iota(jnp.int32, (8, 1), 0)
     first = jnp.sum(acc, 0, keepdims=True)
     second = jnp.sum(square, 0, keepdims=True)
-    width = width_ref[...].astype(jnp.float32).reshape(1, 1)
-    sums_ref[...] = jnp.where(row == 0, first, jnp.where(row == 1, second, width))
-
-
-def finish(coded_ref, exponent, width):
+    sums_ref[...] = jnp.where(row == 0, first, second)
+
+
+def finish(coded_ref, *columns):
     lane = lax.broadcasted_iota(jnp.int32, (coded_ref.shape[0], AUX), 1)
-    extra = jnp.where(lane == 0, exponent, jnp.where(lane == 1, width, 0.0))
+    extra = jnp.zeros(lane.shape, jnp.float32)
+    for k, column in enumerate(columns):
+        extra = jnp.where(lane == k, column, extra)
     coded_ref[:, pl.ds(coded_ref.shape[1] - AUX, AUX)] = extra.astype(jnp.int32).astype(jnp.int16)
 
 
@@ -90,22 +91,37 @@
     return jnp.clip(jnp.round(value), -32767.0, 32767.0).astype(jnp.int32).astype(jnp.int16)
 
 
+def scale_of(peak):
+    exponent = jnp.floor(jnp.log2(jnp.maximum(peak, 1e-30)))
+    return exponent, jnp.exp2(UNIT - exponent)
+
+
 def encode(own_ref, coded_ref, width):
-    peak = jnp.max(jnp.abs(own_ref[...]), 1, keepdims=True)
-    exponent = jnp.floor(jnp.log2(jnp.maximum(peak, 1e-30)))
-    scale = jnp.exp2(UNIT - exponent)
+    exponent, scale = scale_of(jnp.max(jnp.abs(own_ref[...]), 1, keepdims=True))
     for k in range(0, own_ref.shape[1], CHUNK):
         coded_ref[:, pl.ds(k, CHUNK)] = fixed(own_ref[:, pl.ds(k, CHUNK)] * scale)
     finish(coded_ref, exponent, width)
 
 
+def split(value):
+    exponent, scale = scale_of(jnp.abs(value))
+    high = jnp.round(value * scale * 0.5)
+    low = jnp.round((value * scale * 0.5 - high) * 2.0**UNIT)
+    return exponent, high, low
+
+
 def aux(coded_ref):
     extra = coded_ref[:, pl.ds(coded_ref.shape[1] - AUX, AUX)].astype(jnp.int32).astype(jnp.float32)
-    return extra[:, :1], extra[:, 1:2]
-
-
-def unit(exponent, use):
+    return [extra[:, k : k + 1] for k in range(4)]
+
+
+def unit(exponent, use=True):
     return jnp.where(use, jnp.exp2(exponent - UNIT), 0.0)
+
+
+def grid_values(coded_ref):
+    size = coded_ref.shape[1] - AUX
+    return coded_ref[:, pl.ds(0, size)].astype(jnp.int32).astype(jnp.float32) * unit(aux(coded_ref)[0])
 
 
 def values(coded_ref, k):
@@ -122,9 +138,8 @@
         own_ref[:, pl.ds(k, CHUNK)] = both[:rows] + both[rows:]
 
 
-def first_kernel(samples, s0, s1, s2, s3, dosage_ref, start_ref, scaled_ref, own_ref, coded_ref):
+def first_kernel(samples, wide_ref, s0, s1, s2, s3, dosage_ref, start_ref, scaled_ref, own_ref, coded_ref):
     sums = total([s[0:2] for s in (s0, s1, s2, s3)])
-    width = s0[2:3, 0:1]
     center = sums[0:1] / samples
     spread = sums[1:2] / samples - center * center
     factor = lax.rsqrt(spread + 1e-05)
@@ -132,22 +147,22 @@
         part = dosage_ref[pl.ds(k, CHUNK)].astype(jnp.float32)
         scaled_ref[pl.ds(k, CHUNK)] = ((part - center) * factor).astype(jnp.bfloat16)
     project(start_ref[...], scaled_ref, own_ref)
-    encode(own_ref, coded_ref, width)
+    encode(own_ref, coded_ref, wide_ref[0:1, 0:1])
 
 
 def next_kernel(
-    samples, groups, sums_ref, z0, z1, z2, z3, start_ref, scaled_ref, first_ref, parts_ref, own_ref, coded_ref
+    samples, wide_ref, z0, z1, z2, z3, start_ref, scaled_ref, first_ref, parts_ref, own_ref, coded_ref
 ):
-    first = total([z[...] for z in (z0, z1, z2, z3)]) / samples
+    first = total([grid_values(z) for z in (z0, z1, z2, z3)]) / samples
     first_ref[...] = first
     start = start_ref[...]
     lane = lax.broadcasted_iota(jnp.int32, parts_ref.shape, 1)
     parts = jnp.zeros(parts_ref.shape, jnp.float32)
     for k, (a, b) in enumerate(((start, start), (start, first), (first, first))):
-        parts = jnp.where(lane == k, jnp.sum(a * b, 1, keepdims=True) / groups, parts)
+        parts = jnp.where(lane == k, jnp.sum(a * b, 1, keepdims=True), parts)
     parts_ref[...] = parts
     project(first, scaled_ref, own_ref)
-    encode(own_ref, coded_ref, sums_ref[2:3, 0:1])
+    encode(own_ref, coded_ref, wide_ref[0:1, 0:1])
 
 
 def place(count):
@@ -162,9 +177,9 @@
 
 def give_kernel(count, near_ref, own_ref, coded_ref, partner_ref, outer_ref, inner_ref):
     odd = place(count)[0]
-    exponent, width = aux(coded_ref)
-    partner_exponent, partner_width = aux(partner_ref)
-    near = near_ref[2:3, 0:1]
+    exponent, width = aux(coded_ref)[:2]
+    partner_exponent, partner_width = aux(partner_ref)[:2]
+    near = near_ref[0:1, 0:1]
     sent = jnp.maximum(exponent, partner_exponent) + 1.0
     scale = jnp.exp2(UNIT - sent)
     partner_scale = scale * jnp.exp2(partner_exponent - UNIT)
@@ -184,16 +199,15 @@
     finish(inner_ref, sent, width)
 
 
-def window_kernel(samples, count, own_ref, coded_ref, partner_ref, outer_ref, inner_ref, far_ref, scaled_ref, *refs):
+def window_kernel(samples, count, own_ref, coded_ref, partner_ref, outer_ref, inner_ref, far_ref, scaled_ref, sent_ref):
     odd, use_outer, use_inner, use_far = place(count)
-    _, width = aux(coded_ref)
-    partner_exponent, partner_width = aux(partner_ref)
-    far_exponent, far_width = aux(far_ref)
+    width = aux(coded_ref)[1]
+    partner_exponent, partner_width = aux(partner_ref)[:2]
+    far_exponent, far_width = aux(far_ref)[:2]
     partner_scale = unit(partner_exponent, jnp.where(odd, partner_width, width) >= 1)
     outer_scale = unit(aux(outer_ref)[0], use_outer)
     inner_scale = unit(aux(inner_ref)[0], use_inner)
     far_scale = jnp.where(jnp.where(odd, width, far_width) >= 3, unit(far_exponent, use_far), 0.0)
-    out_ref = refs[-1]
     rows = own_ref.shape[0]
     acc = jnp.zeros((2 * rows, scaled_ref.shape[1]), jnp.float32)
     curved = jnp.zeros((rows, CHUNK), jnp.float32)
@@ -210,23 +224,31 @@
             two_terms(mixed), scaled_ref[pl.ds(k, CHUNK)], preferred_element_type=jnp.float32
         )
         curved = curved + own * mixed
-    out_ref[...] = acc[:rows] + acc[rows:]
-    if len(refs) == 3:
-        parts_ref, sums_ref = refs[:2]
-        lane = lax.broadcasted_iota(jnp.int32, parts_ref.shape, 1)
-        sums = jnp.where(lane == 3, jnp.sum(curved, 1, keepdims=True) / samples, parts_ref[...])
-        filled = jnp.concatenate([sums, jnp.zeros((AUX - rows, AUX), jnp.float32)], 0)
-        sums_ref[...] = filled.T[:8]
-
-
-def last_kernel(samples, shrink_ref, p0, p1, p2, p3, z0, z1, start_ref, first_ref, effects_ref, residual_ref):
+    z = acc[:rows] + acc[rows:]
+    exponent, scale = scale_of(jnp.max(jnp.abs(z), 1, keepdims=True))
+    sent_ref[:, pl.ds(0, z.shape[1])] = fixed(z * scale)
+    finish(sent_ref, exponent, *split(jnp.sum(curved, 1, keepdims=True) / samples))
+
+
+def collect_kernel(parts_ref, z0, z1, z2, z3, flat_ref):
+    terms = []
+    for z in (z0, z1, z2, z3):
+        _, exponent, high, low = aux(z)
+        terms.append((high + low * 2.0**-UNIT) * 2.0 * unit(exponent))
+    lane = lax.broadcasted_iota(jnp.int32, parts_ref.shape, 1)
+    parts = jnp.where(lane == 3, total(terms), parts_ref[...])
+    filled = jnp.concatenate([parts, jnp.zeros((AUX - parts.shape[0], AUX), jnp.float32)], 0)
+    flat_ref[...] = filled.T[:8]
+
+
+def last_kernel(samples, shrink_ref, p0, p1, p2, p3, z0, z1, z2, z3, start_ref, first_ref, effects_ref, residual_ref):
     rows = shrink_ref.shape[0]
     flat = total([p[...] for p in (p0, p1, p2, p3)])
     parts = jnp.concatenate([flat, jnp.zeros((AUX - 8, AUX), jnp.float32)], 0).T[:rows]
     bb, bw, ww, wu = (parts[:, k : k + 1] for k in range(4))
     shrink = shrink_ref[...]
     start, first = start_ref[...], first_ref[...]
-    second = (z0[...] + z1[...]) / samples
+    second = total([grid_values(z) for z in (z0, z1, z2, z3)]) / samples
     ratio = bw / bb
     step = 1.0 / (ratio + shrink)
     norm = step * step * (ww - ratio * bw)
@@ -240,17 +262,16 @@
     residual_ref[...] = rest - step2 * image
 
 
-def snp_sum(value):
+def snp_parts(value):
     count = lax.axis_size("snp")
     value = value + swap(value, "snp", 1)
     bit = 2
-    while bit < count:
-        if 2 * bit < count:
-            value = total([value, *partners(value, "snp", bit, 2 * bit)])
-        else:
-            value = value + swap(value, "snp", bit)
+    while 4 * bit < count:
+        value = total([value, *partners(value, "snp", bit, 2 * bit)])
         bit *= 4
-    return value
+    if 2 * bit < count:
+        return [value, *partners(value, "snp", bit, 2 * bit)]
+    return [value, swap(value, "snp", bit), jnp.zeros_like(value), jnp.zeros_like(value)]
 
 
 def shards(dosage, band_width, marginal, penalty):
@@ -259,43 +280,47 @@
     samples = local * groups
     start = marginal.T
     shrink = penalty[:, None]
-    grid, own_shape, flat = (rows, size), (rows, local), (8, AUX)
-    coded_out = ((rows, local + AUX), jnp.int16)
-
-    (sums,) = call(stats_kernel, [((8, size), jnp.float32)], band_width, dosage)
-    others = partners(sums, "samp", 1, 2)
-    near = shifted(sums)
-    others, near = lax.optimization_barrier((others, near))
+    grid, own_shape = (rows, size), (rows, local)
+    own_out, coded_out = (own_shape, jnp.float32), ((rows, local + AUX), jnp.int16)
+
+    sent_out = ((rows, size + AUX), jnp.int16)
+
+    (sums,) = call(stats_kernel, [((8, size), jnp.float32)], dosage)
+    one, two, three = partners(sums, "samp", 1, 2)
+    one, band_width = lax.optimization_barrier((one, band_width))
+    wide = jnp.broadcast_to(band_width.astype(jnp.float32)[:, None], (8, AUX))
+    near = shifted(wide)
+    two, three, near = lax.optimization_barrier((two, three, near))
     scaled, own, coded = call(
         functools.partial(first_kernel, samples),
-        [(dosage.shape, jnp.bfloat16), (own_shape, jnp.float32), coded_out],
-        sums, *others, dosage, start,
+        [(dosage.shape, jnp.bfloat16), own_out, coded_out],
+        wide, sums, one, two, three, dosage, start,
     )
 
-    def window(own, coded, extra, outs):
+    def window(own, coded):
         far = distant(coded)
         partner = swap(coded, "snp", 1)
         outer, inner = call(
             functools.partial(give_kernel, count), [coded_out, coded_out], near, own, coded, partner
         )
-        return call(
-            functools.partial(window_kernel, samples, count), outs,
-            own, coded, partner, crossing(outer, 1), crossing(inner, 0), far, scaled, *extra,
-        )
-
-    (z,) = window(own, coded, (), [(grid, jnp.float32)])
+        (z,) = call(
+            functools.partial(window_kernel, samples, count), [sent_out],
+            own, coded, partner, crossing(outer, 1), crossing(inner, 0), far, scaled,
+        )
+        return [z, *partners(z, "samp", 1, 2)]
+
     first, parts, own, coded = call(
-        functools.partial(next_kernel, samples, groups),
-        [(grid, jnp.float32), ((rows, AUX), jnp.float32), (own_shape, jnp.float32), coded_out],
-        sums, z, *partners(z, "samp", 1, 2), start, scaled,
+        functools.partial(next_kernel, samples),
+        [(grid, jnp.float32), ((rows, AUX), jnp.float32), own_out, coded_out],
+        wide, *window(own, coded), start, scaled,
     )
-    parts, z = window(own, coded, (parts,), [(flat, jnp.float32), (grid, jnp.float32)])
-    z = z + swap(z, "samp", 1)
-    z, parts = lax.optimization_barrier((z, snp_sum(parts)))
+    zs = window(own, coded)
+    (flat,) = call(collect_kernel, [((8, AUX), jnp.float32)], parts, *zs)
+    parts = snp_parts(flat)
     effects, residual = call(
         functools.partial(last_kernel, samples),
         [(grid, jnp.float32), (grid, jnp.float32)],
-        shrink, parts, *partners(parts, "samp", 1, 2), z, swap(z, "samp", 2), start, first,
+        shrink, *parts, *zs, start, first,
     )
     return (effects.T, residual.T)
 

time: 76.6 us -> 73.5 us (0.960)
  starting transfers between devices: 27.1 us -> 23.6 us
    ppermute x17 -> x15, waiting for transfers between devices: 16.2 us -> 13.5 us  [swap(): lax.ppermute(value, axis, [(i, i ^ bits) for i in range(lax.axis_size(axi...]
    ppermute x17 -> x15, starting transfers between devices: 18.9 us -> 16.2 us  [swap(): lax.ppermute(value, axis, [(i, i ^ bits) for i in range(lax.axis_size(axi...]
    ppermute x1, waiting for transfers between devices: 1.16 us -> 3.61 us  [shifted(): lax.ppermute(value, 'snp', [(i, (i + 2) % count) for i in range(count)])]
    ppermute x2, starting transfers between devices: 2.05 us -> 1.2 us  [distant(): return lax.ppermute(value, 'snp', both + [(j, i) for i, j in both])]
    pallas_call x8 -> x9, Pallas kernels: 5.75 us -> 6.47 us  [call(): pl.pallas_call(body, out_shape=outs, in_specs=specs, out_specs=[pl.BlockS...]
  transfers between devices with their start and end apart: 24 -> 22, of which waited for: 17 -> 16; matrix products, arithmetic and copies ran while one was open for 0% -> 0% of each run, Pallas kernels for 1% -> 1%
where the time goes in v6:
time: 73.5 us; the launch traced here: 73.3 us
  waiting for transfers between devices  40.2 us (55%)
  starting transfers between devices  23.6 us (32%)
  Pallas kernels  6.47 us (9%)
  local copies, waits for them, and re-layouts  1.69 us (2%)
  between operations  1.41 us (2%)
    ppermute x15, starting transfers between devices, swap(): lax.ppermute(value, axis, [(i, i ^ bits) for i in range(lax.axis_size(axi...  16.2 us
    ppermute x15, waiting for transfers between devices, swap(): lax.ppermute(value, axis, [(i, i ^ bits) for i in range(lax.axis_size(axi...  13.5 us
    ppermute x2, waiting for transfers between devices, distant(): return lax.ppermute(value, 'snp', both + [(j, i) for i, j in both])  11.8 us
    ppermute x4, waiting for transfers between devices, crossing(): return lax.ppermute(value, 'snp', pairs)  11.4 us
    pallas_call x9, Pallas kernels, call(): pl.pallas_call(body, out_shape=outs, in_specs=specs, out_specs=[pl.BlockS...  6.47 us
    ppermute x4, starting transfers between devices, crossing(): return lax.ppermute(value, 'snp', pairs)  4.08 us
    ppermute x1, waiting for transfers between devices, shifted(): lax.ppermute(value, 'snp', [(i, (i + 2) % count) for i in range(count)])  3.61 us
    ppermute x1, starting transfers between devices, shifted(): lax.ppermute(value, 'snp', [(i, (i + 2) % count) for i in range(count)])  2.09 us
  transfers between devices with their start and end apart: 22, of which 16 were waited for; matrix products, arithmetic and copies ran while one was open for 0% of the time, Pallas kernels for 1%

profile of v6, /device:TPU:0, one launch (start us, length us, event | category | flops | bytes accessed | tf_op | source)
XLA Modules:
  0.0 73.3 jit_solution(12030751471979691760)
XLA Ops:
  0.6 0.0 copy-start
  0.6 1.6 %copy-done = bf16[2048,512]{1,0:T(8,128)(2,1)S(1)} copy-done((bf16[2048,512]{1,0:T(8,128)(2,1)S(1)}, bf16[2048,512]{1,0:T(8,128)(2,1)}, u32[]{:S(2)}) %copy-start) | copy-done | bytes 2097176
  2.2 0.0 copy-start.1
  2.2 0.4 shard_map.59.s0
  2.6 3.0 %collective-permute-start = (f32[8,512]{1,0:T(8,128)S(1)}, f32[8,512]{1,0:T(8,128)S(1)}, u32[]{:S(2)}, u32[]{:S(2)}) collective-permute-start(f32[8,512]{1,0:T(8,128)S(1)} %shard_map.59.s0), channel_id=1, source_target_pairs={{0,8},{8,0},{16,24},{24,16},{1,9},{9,1},{17,25},{25,17},{2,10},{10... | collective-permute-start | bytes 49160 | tf_op jit(solution)/shard_map/ppermute | solution.py:18
  5.6 1.5 %collective-permute-start.1 = (f32[8,512]{1,0:T(8,128)S(1)}, f32[8,512]{1,0:T(8,128)S(1)}, u32[]{:S(2)}, u32[]{:S(2)}) collective-permute-start(f32[8,512]{1,0:T(8,128)S(1)} %shard_map.59.s0), channel_id=1, source_target_pairs={{0,16},{8,24},{16,0},{24,8},{1,17},{9,25},{17,1},{25,9},{2,18},{10... | collective-permute-start | bytes 49160 | tf_op jit(solution)/shard_map/ppermute | solution.py:18
  7.1 0.0 collective-permute-start.2
  7.8 2.1 %collective-permute-start.3 = (f32[8,128]{1,0:T(8,128)S(1)}, f32[8,128]{1,0:T(8,128)S(1)}, u32[]{:S(2)}, u32[]{:S(2)}) collective-permute-start(f32[8,128]{1,0:T(8,128)S(1)} %broadcast_in_dim.13.wide_ref), channel_id=1, source_target_pairs={{0,2},{1,3},{2,4},{3,5},{4,6},{5,7},{6,0},{7,1},{8,10},{9,11},{10,... | collective-permute-start | bytes 12296 | tf_op jit(solution)/shard_map/ppermute | solution.py:38
  9.9 0.0 collective-permute-done.s1
  9.9 3.6 %collective-permute-done.3.near_ref = f32[8,128]{1,0:T(8,128)S(1)} collective-permute-done((f32[8,128]{1,0:T(8,128)S(1)}, f32[8,128]{1,0:T(8,128)S(1)}, u32[]{:S(2)}, u32[]{:S(2)}) %collective-permute-start.3) | collective-permute-done | bytes 4128 | tf_op jit(solution)/shard_map/ppermute | solution.py:38
  13.5 0.0 collective-permute-done.1.s2
  13.5 0.0 collective-permute-done.2.s3
  13.5 0.0 copy-done.1
  13.5 1.0 %shard_map.60 = (bf16[2048,512]{1,0:T(8,128)(2,1)S(1)}, f32[64,2048]{1,0:T(8,128)S(1)}, s16[64,2176]{1,0:T(8,128)(2,1)S(1)}) custom-call(f32[8,128]{1,0:T(8,128)S(1)} %broadcast_in_dim.13.wide_ref, f32[8,512]{1,0:T(8,128)S(1)} %shard_map.59.s0, f32[8,512]{1,0:T(8,128)S(1)} %collective-permute-done.s1, f32[8,512]{1,0:T(8,128)S(1)} %collective-permute-done.1.s2, ...), custom_call_target="tpu_custom_call" | custom-call | tf_op jit(solution)/shard_map/pallas_call | solution.py:53
  14.5 0.1 collective-permute-start.4
  14.6 0.1 collective-permute-start.7
  14.7 1.5 %collective-permute-done.4.partner_ref = s16[64,2176]{1,0:T(8,128)(2,1)S(1)} collective-permute-done((s16[64,2176]{1,0:T(8,128)(2,1)S(1)}, s16[64,2176]{1,0:T(8,128)(2,1)S(1)}, u32[]{:S(2)}, u32[]{:S(2)}) %collective-permute-start.4) | collective-permute-done | bytes 278560 | tf_op jit(solution)/shard_map/ppermute | solution.py:18
  16.2 0.4 shard_map.61
  16.6 0.2 collective-permute-start.5
  16.7 1.9 %collective-permute-start.6 = (s16[64,2176]{1,0:T(8,128)(2,1)S(1)}, s16[64,2176]{1,0:T(8,128)(2,1)S(1)}, u32[]{:S(2)}, u32[]{:S(2)}) collective-permute-start(s16[64,2176]{1,0:T(8,128)(2,1)S(1)} %get-tuple-element.28), channel_id=1, source_target_pairs={{0,2},{1,0},{2,4},{3,1},{4,6},{5,3},{6,7},{7,5},{8,10},{9,8},{10,1... | collective-permute-start | bytes 835592 | tf_op jit(solution)/shard_map/ppermute | solution.py:27
  18.6 5.6 %collective-permute-done.7.far_ref = s16[64,2176]{1,0:T(8,128)(2,1)S(1)} collective-permute-done((s16[64,2176]{1,0:T(8,128)(2,1)S(1)}, s16[64,2176]{1,0:T(8,128)(2,1)S(1)}, u32[]{:S(2)}, u32[]{:S(2)}) %collective-permute-start.7) | collective-permute-done | bytes 278560 | tf_op jit(solution)/shard_map/ppermute | solution.py:33
  24.3 5.9 %collective-permute-done.5.outer_ref = s16[64,2176]{1,0:T(8,128)(2,1)S(1)} collective-permute-done((s16[64,2176]{1,0:T(8,128)(2,1)S(1)}, s16[64,2176]{1,0:T(8,128)(2,1)S(1)}, u32[]{:S(2)}, u32[]{:S(2)}) %collective-permute-start.5) | collective-permute-done | bytes 278560 | tf_op jit(solution)/shard_map/ppermute | solution.py:27
  30.2 0.0 collective-permute-done.6.inner_ref
  30.2 0.9 %shard_map.62.z0 = s16[64,640]{1,0:T(8,128)(2,1)S(1)} custom-call(f32[64,2048]{1,0:T(8,128)S(1)} %get-tuple-element.24.own_ref, s16[64,2176]{1,0:T(8,128)(2,1)S(1)} %get-tuple-element.25.coded_ref, s16[64,2176]{1,0:T(8,128)(2,1)S(1)} %collective-permute-done.4.partner_ref, s16[64,2176]{1,0:T(8,128)(2,1)S(1)} %collective-permute-done.5.outer_ref, ...), custom_call_target="tpu_custom_call" | custom-call | tf_op jit(solution)/shard_map/pallas_call | solution.py:53
  31.1 2.7 %collective-permute-start.10 = (s16[64,640]{1,0:T(8,128)(2,1)S(1)}, s16[64,640]{1,0:T(8,128)(2,1)S(1)}, u32[]{:S(2)}, u32[]{:S(2)}) collective-permute-start(s16[64,640]{1,0:T(8,128)(2,1)S(1)} %shard_map.62.z0), channel_id=1, source_target_pairs={{0,24},{8,16},{16,8},{24,0},{1,25},{9,17},{17,9},{25,1},{2,26},{10... | collective-permute-start | bytes 245768 | tf_op jit(solution)/shard_map/ppermute | solution.py:18
  33.9 0.5 collective-permute-start.8
  34.4 0.3 collective-permute-start.9
  34.7 2.0 %collective-permute-done.10.z3 = s16[64,640]{1,0:T(8,128)(2,1)S(1)} collective-permute-done((s16[64,640]{1,0:T(8,128)(2,1)S(1)}, s16[64,640]{1,0:T(8,128)(2,1)S(1)}, u32[]{:S(2)}, u32[]{:S(2)}) %collective-permute-start.10) | collective-permute-done | bytes 81952 | tf_op jit(solution)/shard_map/ppermute | solution.py:18
  36.6 1.7 %collective-permute-done.8.z1 = s16[64,640]{1,0:T(8,128)(2,1)S(1)} collective-permute-done((s16[64,640]{1,0:T(8,128)(2,1)S(1)}, s16[64,640]{1,0:T(8,128)(2,1)S(1)}, u32[]{:S(2)}, u32[]{:S(2)}) %collective-permute-start.8) | collective-permute-done | bytes 81952 | tf_op jit(solution)/shard_map/ppermute | solution.py:18
  38.3 0.5 collective-permute-done.9.z2
  38.8 1.0 %shard_map.63 = (f32[64,512]{1,0:T(8,128)S(1)}, f32[64,128]{1,0:T(8,128)S(1)}, f32[64,2048]{1,0:T(8,128)S(1)}, s16[64,2176]{1,0:T(8,128)(2,1)S(1)}) custom-call(f32[8,128]{1,0:T(8,128)S(1)} %broadcast_in_dim.13.wide_ref, s16[64,640]{1,0:T(8,128)(2,1)S(1)} %shard_map.62.z0, s16[64,640]{1,0:T(8,128)(2,1)S(1)} %collective-permute-done.8.z1, ...), custom_call_target="tpu_custom_call" | custom-call | tf_op jit(solution)/shard_map/pallas_call | solution.py:53
  39.8 0.1 collective-permute-start.11
  39.9 1.1 %collective-permute-start.14 = (s16[64,2176]{1,0:T(8,128)(2,1)S(1)}, s16[64,2176]{1,0:T(8,128)(2,1)S(1)}, u32[]{:S(2)}, u32[]{:S(2)}) collective-permute-start(s16[64,2176]{1,0:T(8,128)(2,1)S(1)} %get-tuple-element.32.coded_ref), channel_id=1, source_target_pairs={{1,4},{3,6},{0,2},{5,7},{4,1},{6,3},{2,0},{7,5},{9,12},{11,14},{8,... | collective-permute-start | bytes 835592 | tf_op jit(solution)/shard_map/ppermute | solution.py:33
  41.0 0.4 collective-permute-done.11.partner_ref
  41.4 0.4 shard_map.64
  41.8 0.2 collective-permute-start.12
  42.0 0.0 copy-start.2
  42.0 1.9 %collective-permute-start.13 = (s16[64,2176]{1,0:T(8,128)(2,1)S(1)}, s16[64,2176]{1,0:T(8,128)(2,1)S(1)}, u32[]{:S(2)}, u32[]{:S(2)}) collective-permute-start(s16[64,2176]{1,0:T(8,128)(2,1)S(1)} %get-tuple-element.34), channel_id=1, source_target_pairs={{0,2},{1,0},{2,4},{3,1},{4,6},{5,3},{6,7},{7,5},{8,10},{9,8},{10,1... | collective-permute-start | bytes 835592 | tf_op jit(solution)/shard_map/ppermute | solution.py:27
  43.9 6.2 %collective-permute-done.14.far_ref = s16[64,2176]{1,0:T(8,128)(2,1)S(1)} collective-permute-done((s16[64,2176]{1,0:T(8,128)(2,1)S(1)}, s16[64,2176]{1,0:T(8,128)(2,1)S(1)}, u32[]{:S(2)}, u32[]{:S(2)}) %collective-permute-start.14) | collective-permute-done | bytes 278560 | tf_op jit(solution)/shard_map/ppermute | solution.py:33
  50.0 5.4 %collective-permute-done.12.outer_ref = s16[64,2176]{1,0:T(8,128)(2,1)S(1)} collective-permute-done((s16[64,2176]{1,0:T(8,128)(2,1)S(1)}, s16[64,2176]{1,0:T(8,128)(2,1)S(1)}, u32[]{:S(2)}, u32[]{:S(2)}) %collective-permute-start.12) | collective-permute-done | bytes 278560 | tf_op jit(solution)/shard_map/ppermute | solution.py:27
  55.4 0.0 collective-permute-done.13.inner_ref
  55.5 0.9 %shard_map.65.z0 = s16[64,640]{1,0:T(8,128)(2,1)S(1)} custom-call(f32[64,2048]{1,0:T(8,128)S(1)} %get-tuple-element.31.own_ref, s16[64,2176]{1,0:T(8,128)(2,1)S(1)} %get-tuple-element.32.coded_ref, s16[64,2176]{1,0:T(8,128)(2,1)S(1)} %collective-permute-done.11.partner_ref, s16[64,2176]{1,0:T(8,128)(2,1)S(1)} %collective-permute-done.12.outer_ref, ...), custom_call_target="tpu_custom_call" | custom-call | tf_op jit(solution)/shard_map/pallas_call | solution.py:53
  56.4 1.6 %collective-permute-start.15 = (s16[64,640]{1,0:T(8,128)(2,1)S(1)}, s16[64,640]{1,0:T(8,128)(2,1)S(1)}, u32[]{:S(2)}, u32[]{:S(2)}) collective-permute-start(s16[64,640]{1,0:T(8,128)(2,1)S(1)} %shard_map.65.z0), channel_id=1, source_target_pairs={{0,8},{8,0},{16,24},{24,16},{1,9},{9,1},{17,25},{25,17},{2,10},{10... | collective-permute-start | bytes 245768 | tf_op jit(solution)/shard_map/ppermute | solution.py:18
  57.9 0.5 collective-permute-start.16
  58.4 1.5 %collective-permute-start.17 = (s16[64,640]{1,0:T(8,128)(2,1)S(1)}, s16[64,640]{1,0:T(8,128)(2,1)S(1)}, u32[]{:S(2)}, u32[]{:S(2)}) collective-permute-start(s16[64,640]{1,0:T(8,128)(2,1)S(1)} %shard_map.65.z0), channel_id=1, source_target_pairs={{0,24},{8,16},{16,8},{24,0},{1,25},{9,17},{17,9},{25,1},{2,26},{10... | collective-permute-start | bytes 245768 | tf_op jit(solution)/shard_map/ppermute | solution.py:18
  59.9 1.6 %collective-permute-done.15.z1 = s16[64,640]{1,0:T(8,128)(2,1)S(1)} collective-permute-done((s16[64,640]{1,0:T(8,128)(2,1)S(1)}, s16[64,640]{1,0:T(8,128)(2,1)S(1)}, u32[]{:S(2)}, u32[]{:S(2)}) %collective-permute-start.15) | collective-permute-done | bytes 81952 | tf_op jit(solution)/shard_map/ppermute | solution.py:18
  61.6 0.8 %collective-permute-done.16.z2 = s16[64,640]{1,0:T(8,128)(2,1)S(1)} collective-permute-done((s16[64,640]{1,0:T(8,128)(2,1)S(1)}, s16[64,640]{1,0:T(8,128)(2,1)S(1)}, u32[]{:S(2)}, u32[]{:S(2)}) %collective-permute-start.16) | collective-permute-done | bytes 81952 | tf_op jit(solution)/shard_map/ppermute | solution.py:18
  62.4 1.4 %collective-permute-done.17.z3 = s16[64,640]{1,0:T(8,128)(2,1)S(1)} collective-permute-done((s16[64,640]{1,0:T(8,128)(2,1)S(1)}, s16[64,640]{1,0:T(8,128)(2,1)S(1)}, u32[]{:S(2)}, u32[]{:S(2)}) %collective-permute-start.17) | collective-permute-done | bytes 81952 | tf_op jit(solution)/shard_map/ppermute | solution.py:18
  63.8 0.3 shard_map.66
  64.0 0.0 collective-permute-start.18
  64.0 1.2 %collective-permute-done.18 = f32[8,128]{1,0:T(8,128)S(1)} collective-permute-done((f32[8,128]{1,0:T(8,128)S(1)}, f32[8,128]{1,0:T(8,128)S(1)}, u32[]{:S(2)}, u32[]{:S(2)}) %collective-permute-start.18) | collective-permute-done | bytes 4128 | tf_op jit(solution)/shard_map/ppermute | solution.py:18
  65.2 1.5 %collective-permute-start.19 = (f32[8,128]{1,0:T(8,128)S(1)}, f32[8,128]{1,0:T(8,128)S(1)}, u32[]{:S(2)}, u32[]{:S(2)}) collective-permute-start(f32[8,128]{1,0:T(8,128)S(1)} %add.3.p0), channel_id=1, source_target_pairs={{0,2},{1,3},{2,0},{3,1},{4,6},{5,7},{6,4},{7,5},{8,10},{9,11},{10,... | collective-permute-start | bytes 12296 | tf_op jit(solution)/shard_map/ppermute | solution.py:18
  66.7 0.0 collective-permute-start.20
  66.7 2.9 %collective-permute-start.21 = (f32[8,128]{1,0:T(8,128)S(1)}, f32[8,128]{1,0:T(8,128)S(1)}, u32[]{:S(2)}, u32[]{:S(2)}) collective-permute-start(f32[8,128]{1,0:T(8,128)S(1)} %add.3.p0), channel_id=1, source_target_pairs={{0,6},{1,7},{2,4},{3,5},{4,2},{5,3},{6,0},{7,1},{8,14},{9,15},{10,... | collective-permute-start | bytes 12296 | tf_op jit(solution)/shard_map/ppermute | solution.py:18
  69.6 0.0 copy-done.2
  69.6 0.1 copy.6.shrink_ref
  69.7 0.0 collective-permute-done.19.p1
  69.7 1.5 %collective-permute-done.20.p2 = f32[8,128]{1,0:T(8,128)S(1)} collective-permute-done((f32[8,128]{1,0:T(8,128)S(1)}, f32[8,128]{1,0:T(8,128)S(1)}, u32[]{:S(2)}, u32[]{:S(2)}) %collective-permute-start.20) | collective-permute-done | bytes 4128 | tf_op jit(solution)/shard_map/ppermute | solution.py:18
  71.2 0.9 %collective-permute-done.21.p3 = f32[8,128]{1,0:T(8,128)S(1)} collective-permute-done((f32[8,128]{1,0:T(8,128)S(1)}, f32[8,128]{1,0:T(8,128)S(1)}, u32[]{:S(2)}, u32[]{:S(2)}) %collective-permute-start.21) | collective-permute-done | bytes 4128 | tf_op jit(solution)/shard_map/ppermute | solution.py:18
  72.1 1.2 %shard_map.67 = (f32[64,512]{1,0:T(8,128)}, f32[64,512]{1,0:T(8,128)}) custom-call(f32[64,1]{1,0:T(8,128)S(1)} %copy.6.shrink_ref, f32[8,128]{1,0:T(8,128)S(1)} %add.3.p0, f32[8,128]{1,0:T(8,128)S(1)} %collective-permute-done.19.p1, f32[8,128]{1,0:T(8,128)S(1)} %collective-permute-done.20.p2, f32[8,128]{1,0:T(8,128)S(1)} %collective-permute-done.21.p3, ...), custom_call_target="tpu_custom_call" | custom-call | tf_op jit(solution)/shard_map/pallas_call | solution.py:53
  (2 shorter events, 0.0 us)
Async XLA Ops:
  0.6 1.6 %copy-start = (bf16[2048,512]{1,0:T(8,128)(2,1)S(1)}, bf16[2048,512]{1,0:T(8,128)(2,1)}, u32[]{:S(2)}) copy-start(bf16[2048,512]{1,0:T(8,128)(2,1)} %dosage_ref.3) | copy-start | bytes 6291460
  2.2 11.3 %copy-start.1 = (f32[512,64]{0,1:T(8,128)S(1)}, f32[512,64]{0,1:T(8,128)}, u32[]{:S(2)}) copy-start(f32[512,64]{0,1:T(8,128)} %param.6) | copy-start | bytes 393220
  2.6 7.3 %collective-permute-start = (f32[8,512]{1,0:T(8,128)S(1)}, f32[8,512]{1,0:T(8,128)S(1)}, u32[]{:S(2)}, u32[]{:S(2)}) collective-permute-start(f32[8,512]{1,0:T(8,128)S(1)} %shard_map.59.s0), channel_id=1, source_target_pairs={{0,8},{8,0},{16,24},{24,16},{1,9},{9,1},{17,25},{25,17},{2,10},{10... | collective-permute-start | bytes 49160 | tf_op jit(solution)/shard_map/ppermute | solution.py:18
  5.6 7.9 %collective-permute-start.1 = (f32[8,512]{1,0:T(8,128)S(1)}, f32[8,512]{1,0:T(8,128)S(1)}, u32[]{:S(2)}, u32[]{:S(2)}) collective-permute-start(f32[8,512]{1,0:T(8,128)S(1)} %shard_map.59.s0), channel_id=1, source_target_pairs={{0,16},{8,24},{16,0},{24,8},{1,17},{9,25},{17,1},{25,9},{2,18},{10... | collective-permute-start | bytes 49160 | tf_op jit(solution)/shard_map/ppermute | solution.py:18
  7.1 6.4 %collective-permute-start.2 = (f32[8,512]{1,0:T(8,128)S(1)}, f32[8,512]{1,0:T(8,128)S(1)}, u32[]{:S(2)}, u32[]{:S(2)}) collective-permute-start(f32[8,512]{1,0:T(8,128)S(1)} %shard_map.59.s0), channel_id=1, source_target_pairs={{0,24},{8,16},{16,8},{24,0},{1,25},{9,17},{17,9},{25,1},{2,26},{10... | collective-permute-start | bytes 49160 | tf_op jit(solution)/shard_map/ppermute | solution.py:18
  7.8 5.7 %collective-permute-start.3 = (f32[8,128]{1,0:T(8,128)S(1)}, f32[8,128]{1,0:T(8,128)S(1)}, u32[]{:S(2)}, u32[]{:S(2)}) collective-permute-start(f32[8,128]{1,0:T(8,128)S(1)} %broadcast_in_dim.13.wide_ref), channel_id=1, source_target_pairs={{0,2},{1,3},{2,4},{3,5},{4,6},{5,7},{6,0},{7,1},{8,10},{9,11},{10,... | collective-permute-start | bytes 12296 | tf_op jit(solution)/shard_map/ppermute | solution.py:38
  14.5 1.6 %collective-permute-start.4 = (s16[64,2176]{1,0:T(8,128)(2,1)S(1)}, s16[64,2176]{1,0:T(8,128)(2,1)S(1)}, u32[]{:S(2)}, u32[]{:S(2)}) collective-permute-start(s16[64,2176]{1,0:T(8,128)(2,1)S(1)} %get-tuple-element.25.coded_ref), channel_id=1, source_target_pairs={{0,1},{1,0},{2,3},{3,2},{4,5},{5,4},{6,7},{7,6},{8,9},{9,8},{10,11... | collective-permute-start | bytes 835592 | tf_op jit(solution)/shard_map/ppermute | solution.py:18
  14.6 9.6 %collective-permute-start.7 = (s16[64,2176]{1,0:T(8,128)(2,1)S(1)}, s16[64,2176]{1,0:T(8,128)(2,1)S(1)}, u32[]{:S(2)}, u32[]{:S(2)}) collective-permute-start(s16[64,2176]{1,0:T(8,128)(2,1)S(1)} %get-tuple-element.25.coded_ref), channel_id=1, source_target_pairs={{1,4},{3,6},{0,2},{5,7},{4,1},{6,3},{2,0},{7,5},{9,12},{11,14},{8,... | collective-permute-start | bytes 835592 | tf_op jit(solution)/shard_map/ppermute | solution.py:33
  16.6 13.6 %collective-permute-start.5 = (s16[64,2176]{1,0:T(8,128)(2,1)S(1)}, s16[64,2176]{1,0:T(8,128)(2,1)S(1)}, u32[]{:S(2)}, u32[]{:S(2)}) collective-permute-start(s16[64,2176]{1,0:T(8,128)(2,1)S(1)} %get-tuple-element.27), channel_id=1, source_target_pairs={{0,1},{1,3},{2,0},{3,5},{4,2},{5,7},{6,4},{7,6},{8,9},{9,11},{10,8... | collective-permute-start | bytes 835592 | tf_op jit(solution)/shard_map/ppermute | solution.py:27
  16.7 13.5 %collective-permute-start.6 = (s16[64,2176]{1,0:T(8,128)(2,1)S(1)}, s16[64,2176]{1,0:T(8,128)(2,1)S(1)}, u32[]{:S(2)}, u32[]{:S(2)}) collective-permute-start(s16[64,2176]{1,0:T(8,128)(2,1)S(1)} %get-tuple-element.28), channel_id=1, source_target_pairs={{0,2},{1,0},{2,4},{3,1},{4,6},{5,3},{6,7},{7,5},{8,10},{9,8},{10,1... | collective-permute-start | bytes 835592 | tf_op jit(solution)/shard_map/ppermute | solution.py:27
  31.1 5.5 %collective-permute-start.10 = (s16[64,640]{1,0:T(8,128)(2,1)S(1)}, s16[64,640]{1,0:T(8,128)(2,1)S(1)}, u32[]{:S(2)}, u32[]{:S(2)}) collective-permute-start(s16[64,640]{1,0:T(8,128)(2,1)S(1)} %shard_map.62.z0), channel_id=1, source_target_pairs={{0,24},{8,16},{16,8},{24,0},{1,25},{9,17},{17,9},{25,1},{2,26},{10... | collective-permute-start | bytes 245768 | tf_op jit(solution)/shard_map/ppermute | solution.py:18
  33.9 4.4 %collective-permute-start.8 = (s16[64,640]{1,0:T(8,128)(2,1)S(1)}, s16[64,640]{1,0:T(8,128)(2,1)S(1)}, u32[]{:S(2)}, u32[]{:S(2)}) collective-permute-start(s16[64,640]{1,0:T(8,128)(2,1)S(1)} %shard_map.62.z0), channel_id=1, source_target_pairs={{0,8},{8,0},{16,24},{24,16},{1,9},{9,1},{17,25},{25,17},{2,10},{10... | collective-permute-start | bytes 245768 | tf_op jit(solution)/shard_map/ppermute | solution.py:18
  34.4 4.4 %collective-permute-start.9 = (s16[64,640]{1,0:T(8,128)(2,1)S(1)}, s16[64,640]{1,0:T(8,128)(2,1)S(1)}, u32[]{:S(2)}, u32[]{:S(2)}) collective-permute-start(s16[64,640]{1,0:T(8,128)(2,1)S(1)} %shard_map.62.z0), channel_id=1, source_target_pairs={{0,16},{8,24},{16,0},{24,8},{1,17},{9,25},{17,1},{25,9},{2,18},{10... | collective-permute-start | bytes 245768 | tf_op jit(solution)/shard_map/ppermute | solution.py:18
  39.8 1.6 %collective-permute-start.11 = (s16[64,2176]{1,0:T(8,128)(2,1)S(1)}, s16[64,2176]{1,0:T(8,128)(2,1)S(1)}, u32[]{:S(2)}, u32[]{:S(2)}) collective-permute-start(s16[64,2176]{1,0:T(8,128)(2,1)S(1)} %get-tuple-element.32.coded_ref), channel_id=1, source_target_pairs={{0,1},{1,0},{2,3},{3,2},{4,5},{5,4},{6,7},{7,6},{8,9},{9,8},{10,11... | collective-permute-start | bytes 835592 | tf_op jit(solution)/shard_map/ppermute | solution.py:18
  39.9 10.2 %collective-permute-start.14 = (s16[64,2176]{1,0:T(8,128)(2,1)S(1)}, s16[64,2176]{1,0:T(8,128)(2,1)S(1)}, u32[]{:S(2)}, u32[]{:S(2)}) collective-permute-start(s16[64,2176]{1,0:T(8,128)(2,1)S(1)} %get-tuple-element.32.coded_ref), channel_id=1, source_target_pairs={{1,4},{3,6},{0,2},{5,7},{4,1},{6,3},{2,0},{7,5},{9,12},{11,14},{8,... | collective-permute-start | bytes 835592 | tf_op jit(solution)/shard_map/ppermute | solution.py:33
  41.8 13.6 %collective-permute-start.12 = (s16[64,2176]{1,0:T(8,128)(2,1)S(1)}, s16[64,2176]{1,0:T(8,128)(2,1)S(1)}, u32[]{:S(2)}, u32[]{:S(2)}) collective-permute-start(s16[64,2176]{1,0:T(8,128)(2,1)S(1)} %get-tuple-element.33), channel_id=1, source_target_pairs={{0,1},{1,3},{2,0},{3,5},{4,2},{5,7},{6,4},{7,6},{8,9},{9,11},{10,8... | collective-permute-start | bytes 835592 | tf_op jit(solution)/shard_map/ppermute | solution.py:27
  42.0 27.6 %copy-start.2 = (f32[64]{0:T(128)S(1)}, f32[64]{0:T(128)}, u32[]{:S(2)}) copy-start(f32[64]{0:T(128)} %param.7) | copy-start | bytes 772
  42.0 13.5 %collective-permute-start.13 = (s16[64,2176]{1,0:T(8,128)(2,1)S(1)}, s16[64,2176]{1,0:T(8,128)(2,1)S(1)}, u32[]{:S(2)}, u32[]{:S(2)}) collective-permute-start(s16[64,2176]{1,0:T(8,128)(2,1)S(1)} %get-tuple-element.34), channel_id=1, source_target_pairs={{0,2},{1,0},{2,4},{3,1},{4,6},{5,3},{6,7},{7,5},{8,10},{9,8},{10,1... | collective-permute-start | bytes 835592 | tf_op jit(solution)/shard_map/ppermute | solution.py:27
  56.4 5.2 %collective-permute-start.15 = (s16[64,640]{1,0:T(8,128)(2,1)S(1)}, s16[64,640]{1,0:T(8,128)(2,1)S(1)}, u32[]{:S(2)}, u32[]{:S(2)}) collective-permute-start(s16[64,640]{1,0:T(8,128)(2,1)S(1)} %shard_map.65.z0), channel_id=1, source_target_pairs={{0,8},{8,0},{16,24},{24,16},{1,9},{9,1},{17,25},{25,17},{2,10},{10... | collective-permute-start | bytes 245768 | tf_op jit(solution)/shard_map/ppermute | solution.py:18
  57.9 4.4 %collective-permute-start.16 = (s16[64,640]{1,0:T(8,128)(2,1)S(1)}, s16[64,640]{1,0:T(8,128)(2,1)S(1)}, u32[]{:S(2)}, u32[]{:S(2)}) collective-permute-start(s16[64,640]{1,0:T(8,128)(2,1)S(1)} %shard_map.65.z0), channel_id=1, source_target_pairs={{0,16},{8,24},{16,0},{24,8},{1,17},{9,25},{17,1},{25,9},{2,18},{10... | collective-permute-start | bytes 245768 | tf_op jit(solution)/shard_map/ppermute | solution.py:18
  58.4 5.3 %collective-permute-start.17 = (s16[64,640]{1,0:T(8,128)(2,1)S(1)}, s16[64,640]{1,0:T(8,128)(2,1)S(1)}, u32[]{:S(2)}, u32[]{:S(2)}) collective-permute-start(s16[64,640]{1,0:T(8,128)(2,1)S(1)} %shard_map.65.z0), channel_id=1, source_target_pairs={{0,24},{8,16},{16,8},{24,0},{1,25},{9,17},{17,9},{25,1},{2,26},{10... | collective-permute-start | bytes 245768 | tf_op jit(solution)/shard_map/ppermute | solution.py:18
  64.0 1.2 %collective-permute-start.18 = (f32[8,128]{1,0:T(8,128)S(1)}, f32[8,128]{1,0:T(8,128)S(1)}, u32[]{:S(2)}, u32[]{:S(2)}) collective-permute-start(f32[8,128]{1,0:T(8,128)S(1)} %shard_map.66), channel_id=1, source_target_pairs={{0,1},{1,0},{2,3},{3,2},{4,5},{5,4},{6,7},{7,6},{8,9},{9,8},{10,11... | collective-permute-start | bytes 12296 | tf_op jit(solution)/shard_map/ppermute | solution.py:18
  65.2 4.5 %collective-permute-start.19 = (f32[8,128]{1,0:T(8,128)S(1)}, f32[8,128]{1,0:T(8,128)S(1)}, u32[]{:S(2)}, u32[]{:S(2)}) collective-permute-start(f32[8,128]{1,0:T(8,128)S(1)} %add.3.p0), channel_id=1, source_target_pairs={{0,2},{1,3},{2,0},{3,1},{4,6},{5,7},{6,4},{7,5},{8,10},{9,11},{10,... | collective-permute-start | bytes 12296 | tf_op jit(solution)/shard_map/ppermute | solution.py:18
  66.7 4.5 %collective-permute-start.20 = (f32[8,128]{1,0:T(8,128)S(1)}, f32[8,128]{1,0:T(8,128)S(1)}, u32[]{:S(2)}, u32[]{:S(2)}) collective-permute-start(f32[8,128]{1,0:T(8,128)S(1)} %add.3.p0), channel_id=1, source_target_pairs={{0,4},{1,5},{2,6},{3,7},{4,0},{5,1},{6,2},{7,3},{8,12},{9,13},{10,... | collective-permute-start | bytes 12296 | tf_op jit(solution)/shard_map/ppermute | solution.py:18
  66.7 5.4 %collective-permute-start.21 = (f32[8,128]{1,0:T(8,128)S(1)}, f32[8,128]{1,0:T(8,128)S(1)}, u32[]{:S(2)}, u32[]{:S(2)}) collective-permute-start(f32[8,128]{1,0:T(8,128)S(1)} %add.3.p0), channel_id=1, source_target_pairs={{0,6},{1,7},{2,4},{3,5},{4,2},{5,3},{6,0},{7,1},{8,14},{9,15},{10,... | collective-permute-start | bytes 12296 | tf_op jit(solution)/shard_map/ppermute | solution.py:18

commit v7 on v6

--- a/solution.py
+++ b/solution.py
@@ -18,19 +18,24 @@
     return lax.ppermute(value, axis, [(i, i ^ bits) for i in range(lax.axis_size(axis))])
 
 
-def crossing(value, rising):
+def between(value, offset):
     count = lax.axis_size("snp")
     pairs = []
     for i in range(count):
-        target = i + 2 if i % 2 == rising else i - 2
+        target = ((i // 2 + offset ^ 1) - offset) * 2 + i % 2
         pairs.append((i, target if 0 <= target < count else i ^ 1))
     return lax.ppermute(value, "snp", pairs)
 
 
 def distant(value):
-    count = lax.axis_size("snp")
-    both = [(i, i + 3) for i in range(1, count - 3, 2)] + [(0, 2), (count - 3, count - 1)]
-    return lax.ppermute(value, "snp", both + [(j, i) for i, j in both])
+    rows, count = lax.axis_size("samp"), lax.axis_size("snp")
+    pairs = []
+    for row in range(rows):
+        for i in range(count):
+            target = i + 3 if i % 2 else i - 3
+            inside = 0 <= target < count
+            pairs.append((row * count + i, row * count + target if inside else (row ^ 1) * count + i))
+    return lax.ppermute(value, ("samp", "snp"), pairs)
 
 
 def shifted(value):
@@ -167,16 +172,17 @@
 
 def place(count):
     index = lax.axis_index("snp")
-    odd = (index & 1) == 1
-    below, above = (index >= 2).astype(jnp.int32), (index < count - 2).astype(jnp.int32)
-    outer = jnp.where(odd, below, above) == 1
-    inner = jnp.where(odd, above, below) == 1
+    odd, pair = (index & 1) == 1, index >> 1
+    rises = (pair & 1) == 0
+    above, below = (pair < count // 2 - 1).astype(jnp.int32), (pair > 0).astype(jnp.int32)
+    first = jnp.where(rises, above, below) == 1
+    second = jnp.where(rises, below, above) == 1
     far = jnp.where(odd, (index < count - 3).astype(jnp.int32), (index >= 3).astype(jnp.int32)) == 1
-    return odd, outer, inner, far
-
-
-def give_kernel(count, near_ref, own_ref, coded_ref, partner_ref, outer_ref, inner_ref):
-    odd = place(count)[0]
+    return odd, rises, first, second, far
+
+
+def give_kernel(count, near_ref, own_ref, coded_ref, partner_ref, first_ref, second_ref):
+    odd, rises = place(count)[:2]
     exponent, width = aux(coded_ref)[:2]
     partner_exponent, partner_width = aux(partner_ref)[:2]
     near = near_ref[0:1, 0:1]
@@ -188,25 +194,25 @@
     up_partner = flag(partner_width, jnp.where(odd, 3.0, 1.0)) * partner_scale
     down_own = flag(near, 2.0) * scale
     down_partner = flag(near, jnp.where(odd, 1.0, 3.0)) * partner_scale
-    choose = lambda even_case, odd_case: jnp.where(odd, odd_case, even_case)
-    outer_own, outer_partner = choose(down_own, up_own), choose(down_partner, up_partner)
-    inner_own, inner_partner = choose(up_own, down_own), choose(up_partner, down_partner)
+    choose = lambda one, two: jnp.where(rises, one, two)
+    first_own, first_partner = choose(up_own, down_own), choose(up_partner, down_partner)
+    second_own, second_partner = choose(down_own, up_own), choose(down_partner, up_partner)
     for k in range(0, own_ref.shape[1], CHUNK):
         own, partner = own_ref[:, pl.ds(k, CHUNK)], values(partner_ref, k)
-        outer_ref[:, pl.ds(k, CHUNK)] = fixed(own * outer_own + partner * outer_partner)
-        inner_ref[:, pl.ds(k, CHUNK)] = fixed(own * inner_own + partner * inner_partner)
-    finish(outer_ref, sent, width)
-    finish(inner_ref, sent, width)
-
-
-def window_kernel(samples, count, own_ref, coded_ref, partner_ref, outer_ref, inner_ref, far_ref, scaled_ref, sent_ref):
-    odd, use_outer, use_inner, use_far = place(count)
+        first_ref[:, pl.ds(k, CHUNK)] = fixed(own * first_own + partner * first_partner)
+        second_ref[:, pl.ds(k, CHUNK)] = fixed(own * second_own + partner * second_partner)
+    finish(first_ref, sent, width)
+    finish(second_ref, sent, width)
+
+
+def window_kernel(samples, count, own_ref, coded_ref, partner_ref, first_ref, second_ref, far_ref, scaled_ref, sent_ref):
+    odd, _, use_first, use_second, use_far = place(count)
     width = aux(coded_ref)[1]
     partner_exponent, partner_width = aux(partner_ref)[:2]
     far_exponent, far_width = aux(far_ref)[:2]
     partner_scale = unit(partner_exponent, jnp.where(odd, partner_width, width) >= 1)
-    outer_scale = unit(aux(outer_ref)[0], use_outer)
-    inner_scale = unit(aux(inner_ref)[0], use_inner)
+    first_scale = unit(aux(first_ref)[0], use_first)
+    second_scale = unit(aux(second_ref)[0], use_second)
     far_scale = jnp.where(jnp.where(odd, width, far_width) >= 3, unit(far_exponent, use_far), 0.0)
     rows = own_ref.shape[0]
     acc = jnp.zeros((2 * rows, scaled_ref.shape[1]), jnp.float32)
@@ -216,8 +222,8 @@
         mixed = (
             own
             + values(partner_ref, k) * partner_scale
-            + values(outer_ref, k) * outer_scale
-            + values(inner_ref, k) * inner_scale
+            + values(first_ref, k) * first_scale
+            + values(second_ref, k) * second_scale
             + values(far_ref, k) * far_scale
         )
         acc = acc + jnp.dot(
@@ -300,12 +306,14 @@
     def window(own, coded):
         far = distant(coded)
         partner = swap(coded, "snp", 1)
-        outer, inner = call(
+        one, two = call(
             functools.partial(give_kernel, count), [coded_out, coded_out], near, own, coded, partner
         )
+        two = between(two, 1)
+        one = between(one, 0)
         (z,) = call(
             functools.partial(window_kernel, samples, count), [sent_out],
-            own, coded, partner, crossing(outer, 1), crossing(inner, 0), far, scaled,
+            own, coded, partner, one, two, far, scaled,
         )
         return [z, *partners(z, "samp", 1, 2)]
 

time: 73.5 us -> 71.8 us (0.977)
  waiting for transfers between devices: 40.2 us -> 35.7 us
  starting transfers between devices: 23.6 us -> 26.4 us
    ppermute x6, waiting for transfers between devices: 23.1 us -> 19.6 us  [the longest x4 14 us: between(): return lax.ppermute(value, 'snp', pairs)]
    ppermute x6, starting transfers between devices: 5.28 us -> 6.74 us  [the longest x4 3.43 us: between(): return lax.ppermute(value, 'snp', pairs)]
    ppermute x15, starting transfers between devices: 16.2 us -> 17.6 us  [swap(): lax.ppermute(value, axis, [(i, i ^ bits) for i in range(lax.axis_size(axi...]
    ppermute x15, waiting for transfers between devices: 13.5 us -> 12.5 us  [swap(): lax.ppermute(value, axis, [(i, i ^ bits) for i in range(lax.axis_size(axi...]
  transfers between devices with their start and end apart: 22 -> 22, of which waited for: 16 -> 13; matrix products, arithmetic and copies ran while one was open for 0% -> 0% of each run, Pallas kernels for 1% -> 1%
where the time goes in v7:
time: 71.8 us; the launch traced here: 71.6 us
  waiting for transfers between devices  35.7 us (50%)
  starting transfers between devices  26.4 us (37%)
  Pallas kernels  6.45 us (9%)
  local copies, waits for them, and re-layouts  1.69 us (2%)
  between operations  1.4 us (2%)
    ppermute x15, starting transfers between devices, swap(): lax.ppermute(value, axis, [(i, i ^ bits) for i in range(lax.axis_size(axi...  17.6 us
    ppermute x4, waiting for transfers between devices, between(): return lax.ppermute(value, 'snp', pairs)  14 us
    ppermute x15, waiting for transfers between devices, swap(): lax.ppermute(value, axis, [(i, i ^ bits) for i in range(lax.axis_size(axi...  12.5 us
    pallas_call x9, Pallas kernels, call(): pl.pallas_call(body, out_shape=outs, in_specs=specs, out_specs=[pl.BlockS...  6.45 us
    ppermute x2, waiting for transfers between devices, distant(): return lax.ppermute(value, ('samp', 'snp'), pairs)  5.65 us
    ppermute x1, waiting for transfers between devices, shifted(): lax.ppermute(value, 'snp', [(i, (i + 2) % count) for i in range(count)])  3.61 us
    ppermute x4, starting transfers between devices, between(): return lax.ppermute(value, 'snp', pairs)  3.43 us
    ppermute x2, starting transfers between devices, distant(): return lax.ppermute(value, ('samp', 'snp'), pairs)  3.31 us
  transfers between devices with their start and end apart: 22, of which 13 were waited for; matrix products, arithmetic and copies ran while one was open for 0% of the time, Pallas kernels for 1%

profile of v7, /device:TPU:0, one launch (start us, length us, event | category | flops | bytes accessed | tf_op | source)
XLA Modules:
  0.0 71.6 jit_solution(11380568697417750032)
XLA Ops:
  0.6 0.0 copy-start
  0.6 1.6 %copy-done = bf16[2048,512]{1,0:T(8,128)(2,1)S(1)} copy-done((bf16[2048,512]{1,0:T(8,128)(2,1)S(1)}, bf16[2048,512]{1,0:T(8,128)(2,1)}, u32[]{:S(2)}) %copy-start) | copy-done | bytes 2097176
  2.2 0.0 copy-start.1
  2.2 0.4 shard_map.59.s0
  2.6 3.0 %collective-permute-start = (f32[8,512]{1,0:T(8,128)S(1)}, f32[8,512]{1,0:T(8,128)S(1)}, u32[]{:S(2)}, u32[]{:S(2)}) collective-permute-start(f32[8,512]{1,0:T(8,128)S(1)} %shard_map.59.s0), channel_id=1, source_target_pairs={{0,8},{8,0},{16,24},{24,16},{1,9},{9,1},{17,25},{25,17},{2,10},{10... | collective-permute-start | bytes 49160 | tf_op jit(solution)/shard_map/ppermute | solution.py:18
  5.6 1.5 %collective-permute-start.1 = (f32[8,512]{1,0:T(8,128)S(1)}, f32[8,512]{1,0:T(8,128)S(1)}, u32[]{:S(2)}, u32[]{:S(2)}) collective-permute-start(f32[8,512]{1,0:T(8,128)S(1)} %shard_map.59.s0), channel_id=1, source_target_pairs={{0,16},{8,24},{16,0},{24,8},{1,17},{9,25},{17,1},{25,9},{2,18},{10... | collective-permute-start | bytes 49160 | tf_op jit(solution)/shard_map/ppermute | solution.py:18
  7.1 0.0 collective-permute-start.2
  7.8 2.1 %collective-permute-start.3 = (f32[8,128]{1,0:T(8,128)S(1)}, f32[8,128]{1,0:T(8,128)S(1)}, u32[]{:S(2)}, u32[]{:S(2)}) collective-permute-start(f32[8,128]{1,0:T(8,128)S(1)} %broadcast_in_dim.13.wide_ref), channel_id=1, source_target_pairs={{0,2},{1,3},{2,4},{3,5},{4,6},{5,7},{6,0},{7,1},{8,10},{9,11},{10,... | collective-permute-start | bytes 12296 | tf_op jit(solution)/shard_map/ppermute | solution.py:43
  9.9 0.0 collective-permute-done.s1
  9.9 3.6 %collective-permute-done.3.near_ref = f32[8,128]{1,0:T(8,128)S(1)} collective-permute-done((f32[8,128]{1,0:T(8,128)S(1)}, f32[8,128]{1,0:T(8,128)S(1)}, u32[]{:S(2)}, u32[]{:S(2)}) %collective-permute-start.3) | collective-permute-done | bytes 4128 | tf_op jit(solution)/shard_map/ppermute | solution.py:43
  13.5 0.0 collective-permute-done.1.s2
  13.5 0.0 collective-permute-done.2.s3
  13.5 0.0 copy-done.1
  13.5 1.0 %shard_map.60 = (bf16[2048,512]{1,0:T(8,128)(2,1)S(1)}, f32[64,2048]{1,0:T(8,128)S(1)}, s16[64,2176]{1,0:T(8,128)(2,1)S(1)}) custom-call(f32[8,128]{1,0:T(8,128)S(1)} %broadcast_in_dim.13.wide_ref, f32[8,512]{1,0:T(8,128)S(1)} %shard_map.59.s0, f32[8,512]{1,0:T(8,128)S(1)} %collective-permute-done.s1, f32[8,512]{1,0:T(8,128)S(1)} %collective-permute-done.1.s2, ...), custom_call_target="tpu_custom_call" | custom-call | tf_op jit(solution)/shard_map/pallas_call | solution.py:58
  14.5 0.1 collective-permute-start.4
  14.6 1.8 %collective-permute-start.7 = (s16[64,2176]{1,0:T(8,128)(2,1)S(1)}, s16[64,2176]{1,0:T(8,128)(2,1)S(1)}, u32[]{:S(2)}, u32[]{:S(2)}) collective-permute-start(s16[64,2176]{1,0:T(8,128)(2,1)S(1)} %get-tuple-element.25.coded_ref), channel_id=1, source_target_pairs={{0,8},{1,4},{2,10},{3,6},{4,1},{5,13},{6,3},{7,15},{8,0},{9,12},{1... | collective-permute-start | bytes 835592 | tf_op jit(solution)/shard_map/ppermute | solution.py:38
  16.4 0.0 collective-permute-done.4.partner_ref
  16.4 0.4 shard_map.61
  16.8 0.1 collective-permute-start.5
  16.9 0.7 collective-permute-start.6
  17.6 3.7 %collective-permute-done.7.far_ref = s16[64,2176]{1,0:T(8,128)(2,1)S(1)} collective-permute-done((s16[64,2176]{1,0:T(8,128)(2,1)S(1)}, s16[64,2176]{1,0:T(8,128)(2,1)S(1)}, u32[]{:S(2)}, u32[]{:S(2)}) %collective-permute-start.7) | collective-permute-done | bytes 278560 | tf_op jit(solution)/shard_map/ppermute | solution.py:38
  21.2 7.1 %collective-permute-done.5.first_ref = s16[64,2176]{1,0:T(8,128)(2,1)S(1)} collective-permute-done((s16[64,2176]{1,0:T(8,128)(2,1)S(1)}, s16[64,2176]{1,0:T(8,128)(2,1)S(1)}, u32[]{:S(2)}, u32[]{:S(2)}) %collective-permute-start.5) | collective-permute-done | bytes 278560 | tf_op jit(solution)/shard_map/ppermute | solution.py:27
  28.3 0.0 collective-permute-done.6.second_ref
  28.3 0.9 %shard_map.62.z0 = s16[64,640]{1,0:T(8,128)(2,1)S(1)} custom-call(f32[64,2048]{1,0:T(8,128)S(1)} %get-tuple-element.24.own_ref, s16[64,2176]{1,0:T(8,128)(2,1)S(1)} %get-tuple-element.25.coded_ref, s16[64,2176]{1,0:T(8,128)(2,1)S(1)} %collective-permute-done.4.partner_ref, s16[64,2176]{1,0:T(8,128)(2,1)S(1)} %collective-permute-done.5.first_ref, ...), custom_call_target="tpu_custom_call" | custom-call | tf_op jit(solution)/shard_map/pallas_call | solution.py:58
  29.2 2.7 %collective-permute-start.10 = (s16[64,640]{1,0:T(8,128)(2,1)S(1)}, s16[64,640]{1,0:T(8,128)(2,1)S(1)}, u32[]{:S(2)}, u32[]{:S(2)}) collective-permute-start(s16[64,640]{1,0:T(8,128)(2,1)S(1)} %shard_map.62.z0), channel_id=1, source_target_pairs={{0,24},{8,16},{16,8},{24,0},{1,25},{9,17},{17,9},{25,1},{2,26},{10... | collective-permute-start | bytes 245768 | tf_op jit(solution)/shard_map/ppermute | solution.py:18
  32.0 0.6 collective-permute-start.8
  32.5 0.3 collective-permute-start.9
  32.8 2.7 %collective-permute-done.10.z3 = s16[64,640]{1,0:T(8,128)(2,1)S(1)} collective-permute-done((s16[64,640]{1,0:T(8,128)(2,1)S(1)}, s16[64,640]{1,0:T(8,128)(2,1)S(1)}, u32[]{:S(2)}, u32[]{:S(2)}) %collective-permute-start.10) | collective-permute-done | bytes 81952 | tf_op jit(solution)/shard_map/ppermute | solution.py:18
  35.5 1.0 %collective-permute-done.8.z1 = s16[64,640]{1,0:T(8,128)(2,1)S(1)} collective-permute-done((s16[64,640]{1,0:T(8,128)(2,1)S(1)}, s16[64,640]{1,0:T(8,128)(2,1)S(1)}, u32[]{:S(2)}, u32[]{:S(2)}) %collective-permute-start.8) | collective-permute-done | bytes 81952 | tf_op jit(solution)/shard_map/ppermute | solution.py:18
  36.5 0.5 collective-permute-done.9.z2
  36.9 1.0 %shard_map.63 = (f32[64,512]{1,0:T(8,128)S(1)}, f32[64,128]{1,0:T(8,128)S(1)}, f32[64,2048]{1,0:T(8,128)S(1)}, s16[64,2176]{1,0:T(8,128)(2,1)S(1)}) custom-call(f32[8,128]{1,0:T(8,128)S(1)} %broadcast_in_dim.13.wide_ref, s16[64,640]{1,0:T(8,128)(2,1)S(1)} %shard_map.62.z0, s16[64,640]{1,0:T(8,128)(2,1)S(1)} %collective-permute-done.8.z1, ...), custom_call_target="tpu_custom_call" | custom-call | tf_op jit(solution)/shard_map/pallas_call | solution.py:58
  37.9 0.1 collective-permute-start.11
  38.0 1.5 %collective-permute-start.14 = (s16[64,2176]{1,0:T(8,128)(2,1)S(1)}, s16[64,2176]{1,0:T(8,128)(2,1)S(1)}, u32[]{:S(2)}, u32[]{:S(2)}) collective-permute-start(s16[64,2176]{1,0:T(8,128)(2,1)S(1)} %get-tuple-element.32.coded_ref), channel_id=1, source_target_pairs={{0,8},{1,4},{2,10},{3,6},{4,1},{5,13},{6,3},{7,15},{8,0},{9,12},{1... | collective-permute-start | bytes 835592 | tf_op jit(solution)/shard_map/ppermute | solution.py:38
  39.5 0.0 collective-permute-done.11.partner_ref
  39.5 0.4 shard_map.64
  40.0 2.7 %collective-permute-start.12 = (s16[64,2176]{1,0:T(8,128)(2,1)S(1)}, s16[64,2176]{1,0:T(8,128)(2,1)S(1)}, u32[]{:S(2)}, u32[]{:S(2)}) collective-permute-start(s16[64,2176]{1,0:T(8,128)(2,1)S(1)} %get-tuple-element.33), channel_id=1, source_target_pairs={{0,2},{1,3},{2,0},{3,1},{4,6},{5,7},{6,4},{7,5},{8,10},{9,11},{10,... | collective-permute-start | bytes 835592 | tf_op jit(solution)/shard_map/ppermute | solution.py:27
  42.6 0.0 copy-start.2
  42.6 0.0 collective-permute-start.13
  42.6 2.0 %collective-permute-done.14.far_ref = s16[64,2176]{1,0:T(8,128)(2,1)S(1)} collective-permute-done((s16[64,2176]{1,0:T(8,128)(2,1)S(1)}, s16[64,2176]{1,0:T(8,128)(2,1)S(1)}, u32[]{:S(2)}, u32[]{:S(2)}) %collective-permute-start.14) | collective-permute-done | bytes 278560 | tf_op jit(solution)/shard_map/ppermute | solution.py:38
  44.6 6.9 %collective-permute-done.12.first_ref = s16[64,2176]{1,0:T(8,128)(2,1)S(1)} collective-permute-done((s16[64,2176]{1,0:T(8,128)(2,1)S(1)}, s16[64,2176]{1,0:T(8,128)(2,1)S(1)}, u32[]{:S(2)}, u32[]{:S(2)}) %collective-permute-start.12) | collective-permute-done | bytes 278560 | tf_op jit(solution)/shard_map/ppermute | solution.py:27
  51.5 0.0 collective-permute-done.13.second_ref
  51.5 0.9 %shard_map.65.z0 = s16[64,640]{1,0:T(8,128)(2,1)S(1)} custom-call(f32[64,2048]{1,0:T(8,128)S(1)} %get-tuple-element.31.own_ref, s16[64,2176]{1,0:T(8,128)(2,1)S(1)} %get-tuple-element.32.coded_ref, s16[64,2176]{1,0:T(8,128)(2,1)S(1)} %collective-permute-done.11.partner_ref, s16[64,2176]{1,0:T(8,128)(2,1)S(1)} %collective-permute-done.12.first_ref, ...), custom_call_target="tpu_custom_call" | custom-call | tf_op jit(solution)/shard_map/pallas_call | solution.py:58
  52.4 1.5 %collective-permute-start.15 = (s16[64,640]{1,0:T(8,128)(2,1)S(1)}, s16[64,640]{1,0:T(8,128)(2,1)S(1)}, u32[]{:S(2)}, u32[]{:S(2)}) collective-permute-start(s16[64,640]{1,0:T(8,128)(2,1)S(1)} %shard_map.65.z0), channel_id=1, source_target_pairs={{0,8},{8,0},{16,24},{24,16},{1,9},{9,1},{17,25},{25,17},{2,10},{10... | collective-permute-start | bytes 245768 | tf_op jit(solution)/shard_map/ppermute | solution.py:18
  54.0 0.7 collective-permute-start.16
  54.7 1.3 %collective-permute-start.17 = (s16[64,640]{1,0:T(8,128)(2,1)S(1)}, s16[64,640]{1,0:T(8,128)(2,1)S(1)}, u32[]{:S(2)}, u32[]{:S(2)}) collective-permute-start(s16[64,640]{1,0:T(8,128)(2,1)S(1)} %shard_map.65.z0), channel_id=1, source_target_pairs={{0,24},{8,16},{16,8},{24,0},{1,25},{9,17},{17,9},{25,1},{2,26},{10... | collective-permute-start | bytes 245768 | tf_op jit(solution)/shard_map/ppermute | solution.py:18
  56.0 1.0 %collective-permute-done.15.z1 = s16[64,640]{1,0:T(8,128)(2,1)S(1)} collective-permute-done((s16[64,640]{1,0:T(8,128)(2,1)S(1)}, s16[64,640]{1,0:T(8,128)(2,1)S(1)}, u32[]{:S(2)}, u32[]{:S(2)}) %collective-permute-start.15) | collective-permute-done | bytes 81952 | tf_op jit(solution)/shard_map/ppermute | solution.py:18
  56.9 3.2 %collective-permute-done.16.z2 = s16[64,640]{1,0:T(8,128)(2,1)S(1)} collective-permute-done((s16[64,640]{1,0:T(8,128)(2,1)S(1)}, s16[64,640]{1,0:T(8,128)(2,1)S(1)}, u32[]{:S(2)}, u32[]{:S(2)}) %collective-permute-start.16) | collective-permute-done | bytes 81952 | tf_op jit(solution)/shard_map/ppermute | solution.py:18
  60.2 0.0 collective-permute-done.17.z3
  60.2 0.3 shard_map.66
  60.4 0.0 collective-permute-start.18
  60.4 1.2 %collective-permute-done.18 = f32[8,128]{1,0:T(8,128)S(1)} collective-permute-done((f32[8,128]{1,0:T(8,128)S(1)}, f32[8,128]{1,0:T(8,128)S(1)}, u32[]{:S(2)}, u32[]{:S(2)}) %collective-permute-start.18) | collective-permute-done | bytes 4128 | tf_op jit(solution)/shard_map/ppermute | solution.py:18
  61.6 3.4 %collective-permute-start.19 = (f32[8,128]{1,0:T(8,128)S(1)}, f32[8,128]{1,0:T(8,128)S(1)}, u32[]{:S(2)}, u32[]{:S(2)}) collective-permute-start(f32[8,128]{1,0:T(8,128)S(1)} %add.3.p0), channel_id=1, source_target_pairs={{0,2},{1,3},{2,0},{3,1},{4,6},{5,7},{6,4},{7,5},{8,10},{9,11},{10,... | collective-permute-start | bytes 12296 | tf_op jit(solution)/shard_map/ppermute | solution.py:18
  65.0 0.0 collective-permute-start.20
  65.0 2.4 %collective-permute-start.21 = (f32[8,128]{1,0:T(8,128)S(1)}, f32[8,128]{1,0:T(8,128)S(1)}, u32[]{:S(2)}, u32[]{:S(2)}) collective-permute-start(f32[8,128]{1,0:T(8,128)S(1)} %add.3.p0), channel_id=1, source_target_pairs={{0,6},{1,7},{2,4},{3,5},{4,2},{5,3},{6,0},{7,1},{8,14},{9,15},{10,... | collective-permute-start | bytes 12296 | tf_op jit(solution)/shard_map/ppermute | solution.py:18
  67.4 0.0 copy-done.2
  67.4 0.1 copy.6.shrink_ref
  67.5 0.0 collective-permute-done.19.p1
  67.5 2.0 %collective-permute-done.20.p2 = f32[8,128]{1,0:T(8,128)S(1)} collective-permute-done((f32[8,128]{1,0:T(8,128)S(1)}, f32[8,128]{1,0:T(8,128)S(1)}, u32[]{:S(2)}, u32[]{:S(2)}) %collective-permute-start.20) | collective-permute-done | bytes 4128 | tf_op jit(solution)/shard_map/ppermute | solution.py:18
  69.5 0.9 %collective-permute-done.21.p3 = f32[8,128]{1,0:T(8,128)S(1)} collective-permute-done((f32[8,128]{1,0:T(8,128)S(1)}, f32[8,128]{1,0:T(8,128)S(1)}, u32[]{:S(2)}, u32[]{:S(2)}) %collective-permute-start.21) | collective-permute-done | bytes 4128 | tf_op jit(solution)/shard_map/ppermute | solution.py:18
  70.4 1.2 %shard_map.67 = (f32[64,512]{1,0:T(8,128)}, f32[64,512]{1,0:T(8,128)}) custom-call(f32[64,1]{1,0:T(8,128)S(1)} %copy.6.shrink_ref, f32[8,128]{1,0:T(8,128)S(1)} %add.3.p0, f32[8,128]{1,0:T(8,128)S(1)} %collective-permute-done.19.p1, f32[8,128]{1,0:T(8,128)S(1)} %collective-permute-done.20.p2, f32[8,128]{1,0:T(8,128)S(1)} %collective-permute-done.21.p3, ...), custom_call_target="tpu_custom_call" | custom-call | tf_op jit(solution)/shard_map/pallas_call | solution.py:58
  (2 shorter events, 0.0 us)
Async XLA Ops:
  0.6 1.6 %copy-start = (bf16[2048,512]{1,0:T(8,128)(2,1)S(1)}, bf16[2048,512]{1,0:T(8,128)(2,1)}, u32[]{:S(2)}) copy-start(bf16[2048,512]{1,0:T(8,128)(2,1)} %dosage_ref.3) | copy-start | bytes 6291460
  2.2 11.3 %copy-start.1 = (f32[512,64]{0,1:T(8,128)S(1)}, f32[512,64]{0,1:T(8,128)}, u32[]{:S(2)}) copy-start(f32[512,64]{0,1:T(8,128)} %param.6) | copy-start | bytes 393220
  2.6 7.3 %collective-permute-start = (f32[8,512]{1,0:T(8,128)S(1)}, f32[8,512]{1,0:T(8,128)S(1)}, u32[]{:S(2)}, u32[]{:S(2)}) collective-permute-start(f32[8,512]{1,0:T(8,128)S(1)} %shard_map.59.s0), channel_id=1, source_target_pairs={{0,8},{8,0},{16,24},{24,16},{1,9},{9,1},{17,25},{25,17},{2,10},{10... | collective-permute-start | bytes 49160 | tf_op jit(solution)/shard_map/ppermute | solution.py:18
  5.6 7.9 %collective-permute-start.1 = (f32[8,512]{1,0:T(8,128)S(1)}, f32[8,512]{1,0:T(8,128)S(1)}, u32[]{:S(2)}, u32[]{:S(2)}) collective-permute-start(f32[8,512]{1,0:T(8,128)S(1)} %shard_map.59.s0), channel_id=1, source_target_pairs={{0,16},{8,24},{16,0},{24,8},{1,17},{9,25},{17,1},{25,9},{2,18},{10... | collective-permute-start | bytes 49160 | tf_op jit(solution)/shard_map/ppermute | solution.py:18
  7.1 6.4 %collective-permute-start.2 = (f32[8,512]{1,0:T(8,128)S(1)}, f32[8,512]{1,0:T(8,128)S(1)}, u32[]{:S(2)}, u32[]{:S(2)}) collective-permute-start(f32[8,512]{1,0:T(8,128)S(1)} %shard_map.59.s0), channel_id=1, source_target_pairs={{0,24},{8,16},{16,8},{24,0},{1,25},{9,17},{17,9},{25,1},{2,26},{10... | collective-permute-start | bytes 49160 | tf_op jit(solution)/shard_map/ppermute | solution.py:18
  7.8 5.7 %collective-permute-start.3 = (f32[8,128]{1,0:T(8,128)S(1)}, f32[8,128]{1,0:T(8,128)S(1)}, u32[]{:S(2)}, u32[]{:S(2)}) collective-permute-start(f32[8,128]{1,0:T(8,128)S(1)} %broadcast_in_dim.13.wide_ref), channel_id=1, source_target_pairs={{0,2},{1,3},{2,4},{3,5},{4,6},{5,7},{6,0},{7,1},{8,10},{9,11},{10,... | collective-permute-start | bytes 12296 | tf_op jit(solution)/shard_map/ppermute | solution.py:43
  14.5 1.9 %collective-permute-start.4 = (s16[64,2176]{1,0:T(8,128)(2,1)S(1)}, s16[64,2176]{1,0:T(8,128)(2,1)S(1)}, u32[]{:S(2)}, u32[]{:S(2)}) collective-permute-start(s16[64,2176]{1,0:T(8,128)(2,1)S(1)} %get-tuple-element.25.coded_ref), channel_id=1, source_target_pairs={{0,1},{1,0},{2,3},{3,2},{4,5},{5,4},{6,7},{7,6},{8,9},{9,8},{10,11... | collective-permute-start | bytes 835592 | tf_op jit(solution)/shard_map/ppermute | solution.py:18
  14.6 6.6 %collective-permute-start.7 = (s16[64,2176]{1,0:T(8,128)(2,1)S(1)}, s16[64,2176]{1,0:T(8,128)(2,1)S(1)}, u32[]{:S(2)}, u32[]{:S(2)}) collective-permute-start(s16[64,2176]{1,0:T(8,128)(2,1)S(1)} %get-tuple-element.25.coded_ref), channel_id=1, source_target_pairs={{0,8},{1,4},{2,10},{3,6},{4,1},{5,13},{6,3},{7,15},{8,0},{9,12},{1... | collective-permute-start | bytes 835592 | tf_op jit(solution)/shard_map/ppermute | solution.py:38
  16.8 11.5 %collective-permute-start.5 = (s16[64,2176]{1,0:T(8,128)(2,1)S(1)}, s16[64,2176]{1,0:T(8,128)(2,1)S(1)}, u32[]{:S(2)}, u32[]{:S(2)}) collective-permute-start(s16[64,2176]{1,0:T(8,128)(2,1)S(1)} %get-tuple-element.27), channel_id=1, source_target_pairs={{0,2},{1,3},{2,0},{3,1},{4,6},{5,7},{6,4},{7,5},{8,10},{9,11},{10,... | collective-permute-start | bytes 835592 | tf_op jit(solution)/shard_map/ppermute | solution.py:27
  16.9 11.4 %collective-permute-start.6 = (s16[64,2176]{1,0:T(8,128)(2,1)S(1)}, s16[64,2176]{1,0:T(8,128)(2,1)S(1)}, u32[]{:S(2)}, u32[]{:S(2)}) collective-permute-start(s16[64,2176]{1,0:T(8,128)(2,1)S(1)} %get-tuple-element.28), channel_id=1, source_target_pairs={{0,1},{1,0},{2,4},{3,5},{4,2},{5,3},{6,7},{7,6},{8,9},{9,8},{10,12... | collective-permute-start | bytes 835592 | tf_op jit(solution)/shard_map/ppermute | solution.py:27
  29.2 6.2 %collective-permute-start.10 = (s16[64,640]{1,0:T(8,128)(2,1)S(1)}, s16[64,640]{1,0:T(8,128)(2,1)S(1)}, u32[]{:S(2)}, u32[]{:S(2)}) collective-permute-start(s16[64,640]{1,0:T(8,128)(2,1)S(1)} %shard_map.62.z0), channel_id=1, source_target_pairs={{0,24},{8,16},{16,8},{24,0},{1,25},{9,17},{17,9},{25,1},{2,26},{10... | collective-permute-start | bytes 245768 | tf_op jit(solution)/shard_map/ppermute | solution.py:18
  32.0 4.5 %collective-permute-start.8 = (s16[64,640]{1,0:T(8,128)(2,1)S(1)}, s16[64,640]{1,0:T(8,128)(2,1)S(1)}, u32[]{:S(2)}, u32[]{:S(2)}) collective-permute-start(s16[64,640]{1,0:T(8,128)(2,1)S(1)} %shard_map.62.z0), channel_id=1, source_target_pairs={{0,8},{8,0},{16,24},{24,16},{1,9},{9,1},{17,25},{25,17},{2,10},{10... | collective-permute-start | bytes 245768 | tf_op jit(solution)/shard_map/ppermute | solution.py:18
  32.5 4.4 %collective-permute-start.9 = (s16[64,640]{1,0:T(8,128)(2,1)S(1)}, s16[64,640]{1,0:T(8,128)(2,1)S(1)}, u32[]{:S(2)}, u32[]{:S(2)}) collective-permute-start(s16[64,640]{1,0:T(8,128)(2,1)S(1)} %shard_map.62.z0), channel_id=1, source_target_pairs={{0,16},{8,24},{16,0},{24,8},{1,17},{9,25},{17,1},{25,9},{2,18},{10... | collective-permute-start | bytes 245768 | tf_op jit(solution)/shard_map/ppermute | solution.py:18
  37.9 1.6 %collective-permute-start.11 = (s16[64,2176]{1,0:T(8,128)(2,1)S(1)}, s16[64,2176]{1,0:T(8,128)(2,1)S(1)}, u32[]{:S(2)}, u32[]{:S(2)}) collective-permute-start(s16[64,2176]{1,0:T(8,128)(2,1)S(1)} %get-tuple-element.32.coded_ref), channel_id=1, source_target_pairs={{0,1},{1,0},{2,3},{3,2},{4,5},{5,4},{6,7},{7,6},{8,9},{9,8},{10,11... | collective-permute-start | bytes 835592 | tf_op jit(solution)/shard_map/ppermute | solution.py:18
  38.0 6.6 %collective-permute-start.14 = (s16[64,2176]{1,0:T(8,128)(2,1)S(1)}, s16[64,2176]{1,0:T(8,128)(2,1)S(1)}, u32[]{:S(2)}, u32[]{:S(2)}) collective-permute-start(s16[64,2176]{1,0:T(8,128)(2,1)S(1)} %get-tuple-element.32.coded_ref), channel_id=1, source_target_pairs={{0,8},{1,4},{2,10},{3,6},{4,1},{5,13},{6,3},{7,15},{8,0},{9,12},{1... | collective-permute-start | bytes 835592 | tf_op jit(solution)/shard_map/ppermute | solution.py:38
  40.0 11.6 %collective-permute-start.12 = (s16[64,2176]{1,0:T(8,128)(2,1)S(1)}, s16[64,2176]{1,0:T(8,128)(2,1)S(1)}, u32[]{:S(2)}, u32[]{:S(2)}) collective-permute-start(s16[64,2176]{1,0:T(8,128)(2,1)S(1)} %get-tuple-element.33), channel_id=1, source_target_pairs={{0,2},{1,3},{2,0},{3,1},{4,6},{5,7},{6,4},{7,5},{8,10},{9,11},{10,... | collective-permute-start | bytes 835592 | tf_op jit(solution)/shard_map/ppermute | solution.py:27
  42.6 24.8 %copy-start.2 = (f32[64]{0:T(128)S(1)}, f32[64]{0:T(128)}, u32[]{:S(2)}) copy-start(f32[64]{0:T(128)} %param.7) | copy-start | bytes 772
  42.6 8.9 %collective-permute-start.13 = (s16[64,2176]{1,0:T(8,128)(2,1)S(1)}, s16[64,2176]{1,0:T(8,128)(2,1)S(1)}, u32[]{:S(2)}, u32[]{:S(2)}) collective-permute-start(s16[64,2176]{1,0:T(8,128)(2,1)S(1)} %get-tuple-element.34), channel_id=1, source_target_pairs={{0,1},{1,0},{2,4},{3,5},{4,2},{5,3},{6,7},{7,6},{8,9},{9,8},{10,12... | collective-permute-start | bytes 835592 | tf_op jit(solution)/shard_map/ppermute | solution.py:27
  52.4 4.5 %collective-permute-start.15 = (s16[64,640]{1,0:T(8,128)(2,1)S(1)}, s16[64,640]{1,0:T(8,128)(2,1)S(1)}, u32[]{:S(2)}, u32[]{:S(2)}) collective-permute-start(s16[64,640]{1,0:T(8,128)(2,1)S(1)} %shard_map.65.z0), channel_id=1, source_target_pairs={{0,8},{8,0},{16,24},{24,16},{1,9},{9,1},{17,25},{25,17},{2,10},{10... | collective-permute-start | bytes 245768 | tf_op jit(solution)/shard_map/ppermute | solution.py:18
  54.0 6.2 %collective-permute-start.16 = (s16[64,640]{1,0:T(8,128)(2,1)S(1)}, s16[64,640]{1,0:T(8,128)(2,1)S(1)}, u32[]{:S(2)}, u32[]{:S(2)}) collective-permute-start(s16[64,640]{1,0:T(8,128)(2,1)S(1)} %shard_map.65.z0), channel_id=1, source_target_pairs={{0,16},{8,24},{16,0},{24,8},{1,17},{9,25},{17,1},{25,9},{2,18},{10... | collective-permute-start | bytes 245768 | tf_op jit(solution)/shard_map/ppermute | solution.py:18
  54.7 5.5 %collective-permute-start.17 = (s16[64,640]{1,0:T(8,128)(2,1)S(1)}, s16[64,640]{1,0:T(8,128)(2,1)S(1)}, u32[]{:S(2)}, u32[]{:S(2)}) collective-permute-start(s16[64,640]{1,0:T(8,128)(2,1)S(1)} %shard_map.65.z0), channel_id=1, source_target_pairs={{0,24},{8,16},{16,8},{24,0},{1,25},{9,17},{17,9},{25,1},{2,26},{10... | collective-permute-start | bytes 245768 | tf_op jit(solution)/shard_map/ppermute | solution.py:18
  60.4 1.2 %collective-permute-start.18 = (f32[8,128]{1,0:T(8,128)S(1)}, f32[8,128]{1,0:T(8,128)S(1)}, u32[]{:S(2)}, u32[]{:S(2)}) collective-permute-start(f32[8,128]{1,0:T(8,128)S(1)} %shard_map.66), channel_id=1, source_target_pairs={{0,1},{1,0},{2,3},{3,2},{4,5},{5,4},{6,7},{7,6},{8,9},{9,8},{10,11... | collective-permute-start | bytes 12296 | tf_op jit(solution)/shard_map/ppermute | solution.py:18
  61.6 5.9 %collective-permute-start.19 = (f32[8,128]{1,0:T(8,128)S(1)}, f32[8,128]{1,0:T(8,128)S(1)}, u32[]{:S(2)}, u32[]{:S(2)}) collective-permute-start(f32[8,128]{1,0:T(8,128)S(1)} %add.3.p0), channel_id=1, source_target_pairs={{0,2},{1,3},{2,0},{3,1},{4,6},{5,7},{6,4},{7,5},{8,10},{9,11},{10,... | collective-permute-start | bytes 12296 | tf_op jit(solution)/shard_map/ppermute | solution.py:18
  65.0 4.5 %collective-permute-start.20 = (f32[8,128]{1,0:T(8,128)S(1)}, f32[8,128]{1,0:T(8,128)S(1)}, u32[]{:S(2)}, u32[]{:S(2)}) collective-permute-start(f32[8,128]{1,0:T(8,128)S(1)} %add.3.p0), channel_id=1, source_target_pairs={{0,4},{1,5},{2,6},{3,7},{4,0},{5,1},{6,2},{7,3},{8,12},{9,13},{10,... | collective-permute-start | bytes 12296 | tf_op jit(solution)/shard_map/ppermute | solution.py:18
  65.0 5.4 %collective-permute-start.21 = (f32[8,128]{1,0:T(8,128)S(1)}, f32[8,128]{1,0:T(8,128)S(1)}, u32[]{:S(2)}, u32[]{:S(2)}) collective-permute-start(f32[8,128]{1,0:T(8,128)S(1)} %add.3.p0), channel_id=1, source_target_pairs={{0,6},{1,7},{2,4},{3,5},{4,2},{5,3},{6,0},{7,1},{8,14},{9,15},{10,... | collective-permute-start | bytes 12296 | tf_op jit(solution)/shard_map/ppermute | solution.py:18

commit v8 on v6

--- a/solution.py
+++ b/solution.py
@@ -27,10 +27,15 @@
     return lax.ppermute(value, "snp", pairs)
 
 
-def distant(value):
-    count = lax.axis_size("snp")
-    both = [(i, i + 3) for i in range(1, count - 3, 2)] + [(0, 2), (count - 3, count - 1)]
-    return lax.ppermute(value, "snp", both + [(j, i) for i, j in both])
+def adjacent(value):
+    rows, count = lax.axis_size("samp"), lax.axis_size("snp")
+    pairs = []
+    for row in range(rows):
+        for i in range(count):
+            target = i + 1 if i % 2 else i - 1
+            inside = 0 <= target < count
+            pairs.append((row * count + i, row * count + target if inside else (row ^ 1) * count + i))
+    return lax.ppermute(value, ("samp", "snp"), pairs)
 
 
 def shifted(value):
@@ -169,45 +174,36 @@
     index = lax.axis_index("snp")
     odd = (index & 1) == 1
     below, above = (index >= 2).astype(jnp.int32), (index < count - 2).astype(jnp.int32)
-    outer = jnp.where(odd, below, above) == 1
-    inner = jnp.where(odd, above, below) == 1
-    far = jnp.where(odd, (index < count - 3).astype(jnp.int32), (index >= 3).astype(jnp.int32)) == 1
-    return odd, outer, inner, far
-
-
-def give_kernel(count, near_ref, own_ref, coded_ref, partner_ref, outer_ref, inner_ref):
-    odd = place(count)[0]
+    side = jnp.where(odd, above, below) == 1
+    across = jnp.where(odd, below, above) == 1
+    return odd, side, across
+
+
+def give_kernel(count, up, near_ref, own_ref, coded_ref, other_ref, sent_ref):
+    odd, side, _ = place(count)
     exponent, width = aux(coded_ref)[:2]
-    partner_exponent, partner_width = aux(partner_ref)[:2]
+    other_exponent, other_width = aux(other_ref)[:2]
     near = near_ref[0:1, 0:1]
-    sent = jnp.maximum(exponent, partner_exponent) + 1.0
+    sent = jnp.maximum(exponent, other_exponent) + 1.0
     scale = jnp.exp2(UNIT - sent)
-    partner_scale = scale * jnp.exp2(partner_exponent - UNIT)
-    flag = lambda value, least: (value >= least).astype(jnp.float32)
-    up_own = flag(width, 2.0) * scale
-    up_partner = flag(partner_width, jnp.where(odd, 3.0, 1.0)) * partner_scale
-    down_own = flag(near, 2.0) * scale
-    down_partner = flag(near, jnp.where(odd, 1.0, 3.0)) * partner_scale
-    choose = lambda even_case, odd_case: jnp.where(odd, odd_case, even_case)
-    outer_own, outer_partner = choose(down_own, up_own), choose(down_partner, up_partner)
-    inner_own, inner_partner = choose(up_own, down_own), choose(up_partner, down_partner)
+    rises = odd if up else jnp.logical_not(odd)
+    known = True if up else side
+    own_scale = jnp.where(jnp.where(rises, width, near) >= 2, scale, 0.0)
+    other_scale = jnp.where(jnp.where(rises, other_width, near) >= 3, scale * unit(other_exponent, known), 0.0)
     for k in range(0, own_ref.shape[1], CHUNK):
-        own, partner = own_ref[:, pl.ds(k, CHUNK)], values(partner_ref, k)
-        outer_ref[:, pl.ds(k, CHUNK)] = fixed(own * outer_own + partner * outer_partner)
-        inner_ref[:, pl.ds(k, CHUNK)] = fixed(own * inner_own + partner * inner_partner)
-    finish(outer_ref, sent, width)
-    finish(inner_ref, sent, width)
-
-
-def window_kernel(samples, count, own_ref, coded_ref, partner_ref, outer_ref, inner_ref, far_ref, scaled_ref, sent_ref):
-    odd, use_outer, use_inner, use_far = place(count)
+        sent_ref[:, pl.ds(k, CHUNK)] = fixed(own_ref[:, pl.ds(k, CHUNK)] * own_scale + values(other_ref, k) * other_scale)
+    finish(sent_ref, sent, width)
+
+
+def window_kernel(samples, count, own_ref, coded_ref, partner_ref, next_ref, same_ref, cross_ref, scaled_ref, sent_ref):
+    odd, side, across = place(count)
     width = aux(coded_ref)[1]
     partner_exponent, partner_width = aux(partner_ref)[:2]
-    far_exponent, far_width = aux(far_ref)[:2]
+    next_exponent, next_width = aux(next_ref)[:2]
     partner_scale = unit(partner_exponent, jnp.where(odd, partner_width, width) >= 1)
-    outer_scale = unit(aux(outer_ref)[0], use_outer)
-    inner_scale = unit(aux(inner_ref)[0], use_inner)
-    far_scale = jnp.where(jnp.where(odd, width, far_width) >= 3, unit(far_exponent, use_far), 0.0)
+    next_scale = jnp.where(jnp.where(odd, width, next_width) >= 1, unit(next_exponent, side), 0.0)
+    same_scale = unit(aux(same_ref)[0], side)
+    cross_scale = unit(aux(cross_ref)[0], across)
     rows = own_ref.shape[0]
     acc = jnp.zeros((2 * rows, scaled_ref.shape[1]), jnp.float32)
     curved = jnp.zeros((rows, CHUNK), jnp.float32)
@@ -216,9 +212,9 @@
         mixed = (
             own
             + values(partner_ref, k) * partner_scale
-            + values(outer_ref, k) * outer_scale
-            + values(inner_ref, k) * inner_scale
-            + values(far_ref, k) * far_scale
+            + values(next_ref, k) * next_scale
+            + values(same_ref, k) * same_scale
+            + values(cross_ref, k) * cross_scale
         )
         acc = acc + jnp.dot(
             two_terms(mixed), scaled_ref[pl.ds(k, CHUNK)], preferred_element_type=jnp.float32
@@ -297,15 +293,17 @@
         wide, sums, one, two, three, dosage, start,
     )
 
+    def give(up, *args):
+        return call(functools.partial(give_kernel, count, up), [coded_out], near, *args)[0]
+
     def window(own, coded):
-        far = distant(coded)
+        beside = adjacent(coded)
         partner = swap(coded, "snp", 1)
-        outer, inner = call(
-            functools.partial(give_kernel, count), [coded_out, coded_out], near, own, coded, partner
-        )
+        cross = crossing(give(1, own, coded, partner), 1)
+        same = crossing(give(0, own, coded, beside), 0)
         (z,) = call(
             functools.partial(window_kernel, samples, count), [sent_out],
-            own, coded, partner, crossing(outer, 1), crossing(inner, 0), far, scaled,
+            own, coded, partner, beside, same, cross, scaled,
         )
         return [z, *partners(z, "samp", 1, 2)]
 

time: 73.5 us -> 69 us (0.939)
  waiting for transfers between devices: 40.2 us -> 35.9 us
    ppermute x4, waiting for transfers between devices: 11.4 us -> 8.12 us  [crossing(): return lax.ppermute(value, 'snp', pairs)]
    ppermute x2, waiting for transfers between devices: 11.8 us -> 9.04 us  [adjacent(): return lax.ppermute(value, ('samp', 'snp'), pairs)]
    ppermute x4, starting transfers between devices: 4.08 us -> 1.33 us  [crossing(): return lax.ppermute(value, 'snp', pairs)]
    ppermute x2, starting transfers between devices: 1.2 us -> 3.36 us  [adjacent(): return lax.ppermute(value, ('samp', 'snp'), pairs)]
    ppermute x15, waiting for transfers between devices: 13.5 us -> 15.1 us  [swap(): lax.ppermute(value, axis, [(i, i ^ bits) for i in range(lax.axis_size(axi...]
    pallas_call x9 -> x11, Pallas kernels: 6.47 us -> 6.7 us  [call(): pl.pallas_call(body, out_shape=outs, in_specs=specs, out_specs=[pl.BlockS...]
where the time goes in v8:
time: 69 us; the launch traced here: 68.8 us
  waiting for transfers between devices  35.9 us (52%)
  starting transfers between devices  23.1 us (33%)
  Pallas kernels  6.7 us (10%)
  local copies, waits for them, and re-layouts  1.69 us (2%)
  between operations  1.43 us (2%)
    ppermute x15, starting transfers between devices, swap(): lax.ppermute(value, axis, [(i, i ^ bits) for i in range(lax.axis_size(axi...  16.3 us
    ppermute x15, waiting for transfers between devices, swap(): lax.ppermute(value, axis, [(i, i ^ bits) for i in range(lax.axis_size(axi...  15.1 us
    ppermute x2, waiting for transfers between devices, adjacent(): return lax.ppermute(value, ('samp', 'snp'), pairs)  9.04 us
    ppermute x4, waiting for transfers between devices, crossing(): return lax.ppermute(value, 'snp', pairs)  8.12 us
    pallas_call x11, Pallas kernels, call(): pl.pallas_call(body, out_shape=outs, in_specs=specs, out_specs=[pl.BlockS...  6.7 us
    ppermute x1, waiting for transfers between devices, shifted(): lax.ppermute(value, 'snp', [(i, (i + 2) % count) for i in range(count)])  3.61 us
    ppermute x2, starting transfers between devices, adjacent(): return lax.ppermute(value, ('samp', 'snp'), pairs)  3.36 us
    ppermute x1, starting transfers between devices, shifted(): lax.ppermute(value, 'snp', [(i, (i + 2) % count) for i in range(count)])  2.09 us
  transfers between devices with their start and end apart: 22, of which 16 were waited for; matrix products, arithmetic and copies ran while one was open for 0% of the time, Pallas kernels for 1%

profile of v8, /device:TPU:0, one launch (start us, length us, event | category | flops | bytes accessed | tf_op | source)
XLA Modules:
  0.0 68.8 jit_solution(12262067867594417512)
XLA Ops:
  0.6 0.0 copy-start
  0.6 1.6 %copy-done = bf16[2048,512]{1,0:T(8,128)(2,1)S(1)} copy-done((bf16[2048,512]{1,0:T(8,128)(2,1)S(1)}, bf16[2048,512]{1,0:T(8,128)(2,1)}, u32[]{:S(2)}) %copy-start) | copy-done | bytes 2097176
  2.2 0.0 copy-start.1
  2.2 0.4 shard_map.59.s0
  2.6 3.0 %collective-permute-start = (f32[8,512]{1,0:T(8,128)S(1)}, f32[8,512]{1,0:T(8,128)S(1)}, u32[]{:S(2)}, u32[]{:S(2)}) collective-permute-start(f32[8,512]{1,0:T(8,128)S(1)} %shard_map.59.s0), channel_id=1, source_target_pairs={{0,8},{8,0},{16,24},{24,16},{1,9},{9,1},{17,25},{25,17},{2,10},{10... | collective-permute-start | bytes 49160 | tf_op jit(solution)/shard_map/ppermute | solution.py:18
  5.6 1.5 %collective-permute-start.1 = (f32[8,512]{1,0:T(8,128)S(1)}, f32[8,512]{1,0:T(8,128)S(1)}, u32[]{:S(2)}, u32[]{:S(2)}) collective-permute-start(f32[8,512]{1,0:T(8,128)S(1)} %shard_map.59.s0), channel_id=1, source_target_pairs={{0,16},{8,24},{16,0},{24,8},{1,17},{9,25},{17,1},{25,9},{2,18},{10... | collective-permute-start | bytes 49160 | tf_op jit(solution)/shard_map/ppermute | solution.py:18
  7.1 0.0 collective-permute-start.2
  7.8 2.1 %collective-permute-start.3 = (f32[8,128]{1,0:T(8,128)S(1)}, f32[8,128]{1,0:T(8,128)S(1)}, u32[]{:S(2)}, u32[]{:S(2)}) collective-permute-start(f32[8,128]{1,0:T(8,128)S(1)} %broadcast_in_dim.13.wide_ref), channel_id=1, source_target_pairs={{0,2},{1,3},{2,4},{3,5},{4,6},{5,7},{6,0},{7,1},{8,10},{9,11},{10,... | collective-permute-start | bytes 12296 | tf_op jit(solution)/shard_map/ppermute | solution.py:43
  9.9 0.0 collective-permute-done.s1
  9.9 3.6 %collective-permute-done.3.near_ref = f32[8,128]{1,0:T(8,128)S(1)} collective-permute-done((f32[8,128]{1,0:T(8,128)S(1)}, f32[8,128]{1,0:T(8,128)S(1)}, u32[]{:S(2)}, u32[]{:S(2)}) %collective-permute-start.3) | collective-permute-done | bytes 4128 | tf_op jit(solution)/shard_map/ppermute | solution.py:43
  13.5 0.0 collective-permute-done.1.s2
  13.5 0.0 collective-permute-done.2.s3
  13.5 0.0 copy-done.1
  13.5 1.0 %shard_map.60 = (bf16[2048,512]{1,0:T(8,128)(2,1)S(1)}, f32[64,2048]{1,0:T(8,128)S(1)}, s16[64,2176]{1,0:T(8,128)(2,1)S(1)}) custom-call(f32[8,128]{1,0:T(8,128)S(1)} %broadcast_in_dim.13.wide_ref, f32[8,512]{1,0:T(8,128)S(1)} %shard_map.59.s0, f32[8,512]{1,0:T(8,128)S(1)} %collective-permute-done.s1, f32[8,512]{1,0:T(8,128)S(1)} %collective-permute-done.1.s2, ...), custom_call_target="tpu_custom_call" | custom-call | tf_op jit(solution)/shard_map/pallas_call | solution.py:58
  14.5 0.1 collective-permute-start.4
  14.6 1.8 %collective-permute-start.5 = (s16[64,2176]{1,0:T(8,128)(2,1)S(1)}, s16[64,2176]{1,0:T(8,128)(2,1)S(1)}, u32[]{:S(2)}, u32[]{:S(2)}) collective-permute-start(s16[64,2176]{1,0:T(8,128)(2,1)S(1)} %get-tuple-element.21.coded_ref), channel_id=1, source_target_pairs={{0,8},{1,2},{2,1},{3,4},{4,3},{5,6},{6,5},{7,15},{8,0},{9,10},{10,... | collective-permute-start | bytes 835592 | tf_op jit(solution)/shard_map/ppermute | solution.py:38
  16.4 0.0 collective-permute-done.4.other_ref.partner_ref
  16.4 0.3 shard_map.62
  16.7 0.0 collective-permute-start.7
  16.7 4.5 %collective-permute-done.5.other_ref.next_ref = s16[64,2176]{1,0:T(8,128)(2,1)S(1)} collective-permute-done((s16[64,2176]{1,0:T(8,128)(2,1)S(1)}, s16[64,2176]{1,0:T(8,128)(2,1)S(1)}, u32[]{:S(2)}, u32[]{:S(2)}) %collective-permute-start.5) | collective-permute-done | bytes 278560 | tf_op jit(solution)/shard_map/ppermute | solution.py:38
  21.2 0.3 shard_map.61
  21.5 0.0 collective-permute-start.6
  21.5 2.7 %collective-permute-done.7.cross_ref = s16[64,2176]{1,0:T(8,128)(2,1)S(1)} collective-permute-done((s16[64,2176]{1,0:T(8,128)(2,1)S(1)}, s16[64,2176]{1,0:T(8,128)(2,1)S(1)}, u32[]{:S(2)}, u32[]{:S(2)}) %collective-permute-start.7) | collective-permute-done | bytes 278560 | tf_op jit(solution)/shard_map/ppermute | solution.py:27
  24.3 1.3 %collective-permute-done.6.same_ref = s16[64,2176]{1,0:T(8,128)(2,1)S(1)} collective-permute-done((s16[64,2176]{1,0:T(8,128)(2,1)S(1)}, s16[64,2176]{1,0:T(8,128)(2,1)S(1)}, u32[]{:S(2)}, u32[]{:S(2)}) %collective-permute-start.6) | collective-permute-done | bytes 278560 | tf_op jit(solution)/shard_map/ppermute | solution.py:27
  25.6 0.9 %shard_map.63.z0 = s16[64,640]{1,0:T(8,128)(2,1)S(1)} custom-call(f32[64,2048]{1,0:T(8,128)S(1)} %get-tuple-element.20.own_ref, s16[64,2176]{1,0:T(8,128)(2,1)S(1)} %get-tuple-element.21.coded_ref, s16[64,2176]{1,0:T(8,128)(2,1)S(1)} %collective-permute-done.4.other_ref.partner_ref, s16[64,2176]{1,0:T(8,128)(2,1)S(1)} %collective-permute-done.5.other_ref.next_ref, ...), custom_call_target="tpu_custom_call" | custom-call | tf_op jit(solution)/shard_map/pallas_call | solution.py:58
  26.5 2.7 %collective-permute-start.10 = (s16[64,640]{1,0:T(8,128)(2,1)S(1)}, s16[64,640]{1,0:T(8,128)(2,1)S(1)}, u32[]{:S(2)}, u32[]{:S(2)}) collective-permute-start(s16[64,640]{1,0:T(8,128)(2,1)S(1)} %shard_map.63.z0), channel_id=1, source_target_pairs={{0,24},{8,16},{16,8},{24,0},{1,25},{9,17},{17,9},{25,1},{2,26},{10... | collective-permute-start | bytes 245768 | tf_op jit(solution)/shard_map/ppermute | solution.py:18
  29.2 0.6 collective-permute-start.8
  29.8 0.3 collective-permute-start.9
  30.1 2.3 %collective-permute-done.10.z3 = s16[64,640]{1,0:T(8,128)(2,1)S(1)} collective-permute-done((s16[64,640]{1,0:T(8,128)(2,1)S(1)}, s16[64,640]{1,0:T(8,128)(2,1)S(1)}, u32[]{:S(2)}, u32[]{:S(2)}) %collective-permute-start.10) | collective-permute-done | bytes 81952 | tf_op jit(solution)/shard_map/ppermute | solution.py:18
  32.3 2.2 %collective-permute-done.8.z1 = s16[64,640]{1,0:T(8,128)(2,1)S(1)} collective-permute-done((s16[64,640]{1,0:T(8,128)(2,1)S(1)}, s16[64,640]{1,0:T(8,128)(2,1)S(1)}, u32[]{:S(2)}, u32[]{:S(2)}) %collective-permute-start.8) | collective-permute-done | bytes 81952 | tf_op jit(solution)/shard_map/ppermute | solution.py:18
  34.5 0.5 collective-permute-done.9.z2
  35.0 1.0 %shard_map.64 = (f32[64,512]{1,0:T(8,128)S(1)}, f32[64,128]{1,0:T(8,128)S(1)}, f32[64,2048]{1,0:T(8,128)S(1)}, s16[64,2176]{1,0:T(8,128)(2,1)S(1)}) custom-call(f32[8,128]{1,0:T(8,128)S(1)} %broadcast_in_dim.13.wide_ref, s16[64,640]{1,0:T(8,128)(2,1)S(1)} %shard_map.63.z0, s16[64,640]{1,0:T(8,128)(2,1)S(1)} %collective-permute-done.8.z1, ...), custom_call_target="tpu_custom_call" | custom-call | tf_op jit(solution)/shard_map/pallas_call | solution.py:58
  36.0 0.1 collective-permute-start.11
  36.1 1.6 %collective-permute-start.12 = (s16[64,2176]{1,0:T(8,128)(2,1)S(1)}, s16[64,2176]{1,0:T(8,128)(2,1)S(1)}, u32[]{:S(2)}, u32[]{:S(2)}) collective-permute-start(s16[64,2176]{1,0:T(8,128)(2,1)S(1)} %get-tuple-element.26.coded_ref), channel_id=1, source_target_pairs={{0,8},{1,2},{2,1},{3,4},{4,3},{5,6},{6,5},{7,15},{8,0},{9,10},{10,... | collective-permute-start | bytes 835592 | tf_op jit(solution)/shard_map/ppermute | solution.py:38
  37.7 0.0 collective-permute-done.11.other_ref.partner_ref
  37.7 0.3 shard_map.66
  38.0 0.2 collective-permute-start.14
  38.2 4.5 %collective-permute-done.12.other_ref.next_ref = s16[64,2176]{1,0:T(8,128)(2,1)S(1)} collective-permute-done((s16[64,2176]{1,0:T(8,128)(2,1)S(1)}, s16[64,2176]{1,0:T(8,128)(2,1)S(1)}, u32[]{:S(2)}, u32[]{:S(2)}) %collective-permute-start.12) | collective-permute-done | bytes 278560 | tf_op jit(solution)/shard_map/ppermute | solution.py:38
  42.7 0.3 shard_map.65
  43.0 0.0 copy-start.2
  43.0 1.1 %collective-permute-start.13 = (s16[64,2176]{1,0:T(8,128)(2,1)S(1)}, s16[64,2176]{1,0:T(8,128)(2,1)S(1)}, u32[]{:S(2)}, u32[]{:S(2)}) collective-permute-start(s16[64,2176]{1,0:T(8,128)(2,1)S(1)} %shard_map.65), channel_id=1, source_target_pairs={{0,2},{1,0},{2,4},{3,1},{4,6},{5,3},{6,7},{7,5},{8,10},{9,8},{10,1... | collective-permute-start | bytes 835592 | tf_op jit(solution)/shard_map/ppermute | solution.py:27
  44.1 1.7 %collective-permute-done.14.cross_ref = s16[64,2176]{1,0:T(8,128)(2,1)S(1)} collective-permute-done((s16[64,2176]{1,0:T(8,128)(2,1)S(1)}, s16[64,2176]{1,0:T(8,128)(2,1)S(1)}, u32[]{:S(2)}, u32[]{:S(2)}) %collective-permute-start.14) | collective-permute-done | bytes 278560 | tf_op jit(solution)/shard_map/ppermute | solution.py:27
  45.7 2.4 %collective-permute-done.13.same_ref = s16[64,2176]{1,0:T(8,128)(2,1)S(1)} collective-permute-done((s16[64,2176]{1,0:T(8,128)(2,1)S(1)}, s16[64,2176]{1,0:T(8,128)(2,1)S(1)}, u32[]{:S(2)}, u32[]{:S(2)}) %collective-permute-start.13) | collective-permute-done | bytes 278560 | tf_op jit(solution)/shard_map/ppermute | solution.py:27
  48.1 0.9 %shard_map.67.z0 = s16[64,640]{1,0:T(8,128)(2,1)S(1)} custom-call(f32[64,2048]{1,0:T(8,128)S(1)} %get-tuple-element.25.own_ref, s16[64,2176]{1,0:T(8,128)(2,1)S(1)} %get-tuple-element.26.coded_ref, s16[64,2176]{1,0:T(8,128)(2,1)S(1)} %collective-permute-done.11.other_ref.partner_ref, s16[64,2176]{1,0:T(8,128)(2,1)S(1)} %collective-permute-done.12.other_ref.next_ref, ...), custom_call_target="tpu_custom_call" | custom-call | tf_op jit(solution)/shard_map/pallas_call | solution.py:58
  49.1 1.6 %collective-permute-start.15 = (s16[64,640]{1,0:T(8,128)(2,1)S(1)}, s16[64,640]{1,0:T(8,128)(2,1)S(1)}, u32[]{:S(2)}, u32[]{:S(2)}) collective-permute-start(s16[64,640]{1,0:T(8,128)(2,1)S(1)} %shard_map.67.z0), channel_id=1, source_target_pairs={{0,8},{8,0},{16,24},{24,16},{1,9},{9,1},{17,25},{25,17},{2,10},{10... | collective-permute-start | bytes 245768 | tf_op jit(solution)/shard_map/ppermute | solution.py:18
  50.6 0.5 collective-permute-start.16
  51.1 1.5 %collective-permute-start.17 = (s16[64,640]{1,0:T(8,128)(2,1)S(1)}, s16[64,640]{1,0:T(8,128)(2,1)S(1)}, u32[]{:S(2)}, u32[]{:S(2)}) collective-permute-start(s16[64,640]{1,0:T(8,128)(2,1)S(1)} %shard_map.67.z0), channel_id=1, source_target_pairs={{0,24},{8,16},{16,8},{24,0},{1,25},{9,17},{17,9},{25,1},{2,26},{10... | collective-permute-start | bytes 245768 | tf_op jit(solution)/shard_map/ppermute | solution.py:18
  52.6 1.2 %collective-permute-done.15.z1 = s16[64,640]{1,0:T(8,128)(2,1)S(1)} collective-permute-done((s16[64,640]{1,0:T(8,128)(2,1)S(1)}, s16[64,640]{1,0:T(8,128)(2,1)S(1)}, u32[]{:S(2)}, u32[]{:S(2)}) %collective-permute-start.15) | collective-permute-done | bytes 81952 | tf_op jit(solution)/shard_map/ppermute | solution.py:18
  53.9 1.3 %collective-permute-done.16.z2 = s16[64,640]{1,0:T(8,128)(2,1)S(1)} collective-permute-done((s16[64,640]{1,0:T(8,128)(2,1)S(1)}, s16[64,640]{1,0:T(8,128)(2,1)S(1)}, u32[]{:S(2)}, u32[]{:S(2)}) %collective-permute-start.16) | collective-permute-done | bytes 81952 | tf_op jit(solution)/shard_map/ppermute | solution.py:18
  55.2 1.8 %collective-permute-done.17.z3 = s16[64,640]{1,0:T(8,128)(2,1)S(1)} collective-permute-done((s16[64,640]{1,0:T(8,128)(2,1)S(1)}, s16[64,640]{1,0:T(8,128)(2,1)S(1)}, u32[]{:S(2)}, u32[]{:S(2)}) %collective-permute-start.17) | collective-permute-done | bytes 81952 | tf_op jit(solution)/shard_map/ppermute | solution.py:18
  56.9 0.3 shard_map.68
  57.2 0.0 collective-permute-start.18
  57.2 1.2 %collective-permute-done.18 = f32[8,128]{1,0:T(8,128)S(1)} collective-permute-done((f32[8,128]{1,0:T(8,128)S(1)}, f32[8,128]{1,0:T(8,128)S(1)}, u32[]{:S(2)}, u32[]{:S(2)}) %collective-permute-start.18) | collective-permute-done | bytes 4128 | tf_op jit(solution)/shard_map/ppermute | solution.py:18
  58.4 2.1 %collective-permute-start.19 = (f32[8,128]{1,0:T(8,128)S(1)}, f32[8,128]{1,0:T(8,128)S(1)}, u32[]{:S(2)}, u32[]{:S(2)}) collective-permute-start(f32[8,128]{1,0:T(8,128)S(1)} %add.3.p0), channel_id=1, source_target_pairs={{0,2},{1,3},{2,0},{3,1},{4,6},{5,7},{6,4},{7,5},{8,10},{9,11},{10,... | collective-permute-start | bytes 12296 | tf_op jit(solution)/shard_map/ppermute | solution.py:18
  60.4 1.7 %collective-permute-start.20 = (f32[8,128]{1,0:T(8,128)S(1)}, f32[8,128]{1,0:T(8,128)S(1)}, u32[]{:S(2)}, u32[]{:S(2)}) collective-permute-start(f32[8,128]{1,0:T(8,128)S(1)} %add.3.p0), channel_id=1, source_target_pairs={{0,4},{1,5},{2,6},{3,7},{4,0},{5,1},{6,2},{7,3},{8,12},{9,13},{10,... | collective-permute-start | bytes 12296 | tf_op jit(solution)/shard_map/ppermute | solution.py:18
  62.2 0.6 collective-permute-start.21
  62.8 0.0 copy-done.2
  62.8 0.1 copy.6.shrink_ref
  62.9 0.0 collective-permute-done.19.p1
  62.9 2.0 %collective-permute-done.20.p2 = f32[8,128]{1,0:T(8,128)S(1)} collective-permute-done((f32[8,128]{1,0:T(8,128)S(1)}, f32[8,128]{1,0:T(8,128)S(1)}, u32[]{:S(2)}, u32[]{:S(2)}) %collective-permute-start.20) | collective-permute-done | bytes 4128 | tf_op jit(solution)/shard_map/ppermute | solution.py:18
  65.0 2.6 %collective-permute-done.21.p3 = f32[8,128]{1,0:T(8,128)S(1)} collective-permute-done((f32[8,128]{1,0:T(8,128)S(1)}, f32[8,128]{1,0:T(8,128)S(1)}, u32[]{:S(2)}, u32[]{:S(2)}) %collective-permute-start.21) | collective-permute-done | bytes 4128 | tf_op jit(solution)/shard_map/ppermute | solution.py:18
  67.6 1.2 %shard_map.69 = (f32[64,512]{1,0:T(8,128)}, f32[64,512]{1,0:T(8,128)}) custom-call(f32[64,1]{1,0:T(8,128)S(1)} %copy.6.shrink_ref, f32[8,128]{1,0:T(8,128)S(1)} %add.3.p0, f32[8,128]{1,0:T(8,128)S(1)} %collective-permute-done.19.p1, f32[8,128]{1,0:T(8,128)S(1)} %collective-permute-done.20.p2, f32[8,128]{1,0:T(8,128)S(1)} %collective-permute-done.21.p3, ...), custom_call_target="tpu_custom_call" | custom-call | tf_op jit(solution)/shard_map/pallas_call | solution.py:58
  (2 shorter events, 0.0 us)
Async XLA Ops:
  0.6 1.6 %copy-start = (bf16[2048,512]{1,0:T(8,128)(2,1)S(1)}, bf16[2048,512]{1,0:T(8,128)(2,1)}, u32[]{:S(2)}) copy-start(bf16[2048,512]{1,0:T(8,128)(2,1)} %dosage_ref.3) | copy-start | bytes 6291460
  2.2 11.3 %copy-start.1 = (f32[512,64]{0,1:T(8,128)S(1)}, f32[512,64]{0,1:T(8,128)}, u32[]{:S(2)}) copy-start(f32[512,64]{0,1:T(8,128)} %param.6) | copy-start | bytes 393220
  2.6 7.3 %collective-permute-start = (f32[8,512]{1,0:T(8,128)S(1)}, f32[8,512]{1,0:T(8,128)S(1)}, u32[]{:S(2)}, u32[]{:S(2)}) collective-permute-start(f32[8,512]{1,0:T(8,128)S(1)} %shard_map.59.s0), channel_id=1, source_target_pairs={{0,8},{8,0},{16,24},{24,16},{1,9},{9,1},{17,25},{25,17},{2,10},{10... | collective-permute-start | bytes 49160 | tf_op jit(solution)/shard_map/ppermute | solution.py:18
  5.6 7.9 %collective-permute-start.1 = (f32[8,512]{1,0:T(8,128)S(1)}, f32[8,512]{1,0:T(8,128)S(1)}, u32[]{:S(2)}, u32[]{:S(2)}) collective-permute-start(f32[8,512]{1,0:T(8,128)S(1)} %shard_map.59.s0), channel_id=1, source_target_pairs={{0,16},{8,24},{16,0},{24,8},{1,17},{9,25},{17,1},{25,9},{2,18},{10... | collective-permute-start | bytes 49160 | tf_op jit(solution)/shard_map/ppermute | solution.py:18
  7.1 6.4 %collective-permute-start.2 = (f32[8,512]{1,0:T(8,128)S(1)}, f32[8,512]{1,0:T(8,128)S(1)}, u32[]{:S(2)}, u32[]{:S(2)}) collective-permute-start(f32[8,512]{1,0:T(8,128)S(1)} %shard_map.59.s0), channel_id=1, source_target_pairs={{0,24},{8,16},{16,8},{24,0},{1,25},{9,17},{17,9},{25,1},{2,26},{10... | collective-permute-start | bytes 49160 | tf_op jit(solution)/shard_map/ppermute | solution.py:18
  7.8 5.7 %collective-permute-start.3 = (f32[8,128]{1,0:T(8,128)S(1)}, f32[8,128]{1,0:T(8,128)S(1)}, u32[]{:S(2)}, u32[]{:S(2)}) collective-permute-start(f32[8,128]{1,0:T(8,128)S(1)} %broadcast_in_dim.13.wide_ref), channel_id=1, source_target_pairs={{0,2},{1,3},{2,4},{3,5},{4,6},{5,7},{6,0},{7,1},{8,10},{9,11},{10,... | collective-permute-start | bytes 12296 | tf_op jit(solution)/shard_map/ppermute | solution.py:43
  14.5 1.9 %collective-permute-start.4 = (s16[64,2176]{1,0:T(8,128)(2,1)S(1)}, s16[64,2176]{1,0:T(8,128)(2,1)S(1)}, u32[]{:S(2)}, u32[]{:S(2)}) collective-permute-start(s16[64,2176]{1,0:T(8,128)(2,1)S(1)} %get-tuple-element.21.coded_ref), channel_id=1, source_target_pairs={{0,1},{1,0},{2,3},{3,2},{4,5},{5,4},{6,7},{7,6},{8,9},{9,8},{10,11... | collective-permute-start | bytes 835592 | tf_op jit(solution)/shard_map/ppermute | solution.py:18
  14.6 6.6 %collective-permute-start.5 = (s16[64,2176]{1,0:T(8,128)(2,1)S(1)}, s16[64,2176]{1,0:T(8,128)(2,1)S(1)}, u32[]{:S(2)}, u32[]{:S(2)}) collective-permute-start(s16[64,2176]{1,0:T(8,128)(2,1)S(1)} %get-tuple-element.21.coded_ref), channel_id=1, source_target_pairs={{0,8},{1,2},{2,1},{3,4},{4,3},{5,6},{6,5},{7,15},{8,0},{9,10},{10,... | collective-permute-start | bytes 835592 | tf_op jit(solution)/shard_map/ppermute | solution.py:38
  16.7 7.6 %collective-permute-start.7 = (s16[64,2176]{1,0:T(8,128)(2,1)S(1)}, s16[64,2176]{1,0:T(8,128)(2,1)S(1)}, u32[]{:S(2)}, u32[]{:S(2)}) collective-permute-start(s16[64,2176]{1,0:T(8,128)(2,1)S(1)} %shard_map.62), channel_id=1, source_target_pairs={{0,1},{1,3},{2,0},{3,5},{4,2},{5,7},{6,4},{7,6},{8,9},{9,11},{10,8... | collective-permute-start | bytes 835592 | tf_op jit(solution)/shard_map/ppermute | solution.py:27
  21.5 4.1 %collective-permute-start.6 = (s16[64,2176]{1,0:T(8,128)(2,1)S(1)}, s16[64,2176]{1,0:T(8,128)(2,1)S(1)}, u32[]{:S(2)}, u32[]{:S(2)}) collective-permute-start(s16[64,2176]{1,0:T(8,128)(2,1)S(1)} %shard_map.61), channel_id=1, source_target_pairs={{0,2},{1,0},{2,4},{3,1},{4,6},{5,3},{6,7},{7,5},{8,10},{9,8},{10,1... | collective-permute-start | bytes 835592 | tf_op jit(solution)/shard_map/ppermute | solution.py:27
  26.5 5.8 %collective-permute-start.10 = (s16[64,640]{1,0:T(8,128)(2,1)S(1)}, s16[64,640]{1,0:T(8,128)(2,1)S(1)}, u32[]{:S(2)}, u32[]{:S(2)}) collective-permute-start(s16[64,640]{1,0:T(8,128)(2,1)S(1)} %shard_map.63.z0), channel_id=1, source_target_pairs={{0,24},{8,16},{16,8},{24,0},{1,25},{9,17},{17,9},{25,1},{2,26},{10... | collective-permute-start | bytes 245768 | tf_op jit(solution)/shard_map/ppermute | solution.py:18
  29.2 5.3 %collective-permute-start.8 = (s16[64,640]{1,0:T(8,128)(2,1)S(1)}, s16[64,640]{1,0:T(8,128)(2,1)S(1)}, u32[]{:S(2)}, u32[]{:S(2)}) collective-permute-start(s16[64,640]{1,0:T(8,128)(2,1)S(1)} %shard_map.63.z0), channel_id=1, source_target_pairs={{0,8},{8,0},{16,24},{24,16},{1,9},{9,1},{17,25},{25,17},{2,10},{10... | collective-permute-start | bytes 245768 | tf_op jit(solution)/shard_map/ppermute | solution.py:18
  29.8 5.3 %collective-permute-start.9 = (s16[64,640]{1,0:T(8,128)(2,1)S(1)}, s16[64,640]{1,0:T(8,128)(2,1)S(1)}, u32[]{:S(2)}, u32[]{:S(2)}) collective-permute-start(s16[64,640]{1,0:T(8,128)(2,1)S(1)} %shard_map.63.z0), channel_id=1, source_target_pairs={{0,16},{8,24},{16,0},{24,8},{1,17},{9,25},{17,1},{25,9},{2,18},{10... | collective-permute-start | bytes 245768 | tf_op jit(solution)/shard_map/ppermute | solution.py:18
  36.0 1.7 %collective-permute-start.11 = (s16[64,2176]{1,0:T(8,128)(2,1)S(1)}, s16[64,2176]{1,0:T(8,128)(2,1)S(1)}, u32[]{:S(2)}, u32[]{:S(2)}) collective-permute-start(s16[64,2176]{1,0:T(8,128)(2,1)S(1)} %get-tuple-element.26.coded_ref), channel_id=1, source_target_pairs={{0,1},{1,0},{2,3},{3,2},{4,5},{5,4},{6,7},{7,6},{8,9},{9,8},{10,11... | collective-permute-start | bytes 835592 | tf_op jit(solution)/shard_map/ppermute | solution.py:18
  36.1 6.6 %collective-permute-start.12 = (s16[64,2176]{1,0:T(8,128)(2,1)S(1)}, s16[64,2176]{1,0:T(8,128)(2,1)S(1)}, u32[]{:S(2)}, u32[]{:S(2)}) collective-permute-start(s16[64,2176]{1,0:T(8,128)(2,1)S(1)} %get-tuple-element.26.coded_ref), channel_id=1, source_target_pairs={{0,8},{1,2},{2,1},{3,4},{4,3},{5,6},{6,5},{7,15},{8,0},{9,10},{10,... | collective-permute-start | bytes 835592 | tf_op jit(solution)/shard_map/ppermute | solution.py:38
  38.0 7.7 %collective-permute-start.14 = (s16[64,2176]{1,0:T(8,128)(2,1)S(1)}, s16[64,2176]{1,0:T(8,128)(2,1)S(1)}, u32[]{:S(2)}, u32[]{:S(2)}) collective-permute-start(s16[64,2176]{1,0:T(8,128)(2,1)S(1)} %shard_map.66), channel_id=1, source_target_pairs={{0,1},{1,3},{2,0},{3,5},{4,2},{5,7},{6,4},{7,6},{8,9},{9,11},{10,8... | collective-permute-start | bytes 835592 | tf_op jit(solution)/shard_map/ppermute | solution.py:27
  43.0 19.9 %copy-start.2 = (f32[64]{0:T(128)S(1)}, f32[64]{0:T(128)}, u32[]{:S(2)}) copy-start(f32[64]{0:T(128)} %param.7) | copy-start | bytes 772
  43.0 5.2 %collective-permute-start.13 = (s16[64,2176]{1,0:T(8,128)(2,1)S(1)}, s16[64,2176]{1,0:T(8,128)(2,1)S(1)}, u32[]{:S(2)}, u32[]{:S(2)}) collective-permute-start(s16[64,2176]{1,0:T(8,128)(2,1)S(1)} %shard_map.65), channel_id=1, source_target_pairs={{0,2},{1,0},{2,4},{3,1},{4,6},{5,3},{6,7},{7,5},{8,10},{9,8},{10,1... | collective-permute-start | bytes 835592 | tf_op jit(solution)/shard_map/ppermute | solution.py:27
  49.1 4.8 %collective-permute-start.15 = (s16[64,640]{1,0:T(8,128)(2,1)S(1)}, s16[64,640]{1,0:T(8,128)(2,1)S(1)}, u32[]{:S(2)}, u32[]{:S(2)}) collective-permute-start(s16[64,640]{1,0:T(8,128)(2,1)S(1)} %shard_map.67.z0), channel_id=1, source_target_pairs={{0,8},{8,0},{16,24},{24,16},{1,9},{9,1},{17,25},{25,17},{2,10},{10... | collective-permute-start | bytes 245768 | tf_op jit(solution)/shard_map/ppermute | solution.py:18
  50.6 4.5 %collective-permute-start.16 = (s16[64,640]{1,0:T(8,128)(2,1)S(1)}, s16[64,640]{1,0:T(8,128)(2,1)S(1)}, u32[]{:S(2)}, u32[]{:S(2)}) collective-permute-start(s16[64,640]{1,0:T(8,128)(2,1)S(1)} %shard_map.67.z0), channel_id=1, source_target_pairs={{0,16},{8,24},{16,0},{24,8},{1,17},{9,25},{17,1},{25,9},{2,18},{10... | collective-permute-start | bytes 245768 | tf_op jit(solution)/shard_map/ppermute | solution.py:18
  51.1 5.8 %collective-permute-start.17 = (s16[64,640]{1,0:T(8,128)(2,1)S(1)}, s16[64,640]{1,0:T(8,128)(2,1)S(1)}, u32[]{:S(2)}, u32[]{:S(2)}) collective-permute-start(s16[64,640]{1,0:T(8,128)(2,1)S(1)} %shard_map.67.z0), channel_id=1, source_target_pairs={{0,24},{8,16},{16,8},{24,0},{1,25},{9,17},{17,9},{25,1},{2,26},{10... | collective-permute-start | bytes 245768 | tf_op jit(solution)/shard_map/ppermute | solution.py:18
  57.2 1.2 %collective-permute-start.18 = (f32[8,128]{1,0:T(8,128)S(1)}, f32[8,128]{1,0:T(8,128)S(1)}, u32[]{:S(2)}, u32[]{:S(2)}) collective-permute-start(f32[8,128]{1,0:T(8,128)S(1)} %shard_map.68), channel_id=1, source_target_pairs={{0,1},{1,0},{2,3},{3,2},{4,5},{5,4},{6,7},{7,6},{8,9},{9,8},{10,11... | collective-permute-start | bytes 12296 | tf_op jit(solution)/shard_map/ppermute | solution.py:18
  58.4 4.5 %collective-permute-start.19 = (f32[8,128]{1,0:T(8,128)S(1)}, f32[8,128]{1,0:T(8,128)S(1)}, u32[]{:S(2)}, u32[]{:S(2)}) collective-permute-start(f32[8,128]{1,0:T(8,128)S(1)} %add.3.p0), channel_id=1, source_target_pairs={{0,2},{1,3},{2,0},{3,1},{4,6},{5,7},{6,4},{7,5},{8,10},{9,11},{10,... | collective-permute-start | bytes 12296 | tf_op jit(solution)/shard_map/ppermute | solution.py:18
  60.4 4.5 %collective-permute-start.20 = (f32[8,128]{1,0:T(8,128)S(1)}, f32[8,128]{1,0:T(8,128)S(1)}, u32[]{:S(2)}, u32[]{:S(2)}) collective-permute-start(f32[8,128]{1,0:T(8,128)S(1)} %add.3.p0), channel_id=1, source_target_pairs={{0,4},{1,5},{2,6},{3,7},{4,0},{5,1},{6,2},{7,3},{8,12},{9,13},{10,... | collective-permute-start | bytes 12296 | tf_op jit(solution)/shard_map/ppermute | solution.py:18
  62.2 5.4 %collective-permute-start.21 = (f32[8,128]{1,0:T(8,128)S(1)}, f32[8,128]{1,0:T(8,128)S(1)}, u32[]{:S(2)}, u32[]{:S(2)}) collective-permute-start(f32[8,128]{1,0:T(8,128)S(1)} %add.3.p0), channel_id=1, source_target_pairs={{0,6},{1,7},{2,4},{3,5},{4,2},{5,3},{6,0},{7,1},{8,14},{9,15},{10,... | collective-permute-start | bytes 12296 | tf_op jit(solution)/shard_map/ppermute | solution.py:18

commit v9 on v8

--- a/solution.py
+++ b/solution.py
@@ -9,6 +9,7 @@
 
 
 AUX = 128
+LESS = 96
 CHUNK = 512
 UNIT = 14
 ROWS = 128
@@ -68,6 +69,10 @@
     high = value.astype(jnp.bfloat16)
     low = (value - high.astype(jnp.float32)).astype(jnp.bfloat16)
     return jnp.concatenate([high, low], 0)
+
+
+def wide_kernel(width_ref, wide_ref):
+    wide_ref[...] = jnp.full(wide_ref.shape, width_ref[0].astype(jnp.float32))
 
 
 def stats_kernel(dosage_ref, sums_ref):
@@ -85,11 +90,12 @@
 
 
 def finish(coded_ref, *columns):
-    lane = lax.broadcasted_iota(jnp.int32, (coded_ref.shape[0], AUX), 1)
+    count = coded_ref.shape[1] % AUX or AUX
+    lane = lax.broadcasted_iota(jnp.int32, (coded_ref.shape[0], count), 1)
     extra = jnp.zeros(lane.shape, jnp.float32)
     for k, column in enumerate(columns):
         extra = jnp.where(lane == k, column, extra)
-    coded_ref[:, pl.ds(coded_ref.shape[1] - AUX, AUX)] = extra.astype(jnp.int32).astype(jnp.int16)
+    coded_ref[:, pl.ds(coded_ref.shape[1] - count, count)] = extra.astype(jnp.int32).astype(jnp.int16)
 
 
 def fixed(value):
@@ -101,11 +107,14 @@
     return exponent, jnp.exp2(UNIT - exponent)
 
 
-def encode(own_ref, coded_ref, width):
+def encode(own_ref, coded_ref, shared_ref, width):
     exponent, scale = scale_of(jnp.max(jnp.abs(own_ref[...]), 1, keepdims=True))
     for k in range(0, own_ref.shape[1], CHUNK):
-        coded_ref[:, pl.ds(k, CHUNK)] = fixed(own_ref[:, pl.ds(k, CHUNK)] * scale)
+        value = fixed(own_ref[:, pl.ds(k, CHUNK)] * scale)
+        coded_ref[:, pl.ds(k, CHUNK)] = value
+        shared_ref[:, pl.ds(k, CHUNK)] = value
     finish(coded_ref, exponent, width)
+    finish(shared_ref, exponent, width)
 
 
 def split(value):
@@ -116,7 +125,8 @@
 
 
 def aux(coded_ref):
-    extra = coded_ref[:, pl.ds(coded_ref.shape[1] - AUX, AUX)].astype(jnp.int32).astype(jnp.float32)
+    count = coded_ref.shape[1] % AUX or AUX
+    extra = coded_ref[:, pl.ds(coded_ref.shape[1] - count, count)].astype(jnp.int32).astype(jnp.float32)
     return [extra[:, k : k + 1] for k in range(4)]
 
 
@@ -133,30 +143,30 @@
     return coded_ref[:, pl.ds(k, CHUNK)].astype(jnp.int32).astype(jnp.float32)
 
 
-def project(value, scaled_ref, own_ref):
+def project(value, turned_ref, own_ref):
     rows = value.shape[0]
     terms = two_terms(value)
-    for k in range(0, scaled_ref.shape[0], CHUNK):
-        both = lax.dot_general(
-            terms, scaled_ref[pl.ds(k, CHUNK)], (((1,), (1,)), ((), ())), preferred_element_type=jnp.float32
-        )
+    for k in range(0, turned_ref.shape[1], CHUNK):
+        both = jnp.dot(terms, turned_ref[:, pl.ds(k, CHUNK)], preferred_element_type=jnp.float32)
         own_ref[:, pl.ds(k, CHUNK)] = both[:rows] + both[rows:]
 
 
-def first_kernel(samples, wide_ref, s0, s1, s2, s3, dosage_ref, start_ref, scaled_ref, own_ref, coded_ref):
+def first_kernel(samples, wide_ref, s0, s1, s2, s3, dosage_ref, start_ref, scaled_ref, turned_ref, own_ref, coded_ref, shared_ref):
     sums = total([s[0:2] for s in (s0, s1, s2, s3)])
     center = sums[0:1] / samples
     spread = sums[1:2] / samples - center * center
     factor = lax.rsqrt(spread + 1e-05)
     for k in range(0, dosage_ref.shape[0], CHUNK):
         part = dosage_ref[pl.ds(k, CHUNK)].astype(jnp.float32)
-        scaled_ref[pl.ds(k, CHUNK)] = ((part - center) * factor).astype(jnp.bfloat16)
-    project(start_ref[...], scaled_ref, own_ref)
-    encode(own_ref, coded_ref, wide_ref[0:1, 0:1])
+        part = ((part - center) * factor).astype(jnp.bfloat16)
+        scaled_ref[pl.ds(k, CHUNK)] = part
+        turned_ref[:, pl.ds(k, CHUNK)] = part.T
+    project(start_ref[...], turned_ref, own_ref)
+    encode(own_ref, coded_ref, shared_ref, wide_ref[0:1, 0:1])
 
 
 def next_kernel(
-    samples, wide_ref, z0, z1, z2, z3, start_ref, scaled_ref, first_ref, parts_ref, own_ref, coded_ref
+    samples, wide_ref, z0, z1, z2, z3, start_ref, turned_ref, first_ref, parts_ref, own_ref, coded_ref, shared_ref
 ):
     first = total([grid_values(z) for z in (z0, z1, z2, z3)]) / samples
     first_ref[...] = first
@@ -166,8 +176,8 @@
     for k, (a, b) in enumerate(((start, start), (start, first), (first, first))):
         parts = jnp.where(lane == k, jnp.sum(a * b, 1, keepdims=True), parts)
     parts_ref[...] = parts
-    project(first, scaled_ref, own_ref)
-    encode(own_ref, coded_ref, wide_ref[0:1, 0:1])
+    project(first, turned_ref, own_ref)
+    encode(own_ref, coded_ref, shared_ref, wide_ref[0:1, 0:1])
 
 
 def place(count):
@@ -263,11 +273,15 @@
     value = value + swap(value, "snp", 1)
     bit = 2
     while 4 * bit < count:
-        value = total([value, *partners(value, "snp", bit, 2 * bit)])
+        value = total([value, *others(value, bit)])
         bit *= 4
     if 2 * bit < count:
-        return [value, *partners(value, "snp", bit, 2 * bit)]
-    return [value, swap(value, "snp", bit), jnp.zeros_like(value), jnp.zeros_like(value)]
+        return [value, *others(value, bit)]
+    return [value, swap(value, "snp", bit ^ 1), jnp.zeros_like(value), jnp.zeros_like(value)]
+
+
+def others(value, bit):
+    return [swap(value, "snp", k ^ 1) for k in (bit, 2 * bit, 3 * bit)]
 
 
 def shards(dosage, band_width, marginal, penalty):
@@ -278,27 +292,34 @@
     shrink = penalty[:, None]
     grid, own_shape = (rows, size), (rows, local)
     own_out, coded_out = (own_shape, jnp.float32), ((rows, local + AUX), jnp.int16)
+    shared_out = ((rows, local + LESS), jnp.int16)
 
     sent_out = ((rows, size + AUX), jnp.int16)
 
     (sums,) = call(stats_kernel, [((8, size), jnp.float32)], dosage)
     one, two, three = partners(sums, "samp", 1, 2)
     one, band_width = lax.optimization_barrier((one, band_width))
-    wide = jnp.broadcast_to(band_width.astype(jnp.float32)[:, None], (8, AUX))
+    wide = pl.pallas_call(
+        wide_kernel,
+        out_shape=jax.ShapeDtypeStruct((8, size + AUX), jnp.float32),
+        in_specs=[pl.BlockSpec(memory_space=pltpu.SMEM)],
+        out_specs=pl.BlockSpec(memory_space=pltpu.VMEM),
+        cost_estimate=pl.CostEstimate(flops=10**10, bytes_accessed=10**8, transcendentals=0),
+    )(band_width)
     near = shifted(wide)
     two, three, near = lax.optimization_barrier((two, three, near))
-    scaled, own, coded = call(
+    scaled, turned, own, coded, shared = call(
         functools.partial(first_kernel, samples),
-        [(dosage.shape, jnp.bfloat16), own_out, coded_out],
+        [(dosage.shape, jnp.bfloat16), (dosage.shape[::-1], jnp.bfloat16), own_out, coded_out, shared_out],
         wide, sums, one, two, three, dosage, start,
     )
 
     def give(up, *args):
         return call(functools.partial(give_kernel, count, up), [coded_out], near, *args)[0]
 
-    def window(own, coded):
+    def window(own, coded, shared):
         beside = adjacent(coded)
-        partner = swap(coded, "snp", 1)
+        partner = swap(shared, "snp", 1)
         cross = crossing(give(1, own, coded, partner), 1)
         same = crossing(give(0, own, coded, beside), 0)
         (z,) = call(
@@ -307,12 +328,12 @@
         )
         return [z, *partners(z, "samp", 1, 2)]
 
-    first, parts, own, coded = call(
+    first, parts, own, coded, shared = call(
         functools.partial(next_kernel, samples),
-        [(grid, jnp.float32), ((rows, AUX), jnp.float32), own_out, coded_out],
-        wide, *window(own, coded), start, scaled,
+        [(grid, jnp.float32), ((rows, AUX), jnp.float32), own_out, coded_out, shared_out],
+        wide, *window(own, coded, shared), start, turned,
     )
-    zs = window(own, coded)
+    zs = window(own, coded, shared)
     (flat,) = call(collect_kernel, [((8, AUX), jnp.float32)], parts, *zs)
     parts = snp_parts(flat)
     effects, residual = call(

time: 69 us -> 67.3 us (0.975)
  waiting for transfers between devices: 35.9 us -> 33.5 us
  starting transfers between devices: 23.1 us -> 25 us
  local copies, waits for them, and re-layouts: 1.69 us -> 0.11 us
    ppermute x15, waiting for transfers between devices: 15.1 us -> 19.6 us  [swap(): lax.ppermute(value, axis, [(i, i ^ bits) for i in range(lax.axis_size(axi...]
    ppermute x1, waiting for transfers between devices: 3.61 us -> 0.01 us  [shifted(): lax.ppermute(value, 'snp', [(i, (i + 2) % count) for i in range(count)])]
    ppermute x2, waiting for transfers between devices: 9.04 us -> 5.72 us  [adjacent(): return lax.ppermute(value, ('samp', 'snp'), pairs)]
    ppermute x2, starting transfers between devices: 3.36 us -> 1.37 us  [adjacent(): return lax.ppermute(value, ('samp', 'snp'), pairs)]
    ppermute x4, starting transfers between devices: 1.33 us -> 3.11 us  [crossing(): return lax.ppermute(value, 'snp', pairs)]
    unnamed x6 -> x8, local copies, waits for them, and re-layouts: 1.59 us -> 0.02 us
    ppermute x15, starting transfers between devices: 16.3 us -> 17.5 us  [swap(): lax.ppermute(value, axis, [(i, i ^ bits) for i in range(lax.axis_size(axi...]
    ppermute x1, starting transfers between devices: 2.09 us -> 3.02 us  [shifted(): lax.ppermute(value, 'snp', [(i, (i + 2) % count) for i in range(count)])]
  transfers between devices with their start and end apart: 22 -> 22, of which waited for: 16 -> 20; matrix products, arithmetic and copies ran while one was open for 0% -> 0% of each run, Pallas kernels for 1% -> 2%
where the time goes in v9:
time: 67.3 us; the launch traced here: 67.1 us
  waiting for transfers between devices  33.5 us (50%)
  starting transfers between devices  25 us (37%)
  Pallas kernels  7.08 us (11%)
  between operations  1.4 us (2%)
    ppermute x15, waiting for transfers between devices, swap(): lax.ppermute(value, axis, [(i, i ^ bits) for i in range(lax.axis_size(axi...  19.6 us
    ppermute x15, starting transfers between devices, swap(): lax.ppermute(value, axis, [(i, i ^ bits) for i in range(lax.axis_size(axi...  17.5 us
    ppermute x4, waiting for transfers between devices, crossing(): return lax.ppermute(value, 'snp', pairs)  8.13 us
    pallas_call x11, Pallas kernels, call(): pl.pallas_call(body, out_shape=outs, in_specs=specs, out_specs=[pl.BlockS...  6.47 us
    ppermute x2, waiting for transfers between devices, adjacent(): return lax.ppermute(value, ('samp', 'snp'), pairs)  5.72 us
    ppermute x4, starting transfers between devices, crossing(): return lax.ppermute(value, 'snp', pairs)  3.11 us
    ppermute x1, starting transfers between devices, shifted(): lax.ppermute(value, 'snp', [(i, (i + 2) % count) for i in range(count)])  3.02 us
    ppermute x2, starting transfers between devices, adjacent(): return lax.ppermute(value, ('samp', 'snp'), pairs)  1.37 us
  transfers between devices with their start and end apart: 22, of which 20 were waited for; matrix products, arithmetic and copies ran while one was open for 0% of the time, Pallas kernels for 2%

profile of v9, /device:TPU:0, one launch (start us, length us, event | category | flops | bytes accessed | tf_op | source)
XLA Modules:
  0.0 67.1 jit_solution(13437340463143388201)
XLA Ops:
  1.3 0.0 copy-start
  1.3 0.6 shard_map.60.wide_ref
  1.9 0.0 copy-start.1
  1.9 3.0 %collective-permute-start.3 = (f32[8,640]{1,0:T(8,128)}, f32[8,640]{1,0:T(8,128)S(1)}, u32[]{:S(2)}, u32[]{:S(2)}) collective-permute-start(f32[8,640]{1,0:T(8,128)} %shard_map.60.wide_ref), channel_id=1, source_target_pairs={{0,2},{1,3},{2,4},{3,5},{4,6},{5,7},{6,0},{7,1},{8,10},{9,11},{10,... | collective-permute-start | bytes 61448 | tf_op jit(solution)/shard_map/ppermute | solution.py:44
  4.9 0.0 copy-done
  4.9 0.4 shard_map.59.s0
  5.3 1.6 %collective-permute-start = (f32[8,512]{1,0:T(8,128)S(1)}, f32[8,512]{1,0:T(8,128)S(1)}, u32[]{:S(2)}, u32[]{:S(2)}) collective-permute-start(f32[8,512]{1,0:T(8,128)S(1)} %shard_map.59.s0), channel_id=1, source_target_pairs={{0,8},{8,0},{16,24},{24,16},{1,9},{9,1},{17,25},{25,17},{2,10},{10... | collective-permute-start | bytes 49160 | tf_op jit(solution)/shard_map/ppermute | solution.py:19
  6.9 1.5 %collective-permute-start.1 = (f32[8,512]{1,0:T(8,128)S(1)}, f32[8,512]{1,0:T(8,128)S(1)}, u32[]{:S(2)}, u32[]{:S(2)}) collective-permute-start(f32[8,512]{1,0:T(8,128)S(1)} %shard_map.59.s0), channel_id=1, source_target_pairs={{0,16},{8,24},{16,0},{24,8},{1,17},{9,25},{17,1},{25,9},{2,18},{10... | collective-permute-start | bytes 49160 | tf_op jit(solution)/shard_map/ppermute | solution.py:19
  8.4 0.5 collective-permute-start.2
  8.9 0.2 collective-permute-done.s1
  9.1 1.5 %collective-permute-done.1.s2 = f32[8,512]{1,0:T(8,128)S(1)} collective-permute-done((f32[8,512]{1,0:T(8,128)S(1)}, f32[8,512]{1,0:T(8,128)S(1)}, u32[]{:S(2)}, u32[]{:S(2)}) %collective-permute-start.1) | collective-permute-done | bytes 16416 | tf_op jit(solution)/shard_map/ppermute | solution.py:19
  10.6 2.4 %collective-permute-done.2.s3 = f32[8,512]{1,0:T(8,128)S(1)} collective-permute-done((f32[8,512]{1,0:T(8,128)S(1)}, f32[8,512]{1,0:T(8,128)S(1)}, u32[]{:S(2)}, u32[]{:S(2)}) %collective-permute-start.2) | collective-permute-done | bytes 16416 | tf_op jit(solution)/shard_map/ppermute | solution.py:19
  13.0 0.0 collective-permute-done.3.near_ref
  13.0 0.0 copy-done.1
  13.0 0.0 copy-done.2
  13.0 1.1 %shard_map.61 = (bf16[2048,512]{1,0:T(8,128)(2,1)S(1)}, bf16[512,2048]{1,0:T(8,128)(2,1)S(1)}, f32[64,2048]{1,0:T(8,128)S(1)}, s16[64,2176]{1,0:T(8,128)(2,1)S(1)}, s16[64,2144]{1,0:T(8,128)(2,1)S(1)}) custom-call(f32[8,640]{1,0:T(8,128)S(1)} %copy-done.2, f32[8,512]{1,0:T(8,128)S(1)} %shard_map.59.s0, f32[8,512]{1,0:T(8,128)S(1)} %collective-permute-done.s1, ...), custom_call_target="tpu_custom_call" | custom-call | tf_op jit(solution)/shard_map/pallas_call | solution.py:59
  14.1 0.6 collective-permute-start.5
  14.7 1.2 %collective-permute-start.4 = (s16[64,2144]{1,0:T(8,128)(2,1)S(1)}, s16[64,2144]{1,0:T(8,128)(2,1)S(1)}, u32[]{:S(2)}, u32[]{:S(2)}) collective-permute-start(s16[64,2144]{1,0:T(8,128)(2,1)S(1)} %get-tuple-element.25), channel_id=1, source_target_pairs={{0,1},{1,0},{2,3},{3,2},{4,5},{5,4},{6,7},{7,6},{8,9},{9,8},{10,11... | collective-permute-start | bytes 823304 | tf_op jit(solution)/shard_map/ppermute | solution.py:19
  15.9 1.2 %collective-permute-done.4.other_ref.partner_ref = s16[64,2144]{1,0:T(8,128)(2,1)S(1)} collective-permute-done((s16[64,2144]{1,0:T(8,128)(2,1)S(1)}, s16[64,2144]{1,0:T(8,128)(2,1)S(1)}, u32[]{:S(2)}, u32[]{:S(2)}) %collective-permute-start.4) | collective-permute-done | bytes 274464 | tf_op jit(solution)/shard_map/ppermute | solution.py:19
  17.1 0.3 shard_map.63
  17.3 0.4 collective-permute-start.7
  17.7 3.0 %collective-permute-done.5.other_ref.next_ref = s16[64,2176]{1,0:T(8,128)(2,1)S(1)} collective-permute-done((s16[64,2176]{1,0:T(8,128)(2,1)S(1)}, s16[64,2176]{1,0:T(8,128)(2,1)S(1)}, u32[]{:S(2)}, u32[]{:S(2)}) %collective-permute-start.5) | collective-permute-done | bytes 278560 | tf_op jit(solution)/shard_map/ppermute | solution.py:39
  20.7 0.3 shard_map.62
  21.0 1.0 %collective-permute-start.6 = (s16[64,2176]{1,0:T(8,128)(2,1)S(1)}, s16[64,2176]{1,0:T(8,128)(2,1)S(1)}, u32[]{:S(2)}, u32[]{:S(2)}) collective-permute-start(s16[64,2176]{1,0:T(8,128)(2,1)S(1)} %shard_map.62), channel_id=1, source_target_pairs={{0,2},{1,0},{2,4},{3,1},{4,6},{5,3},{6,7},{7,5},{8,10},{9,8},{10,1... | collective-permute-start | bytes 835592 | tf_op jit(solution)/shard_map/ppermute | solution.py:28
  22.0 2.4 %collective-permute-done.7.cross_ref = s16[64,2176]{1,0:T(8,128)(2,1)S(1)} collective-permute-done((s16[64,2176]{1,0:T(8,128)(2,1)S(1)}, s16[64,2176]{1,0:T(8,128)(2,1)S(1)}, u32[]{:S(2)}, u32[]{:S(2)}) %collective-permute-start.7) | collective-permute-done | bytes 278560 | tf_op jit(solution)/shard_map/ppermute | solution.py:28
  24.5 1.6 %collective-permute-done.6.same_ref = s16[64,2176]{1,0:T(8,128)(2,1)S(1)} collective-permute-done((s16[64,2176]{1,0:T(8,128)(2,1)S(1)}, s16[64,2176]{1,0:T(8,128)(2,1)S(1)}, u32[]{:S(2)}, u32[]{:S(2)}) %collective-permute-start.6) | collective-permute-done | bytes 278560 | tf_op jit(solution)/shard_map/ppermute | solution.py:28
  26.1 0.9 %shard_map.64.z0 = s16[64,640]{1,0:T(8,128)(2,1)S(1)} custom-call(f32[64,2048]{1,0:T(8,128)S(1)} %get-tuple-element.23.own_ref, s16[64,2176]{1,0:T(8,128)(2,1)S(1)} %get-tuple-element.24.coded_ref, s16[64,2144]{1,0:T(8,128)(2,1)S(1)} %collective-permute-done.4.other_ref.partner_ref, s16[64,2176]{1,0:T(8,128)(2,1)S(1)} %collective-permute-done.5.other_ref.next_ref, ...), custom_call_target="tpu_custom_call" | custom-call | tf_op jit(solution)/shard_map/pallas_call | solution.py:59
  27.0 0.5 collective-permute-start.10
  27.6 1.5 %collective-permute-start.8 = (s16[64,640]{1,0:T(8,128)(2,1)S(1)}, s16[64,640]{1,0:T(8,128)(2,1)S(1)}, u32[]{:S(2)}, u32[]{:S(2)}) collective-permute-start(s16[64,640]{1,0:T(8,128)(2,1)S(1)} %shard_map.64.z0), channel_id=1, source_target_pairs={{0,8},{8,0},{16,24},{24,16},{1,9},{9,1},{17,25},{25,17},{2,10},{10... | collective-permute-start | bytes 245768 | tf_op jit(solution)/shard_map/ppermute | solution.py:19
  29.0 1.5 %collective-permute-start.9 = (s16[64,640]{1,0:T(8,128)(2,1)S(1)}, s16[64,640]{1,0:T(8,128)(2,1)S(1)}, u32[]{:S(2)}, u32[]{:S(2)}) collective-permute-start(s16[64,640]{1,0:T(8,128)(2,1)S(1)} %shard_map.64.z0), channel_id=1, source_target_pairs={{0,16},{8,24},{16,0},{24,8},{1,17},{9,25},{17,1},{25,9},{2,18},{10... | collective-permute-start | bytes 245768 | tf_op jit(solution)/shard_map/ppermute | solution.py:19
  30.6 2.6 %collective-permute-done.10.z3 = s16[64,640]{1,0:T(8,128)(2,1)S(1)} collective-permute-done((s16[64,640]{1,0:T(8,128)(2,1)S(1)}, s16[64,640]{1,0:T(8,128)(2,1)S(1)}, u32[]{:S(2)}, u32[]{:S(2)}) %collective-permute-start.10) | collective-permute-done | bytes 81952 | tf_op jit(solution)/shard_map/ppermute | solution.py:19
  33.2 0.5 collective-permute-done.8.z1
  33.7 1.0 %collective-permute-done.9.z2 = s16[64,640]{1,0:T(8,128)(2,1)S(1)} collective-permute-done((s16[64,640]{1,0:T(8,128)(2,1)S(1)}, s16[64,640]{1,0:T(8,128)(2,1)S(1)}, u32[]{:S(2)}, u32[]{:S(2)}) %collective-permute-start.9) | collective-permute-done | bytes 81952 | tf_op jit(solution)/shard_map/ppermute | solution.py:19
  34.7 0.7 shard_map.65
  35.4 0.8 %collective-permute-start.12 = (s16[64,2176]{1,0:T(8,128)(2,1)S(1)}, s16[64,2176]{1,0:T(8,128)(2,1)S(1)}, u32[]{:S(2)}, u32[]{:S(2)}) collective-permute-start(s16[64,2176]{1,0:T(8,128)(2,1)S(1)} %get-tuple-element.31.coded_ref), channel_id=1, source_target_pairs={{0,8},{1,2},{2,1},{3,4},{4,3},{5,6},{6,5},{7,15},{8,0},{9,10},{10,... | collective-permute-start | bytes 835592 | tf_op jit(solution)/shard_map/ppermute | solution.py:39
  36.1 1.3 %collective-permute-start.11 = (s16[64,2144]{1,0:T(8,128)(2,1)S(1)}, s16[64,2144]{1,0:T(8,128)(2,1)S(1)}, u32[]{:S(2)}, u32[]{:S(2)}) collective-permute-start(s16[64,2144]{1,0:T(8,128)(2,1)S(1)} %get-tuple-element.32), channel_id=1, source_target_pairs={{0,1},{1,0},{2,3},{3,2},{4,5},{5,4},{6,7},{7,6},{8,9},{9,8},{10,11... | collective-permute-start | bytes 823304 | tf_op jit(solution)/shard_map/ppermute | solution.py:19
  37.4 1.2 %collective-permute-done.11.other_ref.partner_ref = s16[64,2144]{1,0:T(8,128)(2,1)S(1)} collective-permute-done((s16[64,2144]{1,0:T(8,128)(2,1)S(1)}, s16[64,2144]{1,0:T(8,128)(2,1)S(1)}, u32[]{:S(2)}, u32[]{:S(2)}) %collective-permute-start.11) | collective-permute-done | bytes 274464 | tf_op jit(solution)/shard_map/ppermute | solution.py:19
  38.6 0.3 shard_map.67
  38.9 0.4 collective-permute-start.14
  39.3 2.7 %collective-permute-done.12.other_ref.next_ref = s16[64,2176]{1,0:T(8,128)(2,1)S(1)} collective-permute-done((s16[64,2176]{1,0:T(8,128)(2,1)S(1)}, s16[64,2176]{1,0:T(8,128)(2,1)S(1)}, u32[]{:S(2)}, u32[]{:S(2)}) %collective-permute-start.12) | collective-permute-done | bytes 278560 | tf_op jit(solution)/shard_map/ppermute | solution.py:39
  42.0 0.3 shard_map.66
  42.2 0.0 copy-start.3
  42.3 1.3 %collective-permute-start.13 = (s16[64,2176]{1,0:T(8,128)(2,1)S(1)}, s16[64,2176]{1,0:T(8,128)(2,1)S(1)}, u32[]{:S(2)}, u32[]{:S(2)}) collective-permute-start(s16[64,2176]{1,0:T(8,128)(2,1)S(1)} %shard_map.66), channel_id=1, source_target_pairs={{0,2},{1,0},{2,4},{3,1},{4,6},{5,3},{6,7},{7,5},{8,10},{9,8},{10,1... | collective-permute-start | bytes 835592 | tf_op jit(solution)/shard_map/ppermute | solution.py:28
  43.6 2.4 %collective-permute-done.14.cross_ref = s16[64,2176]{1,0:T(8,128)(2,1)S(1)} collective-permute-done((s16[64,2176]{1,0:T(8,128)(2,1)S(1)}, s16[64,2176]{1,0:T(8,128)(2,1)S(1)}, u32[]{:S(2)}, u32[]{:S(2)}) %collective-permute-start.14) | collective-permute-done | bytes 278560 | tf_op jit(solution)/shard_map/ppermute | solution.py:28
  46.0 1.6 %collective-permute-done.13.same_ref = s16[64,2176]{1,0:T(8,128)(2,1)S(1)} collective-permute-done((s16[64,2176]{1,0:T(8,128)(2,1)S(1)}, s16[64,2176]{1,0:T(8,128)(2,1)S(1)}, u32[]{:S(2)}, u32[]{:S(2)}) %collective-permute-start.13) | collective-permute-done | bytes 278560 | tf_op jit(solution)/shard_map/ppermute | solution.py:28
  47.6 0.9 %shard_map.68.z0 = s16[64,640]{1,0:T(8,128)(2,1)S(1)} custom-call(f32[64,2048]{1,0:T(8,128)S(1)} %get-tuple-element.30.own_ref, s16[64,2176]{1,0:T(8,128)(2,1)S(1)} %get-tuple-element.31.coded_ref, s16[64,2144]{1,0:T(8,128)(2,1)S(1)} %collective-permute-done.11.other_ref.partner_ref, s16[64,2176]{1,0:T(8,128)(2,1)S(1)} %collective-permute-done.12.other_ref.next_ref, ...), custom_call_target="tpu_custom_call" | custom-call | tf_op jit(solution)/shard_map/pallas_call | solution.py:59
  48.6 0.6 collective-permute-start.15
  49.2 0.9 %collective-permute-start.16 = (s16[64,640]{1,0:T(8,128)(2,1)S(1)}, s16[64,640]{1,0:T(8,128)(2,1)S(1)}, u32[]{:S(2)}, u32[]{:S(2)}) collective-permute-start(s16[64,640]{1,0:T(8,128)(2,1)S(1)} %shard_map.68.z0), channel_id=1, source_target_pairs={{0,16},{8,24},{16,0},{24,8},{1,17},{9,25},{17,1},{25,9},{2,18},{10... | collective-permute-start | bytes 245768 | tf_op jit(solution)/shard_map/ppermute | solution.py:19
  50.1 2.0 %collective-permute-start.17 = (s16[64,640]{1,0:T(8,128)(2,1)S(1)}, s16[64,640]{1,0:T(8,128)(2,1)S(1)}, u32[]{:S(2)}, u32[]{:S(2)}) collective-permute-start(s16[64,640]{1,0:T(8,128)(2,1)S(1)} %shard_map.68.z0), channel_id=1, source_target_pairs={{0,24},{8,16},{16,8},{24,0},{1,25},{9,17},{17,9},{25,1},{2,26},{10... | collective-permute-start | bytes 245768 | tf_op jit(solution)/shard_map/ppermute | solution.py:19
  52.1 1.7 %collective-permute-done.15.z1 = s16[64,640]{1,0:T(8,128)(2,1)S(1)} collective-permute-done((s16[64,640]{1,0:T(8,128)(2,1)S(1)}, s16[64,640]{1,0:T(8,128)(2,1)S(1)}, u32[]{:S(2)}, u32[]{:S(2)}) %collective-permute-start.15) | collective-permute-done | bytes 81952 | tf_op jit(solution)/shard_map/ppermute | solution.py:19
  53.8 0.2 collective-permute-done.16.z2
  54.0 1.7 %collective-permute-done.17.z3 = s16[64,640]{1,0:T(8,128)(2,1)S(1)} collective-permute-done((s16[64,640]{1,0:T(8,128)(2,1)S(1)}, s16[64,640]{1,0:T(8,128)(2,1)S(1)}, u32[]{:S(2)}, u32[]{:S(2)}) %collective-permute-start.17) | collective-permute-done | bytes 81952 | tf_op jit(solution)/shard_map/ppermute | solution.py:19
  55.7 0.3 shard_map.69
  56.0 0.0 collective-permute-start.18
  56.0 1.2 %collective-permute-done.18 = f32[8,128]{1,0:T(8,128)S(1)} collective-permute-done((f32[8,128]{1,0:T(8,128)S(1)}, f32[8,128]{1,0:T(8,128)S(1)}, u32[]{:S(2)}, u32[]{:S(2)}) %collective-permute-start.18) | collective-permute-done | bytes 4128 | tf_op jit(solution)/shard_map/ppermute | solution.py:19
  57.1 2.0 %collective-permute-start.19 = (f32[8,128]{1,0:T(8,128)S(1)}, f32[8,128]{1,0:T(8,128)S(1)}, u32[]{:S(2)}, u32[]{:S(2)}) collective-permute-start(f32[8,128]{1,0:T(8,128)S(1)} %add.3.p0), channel_id=1, source_target_pairs={{0,3},{1,2},{2,1},{3,0},{4,7},{5,6},{6,5},{7,4},{8,11},{9,10},{10,... | collective-permute-start | bytes 12296 | tf_op jit(solution)/shard_map/ppermute | solution.py:19
  59.1 1.9 %collective-permute-start.20 = (f32[8,128]{1,0:T(8,128)S(1)}, f32[8,128]{1,0:T(8,128)S(1)}, u32[]{:S(2)}, u32[]{:S(2)}) collective-permute-start(f32[8,128]{1,0:T(8,128)S(1)} %add.3.p0), channel_id=1, source_target_pairs={{0,5},{1,4},{2,7},{3,6},{4,1},{5,0},{6,3},{7,2},{8,13},{9,12},{10,... | collective-permute-start | bytes 12296 | tf_op jit(solution)/shard_map/ppermute | solution.py:19
  61.0 0.5 collective-permute-start.21
  61.5 0.0 copy-done.3
  61.5 0.1 copy.6.shrink_ref
  61.6 0.0 collective-permute-done.19.p1
  61.6 1.4 %collective-permute-done.20.p2 = f32[8,128]{1,0:T(8,128)S(1)} collective-permute-done((f32[8,128]{1,0:T(8,128)S(1)}, f32[8,128]{1,0:T(8,128)S(1)}, u32[]{:S(2)}, u32[]{:S(2)}) %collective-permute-start.20) | collective-permute-done | bytes 4128 | tf_op jit(solution)/shard_map/ppermute | solution.py:19
  63.0 2.8 %collective-permute-done.21.p3 = f32[8,128]{1,0:T(8,128)S(1)} collective-permute-done((f32[8,128]{1,0:T(8,128)S(1)}, f32[8,128]{1,0:T(8,128)S(1)}, u32[]{:S(2)}, u32[]{:S(2)}) %collective-permute-start.21) | collective-permute-done | bytes 4128 | tf_op jit(solution)/shard_map/ppermute | solution.py:19
  65.9 1.2 %shard_map.70 = (f32[64,512]{1,0:T(8,128)}, f32[64,512]{1,0:T(8,128)}) custom-call(f32[64,1]{1,0:T(8,128)S(1)} %copy.6.shrink_ref, f32[8,128]{1,0:T(8,128)S(1)} %add.3.p0, f32[8,128]{1,0:T(8,128)S(1)} %collective-permute-done.19.p1, f32[8,128]{1,0:T(8,128)S(1)} %collective-permute-done.20.p2, f32[8,128]{1,0:T(8,128)S(1)} %collective-permute-done.21.p3, ...), custom_call_target="tpu_custom_call" | custom-call | tf_op jit(solution)/shard_map/pallas_call | solution.py:59
  (2 shorter events, 0.0 us)
Async XLA Ops:
  1.3 3.7 %copy-start = (bf16[2048,512]{1,0:T(8,128)(2,1)S(1)}, bf16[2048,512]{1,0:T(8,128)(2,1)}, u32[]{:S(2)}) copy-start(bf16[2048,512]{1,0:T(8,128)(2,1)} %dosage_ref.3) | copy-start | bytes 6291460
  1.9 11.1 %copy-start.1 = (f32[512,64]{0,1:T(8,128)S(1)}, f32[512,64]{0,1:T(8,128)}, u32[]{:S(2)}) copy-start(f32[512,64]{0,1:T(8,128)} %param.6) | copy-start | bytes 393220
  1.9 11.1 %copy-start.2 = (f32[8,640]{1,0:T(8,128)S(1)}, f32[8,640]{1,0:T(8,128)}, u32[]{:S(2)}) copy-start(f32[8,640]{1,0:T(8,128)} %shard_map.60.wide_ref) | copy-start | bytes 61444
  1.9 11.1 %collective-permute-start.3 = (f32[8,640]{1,0:T(8,128)}, f32[8,640]{1,0:T(8,128)S(1)}, u32[]{:S(2)}, u32[]{:S(2)}) collective-permute-start(f32[8,640]{1,0:T(8,128)} %shard_map.60.wide_ref), channel_id=1, source_target_pairs={{0,2},{1,3},{2,4},{3,5},{4,6},{5,7},{6,0},{7,1},{8,10},{9,11},{10,... | collective-permute-start | bytes 61448 | tf_op jit(solution)/shard_map/ppermute | solution.py:44
  5.3 3.8 %collective-permute-start = (f32[8,512]{1,0:T(8,128)S(1)}, f32[8,512]{1,0:T(8,128)S(1)}, u32[]{:S(2)}, u32[]{:S(2)}) collective-permute-start(f32[8,512]{1,0:T(8,128)S(1)} %shard_map.59.s0), channel_id=1, source_target_pairs={{0,8},{8,0},{16,24},{24,16},{1,9},{9,1},{17,25},{25,17},{2,10},{10... | collective-permute-start | bytes 49160 | tf_op jit(solution)/shard_map/ppermute | solution.py:19
  6.9 3.7 %collective-permute-start.1 = (f32[8,512]{1,0:T(8,128)S(1)}, f32[8,512]{1,0:T(8,128)S(1)}, u32[]{:S(2)}, u32[]{:S(2)}) collective-permute-start(f32[8,512]{1,0:T(8,128)S(1)} %shard_map.59.s0), channel_id=1, source_target_pairs={{0,16},{8,24},{16,0},{24,8},{1,17},{9,25},{17,1},{25,9},{2,18},{10... | collective-permute-start | bytes 49160 | tf_op jit(solution)/shard_map/ppermute | solution.py:19
  8.4 4.6 %collective-permute-start.2 = (f32[8,512]{1,0:T(8,128)S(1)}, f32[8,512]{1,0:T(8,128)S(1)}, u32[]{:S(2)}, u32[]{:S(2)}) collective-permute-start(f32[8,512]{1,0:T(8,128)S(1)} %shard_map.59.s0), channel_id=1, source_target_pairs={{0,24},{8,16},{16,8},{24,0},{1,25},{9,17},{17,9},{25,1},{2,26},{10... | collective-permute-start | bytes 49160 | tf_op jit(solution)/shard_map/ppermute | solution.py:19
  14.1 6.6 %collective-permute-start.5 = (s16[64,2176]{1,0:T(8,128)(2,1)S(1)}, s16[64,2176]{1,0:T(8,128)(2,1)S(1)}, u32[]{:S(2)}, u32[]{:S(2)}) collective-permute-start(s16[64,2176]{1,0:T(8,128)(2,1)S(1)} %get-tuple-element.24.coded_ref), channel_id=1, source_target_pairs={{0,8},{1,2},{2,1},{3,4},{4,3},{5,6},{6,5},{7,15},{8,0},{9,10},{10,... | collective-permute-start | bytes 835592 | tf_op jit(solution)/shard_map/ppermute | solution.py:39
  14.7 2.3 %collective-permute-start.4 = (s16[64,2144]{1,0:T(8,128)(2,1)S(1)}, s16[64,2144]{1,0:T(8,128)(2,1)S(1)}, u32[]{:S(2)}, u32[]{:S(2)}) collective-permute-start(s16[64,2144]{1,0:T(8,128)(2,1)S(1)} %get-tuple-element.25), channel_id=1, source_target_pairs={{0,1},{1,0},{2,3},{3,2},{4,5},{5,4},{6,7},{7,6},{8,9},{9,8},{10,11... | collective-permute-start | bytes 823304 | tf_op jit(solution)/shard_map/ppermute | solution.py:19
  17.3 7.1 %collective-permute-start.7 = (s16[64,2176]{1,0:T(8,128)(2,1)S(1)}, s16[64,2176]{1,0:T(8,128)(2,1)S(1)}, u32[]{:S(2)}, u32[]{:S(2)}) collective-permute-start(s16[64,2176]{1,0:T(8,128)(2,1)S(1)} %shard_map.63), channel_id=1, source_target_pairs={{0,1},{1,3},{2,0},{3,5},{4,2},{5,7},{6,4},{7,6},{8,9},{9,11},{10,8... | collective-permute-start | bytes 835592 | tf_op jit(solution)/shard_map/ppermute | solution.py:28
  21.0 5.1 %collective-permute-start.6 = (s16[64,2176]{1,0:T(8,128)(2,1)S(1)}, s16[64,2176]{1,0:T(8,128)(2,1)S(1)}, u32[]{:S(2)}, u32[]{:S(2)}) collective-permute-start(s16[64,2176]{1,0:T(8,128)(2,1)S(1)} %shard_map.62), channel_id=1, source_target_pairs={{0,2},{1,0},{2,4},{3,1},{4,6},{5,3},{6,7},{7,5},{8,10},{9,8},{10,1... | collective-permute-start | bytes 835592 | tf_op jit(solution)/shard_map/ppermute | solution.py:28
  27.0 6.2 %collective-permute-start.10 = (s16[64,640]{1,0:T(8,128)(2,1)S(1)}, s16[64,640]{1,0:T(8,128)(2,1)S(1)}, u32[]{:S(2)}, u32[]{:S(2)}) collective-permute-start(s16[64,640]{1,0:T(8,128)(2,1)S(1)} %shard_map.64.z0), channel_id=1, source_target_pairs={{0,24},{8,16},{16,8},{24,0},{1,25},{9,17},{17,9},{25,1},{2,26},{10... | collective-permute-start | bytes 245768 | tf_op jit(solution)/shard_map/ppermute | solution.py:19
  27.6 6.2 %collective-permute-start.8 = (s16[64,640]{1,0:T(8,128)(2,1)S(1)}, s16[64,640]{1,0:T(8,128)(2,1)S(1)}, u32[]{:S(2)}, u32[]{:S(2)}) collective-permute-start(s16[64,640]{1,0:T(8,128)(2,1)S(1)} %shard_map.64.z0), channel_id=1, source_target_pairs={{0,8},{8,0},{16,24},{24,16},{1,9},{9,1},{17,25},{25,17},{2,10},{10... | collective-permute-start | bytes 245768 | tf_op jit(solution)/shard_map/ppermute | solution.py:19
  29.0 5.6 %collective-permute-start.9 = (s16[64,640]{1,0:T(8,128)(2,1)S(1)}, s16[64,640]{1,0:T(8,128)(2,1)S(1)}, u32[]{:S(2)}, u32[]{:S(2)}) collective-permute-start(s16[64,640]{1,0:T(8,128)(2,1)S(1)} %shard_map.64.z0), channel_id=1, source_target_pairs={{0,16},{8,24},{16,0},{24,8},{1,17},{9,25},{17,1},{25,9},{2,18},{10... | collective-permute-start | bytes 245768 | tf_op jit(solution)/shard_map/ppermute | solution.py:19
  35.4 6.6 %collective-permute-start.12 = (s16[64,2176]{1,0:T(8,128)(2,1)S(1)}, s16[64,2176]{1,0:T(8,128)(2,1)S(1)}, u32[]{:S(2)}, u32[]{:S(2)}) collective-permute-start(s16[64,2176]{1,0:T(8,128)(2,1)S(1)} %get-tuple-element.31.coded_ref), channel_id=1, source_target_pairs={{0,8},{1,2},{2,1},{3,4},{4,3},{5,6},{6,5},{7,15},{8,0},{9,10},{10,... | collective-permute-start | bytes 835592 | tf_op jit(solution)/shard_map/ppermute | solution.py:39
  36.1 2.5 %collective-permute-start.11 = (s16[64,2144]{1,0:T(8,128)(2,1)S(1)}, s16[64,2144]{1,0:T(8,128)(2,1)S(1)}, u32[]{:S(2)}, u32[]{:S(2)}) collective-permute-start(s16[64,2144]{1,0:T(8,128)(2,1)S(1)} %get-tuple-element.32), channel_id=1, source_target_pairs={{0,1},{1,0},{2,3},{3,2},{4,5},{5,4},{6,7},{7,6},{8,9},{9,8},{10,11... | collective-permute-start | bytes 823304 | tf_op jit(solution)/shard_map/ppermute | solution.py:19
  38.9 7.1 %collective-permute-start.14 = (s16[64,2176]{1,0:T(8,128)(2,1)S(1)}, s16[64,2176]{1,0:T(8,128)(2,1)S(1)}, u32[]{:S(2)}, u32[]{:S(2)}) collective-permute-start(s16[64,2176]{1,0:T(8,128)(2,1)S(1)} %shard_map.67), channel_id=1, source_target_pairs={{0,1},{1,3},{2,0},{3,5},{4,2},{5,7},{6,4},{7,6},{8,9},{9,11},{10,8... | collective-permute-start | bytes 835592 | tf_op jit(solution)/shard_map/ppermute | solution.py:28
  42.2 19.3 %copy-start.3 = (f32[64]{0:T(128)S(1)}, f32[64]{0:T(128)}, u32[]{:S(2)}) copy-start(f32[64]{0:T(128)} %param.7) | copy-start | bytes 772
  42.3 5.4 %collective-permute-start.13 = (s16[64,2176]{1,0:T(8,128)(2,1)S(1)}, s16[64,2176]{1,0:T(8,128)(2,1)S(1)}, u32[]{:S(2)}, u32[]{:S(2)}) collective-permute-start(s16[64,2176]{1,0:T(8,128)(2,1)S(1)} %shard_map.66), channel_id=1, source_target_pairs={{0,2},{1,0},{2,4},{3,1},{4,6},{5,3},{6,7},{7,5},{8,10},{9,8},{10,1... | collective-permute-start | bytes 835592 | tf_op jit(solution)/shard_map/ppermute | solution.py:28
  48.6 5.3 %collective-permute-start.15 = (s16[64,640]{1,0:T(8,128)(2,1)S(1)}, s16[64,640]{1,0:T(8,128)(2,1)S(1)}, u32[]{:S(2)}, u32[]{:S(2)}) collective-permute-start(s16[64,640]{1,0:T(8,128)(2,1)S(1)} %shard_map.68.z0), channel_id=1, source_target_pairs={{0,8},{8,0},{16,24},{24,16},{1,9},{9,1},{17,25},{25,17},{2,10},{10... | collective-permute-start | bytes 245768 | tf_op jit(solution)/shard_map/ppermute | solution.py:19
  49.2 4.8 %collective-permute-start.16 = (s16[64,640]{1,0:T(8,128)(2,1)S(1)}, s16[64,640]{1,0:T(8,128)(2,1)S(1)}, u32[]{:S(2)}, u32[]{:S(2)}) collective-permute-start(s16[64,640]{1,0:T(8,128)(2,1)S(1)} %shard_map.68.z0), channel_id=1, source_target_pairs={{0,16},{8,24},{16,0},{24,8},{1,17},{9,25},{17,1},{25,9},{2,18},{10... | collective-permute-start | bytes 245768 | tf_op jit(solution)/shard_map/ppermute | solution.py:19
  50.1 5.6 %collective-permute-start.17 = (s16[64,640]{1,0:T(8,128)(2,1)S(1)}, s16[64,640]{1,0:T(8,128)(2,1)S(1)}, u32[]{:S(2)}, u32[]{:S(2)}) collective-permute-start(s16[64,640]{1,0:T(8,128)(2,1)S(1)} %shard_map.68.z0), channel_id=1, source_target_pairs={{0,24},{8,16},{16,8},{24,0},{1,25},{9,17},{17,9},{25,1},{2,26},{10... | collective-permute-start | bytes 245768 | tf_op jit(solution)/shard_map/ppermute | solution.py:19
  56.0 1.2 %collective-permute-start.18 = (f32[8,128]{1,0:T(8,128)S(1)}, f32[8,128]{1,0:T(8,128)S(1)}, u32[]{:S(2)}, u32[]{:S(2)}) collective-permute-start(f32[8,128]{1,0:T(8,128)S(1)} %shard_map.69), channel_id=1, source_target_pairs={{0,1},{1,0},{2,3},{3,2},{4,5},{5,4},{6,7},{7,6},{8,9},{9,8},{10,11... | collective-permute-start | bytes 12296 | tf_op jit(solution)/shard_map/ppermute | solution.py:19
  57.1 4.5 %collective-permute-start.19 = (f32[8,128]{1,0:T(8,128)S(1)}, f32[8,128]{1,0:T(8,128)S(1)}, u32[]{:S(2)}, u32[]{:S(2)}) collective-permute-start(f32[8,128]{1,0:T(8,128)S(1)} %add.3.p0), channel_id=1, source_target_pairs={{0,3},{1,2},{2,1},{3,0},{4,7},{5,6},{6,5},{7,4},{8,11},{9,10},{10,... | collective-permute-start | bytes 12296 | tf_op jit(solution)/shard_map/ppermute | solution.py:19
  59.1 3.9 %collective-permute-start.20 = (f32[8,128]{1,0:T(8,128)S(1)}, f32[8,128]{1,0:T(8,128)S(1)}, u32[]{:S(2)}, u32[]{:S(2)}) collective-permute-start(f32[8,128]{1,0:T(8,128)S(1)} %add.3.p0), channel_id=1, source_target_pairs={{0,5},{1,4},{2,7},{3,6},{4,1},{5,0},{6,3},{7,2},{8,13},{9,12},{10,... | collective-permute-start | bytes 12296 | tf_op jit(solution)/shard_map/ppermute | solution.py:19
  61.0 4.8 %collective-permute-start.21 = (f32[8,128]{1,0:T(8,128)S(1)}, f32[8,128]{1,0:T(8,128)S(1)}, u32[]{:S(2)}, u32[]{:S(2)}) collective-permute-start(f32[8,128]{1,0:T(8,128)S(1)} %add.3.p0), channel_id=1, source_target_pairs={{0,7},{1,6},{2,5},{3,4},{4,3},{5,2},{6,1},{7,0},{8,15},{9,14},{10,... | collective-permute-start | bytes 12296 | tf_op jit(solution)/shard_map/ppermute | solution.py:19

commit v10 on v9

--- a/solution.py
+++ b/solution.py
@@ -75,7 +75,7 @@
     wide_ref[...] = jnp.full(wide_ref.shape, width_ref[0].astype(jnp.float32))
 
 
-def stats_kernel(dosage_ref, sums_ref):
+def stats_kernel(dosage_ref, sums_ref, brief_ref):
     acc = jnp.zeros((8, dosage_ref.shape[1]), jnp.float32)
     square = acc
     for k in range(0, dosage_ref.shape[0], ROWS):
@@ -86,7 +86,9 @@
     row = lax.broadcasted_iota(jnp.int32, (8, 1), 0)
     first = jnp.sum(acc, 0, keepdims=True)
     second = jnp.sum(square, 0, keepdims=True)
-    sums_ref[...] = jnp.where(row == 0, first, second)
+    both = jnp.where(row == 0, first, second)
+    sums_ref[...] = both
+    brief_ref[...] = both[:2]
 
 
 def finish(coded_ref, *columns):
@@ -243,29 +245,40 @@
         terms.append((high + low * 2.0**-UNIT) * 2.0 * unit(exponent))
     lane = lax.broadcasted_iota(jnp.int32, parts_ref.shape, 1)
     parts = jnp.where(lane == 3, total(terms), parts_ref[...])
-    filled = jnp.concatenate([parts, jnp.zeros((AUX - parts.shape[0], AUX), jnp.float32)], 0)
+    filled = jnp.concatenate([parts, jnp.ones((AUX - parts.shape[0], AUX), jnp.float32)], 0)
     flat_ref[...] = filled.T[:8]
 
 
 def last_kernel(samples, shrink_ref, p0, p1, p2, p3, z0, z1, z2, z3, start_ref, first_ref, effects_ref, residual_ref):
-    rows = shrink_ref.shape[0]
-    flat = total([p[...] for p in (p0, p1, p2, p3)])
-    parts = jnp.concatenate([flat, jnp.zeros((AUX - 8, AUX), jnp.float32)], 0).T[:rows]
-    bb, bw, ww, wu = (parts[:, k : k + 1] for k in range(4))
+    rows = start_ref.shape[0]
+    flat = total([p[0:4] for p in (p0, p1, p2, p3)])
+    bb, bw, ww, wu = (flat[k : k + 1] for k in range(4))
     shrink = shrink_ref[...]
-    start, first = start_ref[...], first_ref[...]
-    second = total([grid_values(z) for z in (z0, z1, z2, z3)]) / samples
     ratio = bw / bb
     step = 1.0 / (ratio + shrink)
-    norm = step * step * (ww - ratio * bw)
+    square = step * step
+    norm = square * (ww - ratio * bw)
     bend = norm / bb
-    curve = step * step * (ratio * (ratio * bw - 2.0 * ww) + wu) + shrink * norm - bend * norm / step
+    curve = square * (ratio * (ratio * bw - 2.0 * ww) + wu) + shrink * norm - bend * norm * (ratio + shrink)
     step2 = jnp.where(curve > 0, norm / curve, 0.0)
-    rest = step * (ratio * start - first)
-    direction = rest + bend * start
-    image = step * (ratio * first - second) + bend * first + shrink * direction
-    effects_ref[...] = step * start + step2 * direction
-    residual_ref[...] = rest - step2 * image
+    lead = step * ratio + bend
+    coefficients = (
+        step + step2 * lead,
+        -step2 * step,
+        step * ratio - step2 * shrink * lead,
+        -step - step2 * (lead - shrink * step),
+        step2 * step,
+    )
+    row = lax.broadcasted_iota(jnp.int32, (AUX, AUX), 0)
+    table = jnp.zeros((AUX, AUX), jnp.float32)
+    for k, value in enumerate(coefficients):
+        table = jnp.where(row == k, value, table)
+    table = table.T[:rows]
+    e_start, e_first, r_start, r_first, r_second = (table[:, k : k + 1] for k in range(5))
+    start, first = start_ref[...], first_ref[...]
+    effects_ref[...] = e_start * start + e_first * first
+    second = total([grid_values(z) for z in (z0, z1, z2, z3)]) / samples
+    residual_ref[...] = r_start * start + r_first * first + r_second * second
 
 
 def snp_parts(value):
@@ -273,7 +286,7 @@
     value = value + swap(value, "snp", 1)
     bit = 2
     while 4 * bit < count:
-        value = total([value, *others(value, bit)])
+        value = jnp.pad(total([part[:4] for part in (value, *others(value, bit))]), ((0, 4), (0, 0)))
         bit *= 4
     if 2 * bit < count:
         return [value, *others(value, bit)]
@@ -281,7 +294,7 @@
 
 
 def others(value, bit):
-    return [swap(value, "snp", k ^ 1) for k in (bit, 2 * bit, 3 * bit)]
+    return [swap(value[:rows], "snp", k ^ 1) for k, rows in ((bit, 4), (2 * bit, 6), (3 * bit, 8))]
 
 
 def shards(dosage, band_width, marginal, penalty):
@@ -289,15 +302,15 @@
     local, size, rows = dosage.shape[0], dosage.shape[1], marginal.shape[1]
     samples = local * groups
     start = marginal.T
-    shrink = penalty[:, None]
+    shrink = jnp.pad(penalty, (0, AUX - rows), constant_values=1.0)[None]
     grid, own_shape = (rows, size), (rows, local)
     own_out, coded_out = (own_shape, jnp.float32), ((rows, local + AUX), jnp.int16)
     shared_out = ((rows, local + LESS), jnp.int16)
 
     sent_out = ((rows, size + AUX), jnp.int16)
 
-    (sums,) = call(stats_kernel, [((8, size), jnp.float32)], dosage)
-    one, two, three = partners(sums, "samp", 1, 2)
+    sums, brief = call(stats_kernel, [((8, size), jnp.float32), ((2, size), jnp.float32)], dosage)
+    one, two, three = swap(brief, "samp", 1), swap(brief, "samp", 2), swap(sums, "samp", 3)
     one, band_width = lax.optimization_barrier((one, band_width))
     wide = pl.pallas_call(
         wide_kernel,

time: 67.3 us -> 65.6 us (0.975)
  starting transfers between devices: 25 us -> 24.2 us
    ppermute x15, starting transfers between devices: 17.5 us -> 15.5 us  [swap(): lax.ppermute(value, axis, [(i, i ^ bits) for i in range(lax.axis_size(axi...]
    ppermute x2, starting transfers between devices: 1.37 us -> 2.93 us  [adjacent(): return lax.ppermute(value, ('samp', 'snp'), pairs)]
  transfers between devices with their start and end apart: 22 -> 22, of which waited for: 20 -> 18; matrix products, arithmetic and copies ran while one was open for 0% -> 0% of each run, Pallas kernels for 2% -> 2%
where the time goes in v10:
time: 65.6 us; the launch traced here: 65.5 us
  waiting for transfers between devices  33 us (50%)
  starting transfers between devices  24.2 us (37%)
  Pallas kernels  6.79 us (10%)
  between operations  1.4 us (2%)
    ppermute x15, waiting for transfers between devices, swap(): lax.ppermute(value, axis, [(i, i ^ bits) for i in range(lax.axis_size(axi...  19 us
    ppermute x15, starting transfers between devices, swap(): lax.ppermute(value, axis, [(i, i ^ bits) for i in range(lax.axis_size(axi...  15.5 us
    ppermute x4, waiting for transfers between devices, crossing(): return lax.ppermute(value, 'snp', pairs)  8.13 us
    pallas_call x11, Pallas kernels, call(): pl.pallas_call(body, out_shape=outs, in_specs=specs, out_specs=[pl.BlockS...  6.18 us
    ppermute x2, waiting for transfers between devices, adjacent(): return lax.ppermute(value, ('samp', 'snp'), pairs)  5.89 us
    ppermute x1, starting transfers between devices, shifted(): lax.ppermute(value, 'snp', [(i, (i + 2) % count) for i in range(count)])  3.02 us
    ppermute x2, starting transfers between devices, adjacent(): return lax.ppermute(value, ('samp', 'snp'), pairs)  2.93 us
    ppermute x4, starting transfers between devices, crossing(): return lax.ppermute(value, 'snp', pairs)  2.77 us
  transfers between devices with their start and end apart: 22, of which 18 were waited for; matrix products, arithmetic and copies ran while one was open for 0% of the time, Pallas kernels for 2%

profile of v10, /device:TPU:0, one launch (start us, length us, event | category | flops | bytes accessed | tf_op | source)
XLA Modules:
  0.0 65.5 jit_solution(6574414693695112854)
XLA Ops:
  1.3 0.0 copy-start
  1.3 0.6 shard_map.60.wide_ref
  1.9 0.0 copy-start.1
  1.9 0.0 copy-start.2
  1.9 3.0 %collective-permute-start.3 = (f32[8,640]{1,0:T(8,128)}, f32[8,640]{1,0:T(8,128)S(1)}, u32[]{:S(2)}, u32[]{:S(2)}) collective-permute-start(f32[8,640]{1,0:T(8,128)} %shard_map.60.wide_ref), channel_id=1, source_target_pairs={{0,2},{1,3},{2,4},{3,5},{4,6},{5,7},{6,0},{7,1},{8,10},{9,11},{10,... | collective-permute-start | bytes 61448 | tf_op jit(solution)/shard_map/ppermute | solution.py:44
  4.9 0.0 copy-done
  4.9 0.4 shard_map.59
  5.3 2.5 %collective-permute-start.2 = (f32[8,512]{1,0:T(8,128)S(1)}, f32[8,512]{1,0:T(8,128)S(1)}, u32[]{:S(2)}, u32[]{:S(2)}) collective-permute-start(f32[8,512]{1,0:T(8,128)S(1)} %get-tuple-element.23.s0), channel_id=1, source_target_pairs={{0,24},{8,16},{16,8},{24,0},{1,25},{9,17},{17,9},{25,1},{2,26},{10... | collective-permute-start | bytes 49160 | tf_op jit(solution)/shard_map/ppermute | solution.py:19
  7.8 0.5 collective-permute-start
  8.4 0.5 collective-permute-start.1
  8.9 2.6 %collective-permute-done.s1 = f32[2,512]{1,0:T(2,128)S(1)} collective-permute-done((f32[2,512]{1,0:T(2,128)S(1)}, f32[2,512]{1,0:T(2,128)S(1)}, u32[]{:S(2)}, u32[]{:S(2)}) %collective-permute-start) | collective-permute-done | bytes 4128 | tf_op jit(solution)/shard_map/ppermute | solution.py:19
  11.4 0.5 collective-permute-done.1.s2
  12.0 0.0 collective-permute-done.2.s3
  12.0 0.0 collective-permute-done.3.near_ref
  12.0 0.0 copy-done.1
  12.0 0.0 copy-done.2
  12.0 1.1 %shard_map.61 = (bf16[2048,512]{1,0:T(8,128)(2,1)S(1)}, bf16[512,2048]{1,0:T(8,128)(2,1)S(1)}, f32[64,2048]{1,0:T(8,128)S(1)}, s16[64,2176]{1,0:T(8,128)(2,1)S(1)}, s16[64,2144]{1,0:T(8,128)(2,1)S(1)}) custom-call(f32[8,640]{1,0:T(8,128)S(1)} %copy-done.2, f32[8,512]{1,0:T(8,128)S(1)} %get-tuple-element.23.s0, f32[2,512]{1,0:T(2,128)S(1)} %collective-permute-done.s1, ...), custom_call_target="tpu_custom_call" | custom-call | tf_op jit(solution)/shard_map/pallas_call | solution.py:59
  13.1 1.6 %collective-permute-start.5 = (s16[64,2176]{1,0:T(8,128)(2,1)S(1)}, s16[64,2176]{1,0:T(8,128)(2,1)S(1)}, u32[]{:S(2)}, u32[]{:S(2)}) collective-permute-start(s16[64,2176]{1,0:T(8,128)(2,1)S(1)} %get-tuple-element.28.coded_ref), channel_id=1, source_target_pairs={{0,8},{1,2},{2,1},{3,4},{4,3},{5,6},{6,5},{7,15},{8,0},{9,10},{10,... | collective-permute-start | bytes 835592 | tf_op jit(solution)/shard_map/ppermute | solution.py:39
  14.6 0.2 collective-permute-start.4
  14.8 1.4 %collective-permute-done.4.other_ref.partner_ref = s16[64,2144]{1,0:T(8,128)(2,1)S(1)} collective-permute-done((s16[64,2144]{1,0:T(8,128)(2,1)S(1)}, s16[64,2144]{1,0:T(8,128)(2,1)S(1)}, u32[]{:S(2)}, u32[]{:S(2)}) %collective-permute-start.4) | collective-permute-done | bytes 274464 | tf_op jit(solution)/shard_map/ppermute | solution.py:19
  16.2 0.3 shard_map.63
  16.5 0.2 collective-permute-start.7
  16.7 3.0 %collective-permute-done.5.other_ref.next_ref = s16[64,2176]{1,0:T(8,128)(2,1)S(1)} collective-permute-done((s16[64,2176]{1,0:T(8,128)(2,1)S(1)}, s16[64,2176]{1,0:T(8,128)(2,1)S(1)}, u32[]{:S(2)}, u32[]{:S(2)}) %collective-permute-start.5) | collective-permute-done | bytes 278560 | tf_op jit(solution)/shard_map/ppermute | solution.py:39
  19.7 0.3 shard_map.62
  20.0 1.0 %collective-permute-start.6 = (s16[64,2176]{1,0:T(8,128)(2,1)S(1)}, s16[64,2176]{1,0:T(8,128)(2,1)S(1)}, u32[]{:S(2)}, u32[]{:S(2)}) collective-permute-start(s16[64,2176]{1,0:T(8,128)(2,1)S(1)} %shard_map.62), channel_id=1, source_target_pairs={{0,2},{1,0},{2,4},{3,1},{4,6},{5,3},{6,7},{7,5},{8,10},{9,8},{10,1... | collective-permute-start | bytes 835592 | tf_op jit(solution)/shard_map/ppermute | solution.py:28
  21.0 2.8 %collective-permute-done.7.cross_ref = s16[64,2176]{1,0:T(8,128)(2,1)S(1)} collective-permute-done((s16[64,2176]{1,0:T(8,128)(2,1)S(1)}, s16[64,2176]{1,0:T(8,128)(2,1)S(1)}, u32[]{:S(2)}, u32[]{:S(2)}) %collective-permute-start.7) | collective-permute-done | bytes 278560 | tf_op jit(solution)/shard_map/ppermute | solution.py:28
  23.8 1.3 %collective-permute-done.6.same_ref = s16[64,2176]{1,0:T(8,128)(2,1)S(1)} collective-permute-done((s16[64,2176]{1,0:T(8,128)(2,1)S(1)}, s16[64,2176]{1,0:T(8,128)(2,1)S(1)}, u32[]{:S(2)}, u32[]{:S(2)}) %collective-permute-start.6) | collective-permute-done | bytes 278560 | tf_op jit(solution)/shard_map/ppermute | solution.py:28
  25.0 0.9 %shard_map.64.z0 = s16[64,640]{1,0:T(8,128)(2,1)S(1)} custom-call(f32[64,2048]{1,0:T(8,128)S(1)} %get-tuple-element.27.own_ref, s16[64,2176]{1,0:T(8,128)(2,1)S(1)} %get-tuple-element.28.coded_ref, s16[64,2144]{1,0:T(8,128)(2,1)S(1)} %collective-permute-done.4.other_ref.partner_ref, s16[64,2176]{1,0:T(8,128)(2,1)S(1)} %collective-permute-done.5.other_ref.next_ref, ...), custom_call_target="tpu_custom_call" | custom-call | tf_op jit(solution)/shard_map/pallas_call | solution.py:59
  26.0 1.5 %collective-permute-start.10 = (s16[64,640]{1,0:T(8,128)(2,1)S(1)}, s16[64,640]{1,0:T(8,128)(2,1)S(1)}, u32[]{:S(2)}, u32[]{:S(2)}) collective-permute-start(s16[64,640]{1,0:T(8,128)(2,1)S(1)} %shard_map.64.z0), channel_id=1, source_target_pairs={{0,24},{8,16},{16,8},{24,0},{1,25},{9,17},{17,9},{25,1},{2,26},{10... | collective-permute-start | bytes 245768 | tf_op jit(solution)/shard_map/ppermute | solution.py:19
  27.5 0.5 collective-permute-start.8
  28.0 1.5 %collective-permute-start.9 = (s16[64,640]{1,0:T(8,128)(2,1)S(1)}, s16[64,640]{1,0:T(8,128)(2,1)S(1)}, u32[]{:S(2)}, u32[]{:S(2)}) collective-permute-start(s16[64,640]{1,0:T(8,128)(2,1)S(1)} %shard_map.64.z0), channel_id=1, source_target_pairs={{0,16},{8,24},{16,0},{24,8},{1,17},{9,25},{17,1},{25,9},{2,18},{10... | collective-permute-start | bytes 245768 | tf_op jit(solution)/shard_map/ppermute | solution.py:19
  29.5 2.7 %collective-permute-done.10.z3 = s16[64,640]{1,0:T(8,128)(2,1)S(1)} collective-permute-done((s16[64,640]{1,0:T(8,128)(2,1)S(1)}, s16[64,640]{1,0:T(8,128)(2,1)S(1)}, u32[]{:S(2)}, u32[]{:S(2)}) %collective-permute-start.10) | collective-permute-done | bytes 81952 | tf_op jit(solution)/shard_map/ppermute | solution.py:19
  32.2 0.6 collective-permute-done.8.z1
  32.9 1.0 %collective-permute-done.9.z2 = s16[64,640]{1,0:T(8,128)(2,1)S(1)} collective-permute-done((s16[64,640]{1,0:T(8,128)(2,1)S(1)}, s16[64,640]{1,0:T(8,128)(2,1)S(1)}, u32[]{:S(2)}, u32[]{:S(2)}) %collective-permute-start.9) | collective-permute-done | bytes 81952 | tf_op jit(solution)/shard_map/ppermute | solution.py:19
  33.8 0.7 %shard_map.65 = (f32[64,512]{1,0:T(8,128)S(1)}, f32[64,128]{1,0:T(8,128)S(1)}, f32[64,2048]{1,0:T(8,128)S(1)}, s16[64,2176]{1,0:T(8,128)(2,1)S(1)}, s16[64,2144]{1,0:T(8,128)(2,1)S(1)}) custom-call(f32[8,640]{1,0:T(8,128)S(1)} %copy-done.2, s16[64,640]{1,0:T(8,128)(2,1)S(1)} %shard_map.64.z0, s16[64,640]{1,0:T(8,128)(2,1)S(1)} %collective-permute-done.8.z1, ...), custom_call_target="tpu_custom_call" | custom-call | tf_op jit(solution)/shard_map/pallas_call | solution.py:59
  34.5 1.4 %collective-permute-start.12 = (s16[64,2176]{1,0:T(8,128)(2,1)S(1)}, s16[64,2176]{1,0:T(8,128)(2,1)S(1)}, u32[]{:S(2)}, u32[]{:S(2)}) collective-permute-start(s16[64,2176]{1,0:T(8,128)(2,1)S(1)} %get-tuple-element.35.coded_ref), channel_id=1, source_target_pairs={{0,8},{1,2},{2,1},{3,4},{4,3},{5,6},{6,5},{7,15},{8,0},{9,10},{10,... | collective-permute-start | bytes 835592 | tf_op jit(solution)/shard_map/ppermute | solution.py:39
  35.9 0.5 collective-permute-start.11
  36.4 1.2 %collective-permute-done.11.other_ref.partner_ref = s16[64,2144]{1,0:T(8,128)(2,1)S(1)} collective-permute-done((s16[64,2144]{1,0:T(8,128)(2,1)S(1)}, s16[64,2144]{1,0:T(8,128)(2,1)S(1)}, u32[]{:S(2)}, u32[]{:S(2)}) %collective-permute-start.11) | collective-permute-done | bytes 274464 | tf_op jit(solution)/shard_map/ppermute | solution.py:19
  37.6 0.3 shard_map.67
  37.8 0.4 collective-permute-start.14
  38.2 2.9 %collective-permute-done.12.other_ref.next_ref = s16[64,2176]{1,0:T(8,128)(2,1)S(1)} collective-permute-done((s16[64,2176]{1,0:T(8,128)(2,1)S(1)}, s16[64,2176]{1,0:T(8,128)(2,1)S(1)}, u32[]{:S(2)}, u32[]{:S(2)}) %collective-permute-start.12) | collective-permute-done | bytes 278560 | tf_op jit(solution)/shard_map/ppermute | solution.py:39
  41.1 0.3 shard_map.66
  41.4 0.0 copy-start.3
  41.4 1.1 %collective-permute-start.13 = (s16[64,2176]{1,0:T(8,128)(2,1)S(1)}, s16[64,2176]{1,0:T(8,128)(2,1)S(1)}, u32[]{:S(2)}, u32[]{:S(2)}) collective-permute-start(s16[64,2176]{1,0:T(8,128)(2,1)S(1)} %shard_map.66), channel_id=1, source_target_pairs={{0,2},{1,0},{2,4},{3,1},{4,6},{5,3},{6,7},{7,5},{8,10},{9,8},{10,1... | collective-permute-start | bytes 835592 | tf_op jit(solution)/shard_map/ppermute | solution.py:28
  42.5 2.4 %collective-permute-done.14.cross_ref = s16[64,2176]{1,0:T(8,128)(2,1)S(1)} collective-permute-done((s16[64,2176]{1,0:T(8,128)(2,1)S(1)}, s16[64,2176]{1,0:T(8,128)(2,1)S(1)}, u32[]{:S(2)}, u32[]{:S(2)}) %collective-permute-start.14) | collective-permute-done | bytes 278560 | tf_op jit(solution)/shard_map/ppermute | solution.py:28
  45.0 1.6 %collective-permute-done.13.same_ref = s16[64,2176]{1,0:T(8,128)(2,1)S(1)} collective-permute-done((s16[64,2176]{1,0:T(8,128)(2,1)S(1)}, s16[64,2176]{1,0:T(8,128)(2,1)S(1)}, u32[]{:S(2)}, u32[]{:S(2)}) %collective-permute-start.13) | collective-permute-done | bytes 278560 | tf_op jit(solution)/shard_map/ppermute | solution.py:28
  46.6 0.9 %shard_map.68.z0 = s16[64,640]{1,0:T(8,128)(2,1)S(1)} custom-call(f32[64,2048]{1,0:T(8,128)S(1)} %get-tuple-element.34.own_ref, s16[64,2176]{1,0:T(8,128)(2,1)S(1)} %get-tuple-element.35.coded_ref, s16[64,2144]{1,0:T(8,128)(2,1)S(1)} %collective-permute-done.11.other_ref.partner_ref, s16[64,2176]{1,0:T(8,128)(2,1)S(1)} %collective-permute-done.12.other_ref.next_ref, ...), custom_call_target="tpu_custom_call" | custom-call | tf_op jit(solution)/shard_map/pallas_call | solution.py:59
  47.5 1.6 %collective-permute-start.15 = (s16[64,640]{1,0:T(8,128)(2,1)S(1)}, s16[64,640]{1,0:T(8,128)(2,1)S(1)}, u32[]{:S(2)}, u32[]{:S(2)}) collective-permute-start(s16[64,640]{1,0:T(8,128)(2,1)S(1)} %shard_map.68.z0), channel_id=1, source_target_pairs={{0,8},{8,0},{16,24},{24,16},{1,9},{9,1},{17,25},{25,17},{2,10},{10... | collective-permute-start | bytes 245768 | tf_op jit(solution)/shard_map/ppermute | solution.py:19
  49.1 0.9 %collective-permute-start.16 = (s16[64,640]{1,0:T(8,128)(2,1)S(1)}, s16[64,640]{1,0:T(8,128)(2,1)S(1)}, u32[]{:S(2)}, u32[]{:S(2)}) collective-permute-start(s16[64,640]{1,0:T(8,128)(2,1)S(1)} %shard_map.68.z0), channel_id=1, source_target_pairs={{0,16},{8,24},{16,0},{24,8},{1,17},{9,25},{17,1},{25,9},{2,18},{10... | collective-permute-start | bytes 245768 | tf_op jit(solution)/shard_map/ppermute | solution.py:19
  50.0 1.1 %collective-permute-start.17 = (s16[64,640]{1,0:T(8,128)(2,1)S(1)}, s16[64,640]{1,0:T(8,128)(2,1)S(1)}, u32[]{:S(2)}, u32[]{:S(2)}) collective-permute-start(s16[64,640]{1,0:T(8,128)(2,1)S(1)} %shard_map.68.z0), channel_id=1, source_target_pairs={{0,24},{8,16},{16,8},{24,0},{1,25},{9,17},{17,9},{25,1},{2,26},{10... | collective-permute-start | bytes 245768 | tf_op jit(solution)/shard_map/ppermute | solution.py:19
  51.1 1.5 %collective-permute-done.15.z1 = s16[64,640]{1,0:T(8,128)(2,1)S(1)} collective-permute-done((s16[64,640]{1,0:T(8,128)(2,1)S(1)}, s16[64,640]{1,0:T(8,128)(2,1)S(1)}, u32[]{:S(2)}, u32[]{:S(2)}) %collective-permute-start.15) | collective-permute-done | bytes 81952 | tf_op jit(solution)/shard_map/ppermute | solution.py:19
  52.5 3.0 %collective-permute-done.16.z2 = s16[64,640]{1,0:T(8,128)(2,1)S(1)} collective-permute-done((s16[64,640]{1,0:T(8,128)(2,1)S(1)}, s16[64,640]{1,0:T(8,128)(2,1)S(1)}, u32[]{:S(2)}, u32[]{:S(2)}) %collective-permute-start.16) | collective-permute-done | bytes 81952 | tf_op jit(solution)/shard_map/ppermute | solution.py:19
  55.5 0.0 collective-permute-done.17.z3
  55.5 0.2 shard_map.69
  55.8 0.0 collective-permute-start.18
  55.8 1.2 %collective-permute-done.18 = f32[8,128]{1,0:T(8,128)S(1)} collective-permute-done((f32[8,128]{1,0:T(8,128)S(1)}, f32[8,128]{1,0:T(8,128)S(1)}, u32[]{:S(2)}, u32[]{:S(2)}) %collective-permute-start.18) | collective-permute-done | bytes 4128 | tf_op jit(solution)/shard_map/ppermute | solution.py:19
  57.0 3.5 %collective-permute-start.21 = (f32[8,128]{1,0:T(8,128)S(1)}, f32[8,128]{1,0:T(8,128)S(1)}, u32[]{:S(2)}, u32[]{:S(2)}) collective-permute-start(f32[8,128]{1,0:T(8,128)S(1)} %add.5.p0), channel_id=1, source_target_pairs={{0,7},{1,6},{2,5},{3,4},{4,3},{5,2},{6,1},{7,0},{8,15},{9,14},{10,... | collective-permute-start | bytes 12296 | tf_op jit(solution)/shard_map/ppermute | solution.py:19
  60.5 0.1 collective-permute-start.19
  60.6 0.5 collective-permute-start.20
  61.0 0.0 copy-done.3
  61.0 2.4 %collective-permute-done.19.p1 = f32[4,128]{1,0:T(4,128)S(1)} collective-permute-done((f32[4,128]{1,0:T(4,128)S(1)}, f32[4,128]{1,0:T(4,128)S(1)}, u32[]{:S(2)}, u32[]{:S(2)}) %collective-permute-start.19) | collective-permute-done | bytes 2080 | tf_op jit(solution)/shard_map/ppermute | solution.py:19
  63.5 1.0 %collective-permute-done.20.p2 = f32[6,128]{1,0:T(8,128)S(1)} collective-permute-done((f32[6,128]{1,0:T(8,128)S(1)}, f32[6,128]{1,0:T(8,128)S(1)}, u32[]{:S(2)}, u32[]{:S(2)}) %collective-permute-start.20) | collective-permute-done | bytes 3104 | tf_op jit(solution)/shard_map/ppermute | solution.py:19
  64.5 0.0 collective-permute-done.21.p3
  64.5 1.0 %shard_map.70 = (f32[64,512]{1,0:T(8,128)}, f32[64,512]{1,0:T(8,128)}) custom-call(f32[1,128]{1,0:T(1,128)S(1)} %pad_bitcast_fusion.shrink_ref, f32[8,128]{1,0:T(8,128)S(1)} %add.5.p0, f32[4,128]{1,0:T(4,128)S(1)} %collective-permute-done.19.p1, f32[6,128]{1,0:T(8,128)S(1)} %collective-permute-done.20.p2, f32[8,128]{1,0:T(8,128)S(1)} %collective-permute-done.21.p3, ...), custom_call_target="tpu_custom_call" | custom-call | tf_op jit(solution)/shard_map/pallas_call | solution.py:59
  (3 shorter events, 0.0 us)
Async XLA Ops:
  1.3 3.7 %copy-start = (bf16[2048,512]{1,0:T(8,128)(2,1)S(1)}, bf16[2048,512]{1,0:T(8,128)(2,1)}, u32[]{:S(2)}) copy-start(bf16[2048,512]{1,0:T(8,128)(2,1)} %dosage_ref.3) | copy-start | bytes 6291460
  1.9 10.1 %copy-start.1 = (f32[512,64]{0,1:T(8,128)S(1)}, f32[512,64]{0,1:T(8,128)}, u32[]{:S(2)}) copy-start(f32[512,64]{0,1:T(8,128)} %param.6) | copy-start | bytes 393220
  1.9 10.1 %copy-start.2 = (f32[8,640]{1,0:T(8,128)S(1)}, f32[8,640]{1,0:T(8,128)}, u32[]{:S(2)}) copy-start(f32[8,640]{1,0:T(8,128)} %shard_map.60.wide_ref) | copy-start | bytes 61444
  1.9 10.1 %collective-permute-start.3 = (f32[8,640]{1,0:T(8,128)}, f32[8,640]{1,0:T(8,128)S(1)}, u32[]{:S(2)}, u32[]{:S(2)}) collective-permute-start(f32[8,640]{1,0:T(8,128)} %shard_map.60.wide_ref), channel_id=1, source_target_pairs={{0,2},{1,3},{2,4},{3,5},{4,6},{5,7},{6,0},{7,1},{8,10},{9,11},{10,... | collective-permute-start | bytes 61448 | tf_op jit(solution)/shard_map/ppermute | solution.py:44
  5.3 6.7 %collective-permute-start.2 = (f32[8,512]{1,0:T(8,128)S(1)}, f32[8,512]{1,0:T(8,128)S(1)}, u32[]{:S(2)}, u32[]{:S(2)}) collective-permute-start(f32[8,512]{1,0:T(8,128)S(1)} %get-tuple-element.23.s0), channel_id=1, source_target_pairs={{0,24},{8,16},{16,8},{24,0},{1,25},{9,17},{17,9},{25,1},{2,26},{10... | collective-permute-start | bytes 49160 | tf_op jit(solution)/shard_map/ppermute | solution.py:19
  7.8 3.6 %collective-permute-start = (f32[2,512]{1,0:T(2,128)S(1)}, f32[2,512]{1,0:T(2,128)S(1)}, u32[]{:S(2)}, u32[]{:S(2)}) collective-permute-start(f32[2,512]{1,0:T(2,128)S(1)} %get-tuple-element.21), channel_id=1, source_target_pairs={{0,8},{8,0},{16,24},{24,16},{1,9},{9,1},{17,25},{25,17},{2,10},{10... | collective-permute-start | bytes 12296 | tf_op jit(solution)/shard_map/ppermute | solution.py:19
  8.4 3.6 %collective-permute-start.1 = (f32[2,512]{1,0:T(2,128)S(1)}, f32[2,512]{1,0:T(2,128)S(1)}, u32[]{:S(2)}, u32[]{:S(2)}) collective-permute-start(f32[2,512]{1,0:T(2,128)S(1)} %get-tuple-element.21), channel_id=1, source_target_pairs={{0,16},{8,24},{16,0},{24,8},{1,17},{9,25},{17,1},{25,9},{2,18},{10... | collective-permute-start | bytes 12296 | tf_op jit(solution)/shard_map/ppermute | solution.py:19
  13.1 6.6 %collective-permute-start.5 = (s16[64,2176]{1,0:T(8,128)(2,1)S(1)}, s16[64,2176]{1,0:T(8,128)(2,1)S(1)}, u32[]{:S(2)}, u32[]{:S(2)}) collective-permute-start(s16[64,2176]{1,0:T(8,128)(2,1)S(1)} %get-tuple-element.28.coded_ref), channel_id=1, source_target_pairs={{0,8},{1,2},{2,1},{3,4},{4,3},{5,6},{6,5},{7,15},{8,0},{9,10},{10,... | collective-permute-start | bytes 835592 | tf_op jit(solution)/shard_map/ppermute | solution.py:39
  14.6 1.6 %collective-permute-start.4 = (s16[64,2144]{1,0:T(8,128)(2,1)S(1)}, s16[64,2144]{1,0:T(8,128)(2,1)S(1)}, u32[]{:S(2)}, u32[]{:S(2)}) collective-permute-start(s16[64,2144]{1,0:T(8,128)(2,1)S(1)} %get-tuple-element.29), channel_id=1, source_target_pairs={{0,1},{1,0},{2,3},{3,2},{4,5},{5,4},{6,7},{7,6},{8,9},{9,8},{10,11... | collective-permute-start | bytes 823304 | tf_op jit(solution)/shard_map/ppermute | solution.py:19
  16.5 7.3 %collective-permute-start.7 = (s16[64,2176]{1,0:T(8,128)(2,1)S(1)}, s16[64,2176]{1,0:T(8,128)(2,1)S(1)}, u32[]{:S(2)}, u32[]{:S(2)}) collective-permute-start(s16[64,2176]{1,0:T(8,128)(2,1)S(1)} %shard_map.63), channel_id=1, source_target_pairs={{0,1},{1,3},{2,0},{3,5},{4,2},{5,7},{6,4},{7,6},{8,9},{9,11},{10,8... | collective-permute-start | bytes 835592 | tf_op jit(solution)/shard_map/ppermute | solution.py:28
  20.0 5.1 %collective-permute-start.6 = (s16[64,2176]{1,0:T(8,128)(2,1)S(1)}, s16[64,2176]{1,0:T(8,128)(2,1)S(1)}, u32[]{:S(2)}, u32[]{:S(2)}) collective-permute-start(s16[64,2176]{1,0:T(8,128)(2,1)S(1)} %shard_map.62), channel_id=1, source_target_pairs={{0,2},{1,0},{2,4},{3,1},{4,6},{5,3},{6,7},{7,5},{8,10},{9,8},{10,1... | collective-permute-start | bytes 835592 | tf_op jit(solution)/shard_map/ppermute | solution.py:28
  26.0 6.3 %collective-permute-start.10 = (s16[64,640]{1,0:T(8,128)(2,1)S(1)}, s16[64,640]{1,0:T(8,128)(2,1)S(1)}, u32[]{:S(2)}, u32[]{:S(2)}) collective-permute-start(s16[64,640]{1,0:T(8,128)(2,1)S(1)} %shard_map.64.z0), channel_id=1, source_target_pairs={{0,24},{8,16},{16,8},{24,0},{1,25},{9,17},{17,9},{25,1},{2,26},{10... | collective-permute-start | bytes 245768 | tf_op jit(solution)/shard_map/ppermute | solution.py:19
  27.5 5.4 %collective-permute-start.8 = (s16[64,640]{1,0:T(8,128)(2,1)S(1)}, s16[64,640]{1,0:T(8,128)(2,1)S(1)}, u32[]{:S(2)}, u32[]{:S(2)}) collective-permute-start(s16[64,640]{1,0:T(8,128)(2,1)S(1)} %shard_map.64.z0), channel_id=1, source_target_pairs={{0,8},{8,0},{16,24},{24,16},{1,9},{9,1},{17,25},{25,17},{2,10},{10... | collective-permute-start | bytes 245768 | tf_op jit(solution)/shard_map/ppermute | solution.py:19
  28.0 5.8 %collective-permute-start.9 = (s16[64,640]{1,0:T(8,128)(2,1)S(1)}, s16[64,640]{1,0:T(8,128)(2,1)S(1)}, u32[]{:S(2)}, u32[]{:S(2)}) collective-permute-start(s16[64,640]{1,0:T(8,128)(2,1)S(1)} %shard_map.64.z0), channel_id=1, source_target_pairs={{0,16},{8,24},{16,0},{24,8},{1,17},{9,25},{17,1},{25,9},{2,18},{10... | collective-permute-start | bytes 245768 | tf_op jit(solution)/shard_map/ppermute | solution.py:19
  34.5 6.6 %collective-permute-start.12 = (s16[64,2176]{1,0:T(8,128)(2,1)S(1)}, s16[64,2176]{1,0:T(8,128)(2,1)S(1)}, u32[]{:S(2)}, u32[]{:S(2)}) collective-permute-start(s16[64,2176]{1,0:T(8,128)(2,1)S(1)} %get-tuple-element.35.coded_ref), channel_id=1, source_target_pairs={{0,8},{1,2},{2,1},{3,4},{4,3},{5,6},{6,5},{7,15},{8,0},{9,10},{10,... | collective-permute-start | bytes 835592 | tf_op jit(solution)/shard_map/ppermute | solution.py:39
  35.9 1.7 %collective-permute-start.11 = (s16[64,2144]{1,0:T(8,128)(2,1)S(1)}, s16[64,2144]{1,0:T(8,128)(2,1)S(1)}, u32[]{:S(2)}, u32[]{:S(2)}) collective-permute-start(s16[64,2144]{1,0:T(8,128)(2,1)S(1)} %get-tuple-element.36), channel_id=1, source_target_pairs={{0,1},{1,0},{2,3},{3,2},{4,5},{5,4},{6,7},{7,6},{8,9},{9,8},{10,11... | collective-permute-start | bytes 823304 | tf_op jit(solution)/shard_map/ppermute | solution.py:19
  37.8 7.1 %collective-permute-start.14 = (s16[64,2176]{1,0:T(8,128)(2,1)S(1)}, s16[64,2176]{1,0:T(8,128)(2,1)S(1)}, u32[]{:S(2)}, u32[]{:S(2)}) collective-permute-start(s16[64,2176]{1,0:T(8,128)(2,1)S(1)} %shard_map.67), channel_id=1, source_target_pairs={{0,1},{1,3},{2,0},{3,5},{4,2},{5,7},{6,4},{7,6},{8,9},{9,11},{10,8... | collective-permute-start | bytes 835592 | tf_op jit(solution)/shard_map/ppermute | solution.py:28
  41.4 19.7 %copy-start.3 = (f32[64]{0:T(128)S(1)}, f32[64]{0:T(128)}, u32[]{:S(2)}) copy-start(f32[64]{0:T(128)} %param.7) | copy-start | bytes 772
  41.4 5.2 %collective-permute-start.13 = (s16[64,2176]{1,0:T(8,128)(2,1)S(1)}, s16[64,2176]{1,0:T(8,128)(2,1)S(1)}, u32[]{:S(2)}, u32[]{:S(2)}) collective-permute-start(s16[64,2176]{1,0:T(8,128)(2,1)S(1)} %shard_map.66), channel_id=1, source_target_pairs={{0,2},{1,0},{2,4},{3,1},{4,6},{5,3},{6,7},{7,5},{8,10},{9,8},{10,1... | collective-permute-start | bytes 835592 | tf_op jit(solution)/shard_map/ppermute | solution.py:28
  47.5 5.0 %collective-permute-start.15 = (s16[64,640]{1,0:T(8,128)(2,1)S(1)}, s16[64,640]{1,0:T(8,128)(2,1)S(1)}, u32[]{:S(2)}, u32[]{:S(2)}) collective-permute-start(s16[64,640]{1,0:T(8,128)(2,1)S(1)} %shard_map.68.z0), channel_id=1, source_target_pairs={{0,8},{8,0},{16,24},{24,16},{1,9},{9,1},{17,25},{25,17},{2,10},{10... | collective-permute-start | bytes 245768 | tf_op jit(solution)/shard_map/ppermute | solution.py:19
  49.1 6.4 %collective-permute-start.16 = (s16[64,640]{1,0:T(8,128)(2,1)S(1)}, s16[64,640]{1,0:T(8,128)(2,1)S(1)}, u32[]{:S(2)}, u32[]{:S(2)}) collective-permute-start(s16[64,640]{1,0:T(8,128)(2,1)S(1)} %shard_map.68.z0), channel_id=1, source_target_pairs={{0,16},{8,24},{16,0},{24,8},{1,17},{9,25},{17,1},{25,9},{2,18},{10... | collective-permute-start | bytes 245768 | tf_op jit(solution)/shard_map/ppermute | solution.py:19
  50.0 5.5 %collective-permute-start.17 = (s16[64,640]{1,0:T(8,128)(2,1)S(1)}, s16[64,640]{1,0:T(8,128)(2,1)S(1)}, u32[]{:S(2)}, u32[]{:S(2)}) collective-permute-start(s16[64,640]{1,0:T(8,128)(2,1)S(1)} %shard_map.68.z0), channel_id=1, source_target_pairs={{0,24},{8,16},{16,8},{24,0},{1,25},{9,17},{17,9},{25,1},{2,26},{10... | collective-permute-start | bytes 245768 | tf_op jit(solution)/shard_map/ppermute | solution.py:19
  55.8 1.2 %collective-permute-start.18 = (f32[8,128]{1,0:T(8,128)S(1)}, f32[8,128]{1,0:T(8,128)S(1)}, u32[]{:S(2)}, u32[]{:S(2)}) collective-permute-start(f32[8,128]{1,0:T(8,128)S(1)} %shard_map.69), channel_id=1, source_target_pairs={{0,1},{1,0},{2,3},{3,2},{4,5},{5,4},{6,7},{7,6},{8,9},{9,8},{10,11... | collective-permute-start | bytes 12296 | tf_op jit(solution)/shard_map/ppermute | solution.py:19
  57.0 7.5 %collective-permute-start.21 = (f32[8,128]{1,0:T(8,128)S(1)}, f32[8,128]{1,0:T(8,128)S(1)}, u32[]{:S(2)}, u32[]{:S(2)}) collective-permute-start(f32[8,128]{1,0:T(8,128)S(1)} %add.5.p0), channel_id=1, source_target_pairs={{0,7},{1,6},{2,5},{3,4},{4,3},{5,2},{6,1},{7,0},{8,15},{9,14},{10,... | collective-permute-start | bytes 12296 | tf_op jit(solution)/shard_map/ppermute | solution.py:19
  60.5 3.0 %collective-permute-start.19 = (f32[4,128]{1,0:T(4,128)S(1)}, f32[4,128]{1,0:T(4,128)S(1)}, u32[]{:S(2)}, u32[]{:S(2)}) collective-permute-start(f32[4,128]{1,0:T(4,128)S(1)} %slice.6), channel_id=1, source_target_pairs={{0,3},{1,2},{2,1},{3,0},{4,7},{5,6},{6,5},{7,4},{8,11},{9,10},{10,... | collective-permute-start | bytes 6152 | tf_op jit(solution)/shard_map/ppermute | solution.py:19
  60.6 3.9 %collective-permute-start.20 = (f32[6,128]{1,0:T(8,128)S(1)}, f32[6,128]{1,0:T(8,128)S(1)}, u32[]{:S(2)}, u32[]{:S(2)}) collective-permute-start(f32[6,128]{1,0:T(8,128)S(1)} %bitcast.9), channel_id=1, source_target_pairs={{0,5},{1,4},{2,7},{3,6},{4,1},{5,0},{6,3},{7,2},{8,13},{9,12},{10,... | collective-permute-start | bytes 9224 | tf_op jit(solution)/shard_map/ppermute | solution.py:19

commit v11 on v10

--- a/solution.py
+++ b/solution.py
@@ -137,7 +137,7 @@
 
 
 def grid_values(coded_ref):
-    size = coded_ref.shape[1] - AUX
+    size = coded_ref.shape[1] - (coded_ref.shape[1] % AUX or AUX)
     return coded_ref[:, pl.ds(0, size)].astype(jnp.int32).astype(jnp.float32) * unit(aux(coded_ref)[0])
 
 
@@ -207,7 +207,7 @@
     finish(sent_ref, sent, width)
 
 
-def window_kernel(samples, count, own_ref, coded_ref, partner_ref, next_ref, same_ref, cross_ref, scaled_ref, sent_ref):
+def window_kernel(samples, count, own_ref, coded_ref, partner_ref, next_ref, same_ref, cross_ref, scaled_ref, sent_ref, brief_ref):
     odd, side, across = place(count)
     width = aux(coded_ref)[1]
     partner_exponent, partner_width = aux(partner_ref)[:2]
@@ -234,8 +234,11 @@
         curved = curved + own * mixed
     z = acc[:rows] + acc[rows:]
     exponent, scale = scale_of(jnp.max(jnp.abs(z), 1, keepdims=True))
-    sent_ref[:, pl.ds(0, z.shape[1])] = fixed(z * scale)
-    finish(sent_ref, exponent, *split(jnp.sum(curved, 1, keepdims=True) / samples))
+    columns = exponent, *split(jnp.sum(curved, 1, keepdims=True) / samples)
+    z = fixed(z * scale)
+    for ref in (sent_ref, brief_ref):
+        ref[:, pl.ds(0, z.shape[1])] = z
+        finish(ref, *columns)
 
 
 def collect_kernel(parts_ref, z0, z1, z2, z3, flat_ref):
@@ -307,7 +310,7 @@
     own_out, coded_out = (own_shape, jnp.float32), ((rows, local + AUX), jnp.int16)
     shared_out = ((rows, local + LESS), jnp.int16)
 
-    sent_out = ((rows, size + AUX), jnp.int16)
+    sent_out, brief_out = ((rows, size + AUX), jnp.int16), ((rows, size + LESS), jnp.int16)
 
     sums, brief = call(stats_kernel, [((8, size), jnp.float32), ((2, size), jnp.float32)], dosage)
     one, two, three = swap(brief, "samp", 1), swap(brief, "samp", 2), swap(sums, "samp", 3)
@@ -335,11 +338,11 @@
         partner = swap(shared, "snp", 1)
         cross = crossing(give(1, own, coded, partner), 1)
         same = crossing(give(0, own, coded, beside), 0)
-        (z,) = call(
-            functools.partial(window_kernel, samples, count), [sent_out],
+        z, brief = call(
+            functools.partial(window_kernel, samples, count), [sent_out, brief_out],
             own, coded, partner, beside, same, cross, scaled,
         )
-        return [z, *partners(z, "samp", 1, 2)]
+        return [z, swap(brief, "samp", 1), swap(brief, "samp", 2), swap(z, "samp", 3)]
 
     first, parts, own, coded, shared = call(
         functools.partial(next_kernel, samples),

time: 65.6 us -> 64.7 us (0.986)
  waiting for transfers between devices: 33 us -> 32.3 us
    ppermute x15, waiting for transfers between devices: 19 us -> 18.3 us  [swap(): lax.ppermute(value, axis, [(i, i ^ bits) for i in range(lax.axis_size(axi...]
  transfers between devices with their start and end apart: 22 -> 22, of which waited for: 18 -> 17; matrix products, arithmetic and copies ran while one was open for 0% -> 0% of each run, Pallas kernels for 2% -> 2%
where the time goes in v11:
time: 64.7 us; the launch traced here: 64.5 us
  waiting for transfers between devices  32.3 us (50%)
  starting transfers between devices  24 us (37%)
  Pallas kernels  6.8 us (11%)
  between operations  1.4 us (2%)
    ppermute x15, waiting for transfers between devices, swap(): lax.ppermute(value, axis, [(i, i ^ bits) for i in range(lax.axis_size(axi...  18.3 us
    ppermute x15, starting transfers between devices, swap(): lax.ppermute(value, axis, [(i, i ^ bits) for i in range(lax.axis_size(axi...  15.3 us
    ppermute x4, waiting for transfers between devices, crossing(): return lax.ppermute(value, 'snp', pairs)  8.13 us
    pallas_call x11, Pallas kernels, call(): pl.pallas_call(body, out_shape=outs, in_specs=specs, out_specs=[pl.BlockS...  6.19 us
    ppermute x2, waiting for transfers between devices, adjacent(): return lax.ppermute(value, ('samp', 'snp'), pairs)  5.89 us
    ppermute x1, starting transfers between devices, shifted(): lax.ppermute(value, 'snp', [(i, (i + 2) % count) for i in range(count)])  3.02 us
    ppermute x2, starting transfers between devices, adjacent(): return lax.ppermute(value, ('samp', 'snp'), pairs)  2.94 us
    ppermute x4, starting transfers between devices, crossing(): return lax.ppermute(value, 'snp', pairs)  2.77 us
  transfers between devices with their start and end apart: 22, of which 17 were waited for; matrix products, arithmetic and copies ran while one was open for 0% of the time, Pallas kernels for 2%

profile of v11, /device:TPU:0, one launch (start us, length us, event | category | flops | bytes accessed | tf_op | source)
XLA Modules:
  0.0 64.5 jit_solution(16056241551511458412)
XLA Ops:
  1.3 0.0 copy-start
  1.3 0.6 shard_map.60.wide_ref
  1.9 0.0 copy-start.1
  1.9 0.0 copy-start.2
  1.9 3.0 %collective-permute-start.3 = (f32[8,640]{1,0:T(8,128)}, f32[8,640]{1,0:T(8,128)S(1)}, u32[]{:S(2)}, u32[]{:S(2)}) collective-permute-start(f32[8,640]{1,0:T(8,128)} %shard_map.60.wide_ref), channel_id=1, source_target_pairs={{0,2},{1,3},{2,4},{3,5},{4,6},{5,7},{6,0},{7,1},{8,10},{9,11},{10,... | collective-permute-start | bytes 61448 | tf_op jit(solution)/shard_map/ppermute | solution.py:44
  4.9 0.0 copy-done
  4.9 0.4 shard_map.59
  5.3 2.5 %collective-permute-start.2 = (f32[8,512]{1,0:T(8,128)S(1)}, f32[8,512]{1,0:T(8,128)S(1)}, u32[]{:S(2)}, u32[]{:S(2)}) collective-permute-start(f32[8,512]{1,0:T(8,128)S(1)} %get-tuple-element.27.s0), channel_id=1, source_target_pairs={{0,24},{8,16},{16,8},{24,0},{1,25},{9,17},{17,9},{25,1},{2,26},{10... | collective-permute-start | bytes 49160 | tf_op jit(solution)/shard_map/ppermute | solution.py:19
  7.8 0.5 collective-permute-start
  8.4 0.5 collective-permute-start.1
  8.9 2.6 %collective-permute-done.s1 = f32[2,512]{1,0:T(2,128)S(1)} collective-permute-done((f32[2,512]{1,0:T(2,128)S(1)}, f32[2,512]{1,0:T(2,128)S(1)}, u32[]{:S(2)}, u32[]{:S(2)}) %collective-permute-start) | collective-permute-done | bytes 4128 | tf_op jit(solution)/shard_map/ppermute | solution.py:19
  11.4 0.5 collective-permute-done.1.s2
  12.0 0.0 collective-permute-done.2.s3
  12.0 0.0 collective-permute-done.3.near_ref
  12.0 0.0 copy-done.1
  12.0 0.0 copy-done.2
  12.0 1.1 %shard_map.61 = (bf16[2048,512]{1,0:T(8,128)(2,1)S(1)}, bf16[512,2048]{1,0:T(8,128)(2,1)S(1)}, f32[64,2048]{1,0:T(8,128)S(1)}, s16[64,2176]{1,0:T(8,128)(2,1)S(1)}, s16[64,2144]{1,0:T(8,128)(2,1)S(1)}) custom-call(f32[8,640]{1,0:T(8,128)S(1)} %copy-done.2, f32[8,512]{1,0:T(8,128)S(1)} %get-tuple-element.27.s0, f32[2,512]{1,0:T(2,128)S(1)} %collective-permute-done.s1, ...), custom_call_target="tpu_custom_call" | custom-call | tf_op jit(solution)/shard_map/pallas_call | solution.py:59
  13.1 1.6 %collective-permute-start.5 = (s16[64,2176]{1,0:T(8,128)(2,1)S(1)}, s16[64,2176]{1,0:T(8,128)(2,1)S(1)}, u32[]{:S(2)}, u32[]{:S(2)}) collective-permute-start(s16[64,2176]{1,0:T(8,128)(2,1)S(1)} %get-tuple-element.32.coded_ref), channel_id=1, source_target_pairs={{0,8},{1,2},{2,1},{3,4},{4,3},{5,6},{6,5},{7,15},{8,0},{9,10},{10,... | collective-permute-start | bytes 835592 | tf_op jit(solution)/shard_map/ppermute | solution.py:39
  14.6 0.2 collective-permute-start.4
  14.8 1.4 %collective-permute-done.4.other_ref.partner_ref = s16[64,2144]{1,0:T(8,128)(2,1)S(1)} collective-permute-done((s16[64,2144]{1,0:T(8,128)(2,1)S(1)}, s16[64,2144]{1,0:T(8,128)(2,1)S(1)}, u32[]{:S(2)}, u32[]{:S(2)}) %collective-permute-start.4) | collective-permute-done | bytes 274464 | tf_op jit(solution)/shard_map/ppermute | solution.py:19
  16.2 0.3 shard_map.63
  16.5 0.2 collective-permute-start.7
  16.7 3.0 %collective-permute-done.5.other_ref.next_ref = s16[64,2176]{1,0:T(8,128)(2,1)S(1)} collective-permute-done((s16[64,2176]{1,0:T(8,128)(2,1)S(1)}, s16[64,2176]{1,0:T(8,128)(2,1)S(1)}, u32[]{:S(2)}, u32[]{:S(2)}) %collective-permute-start.5) | collective-permute-done | bytes 278560 | tf_op jit(solution)/shard_map/ppermute | solution.py:39
  19.7 0.3 shard_map.62
  20.0 1.0 %collective-permute-start.6 = (s16[64,2176]{1,0:T(8,128)(2,1)S(1)}, s16[64,2176]{1,0:T(8,128)(2,1)S(1)}, u32[]{:S(2)}, u32[]{:S(2)}) collective-permute-start(s16[64,2176]{1,0:T(8,128)(2,1)S(1)} %shard_map.62), channel_id=1, source_target_pairs={{0,2},{1,0},{2,4},{3,1},{4,6},{5,3},{6,7},{7,5},{8,10},{9,8},{10,1... | collective-permute-start | bytes 835592 | tf_op jit(solution)/shard_map/ppermute | solution.py:28
  21.0 2.8 %collective-permute-done.7.cross_ref = s16[64,2176]{1,0:T(8,128)(2,1)S(1)} collective-permute-done((s16[64,2176]{1,0:T(8,128)(2,1)S(1)}, s16[64,2176]{1,0:T(8,128)(2,1)S(1)}, u32[]{:S(2)}, u32[]{:S(2)}) %collective-permute-start.7) | collective-permute-done | bytes 278560 | tf_op jit(solution)/shard_map/ppermute | solution.py:28
  23.8 1.3 %collective-permute-done.6.same_ref = s16[64,2176]{1,0:T(8,128)(2,1)S(1)} collective-permute-done((s16[64,2176]{1,0:T(8,128)(2,1)S(1)}, s16[64,2176]{1,0:T(8,128)(2,1)S(1)}, u32[]{:S(2)}, u32[]{:S(2)}) %collective-permute-start.6) | collective-permute-done | bytes 278560 | tf_op jit(solution)/shard_map/ppermute | solution.py:28
  25.0 0.9 %shard_map.64 = (s16[64,640]{1,0:T(8,128)(2,1)S(1)}, s16[64,608]{1,0:T(8,128)(2,1)S(1)}) custom-call(f32[64,2048]{1,0:T(8,128)S(1)} %get-tuple-element.31.own_ref, s16[64,2176]{1,0:T(8,128)(2,1)S(1)} %get-tuple-element.32.coded_ref, s16[64,2144]{1,0:T(8,128)(2,1)S(1)} %collective-permute-done.4.other_ref.partner_ref, ...), custom_call_target="tpu_custom_call" | custom-call | tf_op jit(solution)/shard_map/pallas_call | solution.py:59
  26.0 1.5 %collective-permute-start.10 = (s16[64,640]{1,0:T(8,128)(2,1)S(1)}, s16[64,640]{1,0:T(8,128)(2,1)S(1)}, u32[]{:S(2)}, u32[]{:S(2)}) collective-permute-start(s16[64,640]{1,0:T(8,128)(2,1)S(1)} %get-tuple-element.36.z0), channel_id=1, source_target_pairs={{0,24},{8,16},{16,8},{24,0},{1,25},{9,17},{17,9},{25,1},{2,26},{10... | collective-permute-start | bytes 245768 | tf_op jit(solution)/shard_map/ppermute | solution.py:19
  27.5 0.5 collective-permute-start.8
  28.0 1.5 %collective-permute-start.9 = (s16[64,608]{1,0:T(8,128)(2,1)S(1)}, s16[64,608]{1,0:T(8,128)(2,1)S(1)}, u32[]{:S(2)}, u32[]{:S(2)}) collective-permute-start(s16[64,608]{1,0:T(8,128)(2,1)S(1)} %get-tuple-element.37), channel_id=1, source_target_pairs={{0,16},{8,24},{16,0},{24,8},{1,17},{9,25},{17,1},{25,9},{2,18},{10... | collective-permute-start | bytes 233480 | tf_op jit(solution)/shard_map/ppermute | solution.py:19
  29.5 3.4 %collective-permute-done.8.z1 = s16[64,608]{1,0:T(8,128)(2,1)S(1)} collective-permute-done((s16[64,608]{1,0:T(8,128)(2,1)S(1)}, s16[64,608]{1,0:T(8,128)(2,1)S(1)}, u32[]{:S(2)}, u32[]{:S(2)}) %collective-permute-start.8) | collective-permute-done | bytes 77856 | tf_op jit(solution)/shard_map/ppermute | solution.py:19
  32.9 1.0 %collective-permute-done.9.z2 = s16[64,608]{1,0:T(8,128)(2,1)S(1)} collective-permute-done((s16[64,608]{1,0:T(8,128)(2,1)S(1)}, s16[64,608]{1,0:T(8,128)(2,1)S(1)}, u32[]{:S(2)}, u32[]{:S(2)}) %collective-permute-start.9) | collective-permute-done | bytes 77856 | tf_op jit(solution)/shard_map/ppermute | solution.py:19
  33.8 0.0 collective-permute-done.10.z3
  33.8 0.7 %shard_map.65 = (f32[64,512]{1,0:T(8,128)S(1)}, f32[64,128]{1,0:T(8,128)S(1)}, f32[64,2048]{1,0:T(8,128)S(1)}, s16[64,2176]{1,0:T(8,128)(2,1)S(1)}, s16[64,2144]{1,0:T(8,128)(2,1)S(1)}) custom-call(f32[8,640]{1,0:T(8,128)S(1)} %copy-done.2, s16[64,640]{1,0:T(8,128)(2,1)S(1)} %get-tuple-element.36.z0, s16[64,608]{1,0:T(8,128)(2,1)S(1)} %collective-permute-done.8.z1, ...), custom_call_target="tpu_custom_call" | custom-call | tf_op jit(solution)/shard_map/pallas_call | solution.py:59
  34.5 1.4 %collective-permute-start.12 = (s16[64,2176]{1,0:T(8,128)(2,1)S(1)}, s16[64,2176]{1,0:T(8,128)(2,1)S(1)}, u32[]{:S(2)}, u32[]{:S(2)}) collective-permute-start(s16[64,2176]{1,0:T(8,128)(2,1)S(1)} %get-tuple-element.41.coded_ref), channel_id=1, source_target_pairs={{0,8},{1,2},{2,1},{3,4},{4,3},{5,6},{6,5},{7,15},{8,0},{9,10},{10,... | collective-permute-start | bytes 835592 | tf_op jit(solution)/shard_map/ppermute | solution.py:39
  35.9 0.5 collective-permute-start.11
  36.4 1.2 %collective-permute-done.11.other_ref.partner_ref = s16[64,2144]{1,0:T(8,128)(2,1)S(1)} collective-permute-done((s16[64,2144]{1,0:T(8,128)(2,1)S(1)}, s16[64,2144]{1,0:T(8,128)(2,1)S(1)}, u32[]{:S(2)}, u32[]{:S(2)}) %collective-permute-start.11) | collective-permute-done | bytes 274464 | tf_op jit(solution)/shard_map/ppermute | solution.py:19
  37.6 0.3 shard_map.67
  37.9 0.4 collective-permute-start.14
  38.2 2.9 %collective-permute-done.12.other_ref.next_ref = s16[64,2176]{1,0:T(8,128)(2,1)S(1)} collective-permute-done((s16[64,2176]{1,0:T(8,128)(2,1)S(1)}, s16[64,2176]{1,0:T(8,128)(2,1)S(1)}, u32[]{:S(2)}, u32[]{:S(2)}) %collective-permute-start.12) | collective-permute-done | bytes 278560 | tf_op jit(solution)/shard_map/ppermute | solution.py:39
  41.1 0.3 shard_map.66
  41.4 0.0 copy-start.3
  41.4 1.1 %collective-permute-start.13 = (s16[64,2176]{1,0:T(8,128)(2,1)S(1)}, s16[64,2176]{1,0:T(8,128)(2,1)S(1)}, u32[]{:S(2)}, u32[]{:S(2)}) collective-permute-start(s16[64,2176]{1,0:T(8,128)(2,1)S(1)} %shard_map.66), channel_id=1, source_target_pairs={{0,2},{1,0},{2,4},{3,1},{4,6},{5,3},{6,7},{7,5},{8,10},{9,8},{10,1... | collective-permute-start | bytes 835592 | tf_op jit(solution)/shard_map/ppermute | solution.py:28
  42.5 2.4 %collective-permute-done.14.cross_ref = s16[64,2176]{1,0:T(8,128)(2,1)S(1)} collective-permute-done((s16[64,2176]{1,0:T(8,128)(2,1)S(1)}, s16[64,2176]{1,0:T(8,128)(2,1)S(1)}, u32[]{:S(2)}, u32[]{:S(2)}) %collective-permute-start.14) | collective-permute-done | bytes 278560 | tf_op jit(solution)/shard_map/ppermute | solution.py:28
  45.0 1.6 %collective-permute-done.13.same_ref = s16[64,2176]{1,0:T(8,128)(2,1)S(1)} collective-permute-done((s16[64,2176]{1,0:T(8,128)(2,1)S(1)}, s16[64,2176]{1,0:T(8,128)(2,1)S(1)}, u32[]{:S(2)}, u32[]{:S(2)}) %collective-permute-start.13) | collective-permute-done | bytes 278560 | tf_op jit(solution)/shard_map/ppermute | solution.py:28
  46.6 0.9 %shard_map.68 = (s16[64,640]{1,0:T(8,128)(2,1)S(1)}, s16[64,608]{1,0:T(8,128)(2,1)S(1)}) custom-call(f32[64,2048]{1,0:T(8,128)S(1)} %get-tuple-element.40.own_ref, s16[64,2176]{1,0:T(8,128)(2,1)S(1)} %get-tuple-element.41.coded_ref, s16[64,2144]{1,0:T(8,128)(2,1)S(1)} %collective-permute-done.11.other_ref.partner_ref, ...), custom_call_target="tpu_custom_call" | custom-call | tf_op jit(solution)/shard_map/pallas_call | solution.py:59
  47.5 1.9 %collective-permute-start.17 = (s16[64,640]{1,0:T(8,128)(2,1)S(1)}, s16[64,640]{1,0:T(8,128)(2,1)S(1)}, u32[]{:S(2)}, u32[]{:S(2)}) collective-permute-start(s16[64,640]{1,0:T(8,128)(2,1)S(1)} %get-tuple-element.43.z0), channel_id=1, source_target_pairs={{0,24},{8,16},{16,8},{24,0},{1,25},{9,17},{17,9},{25,1},{2,26},{10... | collective-permute-start | bytes 245768 | tf_op jit(solution)/shard_map/ppermute | solution.py:19
  49.4 0.6 collective-permute-start.15
  50.0 1.1 %collective-permute-start.16 = (s16[64,608]{1,0:T(8,128)(2,1)S(1)}, s16[64,608]{1,0:T(8,128)(2,1)S(1)}, u32[]{:S(2)}, u32[]{:S(2)}) collective-permute-start(s16[64,608]{1,0:T(8,128)(2,1)S(1)} %get-tuple-element.44), channel_id=1, source_target_pairs={{0,16},{8,24},{16,0},{24,8},{1,17},{9,25},{17,1},{25,9},{2,18},{10... | collective-permute-start | bytes 233480 | tf_op jit(solution)/shard_map/ppermute | solution.py:19
  51.1 3.6 %collective-permute-done.15.z1 = s16[64,608]{1,0:T(8,128)(2,1)S(1)} collective-permute-done((s16[64,608]{1,0:T(8,128)(2,1)S(1)}, s16[64,608]{1,0:T(8,128)(2,1)S(1)}, u32[]{:S(2)}, u32[]{:S(2)}) %collective-permute-start.15) | collective-permute-done | bytes 77856 | tf_op jit(solution)/shard_map/ppermute | solution.py:19
  54.7 0.5 collective-permute-done.16.z2
  55.2 0.0 collective-permute-done.17.z3
  55.2 0.2 shard_map.69
  55.5 0.0 collective-permute-start.18
  55.5 1.2 %collective-permute-done.18 = f32[8,128]{1,0:T(8,128)S(1)} collective-permute-done((f32[8,128]{1,0:T(8,128)S(1)}, f32[8,128]{1,0:T(8,128)S(1)}, u32[]{:S(2)}, u32[]{:S(2)}) %collective-permute-start.18) | collective-permute-done | bytes 4128 | tf_op jit(solution)/shard_map/ppermute | solution.py:19
  56.7 2.9 %collective-permute-start.21 = (f32[8,128]{1,0:T(8,128)S(1)}, f32[8,128]{1,0:T(8,128)S(1)}, u32[]{:S(2)}, u32[]{:S(2)}) collective-permute-start(f32[8,128]{1,0:T(8,128)S(1)} %add.5.p0), channel_id=1, source_target_pairs={{0,7},{1,6},{2,5},{3,4},{4,3},{5,2},{6,1},{7,0},{8,15},{9,14},{10,... | collective-permute-start | bytes 12296 | tf_op jit(solution)/shard_map/ppermute | solution.py:19
  59.5 0.1 collective-permute-start.19
  59.6 0.9 %collective-permute-start.20 = (f32[6,128]{1,0:T(8,128)S(1)}, f32[6,128]{1,0:T(8,128)S(1)}, u32[]{:S(2)}, u32[]{:S(2)}) collective-permute-start(f32[6,128]{1,0:T(8,128)S(1)} %bitcast.9), channel_id=1, source_target_pairs={{0,5},{1,4},{2,7},{3,6},{4,1},{5,0},{6,3},{7,2},{8,13},{9,12},{10,... | collective-permute-start | bytes 9224 | tf_op jit(solution)/shard_map/ppermute | solution.py:19
  60.6 0.0 copy-done.3
  60.6 2.0 %collective-permute-done.19.p1 = f32[4,128]{1,0:T(4,128)S(1)} collective-permute-done((f32[4,128]{1,0:T(4,128)S(1)}, f32[4,128]{1,0:T(4,128)S(1)}, u32[]{:S(2)}, u32[]{:S(2)}) %collective-permute-start.19) | collective-permute-done | bytes 2080 | tf_op jit(solution)/shard_map/ppermute | solution.py:19
  62.5 1.0 %collective-permute-done.20.p2 = f32[6,128]{1,0:T(8,128)S(1)} collective-permute-done((f32[6,128]{1,0:T(8,128)S(1)}, f32[6,128]{1,0:T(8,128)S(1)}, u32[]{:S(2)}, u32[]{:S(2)}) %collective-permute-start.20) | collective-permute-done | bytes 3104 | tf_op jit(solution)/shard_map/ppermute | solution.py:19
  63.6 0.0 collective-permute-done.21.p3
  63.6 1.0 %shard_map.70 = (f32[64,512]{1,0:T(8,128)}, f32[64,512]{1,0:T(8,128)}) custom-call(f32[1,128]{1,0:T(1,128)S(1)} %pad_bitcast_fusion.shrink_ref, f32[8,128]{1,0:T(8,128)S(1)} %add.5.p0, f32[4,128]{1,0:T(4,128)S(1)} %collective-permute-done.19.p1, f32[6,128]{1,0:T(8,128)S(1)} %collective-permute-done.20.p2, f32[8,128]{1,0:T(8,128)S(1)} %collective-permute-done.21.p3, ...), custom_call_target="tpu_custom_call" | custom-call | tf_op jit(solution)/shard_map/pallas_call | solution.py:59
  (3 shorter events, 0.0 us)
Async XLA Ops:
  1.3 3.7 %copy-start = (bf16[2048,512]{1,0:T(8,128)(2,1)S(1)}, bf16[2048,512]{1,0:T(8,128)(2,1)}, u32[]{:S(2)}) copy-start(bf16[2048,512]{1,0:T(8,128)(2,1)} %dosage_ref.3) | copy-start | bytes 6291460
  1.9 10.1 %copy-start.1 = (f32[512,64]{0,1:T(8,128)S(1)}, f32[512,64]{0,1:T(8,128)}, u32[]{:S(2)}) copy-start(f32[512,64]{0,1:T(8,128)} %param.6) | copy-start | bytes 393220
  1.9 10.1 %copy-start.2 = (f32[8,640]{1,0:T(8,128)S(1)}, f32[8,640]{1,0:T(8,128)}, u32[]{:S(2)}) copy-start(f32[8,640]{1,0:T(8,128)} %shard_map.60.wide_ref) | copy-start | bytes 61444
  1.9 10.1 %collective-permute-start.3 = (f32[8,640]{1,0:T(8,128)}, f32[8,640]{1,0:T(8,128)S(1)}, u32[]{:S(2)}, u32[]{:S(2)}) collective-permute-start(f32[8,640]{1,0:T(8,128)} %shard_map.60.wide_ref), channel_id=1, source_target_pairs={{0,2},{1,3},{2,4},{3,5},{4,6},{5,7},{6,0},{7,1},{8,10},{9,11},{10,... | collective-permute-start | bytes 61448 | tf_op jit(solution)/shard_map/ppermute | solution.py:44
  5.3 6.7 %collective-permute-start.2 = (f32[8,512]{1,0:T(8,128)S(1)}, f32[8,512]{1,0:T(8,128)S(1)}, u32[]{:S(2)}, u32[]{:S(2)}) collective-permute-start(f32[8,512]{1,0:T(8,128)S(1)} %get-tuple-element.27.s0), channel_id=1, source_target_pairs={{0,24},{8,16},{16,8},{24,0},{1,25},{9,17},{17,9},{25,1},{2,26},{10... | collective-permute-start | bytes 49160 | tf_op jit(solution)/shard_map/ppermute | solution.py:19
  7.8 3.6 %collective-permute-start = (f32[2,512]{1,0:T(2,128)S(1)}, f32[2,512]{1,0:T(2,128)S(1)}, u32[]{:S(2)}, u32[]{:S(2)}) collective-permute-start(f32[2,512]{1,0:T(2,128)S(1)} %get-tuple-element.25), channel_id=1, source_target_pairs={{0,8},{8,0},{16,24},{24,16},{1,9},{9,1},{17,25},{25,17},{2,10},{10... | collective-permute-start | bytes 12296 | tf_op jit(solution)/shard_map/ppermute | solution.py:19
  8.4 3.6 %collective-permute-start.1 = (f32[2,512]{1,0:T(2,128)S(1)}, f32[2,512]{1,0:T(2,128)S(1)}, u32[]{:S(2)}, u32[]{:S(2)}) collective-permute-start(f32[2,512]{1,0:T(2,128)S(1)} %get-tuple-element.25), channel_id=1, source_target_pairs={{0,16},{8,24},{16,0},{24,8},{1,17},{9,25},{17,1},{25,9},{2,18},{10... | collective-permute-start | bytes 12296 | tf_op jit(solution)/shard_map/ppermute | solution.py:19
  13.1 6.6 %collective-permute-start.5 = (s16[64,2176]{1,0:T(8,128)(2,1)S(1)}, s16[64,2176]{1,0:T(8,128)(2,1)S(1)}, u32[]{:S(2)}, u32[]{:S(2)}) collective-permute-start(s16[64,2176]{1,0:T(8,128)(2,1)S(1)} %get-tuple-element.32.coded_ref), channel_id=1, source_target_pairs={{0,8},{1,2},{2,1},{3,4},{4,3},{5,6},{6,5},{7,15},{8,0},{9,10},{10,... | collective-permute-start | bytes 835592 | tf_op jit(solution)/shard_map/ppermute | solution.py:39
  14.6 1.6 %collective-permute-start.4 = (s16[64,2144]{1,0:T(8,128)(2,1)S(1)}, s16[64,2144]{1,0:T(8,128)(2,1)S(1)}, u32[]{:S(2)}, u32[]{:S(2)}) collective-permute-start(s16[64,2144]{1,0:T(8,128)(2,1)S(1)} %get-tuple-element.33), channel_id=1, source_target_pairs={{0,1},{1,0},{2,3},{3,2},{4,5},{5,4},{6,7},{7,6},{8,9},{9,8},{10,11... | collective-permute-start | bytes 823304 | tf_op jit(solution)/shard_map/ppermute | solution.py:19
  16.5 7.3 %collective-permute-start.7 = (s16[64,2176]{1,0:T(8,128)(2,1)S(1)}, s16[64,2176]{1,0:T(8,128)(2,1)S(1)}, u32[]{:S(2)}, u32[]{:S(2)}) collective-permute-start(s16[64,2176]{1,0:T(8,128)(2,1)S(1)} %shard_map.63), channel_id=1, source_target_pairs={{0,1},{1,3},{2,0},{3,5},{4,2},{5,7},{6,4},{7,6},{8,9},{9,11},{10,8... | collective-permute-start | bytes 835592 | tf_op jit(solution)/shard_map/ppermute | solution.py:28
  20.0 5.1 %collective-permute-start.6 = (s16[64,2176]{1,0:T(8,128)(2,1)S(1)}, s16[64,2176]{1,0:T(8,128)(2,1)S(1)}, u32[]{:S(2)}, u32[]{:S(2)}) collective-permute-start(s16[64,2176]{1,0:T(8,128)(2,1)S(1)} %shard_map.62), channel_id=1, source_target_pairs={{0,2},{1,0},{2,4},{3,1},{4,6},{5,3},{6,7},{7,5},{8,10},{9,8},{10,1... | collective-permute-start | bytes 835592 | tf_op jit(solution)/shard_map/ppermute | solution.py:28
  26.0 7.9 %collective-permute-start.10 = (s16[64,640]{1,0:T(8,128)(2,1)S(1)}, s16[64,640]{1,0:T(8,128)(2,1)S(1)}, u32[]{:S(2)}, u32[]{:S(2)}) collective-permute-start(s16[64,640]{1,0:T(8,128)(2,1)S(1)} %get-tuple-element.36.z0), channel_id=1, source_target_pairs={{0,24},{8,16},{16,8},{24,0},{1,25},{9,17},{17,9},{25,1},{2,26},{10... | collective-permute-start | bytes 245768 | tf_op jit(solution)/shard_map/ppermute | solution.py:19
  27.5 5.4 %collective-permute-start.8 = (s16[64,608]{1,0:T(8,128)(2,1)S(1)}, s16[64,608]{1,0:T(8,128)(2,1)S(1)}, u32[]{:S(2)}, u32[]{:S(2)}) collective-permute-start(s16[64,608]{1,0:T(8,128)(2,1)S(1)} %get-tuple-element.37), channel_id=1, source_target_pairs={{0,8},{8,0},{16,24},{24,16},{1,9},{9,1},{17,25},{25,17},{2,10},{10... | collective-permute-start | bytes 233480 | tf_op jit(solution)/shard_map/ppermute | solution.py:19
  28.0 5.8 %collective-permute-start.9 = (s16[64,608]{1,0:T(8,128)(2,1)S(1)}, s16[64,608]{1,0:T(8,128)(2,1)S(1)}, u32[]{:S(2)}, u32[]{:S(2)}) collective-permute-start(s16[64,608]{1,0:T(8,128)(2,1)S(1)} %get-tuple-element.37), channel_id=1, source_target_pairs={{0,16},{8,24},{16,0},{24,8},{1,17},{9,25},{17,1},{25,9},{2,18},{10... | collective-permute-start | bytes 233480 | tf_op jit(solution)/shard_map/ppermute | solution.py:19
  34.5 6.6 %collective-permute-start.12 = (s16[64,2176]{1,0:T(8,128)(2,1)S(1)}, s16[64,2176]{1,0:T(8,128)(2,1)S(1)}, u32[]{:S(2)}, u32[]{:S(2)}) collective-permute-start(s16[64,2176]{1,0:T(8,128)(2,1)S(1)} %get-tuple-element.41.coded_ref), channel_id=1, source_target_pairs={{0,8},{1,2},{2,1},{3,4},{4,3},{5,6},{6,5},{7,15},{8,0},{9,10},{10,... | collective-permute-start | bytes 835592 | tf_op jit(solution)/shard_map/ppermute | solution.py:39
  35.9 1.7 %collective-permute-start.11 = (s16[64,2144]{1,0:T(8,128)(2,1)S(1)}, s16[64,2144]{1,0:T(8,128)(2,1)S(1)}, u32[]{:S(2)}, u32[]{:S(2)}) collective-permute-start(s16[64,2144]{1,0:T(8,128)(2,1)S(1)} %get-tuple-element.42), channel_id=1, source_target_pairs={{0,1},{1,0},{2,3},{3,2},{4,5},{5,4},{6,7},{7,6},{8,9},{9,8},{10,11... | collective-permute-start | bytes 823304 | tf_op jit(solution)/shard_map/ppermute | solution.py:19
  37.9 7.1 %collective-permute-start.14 = (s16[64,2176]{1,0:T(8,128)(2,1)S(1)}, s16[64,2176]{1,0:T(8,128)(2,1)S(1)}, u32[]{:S(2)}, u32[]{:S(2)}) collective-permute-start(s16[64,2176]{1,0:T(8,128)(2,1)S(1)} %shard_map.67), channel_id=1, source_target_pairs={{0,1},{1,3},{2,0},{3,5},{4,2},{5,7},{6,4},{7,6},{8,9},{9,11},{10,8... | collective-permute-start | bytes 835592 | tf_op jit(solution)/shard_map/ppermute | solution.py:28
  41.4 19.2 %copy-start.3 = (f32[64]{0:T(128)S(1)}, f32[64]{0:T(128)}, u32[]{:S(2)}) copy-start(f32[64]{0:T(128)} %param.7) | copy-start | bytes 772
  41.4 5.2 %collective-permute-start.13 = (s16[64,2176]{1,0:T(8,128)(2,1)S(1)}, s16[64,2176]{1,0:T(8,128)(2,1)S(1)}, u32[]{:S(2)}, u32[]{:S(2)}) collective-permute-start(s16[64,2176]{1,0:T(8,128)(2,1)S(1)} %shard_map.66), channel_id=1, source_target_pairs={{0,2},{1,0},{2,4},{3,1},{4,6},{5,3},{6,7},{7,5},{8,10},{9,8},{10,1... | collective-permute-start | bytes 835592 | tf_op jit(solution)/shard_map/ppermute | solution.py:28
  47.5 7.7 %collective-permute-start.17 = (s16[64,640]{1,0:T(8,128)(2,1)S(1)}, s16[64,640]{1,0:T(8,128)(2,1)S(1)}, u32[]{:S(2)}, u32[]{:S(2)}) collective-permute-start(s16[64,640]{1,0:T(8,128)(2,1)S(1)} %get-tuple-element.43.z0), channel_id=1, source_target_pairs={{0,24},{8,16},{16,8},{24,0},{1,25},{9,17},{17,9},{25,1},{2,26},{10... | collective-permute-start | bytes 245768 | tf_op jit(solution)/shard_map/ppermute | solution.py:19
  49.4 5.3 %collective-permute-start.15 = (s16[64,608]{1,0:T(8,128)(2,1)S(1)}, s16[64,608]{1,0:T(8,128)(2,1)S(1)}, u32[]{:S(2)}, u32[]{:S(2)}) collective-permute-start(s16[64,608]{1,0:T(8,128)(2,1)S(1)} %get-tuple-element.44), channel_id=1, source_target_pairs={{0,8},{8,0},{16,24},{24,16},{1,9},{9,1},{17,25},{25,17},{2,10},{10... | collective-permute-start | bytes 233480 | tf_op jit(solution)/shard_map/ppermute | solution.py:19
  50.0 5.2 %collective-permute-start.16 = (s16[64,608]{1,0:T(8,128)(2,1)S(1)}, s16[64,608]{1,0:T(8,128)(2,1)S(1)}, u32[]{:S(2)}, u32[]{:S(2)}) collective-permute-start(s16[64,608]{1,0:T(8,128)(2,1)S(1)} %get-tuple-element.44), channel_id=1, source_target_pairs={{0,16},{8,24},{16,0},{24,8},{1,17},{9,25},{17,1},{25,9},{2,18},{10... | collective-permute-start | bytes 233480 | tf_op jit(solution)/shard_map/ppermute | solution.py:19
  55.5 1.2 %collective-permute-start.18 = (f32[8,128]{1,0:T(8,128)S(1)}, f32[8,128]{1,0:T(8,128)S(1)}, u32[]{:S(2)}, u32[]{:S(2)}) collective-permute-start(f32[8,128]{1,0:T(8,128)S(1)} %shard_map.69), channel_id=1, source_target_pairs={{0,1},{1,0},{2,3},{3,2},{4,5},{5,4},{6,7},{7,6},{8,9},{9,8},{10,11... | collective-permute-start | bytes 12296 | tf_op jit(solution)/shard_map/ppermute | solution.py:19
  56.7 6.9 %collective-permute-start.21 = (f32[8,128]{1,0:T(8,128)S(1)}, f32[8,128]{1,0:T(8,128)S(1)}, u32[]{:S(2)}, u32[]{:S(2)}) collective-permute-start(f32[8,128]{1,0:T(8,128)S(1)} %add.5.p0), channel_id=1, source_target_pairs={{0,7},{1,6},{2,5},{3,4},{4,3},{5,2},{6,1},{7,0},{8,15},{9,14},{10,... | collective-permute-start | bytes 12296 | tf_op jit(solution)/shard_map/ppermute | solution.py:19
  59.5 3.0 %collective-permute-start.19 = (f32[4,128]{1,0:T(4,128)S(1)}, f32[4,128]{1,0:T(4,128)S(1)}, u32[]{:S(2)}, u32[]{:S(2)}) collective-permute-start(f32[4,128]{1,0:T(4,128)S(1)} %slice.6), channel_id=1, source_target_pairs={{0,3},{1,2},{2,1},{3,0},{4,7},{5,6},{6,5},{7,4},{8,11},{9,10},{10,... | collective-permute-start | bytes 6152 | tf_op jit(solution)/shard_map/ppermute | solution.py:19
  59.6 3.9 %collective-permute-start.20 = (f32[6,128]{1,0:T(8,128)S(1)}, f32[6,128]{1,0:T(8,128)S(1)}, u32[]{:S(2)}, u32[]{:S(2)}) collective-permute-start(f32[6,128]{1,0:T(8,128)S(1)} %bitcast.9), channel_id=1, source_target_pairs={{0,5},{1,4},{2,7},{3,6},{4,1},{5,0},{6,3},{7,2},{8,13},{9,12},{10,... | collective-permute-start | bytes 9224 | tf_op jit(solution)/shard_map/ppermute | solution.py:19

commit v12 on v11

--- a/solution.py
+++ b/solution.py
@@ -10,9 +10,10 @@
 
 AUX = 128
 LESS = 96
+LEAST = 64
 CHUNK = 512
 UNIT = 14
-ROWS = 128
+ROWS = 256
 
 
 def swap(value, axis, bits):
@@ -207,36 +208,39 @@
     finish(sent_ref, sent, width)
 
 
-def window_kernel(samples, count, own_ref, coded_ref, partner_ref, next_ref, same_ref, cross_ref, scaled_ref, sent_ref, brief_ref):
-    odd, side, across = place(count)
+def early_kernel(count, own_ref, coded_ref, partner_ref, next_ref, early_ref):
+    odd, side, _ = place(count)
     width = aux(coded_ref)[1]
     partner_exponent, partner_width = aux(partner_ref)[:2]
     next_exponent, next_width = aux(next_ref)[:2]
     partner_scale = unit(partner_exponent, jnp.where(odd, partner_width, width) >= 1)
     next_scale = jnp.where(jnp.where(odd, width, next_width) >= 1, unit(next_exponent, side), 0.0)
+    for k in range(0, own_ref.shape[1], CHUNK):
+        early_ref[:, pl.ds(k, CHUNK)] = (
+            own_ref[:, pl.ds(k, CHUNK)]
+            + values(partner_ref, k) * partner_scale
+            + values(next_ref, k) * next_scale
+        )
+
+
+def window_kernel(samples, count, own_ref, early_ref, same_ref, cross_ref, scaled_ref, *sent_refs):
+    _, side, across = place(count)
     same_scale = unit(aux(same_ref)[0], side)
     cross_scale = unit(aux(cross_ref)[0], across)
     rows = own_ref.shape[0]
     acc = jnp.zeros((2 * rows, scaled_ref.shape[1]), jnp.float32)
     curved = jnp.zeros((rows, CHUNK), jnp.float32)
     for k in range(0, own_ref.shape[1], CHUNK):
-        own = own_ref[:, pl.ds(k, CHUNK)]
-        mixed = (
-            own
-            + values(partner_ref, k) * partner_scale
-            + values(next_ref, k) * next_scale
-            + values(same_ref, k) * same_scale
-            + values(cross_ref, k) * cross_scale
-        )
+        mixed = early_ref[:, pl.ds(k, CHUNK)] + values(same_ref, k) * same_scale + values(cross_ref, k) * cross_scale
         acc = acc + jnp.dot(
             two_terms(mixed), scaled_ref[pl.ds(k, CHUNK)], preferred_element_type=jnp.float32
         )
-        curved = curved + own * mixed
+        curved = curved + own_ref[:, pl.ds(k, CHUNK)] * mixed
     z = acc[:rows] + acc[rows:]
     exponent, scale = scale_of(jnp.max(jnp.abs(z), 1, keepdims=True))
     columns = exponent, *split(jnp.sum(curved, 1, keepdims=True) / samples)
     z = fixed(z * scale)
-    for ref in (sent_ref, brief_ref):
+    for ref in sent_refs:
         ref[:, pl.ds(0, z.shape[1])] = z
         finish(ref, *columns)
 
@@ -252,7 +256,11 @@
     flat_ref[...] = filled.T[:8]
 
 
-def last_kernel(samples, shrink_ref, p0, p1, p2, p3, z0, z1, z2, z3, start_ref, first_ref, effects_ref, residual_ref):
+def second_kernel(samples, z0, z1, z2, z3, second_ref):
+    second_ref[...] = total([grid_values(z) for z in (z0, z1, z2, z3)]) / samples
+
+
+def last_kernel(shrink_ref, p0, p1, p2, p3, second_ref, start_ref, first_ref, effects_ref, residual_ref):
     rows = start_ref.shape[0]
     flat = total([p[0:4] for p in (p0, p1, p2, p3)])
     bb, bw, ww, wu = (flat[k : k + 1] for k in range(4))
@@ -280,8 +288,7 @@
     e_start, e_first, r_start, r_first, r_second = (table[:, k : k + 1] for k in range(5))
     start, first = start_ref[...], first_ref[...]
     effects_ref[...] = e_start * start + e_first * first
-    second = total([grid_values(z) for z in (z0, z1, z2, z3)]) / samples
-    residual_ref[...] = r_start * start + r_first * first + r_second * second
+    residual_ref[...] = r_start * start + r_first * first + r_second * second_ref[...]
 
 
 def snp_parts(value):
@@ -310,7 +317,7 @@
     own_out, coded_out = (own_shape, jnp.float32), ((rows, local + AUX), jnp.int16)
     shared_out = ((rows, local + LESS), jnp.int16)
 
-    sent_out, brief_out = ((rows, size + AUX), jnp.int16), ((rows, size + LESS), jnp.int16)
+    sent_outs = [((rows, size + lanes), jnp.int16) for lanes in (AUX, LESS, LEAST)]
 
     sums, brief = call(stats_kernel, [((8, size), jnp.float32), ((2, size), jnp.float32)], dosage)
     one, two, three = swap(brief, "samp", 1), swap(brief, "samp", 2), swap(sums, "samp", 3)
@@ -338,11 +345,12 @@
         partner = swap(shared, "snp", 1)
         cross = crossing(give(1, own, coded, partner), 1)
         same = crossing(give(0, own, coded, beside), 0)
-        z, brief = call(
-            functools.partial(window_kernel, samples, count), [sent_out, brief_out],
-            own, coded, partner, beside, same, cross, scaled,
+        (early,) = call(functools.partial(early_kernel, count), [own_out], own, coded, partner, beside)
+        z, brief, least = call(
+            functools.partial(window_kernel, samples, count), sent_outs,
+            own, early, same, cross, scaled,
         )
-        return [z, swap(brief, "samp", 1), swap(brief, "samp", 2), swap(z, "samp", 3)]
+        return [z, swap(brief, "samp", 1), swap(least, "samp", 2), swap(z, "samp", 3)]
 
     first, parts, own, coded, shared = call(
         functools.partial(next_kernel, samples),
@@ -352,10 +360,11 @@
     zs = window(own, coded, shared)
     (flat,) = call(collect_kernel, [((8, AUX), jnp.float32)], parts, *zs)
     parts = snp_parts(flat)
+    (second,) = call(functools.partial(second_kernel, samples), [(grid, jnp.float32)], *zs)
     effects, residual = call(
-        functools.partial(last_kernel, samples),
+        last_kernel,
         [(grid, jnp.float32), (grid, jnp.float32)],
-        shrink, *parts, *zs, start, first,
+        shrink, *parts, second, start, first,
     )
     return (effects.T, residual.T)
 

time: 64.7 us -> 64.3 us (level)
  waiting for transfers between devices: 32.3 us -> 31.6 us
    pallas_call x11 -> x14, Pallas kernels: 6.19 us -> 6.46 us  [call(): pl.pallas_call(body, out_shape=outs, in_specs=specs, out_specs=[pl.BlockS...]
  transfers between devices with their start and end apart: 22 -> 22, of which waited for: 17 -> 15; matrix products, arithmetic and copies ran while one was open for 0% -> 0% of each run, Pallas kernels for 2% -> 3%
where the time goes in v12:
time: 64.3 us; the launch traced here: 64.2 us
  waiting for transfers between devices  31.6 us (49%)
  starting transfers between devices  24 us (37%)
  Pallas kernels  7.07 us (11%)
  between operations  1.41 us (2%)
    ppermute x15, waiting for transfers between devices, swap(): lax.ppermute(value, axis, [(i, i ^ bits) for i in range(lax.axis_size(axi...  18.1 us
    ppermute x15, starting transfers between devices, swap(): lax.ppermute(value, axis, [(i, i ^ bits) for i in range(lax.axis_size(axi...  15.3 us
    ppermute x4, waiting for transfers between devices, crossing(): return lax.ppermute(value, 'snp', pairs)  7.62 us
    pallas_call x14, Pallas kernels, call(): pl.pallas_call(body, out_shape=outs, in_specs=specs, out_specs=[pl.BlockS...  6.46 us
    ppermute x2, waiting for transfers between devices, adjacent(): return lax.ppermute(value, ('samp', 'snp'), pairs)  5.88 us
    ppermute x1, starting transfers between devices, shifted(): lax.ppermute(value, 'snp', [(i, (i + 2) % count) for i in range(count)])  3.02 us
    ppermute x2, starting transfers between devices, adjacent(): return lax.ppermute(value, ('samp', 'snp'), pairs)  2.94 us
    ppermute x4, starting transfers between devices, crossing(): return lax.ppermute(value, 'snp', pairs)  2.79 us
  transfers between devices with their start and end apart: 22, of which 15 were waited for; matrix products, arithmetic and copies ran while one was open for 0% of the time, Pallas kernels for 3%

profile of v12, /device:TPU:0, one launch (start us, length us, event | category | flops | bytes accessed | tf_op | source)
XLA Modules:
  0.0 64.2 jit_solution(5447784375289905306)
XLA Ops:
  1.3 0.0 copy-start
  1.3 0.6 shard_map.60.wide_ref
  1.9 3.0 %collective-permute-start.3 = (f32[8,640]{1,0:T(8,128)}, f32[8,640]{1,0:T(8,128)S(1)}, u32[]{:S(2)}, u32[]{:S(2)}) collective-permute-start(f32[8,640]{1,0:T(8,128)} %shard_map.60.wide_ref), channel_id=1, source_target_pairs={{0,2},{1,3},{2,4},{3,5},{4,6},{5,7},{6,0},{7,1},{8,10},{9,11},{10,... | collective-permute-start | bytes 61448 | tf_op jit(solution)/shard_map/ppermute | solution.py:45
  4.9 0.0 copy-done
  4.9 0.4 shard_map.59
  5.3 2.5 %collective-permute-start.2 = (f32[8,512]{1,0:T(8,128)S(1)}, f32[8,512]{1,0:T(8,128)S(1)}, u32[]{:S(2)}, u32[]{:S(2)}) collective-permute-start(f32[8,512]{1,0:T(8,128)S(1)} %get-tuple-element.29.s0), channel_id=1, source_target_pairs={{0,24},{8,16},{16,8},{24,0},{1,25},{9,17},{17,9},{25,1},{2,26},{10... | collective-permute-start | bytes 49160 | tf_op jit(solution)/shard_map/ppermute | solution.py:20
  7.8 0.5 collective-permute-start
  8.3 0.5 collective-permute-start.1
  8.9 2.6 %collective-permute-done.s1 = f32[2,512]{1,0:T(2,128)S(1)} collective-permute-done((f32[2,512]{1,0:T(2,128)S(1)}, f32[2,512]{1,0:T(2,128)S(1)}, u32[]{:S(2)}, u32[]{:S(2)}) %collective-permute-start) | collective-permute-done | bytes 4128 | tf_op jit(solution)/shard_map/ppermute | solution.py:20
  11.4 0.5 collective-permute-done.1.s2
  12.0 0.0 collective-permute-done.2.s3
  12.0 0.0 collective-permute-done.3.near_ref
  12.0 0.0 copy-done.1
  12.0 0.0 copy-done.2
  12.0 1.1 %shard_map.61 = (bf16[2048,512]{1,0:T(8,128)(2,1)S(1)}, bf16[512,2048]{1,0:T(8,128)(2,1)S(1)}, f32[64,2048]{1,0:T(8,128)S(1)}, s16[64,2176]{1,0:T(8,128)(2,1)S(1)}, s16[64,2144]{1,0:T(8,128)(2,1)S(1)}) custom-call(f32[8,640]{1,0:T(8,128)S(1)} %copy-done.2, f32[8,512]{1,0:T(8,128)S(1)} %get-tuple-element.29.s0, f32[2,512]{1,0:T(2,128)S(1)} %collective-permute-done.s1, ...), custom_call_target="tpu_custom_call" | custom-call | tf_op jit(solution)/shard_map/pallas_call | solution.py:60
  13.1 1.6 %collective-permute-start.5 = (s16[64,2176]{1,0:T(8,128)(2,1)S(1)}, s16[64,2176]{1,0:T(8,128)(2,1)S(1)}, u32[]{:S(2)}, u32[]{:S(2)}) collective-permute-start(s16[64,2176]{1,0:T(8,128)(2,1)S(1)} %get-tuple-element.34.coded_ref), channel_id=1, source_target_pairs={{0,8},{1,2},{2,1},{3,4},{4,3},{5,6},{6,5},{7,15},{8,0},{9,10},{10,... | collective-permute-start | bytes 835592 | tf_op jit(solution)/shard_map/ppermute | solution.py:40
  14.6 0.2 collective-permute-start.4
  14.8 1.4 %collective-permute-done.4.partner_ref.other_ref = s16[64,2144]{1,0:T(8,128)(2,1)S(1)} collective-permute-done((s16[64,2144]{1,0:T(8,128)(2,1)S(1)}, s16[64,2144]{1,0:T(8,128)(2,1)S(1)}, u32[]{:S(2)}, u32[]{:S(2)}) %collective-permute-start.4) | collective-permute-done | bytes 274464 | tf_op jit(solution)/shard_map/ppermute | solution.py:20
  16.2 0.3 shard_map.64
  16.5 0.2 collective-permute-start.7
  16.7 3.0 %collective-permute-done.5.next_ref.other_ref = s16[64,2176]{1,0:T(8,128)(2,1)S(1)} collective-permute-done((s16[64,2176]{1,0:T(8,128)(2,1)S(1)}, s16[64,2176]{1,0:T(8,128)(2,1)S(1)}, u32[]{:S(2)}, u32[]{:S(2)}) %collective-permute-start.5) | collective-permute-done | bytes 278560 | tf_op jit(solution)/shard_map/ppermute | solution.py:40
  19.7 0.3 shard_map.63
  19.9 1.0 %collective-permute-start.6 = (s16[64,2176]{1,0:T(8,128)(2,1)S(1)}, s16[64,2176]{1,0:T(8,128)(2,1)S(1)}, u32[]{:S(2)}, u32[]{:S(2)}) collective-permute-start(s16[64,2176]{1,0:T(8,128)(2,1)S(1)} %shard_map.63), channel_id=1, source_target_pairs={{0,2},{1,0},{2,4},{3,1},{4,6},{5,3},{6,7},{7,5},{8,10},{9,8},{10,1... | collective-permute-start | bytes 835592 | tf_op jit(solution)/shard_map/ppermute | solution.py:29
  21.0 0.2 shard_map.62.early_ref
  21.2 2.5 %collective-permute-done.7.cross_ref = s16[64,2176]{1,0:T(8,128)(2,1)S(1)} collective-permute-done((s16[64,2176]{1,0:T(8,128)(2,1)S(1)}, s16[64,2176]{1,0:T(8,128)(2,1)S(1)}, u32[]{:S(2)}, u32[]{:S(2)}) %collective-permute-start.7) | collective-permute-done | bytes 278560 | tf_op jit(solution)/shard_map/ppermute | solution.py:29
  23.7 1.3 %collective-permute-done.6.same_ref = s16[64,2176]{1,0:T(8,128)(2,1)S(1)} collective-permute-done((s16[64,2176]{1,0:T(8,128)(2,1)S(1)}, s16[64,2176]{1,0:T(8,128)(2,1)S(1)}, u32[]{:S(2)}, u32[]{:S(2)}) %collective-permute-start.6) | collective-permute-done | bytes 278560 | tf_op jit(solution)/shard_map/ppermute | solution.py:29
  25.0 0.7 %shard_map.65 = (s16[64,640]{1,0:T(8,128)(2,1)S(1)}, s16[64,608]{1,0:T(8,128)(2,1)S(1)}, s16[64,576]{1,0:T(8,128)(2,1)S(1)}) custom-call(f32[64,2048]{1,0:T(8,128)S(1)} %get-tuple-element.33.own_ref, f32[64,2048]{1,0:T(8,128)S(1)} %shard_map.62.early_ref, s16[64,2176]{1,0:T(8,128)(2,1)S(1)} %collective-permute-done.6.same_ref, ...), custom_call_target="tpu_custom_call" | custom-call | tf_op jit(solution)/shard_map/pallas_call | solution.py:60
  25.8 1.5 %collective-permute-start.10 = (s16[64,640]{1,0:T(8,128)(2,1)S(1)}, s16[64,640]{1,0:T(8,128)(2,1)S(1)}, u32[]{:S(2)}, u32[]{:S(2)}) collective-permute-start(s16[64,640]{1,0:T(8,128)(2,1)S(1)} %get-tuple-element.38.z0), channel_id=1, source_target_pairs={{0,24},{8,16},{16,8},{24,0},{1,25},{9,17},{17,9},{25,1},{2,26},{10... | collective-permute-start | bytes 245768 | tf_op jit(solution)/shard_map/ppermute | solution.py:20
  27.3 0.5 collective-permute-start.8
  27.8 1.5 %collective-permute-start.9 = (s16[64,576]{1,0:T(8,128)(2,1)S(1)}, s16[64,576]{1,0:T(8,128)(2,1)S(1)}, u32[]{:S(2)}, u32[]{:S(2)}) collective-permute-start(s16[64,576]{1,0:T(8,128)(2,1)S(1)} %get-tuple-element.40), channel_id=1, source_target_pairs={{0,16},{8,24},{16,0},{24,8},{1,17},{9,25},{17,1},{25,9},{2,18},{10... | collective-permute-start | bytes 221192 | tf_op jit(solution)/shard_map/ppermute | solution.py:20
  29.3 4.3 %collective-permute-done.9.z2 = s16[64,576]{1,0:T(8,128)(2,1)S(1)} collective-permute-done((s16[64,576]{1,0:T(8,128)(2,1)S(1)}, s16[64,576]{1,0:T(8,128)(2,1)S(1)}, u32[]{:S(2)}, u32[]{:S(2)}) %collective-permute-start.9) | collective-permute-done | bytes 73760 | tf_op jit(solution)/shard_map/ppermute | solution.py:20
  33.6 0.0 collective-permute-done.8.z1
  33.6 0.0 collective-permute-done.10.z3
  33.6 0.7 %shard_map.66 = (f32[64,512]{1,0:T(8,128)S(1)}, f32[64,128]{1,0:T(8,128)S(1)}, f32[64,2048]{1,0:T(8,128)S(1)}, s16[64,2176]{1,0:T(8,128)(2,1)S(1)}, s16[64,2144]{1,0:T(8,128)(2,1)S(1)}) custom-call(f32[8,640]{1,0:T(8,128)S(1)} %copy-done.2, s16[64,640]{1,0:T(8,128)(2,1)S(1)} %get-tuple-element.38.z0, s16[64,608]{1,0:T(8,128)(2,1)S(1)} %collective-permute-done.8.z1, ...), custom_call_target="tpu_custom_call" | custom-call | tf_op jit(solution)/shard_map/pallas_call | solution.py:60
  34.3 1.4 %collective-permute-start.12 = (s16[64,2176]{1,0:T(8,128)(2,1)S(1)}, s16[64,2176]{1,0:T(8,128)(2,1)S(1)}, u32[]{:S(2)}, u32[]{:S(2)}) collective-permute-start(s16[64,2176]{1,0:T(8,128)(2,1)S(1)} %get-tuple-element.44.coded_ref), channel_id=1, source_target_pairs={{0,8},{1,2},{2,1},{3,4},{4,3},{5,6},{6,5},{7,15},{8,0},{9,10},{10,... | collective-permute-start | bytes 835592 | tf_op jit(solution)/shard_map/ppermute | solution.py:40
  35.7 0.5 collective-permute-start.11
  36.2 1.2 %collective-permute-done.11.partner_ref.other_ref = s16[64,2144]{1,0:T(8,128)(2,1)S(1)} collective-permute-done((s16[64,2144]{1,0:T(8,128)(2,1)S(1)}, s16[64,2144]{1,0:T(8,128)(2,1)S(1)}, u32[]{:S(2)}, u32[]{:S(2)}) %collective-permute-start.11) | collective-permute-done | bytes 274464 | tf_op jit(solution)/shard_map/ppermute | solution.py:20
  37.4 0.3 shard_map.69
  37.7 0.4 collective-permute-start.14
  38.1 2.9 %collective-permute-done.12.next_ref.other_ref = s16[64,2176]{1,0:T(8,128)(2,1)S(1)} collective-permute-done((s16[64,2176]{1,0:T(8,128)(2,1)S(1)}, s16[64,2176]{1,0:T(8,128)(2,1)S(1)}, u32[]{:S(2)}, u32[]{:S(2)}) %collective-permute-start.12) | collective-permute-done | bytes 278560 | tf_op jit(solution)/shard_map/ppermute | solution.py:40
  40.9 0.3 shard_map.68
  41.2 1.2 %collective-permute-start.13 = (s16[64,2176]{1,0:T(8,128)(2,1)S(1)}, s16[64,2176]{1,0:T(8,128)(2,1)S(1)}, u32[]{:S(2)}, u32[]{:S(2)}) collective-permute-start(s16[64,2176]{1,0:T(8,128)(2,1)S(1)} %shard_map.68), channel_id=1, source_target_pairs={{0,2},{1,0},{2,4},{3,1},{4,6},{5,3},{6,7},{7,5},{8,10},{9,8},{10,1... | collective-permute-start | bytes 835592 | tf_op jit(solution)/shard_map/ppermute | solution.py:29
  42.3 0.2 shard_map.67.early_ref
  42.6 0.0 copy-start.3
  42.6 2.2 %collective-permute-done.14.cross_ref = s16[64,2176]{1,0:T(8,128)(2,1)S(1)} collective-permute-done((s16[64,2176]{1,0:T(8,128)(2,1)S(1)}, s16[64,2176]{1,0:T(8,128)(2,1)S(1)}, u32[]{:S(2)}, u32[]{:S(2)}) %collective-permute-start.14) | collective-permute-done | bytes 278560 | tf_op jit(solution)/shard_map/ppermute | solution.py:29
  44.8 1.6 %collective-permute-done.13.same_ref = s16[64,2176]{1,0:T(8,128)(2,1)S(1)} collective-permute-done((s16[64,2176]{1,0:T(8,128)(2,1)S(1)}, s16[64,2176]{1,0:T(8,128)(2,1)S(1)}, u32[]{:S(2)}, u32[]{:S(2)}) %collective-permute-start.13) | collective-permute-done | bytes 278560 | tf_op jit(solution)/shard_map/ppermute | solution.py:29
  46.4 0.7 %shard_map.70 = (s16[64,640]{1,0:T(8,128)(2,1)S(1)}, s16[64,608]{1,0:T(8,128)(2,1)S(1)}, s16[64,576]{1,0:T(8,128)(2,1)S(1)}) custom-call(f32[64,2048]{1,0:T(8,128)S(1)} %get-tuple-element.43.own_ref, f32[64,2048]{1,0:T(8,128)S(1)} %shard_map.67.early_ref, s16[64,2176]{1,0:T(8,128)(2,1)S(1)} %collective-permute-done.13.same_ref, ...), custom_call_target="tpu_custom_call" | custom-call | tf_op jit(solution)/shard_map/pallas_call | solution.py:60
  47.2 1.9 %collective-permute-start.17 = (s16[64,640]{1,0:T(8,128)(2,1)S(1)}, s16[64,640]{1,0:T(8,128)(2,1)S(1)}, u32[]{:S(2)}, u32[]{:S(2)}) collective-permute-start(s16[64,640]{1,0:T(8,128)(2,1)S(1)} %get-tuple-element.46.z0), channel_id=1, source_target_pairs={{0,24},{8,16},{16,8},{24,0},{1,25},{9,17},{17,9},{25,1},{2,26},{10... | collective-permute-start | bytes 245768 | tf_op jit(solution)/shard_map/ppermute | solution.py:20
  49.1 0.5 collective-permute-start.15
  49.6 1.1 %collective-permute-start.16 = (s16[64,576]{1,0:T(8,128)(2,1)S(1)}, s16[64,576]{1,0:T(8,128)(2,1)S(1)}, u32[]{:S(2)}, u32[]{:S(2)}) collective-permute-start(s16[64,576]{1,0:T(8,128)(2,1)S(1)} %get-tuple-element.48), channel_id=1, source_target_pairs={{0,16},{8,24},{16,0},{24,8},{1,17},{9,25},{17,1},{25,9},{2,18},{10... | collective-permute-start | bytes 221192 | tf_op jit(solution)/shard_map/ppermute | solution.py:20
  50.7 4.1 %collective-permute-done.16.z2 = s16[64,576]{1,0:T(8,128)(2,1)S(1)} collective-permute-done((s16[64,576]{1,0:T(8,128)(2,1)S(1)}, s16[64,576]{1,0:T(8,128)(2,1)S(1)}, u32[]{:S(2)}, u32[]{:S(2)}) %collective-permute-start.16) | collective-permute-done | bytes 73760 | tf_op jit(solution)/shard_map/ppermute | solution.py:20
  54.9 0.0 collective-permute-done.15.z1
  54.9 0.0 collective-permute-done.17.z3
  54.9 0.2 shard_map.71
  55.1 0.0 collective-permute-start.18
  55.2 1.2 %collective-permute-done.18 = f32[8,128]{1,0:T(8,128)S(1)} collective-permute-done((f32[8,128]{1,0:T(8,128)S(1)}, f32[8,128]{1,0:T(8,128)S(1)}, u32[]{:S(2)}, u32[]{:S(2)}) %collective-permute-start.18) | collective-permute-done | bytes 4128 | tf_op jit(solution)/shard_map/ppermute | solution.py:20
  56.3 2.9 %collective-permute-start.21 = (f32[8,128]{1,0:T(8,128)S(1)}, f32[8,128]{1,0:T(8,128)S(1)}, u32[]{:S(2)}, u32[]{:S(2)}) collective-permute-start(f32[8,128]{1,0:T(8,128)S(1)} %add.5.p0), channel_id=1, source_target_pairs={{0,7},{1,6},{2,5},{3,4},{4,3},{5,2},{6,1},{7,0},{8,15},{9,14},{10,... | collective-permute-start | bytes 12296 | tf_op jit(solution)/shard_map/ppermute | solution.py:20
  59.2 0.1 collective-permute-start.19
  59.3 0.9 %collective-permute-start.20 = (f32[6,128]{1,0:T(8,128)S(1)}, f32[6,128]{1,0:T(8,128)S(1)}, u32[]{:S(2)}, u32[]{:S(2)}) collective-permute-start(f32[6,128]{1,0:T(8,128)S(1)} %bitcast.9), channel_id=1, source_target_pairs={{0,5},{1,4},{2,7},{3,6},{4,1},{5,0},{6,3},{7,2},{8,13},{9,12},{10,... | collective-permute-start | bytes 9224 | tf_op jit(solution)/shard_map/ppermute | solution.py:20
  60.2 0.1 shard_map.72.second_ref
  60.3 1.9 %collective-permute-done.19.p1 = f32[4,128]{1,0:T(4,128)S(1)} collective-permute-done((f32[4,128]{1,0:T(4,128)S(1)}, f32[4,128]{1,0:T(4,128)S(1)}, u32[]{:S(2)}, u32[]{:S(2)}) %collective-permute-start.19) | collective-permute-done | bytes 2080 | tf_op jit(solution)/shard_map/ppermute | solution.py:20
  62.2 1.0 %collective-permute-done.20.p2 = f32[6,128]{1,0:T(8,128)S(1)} collective-permute-done((f32[6,128]{1,0:T(8,128)S(1)}, f32[6,128]{1,0:T(8,128)S(1)}, u32[]{:S(2)}, u32[]{:S(2)}) %collective-permute-start.20) | collective-permute-done | bytes 3104 | tf_op jit(solution)/shard_map/ppermute | solution.py:20
  63.2 0.0 collective-permute-done.21.p3
  63.2 1.0 %shard_map.73 = (f32[64,512]{1,0:T(8,128)}, f32[64,512]{1,0:T(8,128)}) custom-call(f32[1,128]{1,0:T(1,128)S(1)} %pad_bitcast_fusion.shrink_ref, f32[8,128]{1,0:T(8,128)S(1)} %add.5.p0, f32[4,128]{1,0:T(4,128)S(1)} %collective-permute-done.19.p1, f32[6,128]{1,0:T(8,128)S(1)} %collective-permute-done.20.p2, f32[8,128]{1,0:T(8,128)S(1)} %collective-permute-done.21.p3, ...), custom_call_target="tpu_custom_call" | custom-call | tf_op jit(solution)/shard_map/pallas_call | solution.py:60
  (6 shorter events, 0.0 us)
Async XLA Ops:
  1.3 3.7 %copy-start = (bf16[2048,512]{1,0:T(8,128)(2,1)S(1)}, bf16[2048,512]{1,0:T(8,128)(2,1)}, u32[]{:S(2)}) copy-start(bf16[2048,512]{1,0:T(8,128)(2,1)} %dosage_ref.3) | copy-start | bytes 6291460
  1.9 10.1 %copy-start.1 = (f32[512,64]{0,1:T(8,128)S(1)}, f32[512,64]{0,1:T(8,128)}, u32[]{:S(2)}) copy-start(f32[512,64]{0,1:T(8,128)} %param.6) | copy-start | bytes 393220
  1.9 10.1 %copy-start.2 = (f32[8,640]{1,0:T(8,128)S(1)}, f32[8,640]{1,0:T(8,128)}, u32[]{:S(2)}) copy-start(f32[8,640]{1,0:T(8,128)} %shard_map.60.wide_ref) | copy-start | bytes 61444
  1.9 10.1 %collective-permute-start.3 = (f32[8,640]{1,0:T(8,128)}, f32[8,640]{1,0:T(8,128)S(1)}, u32[]{:S(2)}, u32[]{:S(2)}) collective-permute-start(f32[8,640]{1,0:T(8,128)} %shard_map.60.wide_ref), channel_id=1, source_target_pairs={{0,2},{1,3},{2,4},{3,5},{4,6},{5,7},{6,0},{7,1},{8,10},{9,11},{10,... | collective-permute-start | bytes 61448 | tf_op jit(solution)/shard_map/ppermute | solution.py:45
  5.3 6.7 %collective-permute-start.2 = (f32[8,512]{1,0:T(8,128)S(1)}, f32[8,512]{1,0:T(8,128)S(1)}, u32[]{:S(2)}, u32[]{:S(2)}) collective-permute-start(f32[8,512]{1,0:T(8,128)S(1)} %get-tuple-element.29.s0), channel_id=1, source_target_pairs={{0,24},{8,16},{16,8},{24,0},{1,25},{9,17},{17,9},{25,1},{2,26},{10... | collective-permute-start | bytes 49160 | tf_op jit(solution)/shard_map/ppermute | solution.py:20
  7.8 3.6 %collective-permute-start = (f32[2,512]{1,0:T(2,128)S(1)}, f32[2,512]{1,0:T(2,128)S(1)}, u32[]{:S(2)}, u32[]{:S(2)}) collective-permute-start(f32[2,512]{1,0:T(2,128)S(1)} %get-tuple-element.27), channel_id=1, source_target_pairs={{0,8},{8,0},{16,24},{24,16},{1,9},{9,1},{17,25},{25,17},{2,10},{10... | collective-permute-start | bytes 12296 | tf_op jit(solution)/shard_map/ppermute | solution.py:20
  8.3 3.6 %collective-permute-start.1 = (f32[2,512]{1,0:T(2,128)S(1)}, f32[2,512]{1,0:T(2,128)S(1)}, u32[]{:S(2)}, u32[]{:S(2)}) collective-permute-start(f32[2,512]{1,0:T(2,128)S(1)} %get-tuple-element.27), channel_id=1, source_target_pairs={{0,16},{8,24},{16,0},{24,8},{1,17},{9,25},{17,1},{25,9},{2,18},{10... | collective-permute-start | bytes 12296 | tf_op jit(solution)/shard_map/ppermute | solution.py:20
  13.1 6.6 %collective-permute-start.5 = (s16[64,2176]{1,0:T(8,128)(2,1)S(1)}, s16[64,2176]{1,0:T(8,128)(2,1)S(1)}, u32[]{:S(2)}, u32[]{:S(2)}) collective-permute-start(s16[64,2176]{1,0:T(8,128)(2,1)S(1)} %get-tuple-element.34.coded_ref), channel_id=1, source_target_pairs={{0,8},{1,2},{2,1},{3,4},{4,3},{5,6},{6,5},{7,15},{8,0},{9,10},{10,... | collective-permute-start | bytes 835592 | tf_op jit(solution)/shard_map/ppermute | solution.py:40
  14.6 1.6 %collective-permute-start.4 = (s16[64,2144]{1,0:T(8,128)(2,1)S(1)}, s16[64,2144]{1,0:T(8,128)(2,1)S(1)}, u32[]{:S(2)}, u32[]{:S(2)}) collective-permute-start(s16[64,2144]{1,0:T(8,128)(2,1)S(1)} %get-tuple-element.35), channel_id=1, source_target_pairs={{0,1},{1,0},{2,3},{3,2},{4,5},{5,4},{6,7},{7,6},{8,9},{9,8},{10,11... | collective-permute-start | bytes 823304 | tf_op jit(solution)/shard_map/ppermute | solution.py:20
  16.5 7.3 %collective-permute-start.7 = (s16[64,2176]{1,0:T(8,128)(2,1)S(1)}, s16[64,2176]{1,0:T(8,128)(2,1)S(1)}, u32[]{:S(2)}, u32[]{:S(2)}) collective-permute-start(s16[64,2176]{1,0:T(8,128)(2,1)S(1)} %shard_map.64), channel_id=1, source_target_pairs={{0,1},{1,3},{2,0},{3,5},{4,2},{5,7},{6,4},{7,6},{8,9},{9,11},{10,8... | collective-permute-start | bytes 835592 | tf_op jit(solution)/shard_map/ppermute | solution.py:29
  19.9 5.1 %collective-permute-start.6 = (s16[64,2176]{1,0:T(8,128)(2,1)S(1)}, s16[64,2176]{1,0:T(8,128)(2,1)S(1)}, u32[]{:S(2)}, u32[]{:S(2)}) collective-permute-start(s16[64,2176]{1,0:T(8,128)(2,1)S(1)} %shard_map.63), channel_id=1, source_target_pairs={{0,2},{1,0},{2,4},{3,1},{4,6},{5,3},{6,7},{7,5},{8,10},{9,8},{10,1... | collective-permute-start | bytes 835592 | tf_op jit(solution)/shard_map/ppermute | solution.py:29
  25.8 7.9 %collective-permute-start.10 = (s16[64,640]{1,0:T(8,128)(2,1)S(1)}, s16[64,640]{1,0:T(8,128)(2,1)S(1)}, u32[]{:S(2)}, u32[]{:S(2)}) collective-permute-start(s16[64,640]{1,0:T(8,128)(2,1)S(1)} %get-tuple-element.38.z0), channel_id=1, source_target_pairs={{0,24},{8,16},{16,8},{24,0},{1,25},{9,17},{17,9},{25,1},{2,26},{10... | collective-permute-start | bytes 245768 | tf_op jit(solution)/shard_map/ppermute | solution.py:20
  27.3 6.4 %collective-permute-start.8 = (s16[64,608]{1,0:T(8,128)(2,1)S(1)}, s16[64,608]{1,0:T(8,128)(2,1)S(1)}, u32[]{:S(2)}, u32[]{:S(2)}) collective-permute-start(s16[64,608]{1,0:T(8,128)(2,1)S(1)} %get-tuple-element.39), channel_id=1, source_target_pairs={{0,8},{8,0},{16,24},{24,16},{1,9},{9,1},{17,25},{25,17},{2,10},{10... | collective-permute-start | bytes 233480 | tf_op jit(solution)/shard_map/ppermute | solution.py:20
  27.8 5.8 %collective-permute-start.9 = (s16[64,576]{1,0:T(8,128)(2,1)S(1)}, s16[64,576]{1,0:T(8,128)(2,1)S(1)}, u32[]{:S(2)}, u32[]{:S(2)}) collective-permute-start(s16[64,576]{1,0:T(8,128)(2,1)S(1)} %get-tuple-element.40), channel_id=1, source_target_pairs={{0,16},{8,24},{16,0},{24,8},{1,17},{9,25},{17,1},{25,9},{2,18},{10... | collective-permute-start | bytes 221192 | tf_op jit(solution)/shard_map/ppermute | solution.py:20
  34.3 6.6 %collective-permute-start.12 = (s16[64,2176]{1,0:T(8,128)(2,1)S(1)}, s16[64,2176]{1,0:T(8,128)(2,1)S(1)}, u32[]{:S(2)}, u32[]{:S(2)}) collective-permute-start(s16[64,2176]{1,0:T(8,128)(2,1)S(1)} %get-tuple-element.44.coded_ref), channel_id=1, source_target_pairs={{0,8},{1,2},{2,1},{3,4},{4,3},{5,6},{6,5},{7,15},{8,0},{9,10},{10,... | collective-permute-start | bytes 835592 | tf_op jit(solution)/shard_map/ppermute | solution.py:40
  35.7 1.7 %collective-permute-start.11 = (s16[64,2144]{1,0:T(8,128)(2,1)S(1)}, s16[64,2144]{1,0:T(8,128)(2,1)S(1)}, u32[]{:S(2)}, u32[]{:S(2)}) collective-permute-start(s16[64,2144]{1,0:T(8,128)(2,1)S(1)} %get-tuple-element.45), channel_id=1, source_target_pairs={{0,1},{1,0},{2,3},{3,2},{4,5},{5,4},{6,7},{7,6},{8,9},{9,8},{10,11... | collective-permute-start | bytes 823304 | tf_op jit(solution)/shard_map/ppermute | solution.py:20
  37.7 7.1 %collective-permute-start.14 = (s16[64,2176]{1,0:T(8,128)(2,1)S(1)}, s16[64,2176]{1,0:T(8,128)(2,1)S(1)}, u32[]{:S(2)}, u32[]{:S(2)}) collective-permute-start(s16[64,2176]{1,0:T(8,128)(2,1)S(1)} %shard_map.69), channel_id=1, source_target_pairs={{0,1},{1,3},{2,0},{3,5},{4,2},{5,7},{6,4},{7,6},{8,9},{9,11},{10,8... | collective-permute-start | bytes 835592 | tf_op jit(solution)/shard_map/ppermute | solution.py:29
  41.2 5.2 %collective-permute-start.13 = (s16[64,2176]{1,0:T(8,128)(2,1)S(1)}, s16[64,2176]{1,0:T(8,128)(2,1)S(1)}, u32[]{:S(2)}, u32[]{:S(2)}) collective-permute-start(s16[64,2176]{1,0:T(8,128)(2,1)S(1)} %shard_map.68), channel_id=1, source_target_pairs={{0,2},{1,0},{2,4},{3,1},{4,6},{5,3},{6,7},{7,5},{8,10},{9,8},{10,1... | collective-permute-start | bytes 835592 | tf_op jit(solution)/shard_map/ppermute | solution.py:29
  42.6 17.6 %copy-start.3 = (f32[64]{0:T(128)S(1)}, f32[64]{0:T(128)}, u32[]{:S(2)}) copy-start(f32[64]{0:T(128)} %param.7) | copy-start | bytes 772
  47.2 7.7 %collective-permute-start.17 = (s16[64,640]{1,0:T(8,128)(2,1)S(1)}, s16[64,640]{1,0:T(8,128)(2,1)S(1)}, u32[]{:S(2)}, u32[]{:S(2)}) collective-permute-start(s16[64,640]{1,0:T(8,128)(2,1)S(1)} %get-tuple-element.46.z0), channel_id=1, source_target_pairs={{0,24},{8,16},{16,8},{24,0},{1,25},{9,17},{17,9},{25,1},{2,26},{10... | collective-permute-start | bytes 245768 | tf_op jit(solution)/shard_map/ppermute | solution.py:20
  49.1 5.8 %collective-permute-start.15 = (s16[64,608]{1,0:T(8,128)(2,1)S(1)}, s16[64,608]{1,0:T(8,128)(2,1)S(1)}, u32[]{:S(2)}, u32[]{:S(2)}) collective-permute-start(s16[64,608]{1,0:T(8,128)(2,1)S(1)} %get-tuple-element.47), channel_id=1, source_target_pairs={{0,8},{8,0},{16,24},{24,16},{1,9},{9,1},{17,25},{25,17},{2,10},{10... | collective-permute-start | bytes 233480 | tf_op jit(solution)/shard_map/ppermute | solution.py:20
  49.6 5.3 %collective-permute-start.16 = (s16[64,576]{1,0:T(8,128)(2,1)S(1)}, s16[64,576]{1,0:T(8,128)(2,1)S(1)}, u32[]{:S(2)}, u32[]{:S(2)}) collective-permute-start(s16[64,576]{1,0:T(8,128)(2,1)S(1)} %get-tuple-element.48), channel_id=1, source_target_pairs={{0,16},{8,24},{16,0},{24,8},{1,17},{9,25},{17,1},{25,9},{2,18},{10... | collective-permute-start | bytes 221192 | tf_op jit(solution)/shard_map/ppermute | solution.py:20
  55.1 1.2 %collective-permute-start.18 = (f32[8,128]{1,0:T(8,128)S(1)}, f32[8,128]{1,0:T(8,128)S(1)}, u32[]{:S(2)}, u32[]{:S(2)}) collective-permute-start(f32[8,128]{1,0:T(8,128)S(1)} %shard_map.71), channel_id=1, source_target_pairs={{0,1},{1,0},{2,3},{3,2},{4,5},{5,4},{6,7},{7,6},{8,9},{9,8},{10,11... | collective-permute-start | bytes 12296 | tf_op jit(solution)/shard_map/ppermute | solution.py:20
  56.3 6.9 %collective-permute-start.21 = (f32[8,128]{1,0:T(8,128)S(1)}, f32[8,128]{1,0:T(8,128)S(1)}, u32[]{:S(2)}, u32[]{:S(2)}) collective-permute-start(f32[8,128]{1,0:T(8,128)S(1)} %add.5.p0), channel_id=1, source_target_pairs={{0,7},{1,6},{2,5},{3,4},{4,3},{5,2},{6,1},{7,0},{8,15},{9,14},{10,... | collective-permute-start | bytes 12296 | tf_op jit(solution)/shard_map/ppermute | solution.py:20
  59.2 3.0 %collective-permute-start.19 = (f32[4,128]{1,0:T(4,128)S(1)}, f32[4,128]{1,0:T(4,128)S(1)}, u32[]{:S(2)}, u32[]{:S(2)}) collective-permute-start(f32[4,128]{1,0:T(4,128)S(1)} %slice.6), channel_id=1, source_target_pairs={{0,3},{1,2},{2,1},{3,0},{4,7},{5,6},{6,5},{7,4},{8,11},{9,10},{10,... | collective-permute-start | bytes 6152 | tf_op jit(solution)/shard_map/ppermute | solution.py:20
  59.3 3.9 %collective-permute-start.20 = (f32[6,128]{1,0:T(8,128)S(1)}, f32[6,128]{1,0:T(8,128)S(1)}, u32[]{:S(2)}, u32[]{:S(2)}) collective-permute-start(f32[6,128]{1,0:T(8,128)S(1)} %bitcast.9), channel_id=1, source_target_pairs={{0,5},{1,4},{2,7},{3,6},{4,1},{5,0},{6,3},{7,2},{8,13},{9,12},{10,... | collective-permute-start | bytes 9224 | tf_op jit(solution)/shard_map/ppermute | solution.py:20

commit v13 on v12

--- a/solution.py
+++ b/solution.py
@@ -154,18 +154,27 @@
         own_ref[:, pl.ds(k, CHUNK)] = both[:rows] + both[rows:]
 
 
-def first_kernel(samples, wide_ref, s0, s1, s2, s3, dosage_ref, start_ref, scaled_ref, turned_ref, own_ref, coded_ref, shared_ref):
+def first_kernel(samples, wide_ref, s0, s1, s2, s3, dosage_ref, start_ref, scaled_ref, own_ref, coded_ref, shared_ref):
     sums = total([s[0:2] for s in (s0, s1, s2, s3)])
     center = sums[0:1] / samples
     spread = sums[1:2] / samples - center * center
     factor = lax.rsqrt(spread + 1e-05)
     for k in range(0, dosage_ref.shape[0], CHUNK):
         part = dosage_ref[pl.ds(k, CHUNK)].astype(jnp.float32)
-        part = ((part - center) * factor).astype(jnp.bfloat16)
-        scaled_ref[pl.ds(k, CHUNK)] = part
-        turned_ref[:, pl.ds(k, CHUNK)] = part.T
-    project(start_ref[...], turned_ref, own_ref)
+        scaled_ref[pl.ds(k, CHUNK)] = ((part - center) * factor).astype(jnp.bfloat16)
+    terms = two_terms(start_ref[...])
+    rows = start_ref.shape[0]
+    for k in range(0, dosage_ref.shape[0], CHUNK):
+        both = lax.dot_general(
+            terms, scaled_ref[pl.ds(k, CHUNK)], (((1,), (1,)), ((), ())), preferred_element_type=jnp.float32
+        )
+        own_ref[:, pl.ds(k, CHUNK)] = both[:rows] + both[rows:]
     encode(own_ref, coded_ref, shared_ref, wide_ref[0:1, 0:1])
+
+
+def turn_kernel(scaled_ref, turned_ref):
+    for k in range(0, scaled_ref.shape[0], CHUNK):
+        turned_ref[:, pl.ds(k, CHUNK)] = scaled_ref[pl.ds(k, CHUNK)].T
 
 
 def next_kernel(
@@ -223,7 +232,7 @@
         )
 
 
-def window_kernel(samples, count, own_ref, early_ref, same_ref, cross_ref, scaled_ref, *sent_refs):
+def window_kernel(samples, count, last, own_ref, early_ref, same_ref, cross_ref, scaled_ref, *sent_refs):
     _, side, across = place(count)
     same_scale = unit(aux(same_ref)[0], side)
     cross_scale = unit(aux(cross_ref)[0], across)
@@ -235,10 +244,11 @@
         acc = acc + jnp.dot(
             two_terms(mixed), scaled_ref[pl.ds(k, CHUNK)], preferred_element_type=jnp.float32
         )
-        curved = curved + own_ref[:, pl.ds(k, CHUNK)] * mixed
+        if last:
+            curved = curved + own_ref[:, pl.ds(k, CHUNK)] * mixed
     z = acc[:rows] + acc[rows:]
     exponent, scale = scale_of(jnp.max(jnp.abs(z), 1, keepdims=True))
-    columns = exponent, *split(jnp.sum(curved, 1, keepdims=True) / samples)
+    columns = (exponent, *split(jnp.sum(curved, 1, keepdims=True) / samples)) if last else (exponent,)
     z = fixed(z * scale)
     for ref in sent_refs:
         ref[:, pl.ds(0, z.shape[1])] = z
@@ -331,23 +341,25 @@
     )(band_width)
     near = shifted(wide)
     two, three, near = lax.optimization_barrier((two, three, near))
-    scaled, turned, own, coded, shared = call(
+    scaled, own, coded, shared = call(
         functools.partial(first_kernel, samples),
-        [(dosage.shape, jnp.bfloat16), (dosage.shape[::-1], jnp.bfloat16), own_out, coded_out, shared_out],
+        [(dosage.shape, jnp.bfloat16), own_out, coded_out, shared_out],
         wide, sums, one, two, three, dosage, start,
     )
 
+    (turned,) = call(turn_kernel, [(dosage.shape[::-1], jnp.bfloat16)], scaled)
+
     def give(up, *args):
         return call(functools.partial(give_kernel, count, up), [coded_out], near, *args)[0]
 
-    def window(own, coded, shared):
+    def window(own, coded, shared, last):
         beside = adjacent(coded)
         partner = swap(shared, "snp", 1)
         cross = crossing(give(1, own, coded, partner), 1)
         same = crossing(give(0, own, coded, beside), 0)
         (early,) = call(functools.partial(early_kernel, count), [own_out], own, coded, partner, beside)
         z, brief, least = call(
-            functools.partial(window_kernel, samples, count), sent_outs,
+            functools.partial(window_kernel, samples, count, last), sent_outs,
             own, early, same, cross, scaled,
         )
         return [z, swap(brief, "samp", 1), swap(least, "samp", 2), swap(z, "samp", 3)]
@@ -355,9 +367,9 @@
     first, parts, own, coded, shared = call(
         functools.partial(next_kernel, samples),
         [(grid, jnp.float32), ((rows, AUX), jnp.float32), own_out, coded_out, shared_out],
-        wide, *window(own, coded, shared), start, turned,
+        wide, *window(own, coded, shared, False), start, turned,
     )
-    zs = window(own, coded, shared)
+    zs = window(own, coded, shared, True)
     (flat,) = call(collect_kernel, [((8, AUX), jnp.float32)], parts, *zs)
     parts = snp_parts(flat)
     (second,) = call(functools.partial(second_kernel, samples), [(grid, jnp.float32)], *zs)

time: 64.3 us -> 64.1 us (level)
    pallas_call x14 -> x15, Pallas kernels: 6.46 us -> 6.86 us  [call(): pl.pallas_call(body, out_shape=outs, in_specs=specs, out_specs=[pl.BlockS...]
  transfers between devices with their start and end apart: 22 -> 22, of which waited for: 15 -> 15; matrix products, arithmetic and copies ran while one was open for 0% -> 0% of each run, Pallas kernels for 3% -> 4%
where the time goes in v13:
time: 64.1 us; the launch traced here: 63.9 us
  waiting for transfers between devices  31 us (48%)
  starting transfers between devices  24 us (37%)
  Pallas kernels  7.47 us (12%)
  between operations  1.42 us (2%)
    ppermute x15, waiting for transfers between devices, swap(): lax.ppermute(value, axis, [(i, i ^ bits) for i in range(lax.axis_size(axi...  17.5 us
    ppermute x15, starting transfers between devices, swap(): lax.ppermute(value, axis, [(i, i ^ bits) for i in range(lax.axis_size(axi...  15.3 us
    ppermute x4, waiting for transfers between devices, crossing(): return lax.ppermute(value, 'snp', pairs)  7.62 us
    pallas_call x15, Pallas kernels, call(): pl.pallas_call(body, out_shape=outs, in_specs=specs, out_specs=[pl.BlockS...  6.86 us
    ppermute x2, waiting for transfers between devices, adjacent(): return lax.ppermute(value, ('samp', 'snp'), pairs)  5.9 us
    ppermute x1, starting transfers between devices, shifted(): lax.ppermute(value, 'snp', [(i, (i + 2) % count) for i in range(count)])  3.02 us
    ppermute x2, starting transfers between devices, adjacent(): return lax.ppermute(value, ('samp', 'snp'), pairs)  2.93 us
    ppermute x4, starting transfers between devices, crossing(): return lax.ppermute(value, 'snp', pairs)  2.77 us
  transfers between devices with their start and end apart: 22, of which 15 were waited for; matrix products, arithmetic and copies ran while one was open for 0% of the time, Pallas kernels for 4%

profile of v13, /device:TPU:0, one launch (start us, length us, event | category | flops | bytes accessed | tf_op | source)
XLA Modules:
  0.0 63.9 jit_solution(17318637993156494548)
XLA Ops:
  1.3 0.0 copy-start
  1.3 0.6 shard_map.60.wide_ref
  1.9 3.0 %collective-permute-start.3 = (f32[8,640]{1,0:T(8,128)}, f32[8,640]{1,0:T(8,128)S(1)}, u32[]{:S(2)}, u32[]{:S(2)}) collective-permute-start(f32[8,640]{1,0:T(8,128)} %shard_map.60.wide_ref), channel_id=1, source_target_pairs={{0,2},{1,3},{2,4},{3,5},{4,6},{5,7},{6,0},{7,1},{8,10},{9,11},{10,... | collective-permute-start | bytes 61448 | tf_op jit(solution)/shard_map/ppermute | solution.py:45
  4.9 0.0 copy-done
  4.9 0.4 shard_map.59
  5.3 2.5 %collective-permute-start.2 = (f32[8,512]{1,0:T(8,128)S(1)}, f32[8,512]{1,0:T(8,128)S(1)}, u32[]{:S(2)}, u32[]{:S(2)}) collective-permute-start(f32[8,512]{1,0:T(8,128)S(1)} %get-tuple-element.28.s0), channel_id=1, source_target_pairs={{0,24},{8,16},{16,8},{24,0},{1,25},{9,17},{17,9},{25,1},{2,26},{10... | collective-permute-start | bytes 49160 | tf_op jit(solution)/shard_map/ppermute | solution.py:20
  7.8 0.5 collective-permute-start
  8.3 0.5 collective-permute-start.1
  8.9 2.6 %collective-permute-done.s1 = f32[2,512]{1,0:T(2,128)S(1)} collective-permute-done((f32[2,512]{1,0:T(2,128)S(1)}, f32[2,512]{1,0:T(2,128)S(1)}, u32[]{:S(2)}, u32[]{:S(2)}) %collective-permute-start) | collective-permute-done | bytes 4128 | tf_op jit(solution)/shard_map/ppermute | solution.py:20
  11.4 0.5 collective-permute-done.1.s2
  12.0 0.0 collective-permute-done.2.s3
  12.0 0.0 collective-permute-done.3.near_ref
  12.0 0.0 copy-done.2
  12.0 1.0 %shard_map.61 = (bf16[2048,512]{1,0:T(8,128)(2,1)S(1)}, f32[64,2048]{1,0:T(8,128)S(1)}, s16[64,2176]{1,0:T(8,128)(2,1)S(1)}, s16[64,2144]{1,0:T(8,128)(2,1)S(1)}) custom-call(f32[8,640]{1,0:T(8,128)S(1)} %copy-done.2, f32[8,512]{1,0:T(8,128)S(1)} %get-tuple-element.28.s0, f32[2,512]{1,0:T(2,128)S(1)} %collective-permute-done.s1, ...), custom_call_target="tpu_custom_call" | custom-call | tf_op jit(solution)/shard_map/pallas_call | solution.py:60
  13.0 1.6 %collective-permute-start.5 = (s16[64,2176]{1,0:T(8,128)(2,1)S(1)}, s16[64,2176]{1,0:T(8,128)(2,1)S(1)}, u32[]{:S(2)}, u32[]{:S(2)}) collective-permute-start(s16[64,2176]{1,0:T(8,128)(2,1)S(1)} %get-tuple-element.33.coded_ref), channel_id=1, source_target_pairs={{0,8},{1,2},{2,1},{3,4},{4,3},{5,6},{6,5},{7,15},{8,0},{9,10},{10,... | collective-permute-start | bytes 835592 | tf_op jit(solution)/shard_map/ppermute | solution.py:40
  14.5 0.2 collective-permute-start.4
  14.7 1.4 %collective-permute-done.4.partner_ref.other_ref = s16[64,2144]{1,0:T(8,128)(2,1)S(1)} collective-permute-done((s16[64,2144]{1,0:T(8,128)(2,1)S(1)}, s16[64,2144]{1,0:T(8,128)(2,1)S(1)}, u32[]{:S(2)}, u32[]{:S(2)}) %collective-permute-start.4) | collective-permute-done | bytes 274464 | tf_op jit(solution)/shard_map/ppermute | solution.py:20
  16.1 0.3 shard_map.64
  16.4 0.2 collective-permute-start.7
  16.6 3.0 %collective-permute-done.5.next_ref.other_ref = s16[64,2176]{1,0:T(8,128)(2,1)S(1)} collective-permute-done((s16[64,2176]{1,0:T(8,128)(2,1)S(1)}, s16[64,2176]{1,0:T(8,128)(2,1)S(1)}, u32[]{:S(2)}, u32[]{:S(2)}) %collective-permute-start.5) | collective-permute-done | bytes 278560 | tf_op jit(solution)/shard_map/ppermute | solution.py:40
  19.6 0.3 shard_map.63
  19.9 1.0 %collective-permute-start.6 = (s16[64,2176]{1,0:T(8,128)(2,1)S(1)}, s16[64,2176]{1,0:T(8,128)(2,1)S(1)}, u32[]{:S(2)}, u32[]{:S(2)}) collective-permute-start(s16[64,2176]{1,0:T(8,128)(2,1)S(1)} %shard_map.63), channel_id=1, source_target_pairs={{0,2},{1,0},{2,4},{3,1},{4,6},{5,3},{6,7},{7,5},{8,10},{9,8},{10,1... | collective-permute-start | bytes 835592 | tf_op jit(solution)/shard_map/ppermute | solution.py:29
  20.9 0.2 shard_map.62.early_ref
  21.1 2.5 %collective-permute-done.7.cross_ref = s16[64,2176]{1,0:T(8,128)(2,1)S(1)} collective-permute-done((s16[64,2176]{1,0:T(8,128)(2,1)S(1)}, s16[64,2176]{1,0:T(8,128)(2,1)S(1)}, u32[]{:S(2)}, u32[]{:S(2)}) %collective-permute-start.7) | collective-permute-done | bytes 278560 | tf_op jit(solution)/shard_map/ppermute | solution.py:29
  23.7 1.3 %collective-permute-done.6.same_ref = s16[64,2176]{1,0:T(8,128)(2,1)S(1)} collective-permute-done((s16[64,2176]{1,0:T(8,128)(2,1)S(1)}, s16[64,2176]{1,0:T(8,128)(2,1)S(1)}, u32[]{:S(2)}, u32[]{:S(2)}) %collective-permute-start.6) | collective-permute-done | bytes 278560 | tf_op jit(solution)/shard_map/ppermute | solution.py:29
  24.9 0.6 shard_map.65
  25.5 1.5 %collective-permute-start.10 = (s16[64,640]{1,0:T(8,128)(2,1)S(1)}, s16[64,640]{1,0:T(8,128)(2,1)S(1)}, u32[]{:S(2)}, u32[]{:S(2)}) collective-permute-start(s16[64,640]{1,0:T(8,128)(2,1)S(1)} %get-tuple-element.37.z0), channel_id=1, source_target_pairs={{0,24},{8,16},{16,8},{24,0},{1,25},{9,17},{17,9},{25,1},{2,26},{10... | collective-permute-start | bytes 245768 | tf_op jit(solution)/shard_map/ppermute | solution.py:20
  27.0 0.5 collective-permute-start.8
  27.6 1.5 %collective-permute-start.9 = (s16[64,576]{1,0:T(8,128)(2,1)S(1)}, s16[64,576]{1,0:T(8,128)(2,1)S(1)}, u32[]{:S(2)}, u32[]{:S(2)}) collective-permute-start(s16[64,576]{1,0:T(8,128)(2,1)S(1)} %get-tuple-element.39), channel_id=1, source_target_pairs={{0,16},{8,24},{16,0},{24,8},{1,17},{9,25},{17,1},{25,9},{2,18},{10... | collective-permute-start | bytes 221192 | tf_op jit(solution)/shard_map/ppermute | solution.py:20
  29.1 0.6 shard_map.66.turned_ref
  29.7 3.7 %collective-permute-done.9.z2 = s16[64,576]{1,0:T(8,128)(2,1)S(1)} collective-permute-done((s16[64,576]{1,0:T(8,128)(2,1)S(1)}, s16[64,576]{1,0:T(8,128)(2,1)S(1)}, u32[]{:S(2)}, u32[]{:S(2)}) %collective-permute-start.9) | collective-permute-done | bytes 73760 | tf_op jit(solution)/shard_map/ppermute | solution.py:20
  33.4 0.0 collective-permute-done.8.z1
  33.4 0.0 collective-permute-done.10.z3
  33.4 0.7 %shard_map.67 = (f32[64,512]{1,0:T(8,128)S(1)}, f32[64,128]{1,0:T(8,128)S(1)}, f32[64,2048]{1,0:T(8,128)S(1)}, s16[64,2176]{1,0:T(8,128)(2,1)S(1)}, s16[64,2144]{1,0:T(8,128)(2,1)S(1)}) custom-call(f32[8,640]{1,0:T(8,128)S(1)} %copy-done.2, s16[64,640]{1,0:T(8,128)(2,1)S(1)} %get-tuple-element.37.z0, s16[64,608]{1,0:T(8,128)(2,1)S(1)} %collective-permute-done.8.z1, ...), custom_call_target="tpu_custom_call" | custom-call | tf_op jit(solution)/shard_map/pallas_call | solution.py:60
  34.1 1.4 %collective-permute-start.12 = (s16[64,2176]{1,0:T(8,128)(2,1)S(1)}, s16[64,2176]{1,0:T(8,128)(2,1)S(1)}, u32[]{:S(2)}, u32[]{:S(2)}) collective-permute-start(s16[64,2176]{1,0:T(8,128)(2,1)S(1)} %get-tuple-element.42.coded_ref), channel_id=1, source_target_pairs={{0,8},{1,2},{2,1},{3,4},{4,3},{5,6},{6,5},{7,15},{8,0},{9,10},{10,... | collective-permute-start | bytes 835592 | tf_op jit(solution)/shard_map/ppermute | solution.py:40
  35.5 0.5 collective-permute-start.11
  36.0 1.2 %collective-permute-done.11.partner_ref.other_ref = s16[64,2144]{1,0:T(8,128)(2,1)S(1)} collective-permute-done((s16[64,2144]{1,0:T(8,128)(2,1)S(1)}, s16[64,2144]{1,0:T(8,128)(2,1)S(1)}, u32[]{:S(2)}, u32[]{:S(2)}) %collective-permute-start.11) | collective-permute-done | bytes 274464 | tf_op jit(solution)/shard_map/ppermute | solution.py:20
  37.2 0.3 shard_map.70
  37.4 0.4 collective-permute-start.14
  37.8 2.9 %collective-permute-done.12.next_ref.other_ref = s16[64,2176]{1,0:T(8,128)(2,1)S(1)} collective-permute-done((s16[64,2176]{1,0:T(8,128)(2,1)S(1)}, s16[64,2176]{1,0:T(8,128)(2,1)S(1)}, u32[]{:S(2)}, u32[]{:S(2)}) %collective-permute-start.12) | collective-permute-done | bytes 278560 | tf_op jit(solution)/shard_map/ppermute | solution.py:40
  40.7 0.3 shard_map.69
  41.0 1.1 %collective-permute-start.13 = (s16[64,2176]{1,0:T(8,128)(2,1)S(1)}, s16[64,2176]{1,0:T(8,128)(2,1)S(1)}, u32[]{:S(2)}, u32[]{:S(2)}) collective-permute-start(s16[64,2176]{1,0:T(8,128)(2,1)S(1)} %shard_map.69), channel_id=1, source_target_pairs={{0,2},{1,0},{2,4},{3,1},{4,6},{5,3},{6,7},{7,5},{8,10},{9,8},{10,1... | collective-permute-start | bytes 835592 | tf_op jit(solution)/shard_map/ppermute | solution.py:29
  42.1 0.2 shard_map.68.early_ref
  42.4 0.0 copy-start.3
  42.4 2.2 %collective-permute-done.14.cross_ref = s16[64,2176]{1,0:T(8,128)(2,1)S(1)} collective-permute-done((s16[64,2176]{1,0:T(8,128)(2,1)S(1)}, s16[64,2176]{1,0:T(8,128)(2,1)S(1)}, u32[]{:S(2)}, u32[]{:S(2)}) %collective-permute-start.14) | collective-permute-done | bytes 278560 | tf_op jit(solution)/shard_map/ppermute | solution.py:29
  44.5 1.6 %collective-permute-done.13.same_ref = s16[64,2176]{1,0:T(8,128)(2,1)S(1)} collective-permute-done((s16[64,2176]{1,0:T(8,128)(2,1)S(1)}, s16[64,2176]{1,0:T(8,128)(2,1)S(1)}, u32[]{:S(2)}, u32[]{:S(2)}) %collective-permute-start.13) | collective-permute-done | bytes 278560 | tf_op jit(solution)/shard_map/ppermute | solution.py:29
  46.2 0.7 %shard_map.71 = (s16[64,640]{1,0:T(8,128)(2,1)S(1)}, s16[64,608]{1,0:T(8,128)(2,1)S(1)}, s16[64,576]{1,0:T(8,128)(2,1)S(1)}) custom-call(f32[64,2048]{1,0:T(8,128)S(1)} %get-tuple-element.41.own_ref, f32[64,2048]{1,0:T(8,128)S(1)} %shard_map.68.early_ref, s16[64,2176]{1,0:T(8,128)(2,1)S(1)} %collective-permute-done.13.same_ref, ...), custom_call_target="tpu_custom_call" | custom-call | tf_op jit(solution)/shard_map/pallas_call | solution.py:60
  46.9 1.9 %collective-permute-start.17 = (s16[64,640]{1,0:T(8,128)(2,1)S(1)}, s16[64,640]{1,0:T(8,128)(2,1)S(1)}, u32[]{:S(2)}, u32[]{:S(2)}) collective-permute-start(s16[64,640]{1,0:T(8,128)(2,1)S(1)} %get-tuple-element.44.z0), channel_id=1, source_target_pairs={{0,24},{8,16},{16,8},{24,0},{1,25},{9,17},{17,9},{25,1},{2,26},{10... | collective-permute-start | bytes 245768 | tf_op jit(solution)/shard_map/ppermute | solution.py:20
  48.8 0.5 collective-permute-start.15
  49.4 1.1 %collective-permute-start.16 = (s16[64,576]{1,0:T(8,128)(2,1)S(1)}, s16[64,576]{1,0:T(8,128)(2,1)S(1)}, u32[]{:S(2)}, u32[]{:S(2)}) collective-permute-start(s16[64,576]{1,0:T(8,128)(2,1)S(1)} %get-tuple-element.46), channel_id=1, source_target_pairs={{0,16},{8,24},{16,0},{24,8},{1,17},{9,25},{17,1},{25,9},{2,18},{10... | collective-permute-start | bytes 221192 | tf_op jit(solution)/shard_map/ppermute | solution.py:20
  50.5 4.1 %collective-permute-done.16.z2 = s16[64,576]{1,0:T(8,128)(2,1)S(1)} collective-permute-done((s16[64,576]{1,0:T(8,128)(2,1)S(1)}, s16[64,576]{1,0:T(8,128)(2,1)S(1)}, u32[]{:S(2)}, u32[]{:S(2)}) %collective-permute-start.16) | collective-permute-done | bytes 73760 | tf_op jit(solution)/shard_map/ppermute | solution.py:20
  54.6 0.0 collective-permute-done.15.z1
  54.6 0.0 collective-permute-done.17.z3
  54.6 0.2 shard_map.72
  54.9 0.0 collective-permute-start.18
  54.9 1.2 %collective-permute-done.18 = f32[8,128]{1,0:T(8,128)S(1)} collective-permute-done((f32[8,128]{1,0:T(8,128)S(1)}, f32[8,128]{1,0:T(8,128)S(1)}, u32[]{:S(2)}, u32[]{:S(2)}) %collective-permute-start.18) | collective-permute-done | bytes 4128 | tf_op jit(solution)/shard_map/ppermute | solution.py:20
  56.1 2.9 %collective-permute-start.21 = (f32[8,128]{1,0:T(8,128)S(1)}, f32[8,128]{1,0:T(8,128)S(1)}, u32[]{:S(2)}, u32[]{:S(2)}) collective-permute-start(f32[8,128]{1,0:T(8,128)S(1)} %add.5.p0), channel_id=1, source_target_pairs={{0,7},{1,6},{2,5},{3,4},{4,3},{5,2},{6,1},{7,0},{8,15},{9,14},{10,... | collective-permute-start | bytes 12296 | tf_op jit(solution)/shard_map/ppermute | solution.py:20
  58.9 0.1 collective-permute-start.19
  59.0 0.9 %collective-permute-start.20 = (f32[6,128]{1,0:T(8,128)S(1)}, f32[6,128]{1,0:T(8,128)S(1)}, u32[]{:S(2)}, u32[]{:S(2)}) collective-permute-start(f32[6,128]{1,0:T(8,128)S(1)} %bitcast.9), channel_id=1, source_target_pairs={{0,5},{1,4},{2,7},{3,6},{4,1},{5,0},{6,3},{7,2},{8,13},{9,12},{10,... | collective-permute-start | bytes 9224 | tf_op jit(solution)/shard_map/ppermute | solution.py:20
  60.0 0.1 shard_map.73.second_ref
  60.1 1.9 %collective-permute-done.19.p1 = f32[4,128]{1,0:T(4,128)S(1)} collective-permute-done((f32[4,128]{1,0:T(4,128)S(1)}, f32[4,128]{1,0:T(4,128)S(1)}, u32[]{:S(2)}, u32[]{:S(2)}) %collective-permute-start.19) | collective-permute-done | bytes 2080 | tf_op jit(solution)/shard_map/ppermute | solution.py:20
  62.0 1.0 %collective-permute-done.20.p2 = f32[6,128]{1,0:T(8,128)S(1)} collective-permute-done((f32[6,128]{1,0:T(8,128)S(1)}, f32[6,128]{1,0:T(8,128)S(1)}, u32[]{:S(2)}, u32[]{:S(2)}) %collective-permute-start.20) | collective-permute-done | bytes 3104 | tf_op jit(solution)/shard_map/ppermute | solution.py:20
  63.0 0.0 collective-permute-done.21.p3
  63.0 1.0 %shard_map.74 = (f32[64,512]{1,0:T(8,128)}, f32[64,512]{1,0:T(8,128)}) custom-call(f32[1,128]{1,0:T(1,128)S(1)} %pad_bitcast_fusion.shrink_ref, f32[8,128]{1,0:T(8,128)S(1)} %add.5.p0, f32[4,128]{1,0:T(4,128)S(1)} %collective-permute-done.19.p1, f32[6,128]{1,0:T(8,128)S(1)} %collective-permute-done.20.p2, f32[8,128]{1,0:T(8,128)S(1)} %collective-permute-done.21.p3, ...), custom_call_target="tpu_custom_call" | custom-call | tf_op jit(solution)/shard_map/pallas_call | solution.py:60
  (7 shorter events, 0.0 us)
Async XLA Ops:
  1.3 3.7 %copy-start = (bf16[2048,512]{1,0:T(8,128)(2,1)S(1)}, bf16[2048,512]{1,0:T(8,128)(2,1)}, u32[]{:S(2)}) copy-start(bf16[2048,512]{1,0:T(8,128)(2,1)} %dosage_ref.3) | copy-start | bytes 6291460
  1.9 10.1 %copy-start.1 = (f32[512,64]{0,1:T(8,128)S(1)}, f32[512,64]{0,1:T(8,128)}, u32[]{:S(2)}) copy-start(f32[512,64]{0,1:T(8,128)} %param.6) | copy-start | bytes 393220
  1.9 10.1 %copy-start.2 = (f32[8,640]{1,0:T(8,128)S(1)}, f32[8,640]{1,0:T(8,128)}, u32[]{:S(2)}) copy-start(f32[8,640]{1,0:T(8,128)} %shard_map.60.wide_ref) | copy-start | bytes 61444
  1.9 10.1 %collective-permute-start.3 = (f32[8,640]{1,0:T(8,128)}, f32[8,640]{1,0:T(8,128)S(1)}, u32[]{:S(2)}, u32[]{:S(2)}) collective-permute-start(f32[8,640]{1,0:T(8,128)} %shard_map.60.wide_ref), channel_id=1, source_target_pairs={{0,2},{1,3},{2,4},{3,5},{4,6},{5,7},{6,0},{7,1},{8,10},{9,11},{10,... | collective-permute-start | bytes 61448 | tf_op jit(solution)/shard_map/ppermute | solution.py:45
  5.3 6.7 %collective-permute-start.2 = (f32[8,512]{1,0:T(8,128)S(1)}, f32[8,512]{1,0:T(8,128)S(1)}, u32[]{:S(2)}, u32[]{:S(2)}) collective-permute-start(f32[8,512]{1,0:T(8,128)S(1)} %get-tuple-element.28.s0), channel_id=1, source_target_pairs={{0,24},{8,16},{16,8},{24,0},{1,25},{9,17},{17,9},{25,1},{2,26},{10... | collective-permute-start | bytes 49160 | tf_op jit(solution)/shard_map/ppermute | solution.py:20
  7.8 3.6 %collective-permute-start = (f32[2,512]{1,0:T(2,128)S(1)}, f32[2,512]{1,0:T(2,128)S(1)}, u32[]{:S(2)}, u32[]{:S(2)}) collective-permute-start(f32[2,512]{1,0:T(2,128)S(1)} %get-tuple-element.26), channel_id=1, source_target_pairs={{0,8},{8,0},{16,24},{24,16},{1,9},{9,1},{17,25},{25,17},{2,10},{10... | collective-permute-start | bytes 12296 | tf_op jit(solution)/shard_map/ppermute | solution.py:20
  8.3 3.6 %collective-permute-start.1 = (f32[2,512]{1,0:T(2,128)S(1)}, f32[2,512]{1,0:T(2,128)S(1)}, u32[]{:S(2)}, u32[]{:S(2)}) collective-permute-start(f32[2,512]{1,0:T(2,128)S(1)} %get-tuple-element.26), channel_id=1, source_target_pairs={{0,16},{8,24},{16,0},{24,8},{1,17},{9,25},{17,1},{25,9},{2,18},{10... | collective-permute-start | bytes 12296 | tf_op jit(solution)/shard_map/ppermute | solution.py:20
  13.0 6.6 %collective-permute-start.5 = (s16[64,2176]{1,0:T(8,128)(2,1)S(1)}, s16[64,2176]{1,0:T(8,128)(2,1)S(1)}, u32[]{:S(2)}, u32[]{:S(2)}) collective-permute-start(s16[64,2176]{1,0:T(8,128)(2,1)S(1)} %get-tuple-element.33.coded_ref), channel_id=1, source_target_pairs={{0,8},{1,2},{2,1},{3,4},{4,3},{5,6},{6,5},{7,15},{8,0},{9,10},{10,... | collective-permute-start | bytes 835592 | tf_op jit(solution)/shard_map/ppermute | solution.py:40
  14.5 1.6 %collective-permute-start.4 = (s16[64,2144]{1,0:T(8,128)(2,1)S(1)}, s16[64,2144]{1,0:T(8,128)(2,1)S(1)}, u32[]{:S(2)}, u32[]{:S(2)}) collective-permute-start(s16[64,2144]{1,0:T(8,128)(2,1)S(1)} %get-tuple-element.34), channel_id=1, source_target_pairs={{0,1},{1,0},{2,3},{3,2},{4,5},{5,4},{6,7},{7,6},{8,9},{9,8},{10,11... | collective-permute-start | bytes 823304 | tf_op jit(solution)/shard_map/ppermute | solution.py:20
  16.4 7.3 %collective-permute-start.7 = (s16[64,2176]{1,0:T(8,128)(2,1)S(1)}, s16[64,2176]{1,0:T(8,128)(2,1)S(1)}, u32[]{:S(2)}, u32[]{:S(2)}) collective-permute-start(s16[64,2176]{1,0:T(8,128)(2,1)S(1)} %shard_map.64), channel_id=1, source_target_pairs={{0,1},{1,3},{2,0},{3,5},{4,2},{5,7},{6,4},{7,6},{8,9},{9,11},{10,8... | collective-permute-start | bytes 835592 | tf_op jit(solution)/shard_map/ppermute | solution.py:29
  19.9 5.1 %collective-permute-start.6 = (s16[64,2176]{1,0:T(8,128)(2,1)S(1)}, s16[64,2176]{1,0:T(8,128)(2,1)S(1)}, u32[]{:S(2)}, u32[]{:S(2)}) collective-permute-start(s16[64,2176]{1,0:T(8,128)(2,1)S(1)} %shard_map.63), channel_id=1, source_target_pairs={{0,2},{1,0},{2,4},{3,1},{4,6},{5,3},{6,7},{7,5},{8,10},{9,8},{10,1... | collective-permute-start | bytes 835592 | tf_op jit(solution)/shard_map/ppermute | solution.py:29
  25.5 7.9 %collective-permute-start.10 = (s16[64,640]{1,0:T(8,128)(2,1)S(1)}, s16[64,640]{1,0:T(8,128)(2,1)S(1)}, u32[]{:S(2)}, u32[]{:S(2)}) collective-permute-start(s16[64,640]{1,0:T(8,128)(2,1)S(1)} %get-tuple-element.37.z0), channel_id=1, source_target_pairs={{0,24},{8,16},{16,8},{24,0},{1,25},{9,17},{17,9},{25,1},{2,26},{10... | collective-permute-start | bytes 245768 | tf_op jit(solution)/shard_map/ppermute | solution.py:20
  27.0 6.4 %collective-permute-start.8 = (s16[64,608]{1,0:T(8,128)(2,1)S(1)}, s16[64,608]{1,0:T(8,128)(2,1)S(1)}, u32[]{:S(2)}, u32[]{:S(2)}) collective-permute-start(s16[64,608]{1,0:T(8,128)(2,1)S(1)} %get-tuple-element.38), channel_id=1, source_target_pairs={{0,8},{8,0},{16,24},{24,16},{1,9},{9,1},{17,25},{25,17},{2,10},{10... | collective-permute-start | bytes 233480 | tf_op jit(solution)/shard_map/ppermute | solution.py:20
  27.6 5.8 %collective-permute-start.9 = (s16[64,576]{1,0:T(8,128)(2,1)S(1)}, s16[64,576]{1,0:T(8,128)(2,1)S(1)}, u32[]{:S(2)}, u32[]{:S(2)}) collective-permute-start(s16[64,576]{1,0:T(8,128)(2,1)S(1)} %get-tuple-element.39), channel_id=1, source_target_pairs={{0,16},{8,24},{16,0},{24,8},{1,17},{9,25},{17,1},{25,9},{2,18},{10... | collective-permute-start | bytes 221192 | tf_op jit(solution)/shard_map/ppermute | solution.py:20
  34.1 6.6 %collective-permute-start.12 = (s16[64,2176]{1,0:T(8,128)(2,1)S(1)}, s16[64,2176]{1,0:T(8,128)(2,1)S(1)}, u32[]{:S(2)}, u32[]{:S(2)}) collective-permute-start(s16[64,2176]{1,0:T(8,128)(2,1)S(1)} %get-tuple-element.42.coded_ref), channel_id=1, source_target_pairs={{0,8},{1,2},{2,1},{3,4},{4,3},{5,6},{6,5},{7,15},{8,0},{9,10},{10,... | collective-permute-start | bytes 835592 | tf_op jit(solution)/shard_map/ppermute | solution.py:40
  35.5 1.7 %collective-permute-start.11 = (s16[64,2144]{1,0:T(8,128)(2,1)S(1)}, s16[64,2144]{1,0:T(8,128)(2,1)S(1)}, u32[]{:S(2)}, u32[]{:S(2)}) collective-permute-start(s16[64,2144]{1,0:T(8,128)(2,1)S(1)} %get-tuple-element.43), channel_id=1, source_target_pairs={{0,1},{1,0},{2,3},{3,2},{4,5},{5,4},{6,7},{7,6},{8,9},{9,8},{10,11... | collective-permute-start | bytes 823304 | tf_op jit(solution)/shard_map/ppermute | solution.py:20
  37.4 7.1 %collective-permute-start.14 = (s16[64,2176]{1,0:T(8,128)(2,1)S(1)}, s16[64,2176]{1,0:T(8,128)(2,1)S(1)}, u32[]{:S(2)}, u32[]{:S(2)}) collective-permute-start(s16[64,2176]{1,0:T(8,128)(2,1)S(1)} %shard_map.70), channel_id=1, source_target_pairs={{0,1},{1,3},{2,0},{3,5},{4,2},{5,7},{6,4},{7,6},{8,9},{9,11},{10,8... | collective-permute-start | bytes 835592 | tf_op jit(solution)/shard_map/ppermute | solution.py:29
  41.0 5.2 %collective-permute-start.13 = (s16[64,2176]{1,0:T(8,128)(2,1)S(1)}, s16[64,2176]{1,0:T(8,128)(2,1)S(1)}, u32[]{:S(2)}, u32[]{:S(2)}) collective-permute-start(s16[64,2176]{1,0:T(8,128)(2,1)S(1)} %shard_map.69), channel_id=1, source_target_pairs={{0,2},{1,0},{2,4},{3,1},{4,6},{5,3},{6,7},{7,5},{8,10},{9,8},{10,1... | collective-permute-start | bytes 835592 | tf_op jit(solution)/shard_map/ppermute | solution.py:29
  42.4 17.6 %copy-start.3 = (f32[64]{0:T(128)S(1)}, f32[64]{0:T(128)}, u32[]{:S(2)}) copy-start(f32[64]{0:T(128)} %param.7) | copy-start | bytes 772
  46.9 7.7 %collective-permute-start.17 = (s16[64,640]{1,0:T(8,128)(2,1)S(1)}, s16[64,640]{1,0:T(8,128)(2,1)S(1)}, u32[]{:S(2)}, u32[]{:S(2)}) collective-permute-start(s16[64,640]{1,0:T(8,128)(2,1)S(1)} %get-tuple-element.44.z0), channel_id=1, source_target_pairs={{0,24},{8,16},{16,8},{24,0},{1,25},{9,17},{17,9},{25,1},{2,26},{10... | collective-permute-start | bytes 245768 | tf_op jit(solution)/shard_map/ppermute | solution.py:20
  48.8 5.8 %collective-permute-start.15 = (s16[64,608]{1,0:T(8,128)(2,1)S(1)}, s16[64,608]{1,0:T(8,128)(2,1)S(1)}, u32[]{:S(2)}, u32[]{:S(2)}) collective-permute-start(s16[64,608]{1,0:T(8,128)(2,1)S(1)} %get-tuple-element.45), channel_id=1, source_target_pairs={{0,8},{8,0},{16,24},{24,16},{1,9},{9,1},{17,25},{25,17},{2,10},{10... | collective-permute-start | bytes 233480 | tf_op jit(solution)/shard_map/ppermute | solution.py:20
  49.4 5.2 %collective-permute-start.16 = (s16[64,576]{1,0:T(8,128)(2,1)S(1)}, s16[64,576]{1,0:T(8,128)(2,1)S(1)}, u32[]{:S(2)}, u32[]{:S(2)}) collective-permute-start(s16[64,576]{1,0:T(8,128)(2,1)S(1)} %get-tuple-element.46), channel_id=1, source_target_pairs={{0,16},{8,24},{16,0},{24,8},{1,17},{9,25},{17,1},{25,9},{2,18},{10... | collective-permute-start | bytes 221192 | tf_op jit(solution)/shard_map/ppermute | solution.py:20
  54.9 1.2 %collective-permute-start.18 = (f32[8,128]{1,0:T(8,128)S(1)}, f32[8,128]{1,0:T(8,128)S(1)}, u32[]{:S(2)}, u32[]{:S(2)}) collective-permute-start(f32[8,128]{1,0:T(8,128)S(1)} %shard_map.72), channel_id=1, source_target_pairs={{0,1},{1,0},{2,3},{3,2},{4,5},{5,4},{6,7},{7,6},{8,9},{9,8},{10,11... | collective-permute-start | bytes 12296 | tf_op jit(solution)/shard_map/ppermute | solution.py:20
  56.1 6.9 %collective-permute-start.21 = (f32[8,128]{1,0:T(8,128)S(1)}, f32[8,128]{1,0:T(8,128)S(1)}, u32[]{:S(2)}, u32[]{:S(2)}) collective-permute-start(f32[8,128]{1,0:T(8,128)S(1)} %add.5.p0), channel_id=1, source_target_pairs={{0,7},{1,6},{2,5},{3,4},{4,3},{5,2},{6,1},{7,0},{8,15},{9,14},{10,... | collective-permute-start | bytes 12296 | tf_op jit(solution)/shard_map/ppermute | solution.py:20
  58.9 3.0 %collective-permute-start.19 = (f32[4,128]{1,0:T(4,128)S(1)}, f32[4,128]{1,0:T(4,128)S(1)}, u32[]{:S(2)}, u32[]{:S(2)}) collective-permute-start(f32[4,128]{1,0:T(4,128)S(1)} %slice.6), channel_id=1, source_target_pairs={{0,3},{1,2},{2,1},{3,0},{4,7},{5,6},{6,5},{7,4},{8,11},{9,10},{10,... | collective-permute-start | bytes 6152 | tf_op jit(solution)/shard_map/ppermute | solution.py:20
  59.0 3.9 %collective-permute-start.20 = (f32[6,128]{1,0:T(8,128)S(1)}, f32[6,128]{1,0:T(8,128)S(1)}, u32[]{:S(2)}, u32[]{:S(2)}) collective-permute-start(f32[6,128]{1,0:T(8,128)S(1)} %bitcast.9), channel_id=1, source_target_pairs={{0,5},{1,4},{2,7},{3,6},{4,1},{5,0},{6,3},{7,2},{8,13},{9,12},{10,... | collective-permute-start | bytes 9224 | tf_op jit(solution)/shard_map/ppermute | solution.py:20

commit v14 on v13

--- a/solution.py
+++ b/solution.py
@@ -177,17 +177,21 @@
         turned_ref[:, pl.ds(k, CHUNK)] = scaled_ref[pl.ds(k, CHUNK)].T
 
 
-def next_kernel(
-    samples, wide_ref, z0, z1, z2, z3, start_ref, turned_ref, first_ref, parts_ref, own_ref, coded_ref, shared_ref
-):
-    first = total([grid_values(z) for z in (z0, z1, z2, z3)]) / samples
-    first_ref[...] = first
+def parts_kernel(start_ref, first_ref, parts_ref):
+    first = first_ref[...]
     start = start_ref[...]
     lane = lax.broadcasted_iota(jnp.int32, parts_ref.shape, 1)
     parts = jnp.zeros(parts_ref.shape, jnp.float32)
     for k, (a, b) in enumerate(((start, start), (start, first), (first, first))):
         parts = jnp.where(lane == k, jnp.sum(a * b, 1, keepdims=True), parts)
     parts_ref[...] = parts
+
+
+def next_kernel(
+    samples, wide_ref, z0, z1, z2, z3, turned_ref, first_ref, own_ref, coded_ref, shared_ref
+):
+    first = total([grid_values(z) for z in (z0, z1, z2, z3)]) / samples
+    first_ref[...] = first
     project(first, turned_ref, own_ref)
     encode(own_ref, coded_ref, shared_ref, wide_ref[0:1, 0:1])
 
@@ -364,11 +368,12 @@
         )
         return [z, swap(brief, "samp", 1), swap(least, "samp", 2), swap(z, "samp", 3)]
 
-    first, parts, own, coded, shared = call(
+    first, own, coded, shared = call(
         functools.partial(next_kernel, samples),
-        [(grid, jnp.float32), ((rows, AUX), jnp.float32), own_out, coded_out, shared_out],
-        wide, *window(own, coded, shared, False), start, turned,
+        [(grid, jnp.float32), own_out, coded_out, shared_out],
+        wide, *window(own, coded, shared, False), turned,
     )
+    (parts,) = call(parts_kernel, [((rows, AUX), jnp.float32)], start, first)
     zs = window(own, coded, shared, True)
     (flat,) = call(collect_kernel, [((8, AUX), jnp.float32)], parts, *zs)
     parts = snp_parts(flat)

time: 64.1 us -> 64.1 us (level)
    pallas_call x15 -> x16, Pallas kernels: 6.86 us -> 6.95 us  [call(): pl.pallas_call(body, out_shape=outs, in_specs=specs, out_specs=[pl.BlockS...]
where the time goes in v14:
time: 64.1 us; the launch traced here: 63.9 us
  waiting for transfers between devices  30.9 us (48%)
  starting transfers between devices  24 us (37%)
  Pallas kernels  7.56 us (12%)
  between operations  1.42 us (2%)
    ppermute x15, waiting for transfers between devices, swap(): lax.ppermute(value, axis, [(i, i ^ bits) for i in range(lax.axis_size(axi...  17.4 us
    ppermute x15, starting transfers between devices, swap(): lax.ppermute(value, axis, [(i, i ^ bits) for i in range(lax.axis_size(axi...  15.3 us
    ppermute x4, waiting for transfers between devices, crossing(): return lax.ppermute(value, 'snp', pairs)  7.62 us
    pallas_call x16, Pallas kernels, call(): pl.pallas_call(body, out_shape=outs, in_specs=specs, out_specs=[pl.BlockS...  6.95 us
    ppermute x2, waiting for transfers between devices, adjacent(): return lax.ppermute(value, ('samp', 'snp'), pairs)  5.9 us
    ppermute x1, starting transfers between devices, shifted(): lax.ppermute(value, 'snp', [(i, (i + 2) % count) for i in range(count)])  3.02 us
    ppermute x2, starting transfers between devices, adjacent(): return lax.ppermute(value, ('samp', 'snp'), pairs)  2.93 us
    ppermute x4, starting transfers between devices, crossing(): return lax.ppermute(value, 'snp', pairs)  2.77 us
  transfers between devices with their start and end apart: 22, of which 15 were waited for; matrix products, arithmetic and copies ran while one was open for 0% of the time, Pallas kernels for 4%

profile of v14, /device:TPU:0, one launch (start us, length us, event | category | flops | bytes accessed | tf_op | source)
XLA Modules:
  0.0 63.9 jit_solution(1663189097855465806)
XLA Ops:
  1.3 0.0 copy-start
  1.3 0.6 shard_map.60.wide_ref
  1.9 3.0 %collective-permute-start.3 = (f32[8,640]{1,0:T(8,128)}, f32[8,640]{1,0:T(8,128)S(1)}, u32[]{:S(2)}, u32[]{:S(2)}) collective-permute-start(f32[8,640]{1,0:T(8,128)} %shard_map.60.wide_ref), channel_id=1, source_target_pairs={{0,2},{1,3},{2,4},{3,5},{4,6},{5,7},{6,0},{7,1},{8,10},{9,11},{10,... | collective-permute-start | bytes 61448 | tf_op jit(solution)/shard_map/ppermute | solution.py:45
  4.9 0.0 copy-done
  4.9 0.4 shard_map.59
  5.3 2.5 %collective-permute-start.2 = (f32[8,512]{1,0:T(8,128)S(1)}, f32[8,512]{1,0:T(8,128)S(1)}, u32[]{:S(2)}, u32[]{:S(2)}) collective-permute-start(f32[8,512]{1,0:T(8,128)S(1)} %get-tuple-element.27.s0), channel_id=1, source_target_pairs={{0,24},{8,16},{16,8},{24,0},{1,25},{9,17},{17,9},{25,1},{2,26},{10... | collective-permute-start | bytes 49160 | tf_op jit(solution)/shard_map/ppermute | solution.py:20
  7.8 0.5 collective-permute-start
  8.3 0.5 collective-permute-start.1
  8.9 2.6 %collective-permute-done.s1 = f32[2,512]{1,0:T(2,128)S(1)} collective-permute-done((f32[2,512]{1,0:T(2,128)S(1)}, f32[2,512]{1,0:T(2,128)S(1)}, u32[]{:S(2)}, u32[]{:S(2)}) %collective-permute-start) | collective-permute-done | bytes 4128 | tf_op jit(solution)/shard_map/ppermute | solution.py:20
  11.4 0.5 collective-permute-done.1.s2
  12.0 0.0 collective-permute-done.2.s3
  12.0 0.0 collective-permute-done.3.near_ref
  12.0 1.0 %shard_map.61 = (bf16[2048,512]{1,0:T(8,128)(2,1)S(1)}, f32[64,2048]{1,0:T(8,128)S(1)}, s16[64,2176]{1,0:T(8,128)(2,1)S(1)}, s16[64,2144]{1,0:T(8,128)(2,1)S(1)}) custom-call(f32[8,640]{1,0:T(8,128)S(1)} %copy-done.2, f32[8,512]{1,0:T(8,128)S(1)} %get-tuple-element.27.s0, f32[2,512]{1,0:T(2,128)S(1)} %collective-permute-done.s1, ...), custom_call_target="tpu_custom_call" | custom-call | tf_op jit(solution)/shard_map/pallas_call | solution.py:60
  13.0 1.6 %collective-permute-start.5 = (s16[64,2176]{1,0:T(8,128)(2,1)S(1)}, s16[64,2176]{1,0:T(8,128)(2,1)S(1)}, u32[]{:S(2)}, u32[]{:S(2)}) collective-permute-start(s16[64,2176]{1,0:T(8,128)(2,1)S(1)} %get-tuple-element.32.coded_ref), channel_id=1, source_target_pairs={{0,8},{1,2},{2,1},{3,4},{4,3},{5,6},{6,5},{7,15},{8,0},{9,10},{10,... | collective-permute-start | bytes 835592 | tf_op jit(solution)/shard_map/ppermute | solution.py:40
  14.5 0.2 collective-permute-start.4
  14.7 1.4 %collective-permute-done.4.partner_ref.other_ref = s16[64,2144]{1,0:T(8,128)(2,1)S(1)} collective-permute-done((s16[64,2144]{1,0:T(8,128)(2,1)S(1)}, s16[64,2144]{1,0:T(8,128)(2,1)S(1)}, u32[]{:S(2)}, u32[]{:S(2)}) %collective-permute-start.4) | collective-permute-done | bytes 274464 | tf_op jit(solution)/shard_map/ppermute | solution.py:20
  16.1 0.3 shard_map.64
  16.4 0.2 collective-permute-start.7
  16.6 3.0 %collective-permute-done.5.next_ref.other_ref = s16[64,2176]{1,0:T(8,128)(2,1)S(1)} collective-permute-done((s16[64,2176]{1,0:T(8,128)(2,1)S(1)}, s16[64,2176]{1,0:T(8,128)(2,1)S(1)}, u32[]{:S(2)}, u32[]{:S(2)}) %collective-permute-start.5) | collective-permute-done | bytes 278560 | tf_op jit(solution)/shard_map/ppermute | solution.py:40
  19.6 0.3 shard_map.63
  19.9 1.0 %collective-permute-start.6 = (s16[64,2176]{1,0:T(8,128)(2,1)S(1)}, s16[64,2176]{1,0:T(8,128)(2,1)S(1)}, u32[]{:S(2)}, u32[]{:S(2)}) collective-permute-start(s16[64,2176]{1,0:T(8,128)(2,1)S(1)} %shard_map.63), channel_id=1, source_target_pairs={{0,2},{1,0},{2,4},{3,1},{4,6},{5,3},{6,7},{7,5},{8,10},{9,8},{10,1... | collective-permute-start | bytes 835592 | tf_op jit(solution)/shard_map/ppermute | solution.py:29
  20.9 0.2 shard_map.62.early_ref
  21.1 2.5 %collective-permute-done.7.cross_ref = s16[64,2176]{1,0:T(8,128)(2,1)S(1)} collective-permute-done((s16[64,2176]{1,0:T(8,128)(2,1)S(1)}, s16[64,2176]{1,0:T(8,128)(2,1)S(1)}, u32[]{:S(2)}, u32[]{:S(2)}) %collective-permute-start.7) | collective-permute-done | bytes 278560 | tf_op jit(solution)/shard_map/ppermute | solution.py:29
  23.7 1.3 %collective-permute-done.6.same_ref = s16[64,2176]{1,0:T(8,128)(2,1)S(1)} collective-permute-done((s16[64,2176]{1,0:T(8,128)(2,1)S(1)}, s16[64,2176]{1,0:T(8,128)(2,1)S(1)}, u32[]{:S(2)}, u32[]{:S(2)}) %collective-permute-start.6) | collective-permute-done | bytes 278560 | tf_op jit(solution)/shard_map/ppermute | solution.py:29
  24.9 0.6 shard_map.65
  25.5 1.5 %collective-permute-start.10 = (s16[64,640]{1,0:T(8,128)(2,1)S(1)}, s16[64,640]{1,0:T(8,128)(2,1)S(1)}, u32[]{:S(2)}, u32[]{:S(2)}) collective-permute-start(s16[64,640]{1,0:T(8,128)(2,1)S(1)} %get-tuple-element.36.z0), channel_id=1, source_target_pairs={{0,24},{8,16},{16,8},{24,0},{1,25},{9,17},{17,9},{25,1},{2,26},{10... | collective-permute-start | bytes 245768 | tf_op jit(solution)/shard_map/ppermute | solution.py:20
  27.0 0.5 collective-permute-start.8
  27.6 1.5 %collective-permute-start.9 = (s16[64,576]{1,0:T(8,128)(2,1)S(1)}, s16[64,576]{1,0:T(8,128)(2,1)S(1)}, u32[]{:S(2)}, u32[]{:S(2)}) collective-permute-start(s16[64,576]{1,0:T(8,128)(2,1)S(1)} %get-tuple-element.38), channel_id=1, source_target_pairs={{0,16},{8,24},{16,0},{24,8},{1,17},{9,25},{17,1},{25,9},{2,18},{10... | collective-permute-start | bytes 221192 | tf_op jit(solution)/shard_map/ppermute | solution.py:20
  29.1 0.6 shard_map.66.turned_ref
  29.7 3.7 %collective-permute-done.9.z2 = s16[64,576]{1,0:T(8,128)(2,1)S(1)} collective-permute-done((s16[64,576]{1,0:T(8,128)(2,1)S(1)}, s16[64,576]{1,0:T(8,128)(2,1)S(1)}, u32[]{:S(2)}, u32[]{:S(2)}) %collective-permute-start.9) | collective-permute-done | bytes 73760 | tf_op jit(solution)/shard_map/ppermute | solution.py:20
  33.4 0.0 collective-permute-done.8.z1
  33.4 0.0 collective-permute-done.10.z3
  33.4 0.7 %shard_map.67 = (f32[64,512]{1,0:T(8,128)S(1)}, f32[64,2048]{1,0:T(8,128)S(1)}, s16[64,2176]{1,0:T(8,128)(2,1)S(1)}, s16[64,2144]{1,0:T(8,128)(2,1)S(1)}) custom-call(f32[8,640]{1,0:T(8,128)S(1)} %copy-done.2, s16[64,640]{1,0:T(8,128)(2,1)S(1)} %get-tuple-element.36.z0, s16[64,608]{1,0:T(8,128)(2,1)S(1)} %collective-permute-done.8.z1, ...), custom_call_target="tpu_custom_call" | custom-call | tf_op jit(solution)/shard_map/pallas_call | solution.py:60
  34.1 1.4 %collective-permute-start.12 = (s16[64,2176]{1,0:T(8,128)(2,1)S(1)}, s16[64,2176]{1,0:T(8,128)(2,1)S(1)}, u32[]{:S(2)}, u32[]{:S(2)}) collective-permute-start(s16[64,2176]{1,0:T(8,128)(2,1)S(1)} %get-tuple-element.41.coded_ref), channel_id=1, source_target_pairs={{0,8},{1,2},{2,1},{3,4},{4,3},{5,6},{6,5},{7,15},{8,0},{9,10},{10,... | collective-permute-start | bytes 835592 | tf_op jit(solution)/shard_map/ppermute | solution.py:40
  35.5 0.5 collective-permute-start.11
  36.0 1.2 %collective-permute-done.11.partner_ref.other_ref = s16[64,2144]{1,0:T(8,128)(2,1)S(1)} collective-permute-done((s16[64,2144]{1,0:T(8,128)(2,1)S(1)}, s16[64,2144]{1,0:T(8,128)(2,1)S(1)}, u32[]{:S(2)}, u32[]{:S(2)}) %collective-permute-start.11) | collective-permute-done | bytes 274464 | tf_op jit(solution)/shard_map/ppermute | solution.py:20
  37.2 0.3 shard_map.71
  37.4 0.4 collective-permute-start.14
  37.8 2.9 %collective-permute-done.12.next_ref.other_ref = s16[64,2176]{1,0:T(8,128)(2,1)S(1)} collective-permute-done((s16[64,2176]{1,0:T(8,128)(2,1)S(1)}, s16[64,2176]{1,0:T(8,128)(2,1)S(1)}, u32[]{:S(2)}, u32[]{:S(2)}) %collective-permute-start.12) | collective-permute-done | bytes 278560 | tf_op jit(solution)/shard_map/ppermute | solution.py:40
  40.7 0.3 shard_map.70
  41.0 1.1 %collective-permute-start.13 = (s16[64,2176]{1,0:T(8,128)(2,1)S(1)}, s16[64,2176]{1,0:T(8,128)(2,1)S(1)}, u32[]{:S(2)}, u32[]{:S(2)}) collective-permute-start(s16[64,2176]{1,0:T(8,128)(2,1)S(1)} %shard_map.70), channel_id=1, source_target_pairs={{0,2},{1,0},{2,4},{3,1},{4,6},{5,3},{6,7},{7,5},{8,10},{9,8},{10,1... | collective-permute-start | bytes 835592 | tf_op jit(solution)/shard_map/ppermute | solution.py:29
  42.1 0.2 shard_map.69.early_ref
  42.4 0.0 copy-start.3
  42.4 2.2 %collective-permute-done.14.cross_ref = s16[64,2176]{1,0:T(8,128)(2,1)S(1)} collective-permute-done((s16[64,2176]{1,0:T(8,128)(2,1)S(1)}, s16[64,2176]{1,0:T(8,128)(2,1)S(1)}, u32[]{:S(2)}, u32[]{:S(2)}) %collective-permute-start.14) | collective-permute-done | bytes 278560 | tf_op jit(solution)/shard_map/ppermute | solution.py:29
  44.5 1.6 %collective-permute-done.13.same_ref = s16[64,2176]{1,0:T(8,128)(2,1)S(1)} collective-permute-done((s16[64,2176]{1,0:T(8,128)(2,1)S(1)}, s16[64,2176]{1,0:T(8,128)(2,1)S(1)}, u32[]{:S(2)}, u32[]{:S(2)}) %collective-permute-start.13) | collective-permute-done | bytes 278560 | tf_op jit(solution)/shard_map/ppermute | solution.py:29
  46.2 0.7 %shard_map.72 = (s16[64,640]{1,0:T(8,128)(2,1)S(1)}, s16[64,608]{1,0:T(8,128)(2,1)S(1)}, s16[64,576]{1,0:T(8,128)(2,1)S(1)}) custom-call(f32[64,2048]{1,0:T(8,128)S(1)} %get-tuple-element.40.own_ref, f32[64,2048]{1,0:T(8,128)S(1)} %shard_map.69.early_ref, s16[64,2176]{1,0:T(8,128)(2,1)S(1)} %collective-permute-done.13.same_ref, ...), custom_call_target="tpu_custom_call" | custom-call | tf_op jit(solution)/shard_map/pallas_call | solution.py:60
  46.9 1.9 %collective-permute-start.17 = (s16[64,640]{1,0:T(8,128)(2,1)S(1)}, s16[64,640]{1,0:T(8,128)(2,1)S(1)}, u32[]{:S(2)}, u32[]{:S(2)}) collective-permute-start(s16[64,640]{1,0:T(8,128)(2,1)S(1)} %get-tuple-element.43.z0), channel_id=1, source_target_pairs={{0,24},{8,16},{16,8},{24,0},{1,25},{9,17},{17,9},{25,1},{2,26},{10... | collective-permute-start | bytes 245768 | tf_op jit(solution)/shard_map/ppermute | solution.py:20
  48.8 0.5 collective-permute-start.15
  49.4 1.1 %collective-permute-start.16 = (s16[64,576]{1,0:T(8,128)(2,1)S(1)}, s16[64,576]{1,0:T(8,128)(2,1)S(1)}, u32[]{:S(2)}, u32[]{:S(2)}) collective-permute-start(s16[64,576]{1,0:T(8,128)(2,1)S(1)} %get-tuple-element.45), channel_id=1, source_target_pairs={{0,16},{8,24},{16,0},{24,8},{1,17},{9,25},{17,1},{25,9},{2,18},{10... | collective-permute-start | bytes 221192 | tf_op jit(solution)/shard_map/ppermute | solution.py:20
  50.5 0.1 shard_map.68.parts_ref
  50.6 4.0 %collective-permute-done.16.z2 = s16[64,576]{1,0:T(8,128)(2,1)S(1)} collective-permute-done((s16[64,576]{1,0:T(8,128)(2,1)S(1)}, s16[64,576]{1,0:T(8,128)(2,1)S(1)}, u32[]{:S(2)}, u32[]{:S(2)}) %collective-permute-start.16) | collective-permute-done | bytes 73760 | tf_op jit(solution)/shard_map/ppermute | solution.py:20
  54.6 0.0 collective-permute-done.15.z1
  54.6 0.0 collective-permute-done.17.z3
  54.6 0.2 shard_map.73
  54.9 0.0 collective-permute-start.18
  54.9 1.2 %collective-permute-done.18 = f32[8,128]{1,0:T(8,128)S(1)} collective-permute-done((f32[8,128]{1,0:T(8,128)S(1)}, f32[8,128]{1,0:T(8,128)S(1)}, u32[]{:S(2)}, u32[]{:S(2)}) %collective-permute-start.18) | collective-permute-done | bytes 4128 | tf_op jit(solution)/shard_map/ppermute | solution.py:20
  56.1 2.9 %collective-permute-start.21 = (f32[8,128]{1,0:T(8,128)S(1)}, f32[8,128]{1,0:T(8,128)S(1)}, u32[]{:S(2)}, u32[]{:S(2)}) collective-permute-start(f32[8,128]{1,0:T(8,128)S(1)} %add.5.p0), channel_id=1, source_target_pairs={{0,7},{1,6},{2,5},{3,4},{4,3},{5,2},{6,1},{7,0},{8,15},{9,14},{10,... | collective-permute-start | bytes 12296 | tf_op jit(solution)/shard_map/ppermute | solution.py:20
  58.9 0.1 collective-permute-start.19
  59.1 0.9 %collective-permute-start.20 = (f32[6,128]{1,0:T(8,128)S(1)}, f32[6,128]{1,0:T(8,128)S(1)}, u32[]{:S(2)}, u32[]{:S(2)}) collective-permute-start(f32[6,128]{1,0:T(8,128)S(1)} %bitcast.9), channel_id=1, source_target_pairs={{0,5},{1,4},{2,7},{3,6},{4,1},{5,0},{6,3},{7,2},{8,13},{9,12},{10,... | collective-permute-start | bytes 9224 | tf_op jit(solution)/shard_map/ppermute | solution.py:20
  60.0 0.1 shard_map.74.second_ref
  60.1 1.9 %collective-permute-done.19.p1 = f32[4,128]{1,0:T(4,128)S(1)} collective-permute-done((f32[4,128]{1,0:T(4,128)S(1)}, f32[4,128]{1,0:T(4,128)S(1)}, u32[]{:S(2)}, u32[]{:S(2)}) %collective-permute-start.19) | collective-permute-done | bytes 2080 | tf_op jit(solution)/shard_map/ppermute | solution.py:20
  62.0 1.0 %collective-permute-done.20.p2 = f32[6,128]{1,0:T(8,128)S(1)} collective-permute-done((f32[6,128]{1,0:T(8,128)S(1)}, f32[6,128]{1,0:T(8,128)S(1)}, u32[]{:S(2)}, u32[]{:S(2)}) %collective-permute-start.20) | collective-permute-done | bytes 3104 | tf_op jit(solution)/shard_map/ppermute | solution.py:20
  63.0 0.0 collective-permute-done.21.p3
  63.0 1.0 %shard_map.75 = (f32[64,512]{1,0:T(8,128)}, f32[64,512]{1,0:T(8,128)}) custom-call(f32[1,128]{1,0:T(1,128)S(1)} %pad_bitcast_fusion.shrink_ref, f32[8,128]{1,0:T(8,128)S(1)} %add.5.p0, f32[4,128]{1,0:T(4,128)S(1)} %collective-permute-done.19.p1, f32[6,128]{1,0:T(8,128)S(1)} %collective-permute-done.20.p2, f32[8,128]{1,0:T(8,128)S(1)} %collective-permute-done.21.p3, ...), custom_call_target="tpu_custom_call" | custom-call | tf_op jit(solution)/shard_map/pallas_call | solution.py:60
  (8 shorter events, 0.0 us)
Async XLA Ops:
  1.3 3.7 %copy-start = (bf16[2048,512]{1,0:T(8,128)(2,1)S(1)}, bf16[2048,512]{1,0:T(8,128)(2,1)}, u32[]{:S(2)}) copy-start(bf16[2048,512]{1,0:T(8,128)(2,1)} %dosage_ref.3) | copy-start | bytes 6291460
  1.9 10.1 %copy-start.1 = (f32[512,64]{0,1:T(8,128)S(1)}, f32[512,64]{0,1:T(8,128)}, u32[]{:S(2)}) copy-start(f32[512,64]{0,1:T(8,128)} %param.6) | copy-start | bytes 393220
  1.9 10.1 %copy-start.2 = (f32[8,640]{1,0:T(8,128)S(1)}, f32[8,640]{1,0:T(8,128)}, u32[]{:S(2)}) copy-start(f32[8,640]{1,0:T(8,128)} %shard_map.60.wide_ref) | copy-start | bytes 61444
  1.9 10.1 %collective-permute-start.3 = (f32[8,640]{1,0:T(8,128)}, f32[8,640]{1,0:T(8,128)S(1)}, u32[]{:S(2)}, u32[]{:S(2)}) collective-permute-start(f32[8,640]{1,0:T(8,128)} %shard_map.60.wide_ref), channel_id=1, source_target_pairs={{0,2},{1,3},{2,4},{3,5},{4,6},{5,7},{6,0},{7,1},{8,10},{9,11},{10,... | collective-permute-start | bytes 61448 | tf_op jit(solution)/shard_map/ppermute | solution.py:45
  5.3 6.7 %collective-permute-start.2 = (f32[8,512]{1,0:T(8,128)S(1)}, f32[8,512]{1,0:T(8,128)S(1)}, u32[]{:S(2)}, u32[]{:S(2)}) collective-permute-start(f32[8,512]{1,0:T(8,128)S(1)} %get-tuple-element.27.s0), channel_id=1, source_target_pairs={{0,24},{8,16},{16,8},{24,0},{1,25},{9,17},{17,9},{25,1},{2,26},{10... | collective-permute-start | bytes 49160 | tf_op jit(solution)/shard_map/ppermute | solution.py:20
  7.8 3.6 %collective-permute-start = (f32[2,512]{1,0:T(2,128)S(1)}, f32[2,512]{1,0:T(2,128)S(1)}, u32[]{:S(2)}, u32[]{:S(2)}) collective-permute-start(f32[2,512]{1,0:T(2,128)S(1)} %get-tuple-element.25), channel_id=1, source_target_pairs={{0,8},{8,0},{16,24},{24,16},{1,9},{9,1},{17,25},{25,17},{2,10},{10... | collective-permute-start | bytes 12296 | tf_op jit(solution)/shard_map/ppermute | solution.py:20
  8.3 3.6 %collective-permute-start.1 = (f32[2,512]{1,0:T(2,128)S(1)}, f32[2,512]{1,0:T(2,128)S(1)}, u32[]{:S(2)}, u32[]{:S(2)}) collective-permute-start(f32[2,512]{1,0:T(2,128)S(1)} %get-tuple-element.25), channel_id=1, source_target_pairs={{0,16},{8,24},{16,0},{24,8},{1,17},{9,25},{17,1},{25,9},{2,18},{10... | collective-permute-start | bytes 12296 | tf_op jit(solution)/shard_map/ppermute | solution.py:20
  13.0 6.6 %collective-permute-start.5 = (s16[64,2176]{1,0:T(8,128)(2,1)S(1)}, s16[64,2176]{1,0:T(8,128)(2,1)S(1)}, u32[]{:S(2)}, u32[]{:S(2)}) collective-permute-start(s16[64,2176]{1,0:T(8,128)(2,1)S(1)} %get-tuple-element.32.coded_ref), channel_id=1, source_target_pairs={{0,8},{1,2},{2,1},{3,4},{4,3},{5,6},{6,5},{7,15},{8,0},{9,10},{10,... | collective-permute-start | bytes 835592 | tf_op jit(solution)/shard_map/ppermute | solution.py:40
  14.5 1.6 %collective-permute-start.4 = (s16[64,2144]{1,0:T(8,128)(2,1)S(1)}, s16[64,2144]{1,0:T(8,128)(2,1)S(1)}, u32[]{:S(2)}, u32[]{:S(2)}) collective-permute-start(s16[64,2144]{1,0:T(8,128)(2,1)S(1)} %get-tuple-element.33), channel_id=1, source_target_pairs={{0,1},{1,0},{2,3},{3,2},{4,5},{5,4},{6,7},{7,6},{8,9},{9,8},{10,11... | collective-permute-start | bytes 823304 | tf_op jit(solution)/shard_map/ppermute | solution.py:20
  16.4 7.3 %collective-permute-start.7 = (s16[64,2176]{1,0:T(8,128)(2,1)S(1)}, s16[64,2176]{1,0:T(8,128)(2,1)S(1)}, u32[]{:S(2)}, u32[]{:S(2)}) collective-permute-start(s16[64,2176]{1,0:T(8,128)(2,1)S(1)} %shard_map.64), channel_id=1, source_target_pairs={{0,1},{1,3},{2,0},{3,5},{4,2},{5,7},{6,4},{7,6},{8,9},{9,11},{10,8... | collective-permute-start | bytes 835592 | tf_op jit(solution)/shard_map/ppermute | solution.py:29
  19.9 5.1 %collective-permute-start.6 = (s16[64,2176]{1,0:T(8,128)(2,1)S(1)}, s16[64,2176]{1,0:T(8,128)(2,1)S(1)}, u32[]{:S(2)}, u32[]{:S(2)}) collective-permute-start(s16[64,2176]{1,0:T(8,128)(2,1)S(1)} %shard_map.63), channel_id=1, source_target_pairs={{0,2},{1,0},{2,4},{3,1},{4,6},{5,3},{6,7},{7,5},{8,10},{9,8},{10,1... | collective-permute-start | bytes 835592 | tf_op jit(solution)/shard_map/ppermute | solution.py:29
  25.5 7.9 %collective-permute-start.10 = (s16[64,640]{1,0:T(8,128)(2,1)S(1)}, s16[64,640]{1,0:T(8,128)(2,1)S(1)}, u32[]{:S(2)}, u32[]{:S(2)}) collective-permute-start(s16[64,640]{1,0:T(8,128)(2,1)S(1)} %get-tuple-element.36.z0), channel_id=1, source_target_pairs={{0,24},{8,16},{16,8},{24,0},{1,25},{9,17},{17,9},{25,1},{2,26},{10... | collective-permute-start | bytes 245768 | tf_op jit(solution)/shard_map/ppermute | solution.py:20
  27.0 6.4 %collective-permute-start.8 = (s16[64,608]{1,0:T(8,128)(2,1)S(1)}, s16[64,608]{1,0:T(8,128)(2,1)S(1)}, u32[]{:S(2)}, u32[]{:S(2)}) collective-permute-start(s16[64,608]{1,0:T(8,128)(2,1)S(1)} %get-tuple-element.37), channel_id=1, source_target_pairs={{0,8},{8,0},{16,24},{24,16},{1,9},{9,1},{17,25},{25,17},{2,10},{10... | collective-permute-start | bytes 233480 | tf_op jit(solution)/shard_map/ppermute | solution.py:20
  27.6 5.8 %collective-permute-start.9 = (s16[64,576]{1,0:T(8,128)(2,1)S(1)}, s16[64,576]{1,0:T(8,128)(2,1)S(1)}, u32[]{:S(2)}, u32[]{:S(2)}) collective-permute-start(s16[64,576]{1,0:T(8,128)(2,1)S(1)} %get-tuple-element.38), channel_id=1, source_target_pairs={{0,16},{8,24},{16,0},{24,8},{1,17},{9,25},{17,1},{25,9},{2,18},{10... | collective-permute-start | bytes 221192 | tf_op jit(solution)/shard_map/ppermute | solution.py:20
  34.1 6.6 %collective-permute-start.12 = (s16[64,2176]{1,0:T(8,128)(2,1)S(1)}, s16[64,2176]{1,0:T(8,128)(2,1)S(1)}, u32[]{:S(2)}, u32[]{:S(2)}) collective-permute-start(s16[64,2176]{1,0:T(8,128)(2,1)S(1)} %get-tuple-element.41.coded_ref), channel_id=1, source_target_pairs={{0,8},{1,2},{2,1},{3,4},{4,3},{5,6},{6,5},{7,15},{8,0},{9,10},{10,... | collective-permute-start | bytes 835592 | tf_op jit(solution)/shard_map/ppermute | solution.py:40
  35.5 1.7 %collective-permute-start.11 = (s16[64,2144]{1,0:T(8,128)(2,1)S(1)}, s16[64,2144]{1,0:T(8,128)(2,1)S(1)}, u32[]{:S(2)}, u32[]{:S(2)}) collective-permute-start(s16[64,2144]{1,0:T(8,128)(2,1)S(1)} %get-tuple-element.42), channel_id=1, source_target_pairs={{0,1},{1,0},{2,3},{3,2},{4,5},{5,4},{6,7},{7,6},{8,9},{9,8},{10,11... | collective-permute-start | bytes 823304 | tf_op jit(solution)/shard_map/ppermute | solution.py:20
  37.4 7.1 %collective-permute-start.14 = (s16[64,2176]{1,0:T(8,128)(2,1)S(1)}, s16[64,2176]{1,0:T(8,128)(2,1)S(1)}, u32[]{:S(2)}, u32[]{:S(2)}) collective-permute-start(s16[64,2176]{1,0:T(8,128)(2,1)S(1)} %shard_map.71), channel_id=1, source_target_pairs={{0,1},{1,3},{2,0},{3,5},{4,2},{5,7},{6,4},{7,6},{8,9},{9,11},{10,8... | collective-permute-start | bytes 835592 | tf_op jit(solution)/shard_map/ppermute | solution.py:29
  41.0 5.2 %collective-permute-start.13 = (s16[64,2176]{1,0:T(8,128)(2,1)S(1)}, s16[64,2176]{1,0:T(8,128)(2,1)S(1)}, u32[]{:S(2)}, u32[]{:S(2)}) collective-permute-start(s16[64,2176]{1,0:T(8,128)(2,1)S(1)} %shard_map.70), channel_id=1, source_target_pairs={{0,2},{1,0},{2,4},{3,1},{4,6},{5,3},{6,7},{7,5},{8,10},{9,8},{10,1... | collective-permute-start | bytes 835592 | tf_op jit(solution)/shard_map/ppermute | solution.py:29
  42.4 17.6 %copy-start.3 = (f32[64]{0:T(128)S(1)}, f32[64]{0:T(128)}, u32[]{:S(2)}) copy-start(f32[64]{0:T(128)} %param.7) | copy-start | bytes 772
  46.9 7.7 %collective-permute-start.17 = (s16[64,640]{1,0:T(8,128)(2,1)S(1)}, s16[64,640]{1,0:T(8,128)(2,1)S(1)}, u32[]{:S(2)}, u32[]{:S(2)}) collective-permute-start(s16[64,640]{1,0:T(8,128)(2,1)S(1)} %get-tuple-element.43.z0), channel_id=1, source_target_pairs={{0,24},{8,16},{16,8},{24,0},{1,25},{9,17},{17,9},{25,1},{2,26},{10... | collective-permute-start | bytes 245768 | tf_op jit(solution)/shard_map/ppermute | solution.py:20
  48.8 5.8 %collective-permute-start.15 = (s16[64,608]{1,0:T(8,128)(2,1)S(1)}, s16[64,608]{1,0:T(8,128)(2,1)S(1)}, u32[]{:S(2)}, u32[]{:S(2)}) collective-permute-start(s16[64,608]{1,0:T(8,128)(2,1)S(1)} %get-tuple-element.44), channel_id=1, source_target_pairs={{0,8},{8,0},{16,24},{24,16},{1,9},{9,1},{17,25},{25,17},{2,10},{10... | collective-permute-start | bytes 233480 | tf_op jit(solution)/shard_map/ppermute | solution.py:20
  49.4 5.2 %collective-permute-start.16 = (s16[64,576]{1,0:T(8,128)(2,1)S(1)}, s16[64,576]{1,0:T(8,128)(2,1)S(1)}, u32[]{:S(2)}, u32[]{:S(2)}) collective-permute-start(s16[64,576]{1,0:T(8,128)(2,1)S(1)} %get-tuple-element.45), channel_id=1, source_target_pairs={{0,16},{8,24},{16,0},{24,8},{1,17},{9,25},{17,1},{25,9},{2,18},{10... | collective-permute-start | bytes 221192 | tf_op jit(solution)/shard_map/ppermute | solution.py:20
  54.9 1.2 %collective-permute-start.18 = (f32[8,128]{1,0:T(8,128)S(1)}, f32[8,128]{1,0:T(8,128)S(1)}, u32[]{:S(2)}, u32[]{:S(2)}) collective-permute-start(f32[8,128]{1,0:T(8,128)S(1)} %shard_map.73), channel_id=1, source_target_pairs={{0,1},{1,0},{2,3},{3,2},{4,5},{5,4},{6,7},{7,6},{8,9},{9,8},{10,11... | collective-permute-start | bytes 12296 | tf_op jit(solution)/shard_map/ppermute | solution.py:20
  56.1 6.9 %collective-permute-start.21 = (f32[8,128]{1,0:T(8,128)S(1)}, f32[8,128]{1,0:T(8,128)S(1)}, u32[]{:S(2)}, u32[]{:S(2)}) collective-permute-start(f32[8,128]{1,0:T(8,128)S(1)} %add.5.p0), channel_id=1, source_target_pairs={{0,7},{1,6},{2,5},{3,4},{4,3},{5,2},{6,1},{7,0},{8,15},{9,14},{10,... | collective-permute-start | bytes 12296 | tf_op jit(solution)/shard_map/ppermute | solution.py:20
  58.9 3.0 %collective-permute-start.19 = (f32[4,128]{1,0:T(4,128)S(1)}, f32[4,128]{1,0:T(4,128)S(1)}, u32[]{:S(2)}, u32[]{:S(2)}) collective-permute-start(f32[4,128]{1,0:T(4,128)S(1)} %slice.6), channel_id=1, source_target_pairs={{0,3},{1,2},{2,1},{3,0},{4,7},{5,6},{6,5},{7,4},{8,11},{9,10},{10,... | collective-permute-start | bytes 6152 | tf_op jit(solution)/shard_map/ppermute | solution.py:20
  59.1 3.9 %collective-permute-start.20 = (f32[6,128]{1,0:T(8,128)S(1)}, f32[6,128]{1,0:T(8,128)S(1)}, u32[]{:S(2)}, u32[]{:S(2)}) collective-permute-start(f32[6,128]{1,0:T(8,128)S(1)} %bitcast.9), channel_id=1, source_target_pairs={{0,5},{1,4},{2,7},{3,6},{4,1},{5,0},{6,3},{7,2},{8,13},{9,12},{10,... | collective-permute-start | bytes 9224 | tf_op jit(solution)/shard_map/ppermute | solution.py:20

commit v15 on v14

--- a/solution.py
+++ b/solution.py
@@ -13,6 +13,7 @@
 LEAST = 64
 CHUNK = 512
 UNIT = 14
+SAFE = 1.0 - 2.0**-13
 ROWS = 256
 
 
@@ -102,12 +103,12 @@
 
 
 def fixed(value):
-    return jnp.clip(jnp.round(value), -32767.0, 32767.0).astype(jnp.int32).astype(jnp.int16)
+    return jnp.round(value).astype(jnp.int32).astype(jnp.int16)
 
 
 def scale_of(peak):
     exponent = jnp.floor(jnp.log2(jnp.maximum(peak, 1e-30)))
-    return exponent, jnp.exp2(UNIT - exponent)
+    return exponent, jnp.exp2(UNIT - exponent) * SAFE
 
 
 def encode(own_ref, coded_ref, shared_ref, width):
@@ -134,7 +135,7 @@
 
 
 def unit(exponent, use=True):
-    return jnp.where(use, jnp.exp2(exponent - UNIT), 0.0)
+    return jnp.where(use, jnp.exp2(exponent - UNIT) / SAFE, 0.0)
 
 
 def grid_values(coded_ref):
@@ -211,7 +212,7 @@
     other_exponent, other_width = aux(other_ref)[:2]
     near = near_ref[0:1, 0:1]
     sent = jnp.maximum(exponent, other_exponent) + 1.0
-    scale = jnp.exp2(UNIT - sent)
+    scale = jnp.exp2(UNIT - sent) * SAFE
     rises = odd if up else jnp.logical_not(odd)
     known = True if up else side
     own_scale = jnp.where(jnp.where(rises, width, near) >= 2, scale, 0.0)

time: 64.1 us -> 64 us (level)
  no operation moved by 1% of the time
where the time goes in v15:
time: 64 us; the launch traced here: 63.9 us
  waiting for transfers between devices  30.9 us (48%)
  starting transfers between devices  24 us (38%)
  Pallas kernels  7.45 us (12%)
  between operations  1.42 us (2%)
    ppermute x15, waiting for transfers between devices, swap(): lax.ppermute(value, axis, [(i, i ^ bits) for i in range(lax.axis_size(axi...  17.4 us
    ppermute x15, starting transfers between devices, swap(): lax.ppermute(value, axis, [(i, i ^ bits) for i in range(lax.axis_size(axi...  15.3 us
    ppermute x4, waiting for transfers between devices, crossing(): return lax.ppermute(value, 'snp', pairs)  7.62 us
    pallas_call x16, Pallas kernels, call(): pl.pallas_call(body, out_shape=outs, in_specs=specs, out_specs=[pl.BlockS...  6.84 us
    ppermute x2, waiting for transfers between devices, adjacent(): return lax.ppermute(value, ('samp', 'snp'), pairs)  5.93 us
    ppermute x1, starting transfers between devices, shifted(): lax.ppermute(value, 'snp', [(i, (i + 2) % count) for i in range(count)])  3.02 us
    ppermute x2, starting transfers between devices, adjacent(): return lax.ppermute(value, ('samp', 'snp'), pairs)  2.94 us
    ppermute x4, starting transfers between devices, crossing(): return lax.ppermute(value, 'snp', pairs)  2.77 us
  transfers between devices with their start and end apart: 22, of which 15 were waited for; matrix products, arithmetic and copies ran while one was open for 0% of the time, Pallas kernels for 4%

profile of v15, /device:TPU:0, one launch (start us, length us, event | category | flops | bytes accessed | tf_op | source)
XLA Modules:
  0.0 63.9 jit_solution(13310573102404418813)
XLA Ops:
  1.3 0.0 copy-start
  1.3 0.6 shard_map.60.wide_ref
  1.9 3.0 %collective-permute-start.3 = (f32[8,640]{1,0:T(8,128)}, f32[8,640]{1,0:T(8,128)S(1)}, u32[]{:S(2)}, u32[]{:S(2)}) collective-permute-start(f32[8,640]{1,0:T(8,128)} %shard_map.60.wide_ref), channel_id=1, source_target_pairs={{0,2},{1,3},{2,4},{3,5},{4,6},{5,7},{6,0},{7,1},{8,10},{9,11},{10,... | collective-permute-start | bytes 61448 | tf_op jit(solution)/shard_map/ppermute | solution.py:46
  4.9 0.0 copy-done
  4.9 0.4 shard_map.59
  5.3 2.5 %collective-permute-start.2 = (f32[8,512]{1,0:T(8,128)S(1)}, f32[8,512]{1,0:T(8,128)S(1)}, u32[]{:S(2)}, u32[]{:S(2)}) collective-permute-start(f32[8,512]{1,0:T(8,128)S(1)} %get-tuple-element.27.s0), channel_id=1, source_target_pairs={{0,24},{8,16},{16,8},{24,0},{1,25},{9,17},{17,9},{25,1},{2,26},{10... | collective-permute-start | bytes 49160 | tf_op jit(solution)/shard_map/ppermute | solution.py:21
  7.8 0.5 collective-permute-start
  8.3 0.5 collective-permute-start.1
  8.9 2.6 %collective-permute-done.s1 = f32[2,512]{1,0:T(2,128)S(1)} collective-permute-done((f32[2,512]{1,0:T(2,128)S(1)}, f32[2,512]{1,0:T(2,128)S(1)}, u32[]{:S(2)}, u32[]{:S(2)}) %collective-permute-start) | collective-permute-done | bytes 4128 | tf_op jit(solution)/shard_map/ppermute | solution.py:21
  11.4 0.5 collective-permute-done.1.s2
  12.0 0.0 collective-permute-done.2.s3
  12.0 0.0 collective-permute-done.3.near_ref
  12.0 1.0 %shard_map.61 = (bf16[2048,512]{1,0:T(8,128)(2,1)S(1)}, f32[64,2048]{1,0:T(8,128)S(1)}, s16[64,2176]{1,0:T(8,128)(2,1)S(1)}, s16[64,2144]{1,0:T(8,128)(2,1)S(1)}) custom-call(f32[8,640]{1,0:T(8,128)S(1)} %copy-done.2, f32[8,512]{1,0:T(8,128)S(1)} %get-tuple-element.27.s0, f32[2,512]{1,0:T(2,128)S(1)} %collective-permute-done.s1, ...), custom_call_target="tpu_custom_call" | custom-call | tf_op jit(solution)/shard_map/pallas_call | solution.py:61
  13.0 1.6 %collective-permute-start.5 = (s16[64,2176]{1,0:T(8,128)(2,1)S(1)}, s16[64,2176]{1,0:T(8,128)(2,1)S(1)}, u32[]{:S(2)}, u32[]{:S(2)}) collective-permute-start(s16[64,2176]{1,0:T(8,128)(2,1)S(1)} %get-tuple-element.32.coded_ref), channel_id=1, source_target_pairs={{0,8},{1,2},{2,1},{3,4},{4,3},{5,6},{6,5},{7,15},{8,0},{9,10},{10,... | collective-permute-start | bytes 835592 | tf_op jit(solution)/shard_map/ppermute | solution.py:41
  14.5 0.2 collective-permute-start.4
  14.7 1.4 %collective-permute-done.4.partner_ref.other_ref = s16[64,2144]{1,0:T(8,128)(2,1)S(1)} collective-permute-done((s16[64,2144]{1,0:T(8,128)(2,1)S(1)}, s16[64,2144]{1,0:T(8,128)(2,1)S(1)}, u32[]{:S(2)}, u32[]{:S(2)}) %collective-permute-start.4) | collective-permute-done | bytes 274464 | tf_op jit(solution)/shard_map/ppermute | solution.py:21
  16.1 0.2 shard_map.64
  16.3 0.2 collective-permute-start.7
  16.5 3.0 %collective-permute-done.5.next_ref.other_ref = s16[64,2176]{1,0:T(8,128)(2,1)S(1)} collective-permute-done((s16[64,2176]{1,0:T(8,128)(2,1)S(1)}, s16[64,2176]{1,0:T(8,128)(2,1)S(1)}, u32[]{:S(2)}, u32[]{:S(2)}) %collective-permute-start.5) | collective-permute-done | bytes 278560 | tf_op jit(solution)/shard_map/ppermute | solution.py:41
  19.6 0.2 shard_map.63
  19.8 1.0 %collective-permute-start.6 = (s16[64,2176]{1,0:T(8,128)(2,1)S(1)}, s16[64,2176]{1,0:T(8,128)(2,1)S(1)}, u32[]{:S(2)}, u32[]{:S(2)}) collective-permute-start(s16[64,2176]{1,0:T(8,128)(2,1)S(1)} %shard_map.63), channel_id=1, source_target_pairs={{0,2},{1,0},{2,4},{3,1},{4,6},{5,3},{6,7},{7,5},{8,10},{9,8},{10,1... | collective-permute-start | bytes 835592 | tf_op jit(solution)/shard_map/ppermute | solution.py:30
  20.8 0.2 shard_map.62.early_ref
  21.1 2.5 %collective-permute-done.7.cross_ref = s16[64,2176]{1,0:T(8,128)(2,1)S(1)} collective-permute-done((s16[64,2176]{1,0:T(8,128)(2,1)S(1)}, s16[64,2176]{1,0:T(8,128)(2,1)S(1)}, u32[]{:S(2)}, u32[]{:S(2)}) %collective-permute-start.7) | collective-permute-done | bytes 278560 | tf_op jit(solution)/shard_map/ppermute | solution.py:30
  23.6 1.3 %collective-permute-done.6.same_ref = s16[64,2176]{1,0:T(8,128)(2,1)S(1)} collective-permute-done((s16[64,2176]{1,0:T(8,128)(2,1)S(1)}, s16[64,2176]{1,0:T(8,128)(2,1)S(1)}, u32[]{:S(2)}, u32[]{:S(2)}) %collective-permute-start.6) | collective-permute-done | bytes 278560 | tf_op jit(solution)/shard_map/ppermute | solution.py:30
  24.9 0.6 shard_map.65
  25.5 1.5 %collective-permute-start.10 = (s16[64,640]{1,0:T(8,128)(2,1)S(1)}, s16[64,640]{1,0:T(8,128)(2,1)S(1)}, u32[]{:S(2)}, u32[]{:S(2)}) collective-permute-start(s16[64,640]{1,0:T(8,128)(2,1)S(1)} %get-tuple-element.36.z0), channel_id=1, source_target_pairs={{0,24},{8,16},{16,8},{24,0},{1,25},{9,17},{17,9},{25,1},{2,26},{10... | collective-permute-start | bytes 245768 | tf_op jit(solution)/shard_map/ppermute | solution.py:21
  27.0 0.5 collective-permute-start.8
  27.5 1.5 %collective-permute-start.9 = (s16[64,576]{1,0:T(8,128)(2,1)S(1)}, s16[64,576]{1,0:T(8,128)(2,1)S(1)}, u32[]{:S(2)}, u32[]{:S(2)}) collective-permute-start(s16[64,576]{1,0:T(8,128)(2,1)S(1)} %get-tuple-element.38), channel_id=1, source_target_pairs={{0,16},{8,24},{16,0},{24,8},{1,17},{9,25},{17,1},{25,9},{2,18},{10... | collective-permute-start | bytes 221192 | tf_op jit(solution)/shard_map/ppermute | solution.py:21
  29.1 0.6 shard_map.66.turned_ref
  29.7 3.7 %collective-permute-done.9.z2 = s16[64,576]{1,0:T(8,128)(2,1)S(1)} collective-permute-done((s16[64,576]{1,0:T(8,128)(2,1)S(1)}, s16[64,576]{1,0:T(8,128)(2,1)S(1)}, u32[]{:S(2)}, u32[]{:S(2)}) %collective-permute-start.9) | collective-permute-done | bytes 73760 | tf_op jit(solution)/shard_map/ppermute | solution.py:21
  33.4 0.0 collective-permute-done.8.z1
  33.4 0.0 collective-permute-done.10.z3
  33.4 0.7 %shard_map.67 = (f32[64,512]{1,0:T(8,128)S(1)}, f32[64,2048]{1,0:T(8,128)S(1)}, s16[64,2176]{1,0:T(8,128)(2,1)S(1)}, s16[64,2144]{1,0:T(8,128)(2,1)S(1)}) custom-call(f32[8,640]{1,0:T(8,128)S(1)} %copy-done.2, s16[64,640]{1,0:T(8,128)(2,1)S(1)} %get-tuple-element.36.z0, s16[64,608]{1,0:T(8,128)(2,1)S(1)} %collective-permute-done.8.z1, ...), custom_call_target="tpu_custom_call" | custom-call | tf_op jit(solution)/shard_map/pallas_call | solution.py:61
  34.0 1.4 %collective-permute-start.12 = (s16[64,2176]{1,0:T(8,128)(2,1)S(1)}, s16[64,2176]{1,0:T(8,128)(2,1)S(1)}, u32[]{:S(2)}, u32[]{:S(2)}) collective-permute-start(s16[64,2176]{1,0:T(8,128)(2,1)S(1)} %get-tuple-element.41.coded_ref), channel_id=1, source_target_pairs={{0,8},{1,2},{2,1},{3,4},{4,3},{5,6},{6,5},{7,15},{8,0},{9,10},{10,... | collective-permute-start | bytes 835592 | tf_op jit(solution)/shard_map/ppermute | solution.py:41
  35.4 0.5 collective-permute-start.11
  35.9 1.2 %collective-permute-done.11.partner_ref.other_ref = s16[64,2144]{1,0:T(8,128)(2,1)S(1)} collective-permute-done((s16[64,2144]{1,0:T(8,128)(2,1)S(1)}, s16[64,2144]{1,0:T(8,128)(2,1)S(1)}, u32[]{:S(2)}, u32[]{:S(2)}) %collective-permute-start.11) | collective-permute-done | bytes 274464 | tf_op jit(solution)/shard_map/ppermute | solution.py:21
  37.1 0.2 shard_map.71
  37.4 0.4 collective-permute-start.14
  37.7 2.9 %collective-permute-done.12.next_ref.other_ref = s16[64,2176]{1,0:T(8,128)(2,1)S(1)} collective-permute-done((s16[64,2176]{1,0:T(8,128)(2,1)S(1)}, s16[64,2176]{1,0:T(8,128)(2,1)S(1)}, u32[]{:S(2)}, u32[]{:S(2)}) %collective-permute-start.12) | collective-permute-done | bytes 278560 | tf_op jit(solution)/shard_map/ppermute | solution.py:41
  40.6 0.2 shard_map.70
  40.9 1.1 %collective-permute-start.13 = (s16[64,2176]{1,0:T(8,128)(2,1)S(1)}, s16[64,2176]{1,0:T(8,128)(2,1)S(1)}, u32[]{:S(2)}, u32[]{:S(2)}) collective-permute-start(s16[64,2176]{1,0:T(8,128)(2,1)S(1)} %shard_map.70), channel_id=1, source_target_pairs={{0,2},{1,0},{2,4},{3,1},{4,6},{5,3},{6,7},{7,5},{8,10},{9,8},{10,1... | collective-permute-start | bytes 835592 | tf_op jit(solution)/shard_map/ppermute | solution.py:30
  42.0 0.2 shard_map.69.early_ref
  42.3 0.0 copy-start.3
  42.3 2.2 %collective-permute-done.14.cross_ref = s16[64,2176]{1,0:T(8,128)(2,1)S(1)} collective-permute-done((s16[64,2176]{1,0:T(8,128)(2,1)S(1)}, s16[64,2176]{1,0:T(8,128)(2,1)S(1)}, u32[]{:S(2)}, u32[]{:S(2)}) %collective-permute-start.14) | collective-permute-done | bytes 278560 | tf_op jit(solution)/shard_map/ppermute | solution.py:30
  44.5 1.6 %collective-permute-done.13.same_ref = s16[64,2176]{1,0:T(8,128)(2,1)S(1)} collective-permute-done((s16[64,2176]{1,0:T(8,128)(2,1)S(1)}, s16[64,2176]{1,0:T(8,128)(2,1)S(1)}, u32[]{:S(2)}, u32[]{:S(2)}) %collective-permute-start.13) | collective-permute-done | bytes 278560 | tf_op jit(solution)/shard_map/ppermute | solution.py:30
  46.1 0.7 %shard_map.72 = (s16[64,640]{1,0:T(8,128)(2,1)S(1)}, s16[64,608]{1,0:T(8,128)(2,1)S(1)}, s16[64,576]{1,0:T(8,128)(2,1)S(1)}) custom-call(f32[64,2048]{1,0:T(8,128)S(1)} %get-tuple-element.40.own_ref, f32[64,2048]{1,0:T(8,128)S(1)} %shard_map.69.early_ref, s16[64,2176]{1,0:T(8,128)(2,1)S(1)} %collective-permute-done.13.same_ref, ...), custom_call_target="tpu_custom_call" | custom-call | tf_op jit(solution)/shard_map/pallas_call | solution.py:61
  46.8 1.9 %collective-permute-start.17 = (s16[64,640]{1,0:T(8,128)(2,1)S(1)}, s16[64,640]{1,0:T(8,128)(2,1)S(1)}, u32[]{:S(2)}, u32[]{:S(2)}) collective-permute-start(s16[64,640]{1,0:T(8,128)(2,1)S(1)} %get-tuple-element.43.z0), channel_id=1, source_target_pairs={{0,24},{8,16},{16,8},{24,0},{1,25},{9,17},{17,9},{25,1},{2,26},{10... | collective-permute-start | bytes 245768 | tf_op jit(solution)/shard_map/ppermute | solution.py:21
  48.8 0.5 collective-permute-start.15
  49.3 1.1 %collective-permute-start.16 = (s16[64,576]{1,0:T(8,128)(2,1)S(1)}, s16[64,576]{1,0:T(8,128)(2,1)S(1)}, u32[]{:S(2)}, u32[]{:S(2)}) collective-permute-start(s16[64,576]{1,0:T(8,128)(2,1)S(1)} %get-tuple-element.45), channel_id=1, source_target_pairs={{0,16},{8,24},{16,0},{24,8},{1,17},{9,25},{17,1},{25,9},{2,18},{10... | collective-permute-start | bytes 221192 | tf_op jit(solution)/shard_map/ppermute | solution.py:21
  50.4 0.1 shard_map.68.parts_ref
  50.5 4.0 %collective-permute-done.16.z2 = s16[64,576]{1,0:T(8,128)(2,1)S(1)} collective-permute-done((s16[64,576]{1,0:T(8,128)(2,1)S(1)}, s16[64,576]{1,0:T(8,128)(2,1)S(1)}, u32[]{:S(2)}, u32[]{:S(2)}) %collective-permute-start.16) | collective-permute-done | bytes 73760 | tf_op jit(solution)/shard_map/ppermute | solution.py:21
  54.5 0.0 collective-permute-done.15.z1
  54.5 0.0 collective-permute-done.17.z3
  54.5 0.2 shard_map.73
  54.8 0.0 collective-permute-start.18
  54.8 1.2 %collective-permute-done.18 = f32[8,128]{1,0:T(8,128)S(1)} collective-permute-done((f32[8,128]{1,0:T(8,128)S(1)}, f32[8,128]{1,0:T(8,128)S(1)}, u32[]{:S(2)}, u32[]{:S(2)}) %collective-permute-start.18) | collective-permute-done | bytes 4128 | tf_op jit(solution)/shard_map/ppermute | solution.py:21
  56.0 2.9 %collective-permute-start.21 = (f32[8,128]{1,0:T(8,128)S(1)}, f32[8,128]{1,0:T(8,128)S(1)}, u32[]{:S(2)}, u32[]{:S(2)}) collective-permute-start(f32[8,128]{1,0:T(8,128)S(1)} %add.5.p0), channel_id=1, source_target_pairs={{0,7},{1,6},{2,5},{3,4},{4,3},{5,2},{6,1},{7,0},{8,15},{9,14},{10,... | collective-permute-start | bytes 12296 | tf_op jit(solution)/shard_map/ppermute | solution.py:21
  58.9 0.1 collective-permute-start.19
  59.0 0.9 %collective-permute-start.20 = (f32[6,128]{1,0:T(8,128)S(1)}, f32[6,128]{1,0:T(8,128)S(1)}, u32[]{:S(2)}, u32[]{:S(2)}) collective-permute-start(f32[6,128]{1,0:T(8,128)S(1)} %bitcast.9), channel_id=1, source_target_pairs={{0,5},{1,4},{2,7},{3,6},{4,1},{5,0},{6,3},{7,2},{8,13},{9,12},{10,... | collective-permute-start | bytes 9224 | tf_op jit(solution)/shard_map/ppermute | solution.py:21
  59.9 0.1 shard_map.74.second_ref
  60.0 1.9 %collective-permute-done.19.p1 = f32[4,128]{1,0:T(4,128)S(1)} collective-permute-done((f32[4,128]{1,0:T(4,128)S(1)}, f32[4,128]{1,0:T(4,128)S(1)}, u32[]{:S(2)}, u32[]{:S(2)}) %collective-permute-start.19) | collective-permute-done | bytes 2080 | tf_op jit(solution)/shard_map/ppermute | solution.py:21
  61.9 1.0 %collective-permute-done.20.p2 = f32[6,128]{1,0:T(8,128)S(1)} collective-permute-done((f32[6,128]{1,0:T(8,128)S(1)}, f32[6,128]{1,0:T(8,128)S(1)}, u32[]{:S(2)}, u32[]{:S(2)}) %collective-permute-start.20) | collective-permute-done | bytes 3104 | tf_op jit(solution)/shard_map/ppermute | solution.py:21
  62.9 0.0 collective-permute-done.21.p3
  62.9 1.0 %shard_map.75 = (f32[64,512]{1,0:T(8,128)}, f32[64,512]{1,0:T(8,128)}) custom-call(f32[1,128]{1,0:T(1,128)S(1)} %pad_bitcast_fusion.shrink_ref, f32[8,128]{1,0:T(8,128)S(1)} %add.5.p0, f32[4,128]{1,0:T(4,128)S(1)} %collective-permute-done.19.p1, f32[6,128]{1,0:T(8,128)S(1)} %collective-permute-done.20.p2, f32[8,128]{1,0:T(8,128)S(1)} %collective-permute-done.21.p3, ...), custom_call_target="tpu_custom_call" | custom-call | tf_op jit(solution)/shard_map/pallas_call | solution.py:61
  (8 shorter events, 0.0 us)
Async XLA Ops:
  1.3 3.7 %copy-start = (bf16[2048,512]{1,0:T(8,128)(2,1)S(1)}, bf16[2048,512]{1,0:T(8,128)(2,1)}, u32[]{:S(2)}) copy-start(bf16[2048,512]{1,0:T(8,128)(2,1)} %dosage_ref.3) | copy-start | bytes 6291460
  1.9 10.1 %copy-start.1 = (f32[512,64]{0,1:T(8,128)S(1)}, f32[512,64]{0,1:T(8,128)}, u32[]{:S(2)}) copy-start(f32[512,64]{0,1:T(8,128)} %param.6) | copy-start | bytes 393220
  1.9 10.1 %copy-start.2 = (f32[8,640]{1,0:T(8,128)S(1)}, f32[8,640]{1,0:T(8,128)}, u32[]{:S(2)}) copy-start(f32[8,640]{1,0:T(8,128)} %shard_map.60.wide_ref) | copy-start | bytes 61444
  1.9 10.1 %collective-permute-start.3 = (f32[8,640]{1,0:T(8,128)}, f32[8,640]{1,0:T(8,128)S(1)}, u32[]{:S(2)}, u32[]{:S(2)}) collective-permute-start(f32[8,640]{1,0:T(8,128)} %shard_map.60.wide_ref), channel_id=1, source_target_pairs={{0,2},{1,3},{2,4},{3,5},{4,6},{5,7},{6,0},{7,1},{8,10},{9,11},{10,... | collective-permute-start | bytes 61448 | tf_op jit(solution)/shard_map/ppermute | solution.py:46
  5.3 6.7 %collective-permute-start.2 = (f32[8,512]{1,0:T(8,128)S(1)}, f32[8,512]{1,0:T(8,128)S(1)}, u32[]{:S(2)}, u32[]{:S(2)}) collective-permute-start(f32[8,512]{1,0:T(8,128)S(1)} %get-tuple-element.27.s0), channel_id=1, source_target_pairs={{0,24},{8,16},{16,8},{24,0},{1,25},{9,17},{17,9},{25,1},{2,26},{10... | collective-permute-start | bytes 49160 | tf_op jit(solution)/shard_map/ppermute | solution.py:21
  7.8 3.6 %collective-permute-start = (f32[2,512]{1,0:T(2,128)S(1)}, f32[2,512]{1,0:T(2,128)S(1)}, u32[]{:S(2)}, u32[]{:S(2)}) collective-permute-start(f32[2,512]{1,0:T(2,128)S(1)} %get-tuple-element.25), channel_id=1, source_target_pairs={{0,8},{8,0},{16,24},{24,16},{1,9},{9,1},{17,25},{25,17},{2,10},{10... | collective-permute-start | bytes 12296 | tf_op jit(solution)/shard_map/ppermute | solution.py:21
  8.3 3.6 %collective-permute-start.1 = (f32[2,512]{1,0:T(2,128)S(1)}, f32[2,512]{1,0:T(2,128)S(1)}, u32[]{:S(2)}, u32[]{:S(2)}) collective-permute-start(f32[2,512]{1,0:T(2,128)S(1)} %get-tuple-element.25), channel_id=1, source_target_pairs={{0,16},{8,24},{16,0},{24,8},{1,17},{9,25},{17,1},{25,9},{2,18},{10... | collective-permute-start | bytes 12296 | tf_op jit(solution)/shard_map/ppermute | solution.py:21
  13.0 6.6 %collective-permute-start.5 = (s16[64,2176]{1,0:T(8,128)(2,1)S(1)}, s16[64,2176]{1,0:T(8,128)(2,1)S(1)}, u32[]{:S(2)}, u32[]{:S(2)}) collective-permute-start(s16[64,2176]{1,0:T(8,128)(2,1)S(1)} %get-tuple-element.32.coded_ref), channel_id=1, source_target_pairs={{0,8},{1,2},{2,1},{3,4},{4,3},{5,6},{6,5},{7,15},{8,0},{9,10},{10,... | collective-permute-start | bytes 835592 | tf_op jit(solution)/shard_map/ppermute | solution.py:41
  14.5 1.6 %collective-permute-start.4 = (s16[64,2144]{1,0:T(8,128)(2,1)S(1)}, s16[64,2144]{1,0:T(8,128)(2,1)S(1)}, u32[]{:S(2)}, u32[]{:S(2)}) collective-permute-start(s16[64,2144]{1,0:T(8,128)(2,1)S(1)} %get-tuple-element.33), channel_id=1, source_target_pairs={{0,1},{1,0},{2,3},{3,2},{4,5},{5,4},{6,7},{7,6},{8,9},{9,8},{10,11... | collective-permute-start | bytes 823304 | tf_op jit(solution)/shard_map/ppermute | solution.py:21
  16.3 7.3 %collective-permute-start.7 = (s16[64,2176]{1,0:T(8,128)(2,1)S(1)}, s16[64,2176]{1,0:T(8,128)(2,1)S(1)}, u32[]{:S(2)}, u32[]{:S(2)}) collective-permute-start(s16[64,2176]{1,0:T(8,128)(2,1)S(1)} %shard_map.64), channel_id=1, source_target_pairs={{0,1},{1,3},{2,0},{3,5},{4,2},{5,7},{6,4},{7,6},{8,9},{9,11},{10,8... | collective-permute-start | bytes 835592 | tf_op jit(solution)/shard_map/ppermute | solution.py:30
  19.8 5.1 %collective-permute-start.6 = (s16[64,2176]{1,0:T(8,128)(2,1)S(1)}, s16[64,2176]{1,0:T(8,128)(2,1)S(1)}, u32[]{:S(2)}, u32[]{:S(2)}) collective-permute-start(s16[64,2176]{1,0:T(8,128)(2,1)S(1)} %shard_map.63), channel_id=1, source_target_pairs={{0,2},{1,0},{2,4},{3,1},{4,6},{5,3},{6,7},{7,5},{8,10},{9,8},{10,1... | collective-permute-start | bytes 835592 | tf_op jit(solution)/shard_map/ppermute | solution.py:30
  25.5 7.9 %collective-permute-start.10 = (s16[64,640]{1,0:T(8,128)(2,1)S(1)}, s16[64,640]{1,0:T(8,128)(2,1)S(1)}, u32[]{:S(2)}, u32[]{:S(2)}) collective-permute-start(s16[64,640]{1,0:T(8,128)(2,1)S(1)} %get-tuple-element.36.z0), channel_id=1, source_target_pairs={{0,24},{8,16},{16,8},{24,0},{1,25},{9,17},{17,9},{25,1},{2,26},{10... | collective-permute-start | bytes 245768 | tf_op jit(solution)/shard_map/ppermute | solution.py:21
  27.0 6.4 %collective-permute-start.8 = (s16[64,608]{1,0:T(8,128)(2,1)S(1)}, s16[64,608]{1,0:T(8,128)(2,1)S(1)}, u32[]{:S(2)}, u32[]{:S(2)}) collective-permute-start(s16[64,608]{1,0:T(8,128)(2,1)S(1)} %get-tuple-element.37), channel_id=1, source_target_pairs={{0,8},{8,0},{16,24},{24,16},{1,9},{9,1},{17,25},{25,17},{2,10},{10... | collective-permute-start | bytes 233480 | tf_op jit(solution)/shard_map/ppermute | solution.py:21
  27.5 5.8 %collective-permute-start.9 = (s16[64,576]{1,0:T(8,128)(2,1)S(1)}, s16[64,576]{1,0:T(8,128)(2,1)S(1)}, u32[]{:S(2)}, u32[]{:S(2)}) collective-permute-start(s16[64,576]{1,0:T(8,128)(2,1)S(1)} %get-tuple-element.38), channel_id=1, source_target_pairs={{0,16},{8,24},{16,0},{24,8},{1,17},{9,25},{17,1},{25,9},{2,18},{10... | collective-permute-start | bytes 221192 | tf_op jit(solution)/shard_map/ppermute | solution.py:21
  34.0 6.6 %collective-permute-start.12 = (s16[64,2176]{1,0:T(8,128)(2,1)S(1)}, s16[64,2176]{1,0:T(8,128)(2,1)S(1)}, u32[]{:S(2)}, u32[]{:S(2)}) collective-permute-start(s16[64,2176]{1,0:T(8,128)(2,1)S(1)} %get-tuple-element.41.coded_ref), channel_id=1, source_target_pairs={{0,8},{1,2},{2,1},{3,4},{4,3},{5,6},{6,5},{7,15},{8,0},{9,10},{10,... | collective-permute-start | bytes 835592 | tf_op jit(solution)/shard_map/ppermute | solution.py:41
  35.4 1.7 %collective-permute-start.11 = (s16[64,2144]{1,0:T(8,128)(2,1)S(1)}, s16[64,2144]{1,0:T(8,128)(2,1)S(1)}, u32[]{:S(2)}, u32[]{:S(2)}) collective-permute-start(s16[64,2144]{1,0:T(8,128)(2,1)S(1)} %get-tuple-element.42), channel_id=1, source_target_pairs={{0,1},{1,0},{2,3},{3,2},{4,5},{5,4},{6,7},{7,6},{8,9},{9,8},{10,11... | collective-permute-start | bytes 823304 | tf_op jit(solution)/shard_map/ppermute | solution.py:21
  37.4 7.1 %collective-permute-start.14 = (s16[64,2176]{1,0:T(8,128)(2,1)S(1)}, s16[64,2176]{1,0:T(8,128)(2,1)S(1)}, u32[]{:S(2)}, u32[]{:S(2)}) collective-permute-start(s16[64,2176]{1,0:T(8,128)(2,1)S(1)} %shard_map.71), channel_id=1, source_target_pairs={{0,1},{1,3},{2,0},{3,5},{4,2},{5,7},{6,4},{7,6},{8,9},{9,11},{10,8... | collective-permute-start | bytes 835592 | tf_op jit(solution)/shard_map/ppermute | solution.py:30
  40.9 5.2 %collective-permute-start.13 = (s16[64,2176]{1,0:T(8,128)(2,1)S(1)}, s16[64,2176]{1,0:T(8,128)(2,1)S(1)}, u32[]{:S(2)}, u32[]{:S(2)}) collective-permute-start(s16[64,2176]{1,0:T(8,128)(2,1)S(1)} %shard_map.70), channel_id=1, source_target_pairs={{0,2},{1,0},{2,4},{3,1},{4,6},{5,3},{6,7},{7,5},{8,10},{9,8},{10,1... | collective-permute-start | bytes 835592 | tf_op jit(solution)/shard_map/ppermute | solution.py:30
  42.3 17.6 %copy-start.3 = (f32[64]{0:T(128)S(1)}, f32[64]{0:T(128)}, u32[]{:S(2)}) copy-start(f32[64]{0:T(128)} %param.7) | copy-start | bytes 772
  46.8 7.7 %collective-permute-start.17 = (s16[64,640]{1,0:T(8,128)(2,1)S(1)}, s16[64,640]{1,0:T(8,128)(2,1)S(1)}, u32[]{:S(2)}, u32[]{:S(2)}) collective-permute-start(s16[64,640]{1,0:T(8,128)(2,1)S(1)} %get-tuple-element.43.z0), channel_id=1, source_target_pairs={{0,24},{8,16},{16,8},{24,0},{1,25},{9,17},{17,9},{25,1},{2,26},{10... | collective-permute-start | bytes 245768 | tf_op jit(solution)/shard_map/ppermute | solution.py:21
  48.8 5.8 %collective-permute-start.15 = (s16[64,608]{1,0:T(8,128)(2,1)S(1)}, s16[64,608]{1,0:T(8,128)(2,1)S(1)}, u32[]{:S(2)}, u32[]{:S(2)}) collective-permute-start(s16[64,608]{1,0:T(8,128)(2,1)S(1)} %get-tuple-element.44), channel_id=1, source_target_pairs={{0,8},{8,0},{16,24},{24,16},{1,9},{9,1},{17,25},{25,17},{2,10},{10... | collective-permute-start | bytes 233480 | tf_op jit(solution)/shard_map/ppermute | solution.py:21
  49.3 5.2 %collective-permute-start.16 = (s16[64,576]{1,0:T(8,128)(2,1)S(1)}, s16[64,576]{1,0:T(8,128)(2,1)S(1)}, u32[]{:S(2)}, u32[]{:S(2)}) collective-permute-start(s16[64,576]{1,0:T(8,128)(2,1)S(1)} %get-tuple-element.45), channel_id=1, source_target_pairs={{0,16},{8,24},{16,0},{24,8},{1,17},{9,25},{17,1},{25,9},{2,18},{10... | collective-permute-start | bytes 221192 | tf_op jit(solution)/shard_map/ppermute | solution.py:21
  54.8 1.2 %collective-permute-start.18 = (f32[8,128]{1,0:T(8,128)S(1)}, f32[8,128]{1,0:T(8,128)S(1)}, u32[]{:S(2)}, u32[]{:S(2)}) collective-permute-start(f32[8,128]{1,0:T(8,128)S(1)} %shard_map.73), channel_id=1, source_target_pairs={{0,1},{1,0},{2,3},{3,2},{4,5},{5,4},{6,7},{7,6},{8,9},{9,8},{10,11... | collective-permute-start | bytes 12296 | tf_op jit(solution)/shard_map/ppermute | solution.py:21
  56.0 6.9 %collective-permute-start.21 = (f32[8,128]{1,0:T(8,128)S(1)}, f32[8,128]{1,0:T(8,128)S(1)}, u32[]{:S(2)}, u32[]{:S(2)}) collective-permute-start(f32[8,128]{1,0:T(8,128)S(1)} %add.5.p0), channel_id=1, source_target_pairs={{0,7},{1,6},{2,5},{3,4},{4,3},{5,2},{6,1},{7,0},{8,15},{9,14},{10,... | collective-permute-start | bytes 12296 | tf_op jit(solution)/shard_map/ppermute | solution.py:21
  58.9 3.0 %collective-permute-start.19 = (f32[4,128]{1,0:T(4,128)S(1)}, f32[4,128]{1,0:T(4,128)S(1)}, u32[]{:S(2)}, u32[]{:S(2)}) collective-permute-start(f32[4,128]{1,0:T(4,128)S(1)} %slice.6), channel_id=1, source_target_pairs={{0,3},{1,2},{2,1},{3,0},{4,7},{5,6},{6,5},{7,4},{8,11},{9,10},{10,... | collective-permute-start | bytes 6152 | tf_op jit(solution)/shard_map/ppermute | solution.py:21
  59.0 3.9 %collective-permute-start.20 = (f32[6,128]{1,0:T(8,128)S(1)}, f32[6,128]{1,0:T(8,128)S(1)}, u32[]{:S(2)}, u32[]{:S(2)}) collective-permute-start(f32[6,128]{1,0:T(8,128)S(1)} %bitcast.9), channel_id=1, source_target_pairs={{0,5},{1,4},{2,7},{3,6},{4,1},{5,0},{6,3},{7,2},{8,13},{9,12},{10,... | collective-permute-start | bytes 9224 | tf_op jit(solution)/shard_map/ppermute | solution.py:21
